TPU v7x, 32 devices: a whole 2x2x4 slice. The times are simulated.
32 devices in a mesh: group: 2 (over x), expert: 16 (over z, y, core).
Axes of the slice: x: 2, y: 2, z: 4, core: 2. Of those that a mesh axis runs over, the one named last changes fastest.
Arguments:
- tokens: bfloat16 [4096, 3584], P(('group', 'expert')), parts along dimension 0, may hold values from -6 to 6
- norm_gain: float32 [3584], replicated, may hold values from 0.1 to 1.9
- final_gain: float32 [3584], replicated, may hold values from 0.1 to 1.9
- gate_weight: bfloat16 [3584, 8192], P(None, 'expert'), may hold values from -0.09375 to 0.09375
- up_weight: bfloat16 [3584, 8192], P(None, 'expert'), may hold values from -0.09375 to 0.09375
- down_weight: bfloat16 [8192, 3584], P('expert'), may hold values from -0.125 to 0.125
- picks: int32 [4096, 2], P(('group', 'expert')), parts along dimension 0, may hold values from 0 to 3, all different within a row; in each aligned block of 128 rows (0 to 127, 128 to 255, ...) at most 80 rows name the same one
- gates: float32 [4096, 2], P(('group', 'expert')), parts along dimension 0, may hold values from 0.2 to 1
- target_rows: bfloat16 [4096, 3584], P(('group', 'expert')), parts along dimension 0, may hold values from -0.09375 to 0.09375
- rest_lse: float32 [4096], P(('group', 'expert')), parts along dimension 0, may hold values from -2 to 4
- segment_ids: int32 [4096], P(('group', 'expert')), parts along dimension 0, may hold values from 0 to 15, never falling along the last dimension, each value on 1 to 256 neighbouring positions
- ref_logps: float32 [32], P('group'), parts along dimension 0, may hold values from -192 to 192
Outputs:
- sequence_logps: float32 [32], P('group'), parts along dimension 0
- pair_loss: float32 [16], P('group'), parts along dimension 0
There are 2 independent parts, one for each index of `group`. A program takes and returns all parts, laid end to end along the dimension named above; an argument that names none is the same for every part. Nothing has to cross between parts.
Inputs may be any that keep to these rules, and one draw needn't show every extreme that they name: Among the rows of one device no expert is picked more than 80 times, a bound that some block reaches; the picks of one token differ. `segment_ids`: never falling along the tokens; each sequence has 1 to 256 tokens and one has exactly that many; sequence 2p is the chosen and 2p + 1 the rejected answer of pair p.
All inputs are finite; a program needn't handle non-finite values.
Results may differ from a plain program's by a relative error of at most 0.0005.
Values may be sent and summed in bfloat16 or wider, within the bound.
No kernel may reach another device: no remote copies, remote signals or barrier semaphores. Data moves between devices by JAX's collectives and lax.ppermute only.
A program may use at most 128 MiB of HBM per device.

v0:
```python
import jax
import jax.numpy as jnp
from jax import lax
from jax.sharding import PartitionSpec as P

FFE = 2048
HID_DEV = 512
TOPK = 2


EPS = 1e-06
BETA = 0.01


def partner(value, axis, distance):
    mask = 2**distance
    pairs = [(source, source ^ mask) for source in range(lax.axis_size(axis))]
    return lax.ppermute(value, axis, pairs)


def rms_scale(rows, gain):
    values = rows.astype(jnp.float32)
    scale = lax.rsqrt(jnp.mean(values * values, axis=-1, keepdims=True) + EPS)
    return values * scale * gain


def per_device(
    tokens,
    norm_gain,
    final_gain,
    gate_weight,
    up_weight,
    down_weight,
    picks,
    gates,
    target_rows,
    rest_lse,
    segment_ids,
    ref_logps,
):
    width = tokens.shape[1]
    tok_rows = tokens.shape[0]
    spread = FFE // HID_DEV
    devices = lax.axis_size("expert")
    experts = devices // spread
    capacity = (tok_rows * TOPK * 5 // (experts * 4) + 3) // 4 * 4
    quarter = capacity // spread
    bits = spread.bit_length() - 1
    position = lax.axis_index("expert")
    normed = rms_scale(tokens, norm_gain).astype(jnp.bfloat16)
    flat_picks = picks.reshape(-1)
    onehot = (flat_picks[:, None] == jnp.arange(experts, dtype=jnp.int32)[None, :]).astype(
        jnp.int32
    )
    slot = jnp.sum((jnp.cumsum(onehot, axis=0) - onehot) * onehot, axis=1)
    row_ids = jnp.repeat(jnp.arange(tok_rows, dtype=jnp.int32), TOPK)
    buffer = (
        jnp.zeros((experts, capacity, width), jnp.bfloat16)
        .at[flat_picks, slot]
        .set(normed[row_ids])
    )
    outgoing = buffer.reshape(devices, quarter, width)
    gathered = lax.all_to_all(outgoing, "expert", split_axis=0, concat_axis=0, tiled=True)
    for bit in range(bits):
        theirs = partner(gathered, "expert", bit)
        upper = position >> bit & 1 == 1
        first = jnp.where(upper, theirs, gathered)
        second = jnp.where(upper, gathered, theirs)
        gathered = jnp.concatenate([first, second], axis=1)
    shape = gathered.shape
    flat = gathered.reshape(-1, width)
    gate = jnp.dot(flat, gate_weight, preferred_element_type=jnp.float32)
    up = jnp.dot(flat, up_weight, preferred_element_type=jnp.float32)
    hidden = (jax.nn.silu(gate) * up).astype(jnp.bfloat16)
    part = jnp.dot(hidden, down_weight, preferred_element_type=jnp.float32)
    partial_value = part.astype(jnp.bfloat16).reshape(shape)
    returned = lax.all_to_all(partial_value, "expert", split_axis=0, concat_axis=0, tiled=True)
    expert_out = jnp.sum(
        returned.reshape(experts, spread, capacity, width).astype(jnp.float32), axis=1
    )
    flat_out = expert_out.reshape(experts * capacity, width)
    picked = flat_out[flat_picks * capacity + slot].reshape(tok_rows, TOPK, width)
    moe = jnp.sum(gates[:, :, None] * picked, axis=1)
    stream = tokens.astype(jnp.float32) + moe
    final = rms_scale(stream, final_gain).astype(jnp.bfloat16)
    logit = jnp.sum(final.astype(jnp.float32) * target_rows.astype(jnp.float32), axis=1)
    token_logp = logit - jnp.logaddexp(logit, rest_lse)
    sequences = ref_logps.shape[0]
    member = (segment_ids[:, None] == jnp.arange(sequences, dtype=jnp.int32)[None, :]).astype(
        jnp.float32
    )
    local_sums = jnp.dot(token_logp, member, precision=lax.Precision.HIGHEST)
    sequence_logps = lax.psum(local_sums, "expert")
    margin = sequence_logps[0::2] - ref_logps[0::2] - (sequence_logps[1::2] - ref_logps[1::2])
    pair_loss = -jax.nn.log_sigmoid(BETA * margin)
    return (sequence_logps, pair_loss)


def solution(mesh):
    placed = (
        P(("group", "expert"), None),
        P(),
        P(),
        P(None, "expert"),
        P(None, "expert"),
        P("expert", None),
        P(("group", "expert"), None),
        P(("group", "expert"), None),
        P(("group", "expert"), None),
        P(("group", "expert")),
        P(("group", "expert")),
        P("group"),
    )
    return jax.shard_map(
        per_device, mesh=mesh, in_specs=placed, out_specs=(P("group"), P("group")), check_vma=False
    )
```

profile of v0, /device:TPU:0, one launch (start us, length us, event | category | flops | bytes accessed | tf_op | source)
XLA Modules:
  0.0 542.2 jit_solution(12626384341665064358)
XLA Ops:
  0.6 0.8 copy.24
  1.9 1.2 reduce-window.6
  3.5 1.4 fusion
  5.1 1.5 fusion.2
  6.6 3.0 gather_fusion
  9.8 45.1 %scatter_fusion = bf16[4,80,3584]{2,1,0:T(8,128)(2,1)S(1)} fusion(bf16[4,80,3584]{2,1,0:T(8,128)(2,1)S(1)} %broadcast_in_dim.4, s32[256]{0:T(256)S(1)} %bitcast.48, bf16[256,3584]{1,0:T(8,128)(2,1)} %gather_fusion), kind=kCustom, calls=%fused_computation.2 | custom fusion | bytes 5507072 | tf_op jit(solution)/shard_map/scatter | solution.py:60
  54.9 2.2 reshape.163
  57.2 70.6 %all_to_all.10 = bf16[16,20,3584]{2,1,0:T(8,128)(2,1)S(1)} all-to-all(bf16[16,20,3584]{2,1,0:T(8,128)(2,1)} %reshape.163), channel_id=1, replica_groups=mesh['group'=2,'expert'=16] {'expert'}, dimensions={0} | all-to-all | bytes 4587520 | tf_op jit(solution)/shard_map/all_to_all | solution.py:63
  127.7 2.1 copy.29
  130.1 4.5 collective-permute-done
  134.6 4.2 broadcast_select_fusion.3
  138.8 3.5 pad_maximum_fusion.1
  143.4 100.8 %collective-permute-done.1 = bf16[16,40,3584]{2,1,0:T(8,128)(2,1)} collective-permute-done((bf16[16,40,3584]{2,1,0:T(8,128)(2,1)}, bf16[16,40,3584]{2,1,0:T(8,128)(2,1)}, u32[]{:S(2)}, u32[]{:S(2)}) %collective-permute-start.1) | collective-permute-done | bytes 4587552 | tf_op jit(solution)/shard_map/ppermute | solution.py:18
  244.1 5.1 broadcast_select_fusion.1
  250.1 3.5 copy-done.3
  253.6 5.0 fusion.13
  258.6 16.5 %convolution_convert_fusion = bf16[1280,3584]{1,0:T(8,128)(2,1)} fusion(bf16[512,3584]{1,0:T(8,128)(2,1)} %param.17, f32[1280,512]{1,0:T(8,128)S(1)} %fusion.13, bf16[1280,3584]{1,0:T(8,128)(2,1)} %bitcast.51, bf16[3584,512]{1,0:T(8,128)(2,1)} %param.16), kind=kOutput, calls=%fused_computation.4 | convolution fusion | flops 9403760640 | bytes 28311552 | tf_op jit(solution)/shard_map/dot_general | solution.py:75
  275.2 5.1 all-to-all-start.1
  280.5 163.9 %all-to-all-done.1 = bf16[16,80,3584]{2,1,0:T(8,128)(2,1)} async-done(((bf16[16,80,3584]{2,1,0:T(8,128)(2,1)}), bf16[16,80,3584]{2,1,0:T(8,128)(2,1)}, u32[]{:S(2)}, u32[]{:S(2)}) %all-to-all-start.1) | async-done | bytes 9175072 | tf_op jit(solution)/shard_map/all_to_all | solution.py:77
  444.4 7.7 %convert_reduce_fusion = f32[4,80,3584]{2,1,0:T(8,128)} fusion(bf16[16,80,3584]{2,1,0:T(8,128)(2,1)} %all-to-all-done.1), kind=kLoop, calls=%fused_computation.3 | loop fusion | flops 8028160 | bytes 13762560 | tf_op jit(solution)/shard_map/reduce_sum | solution.py:78
  452.1 7.5 %gather_fusion.1 = f32[256,3584]{1,0:T(8,128)} fusion(f32[320,3584]{1,0:T(8,128)} %bitcast.47, s32[1024]{0:T(1024)S(1)} %pad_clamp_fusion), kind=kCustom, calls=%fused_computation.1 | custom fusion | bytes 7341056 | tf_op jit(solution)/shard_map/gather | solution.py:82
  459.5 5.6 %reshape.167 = f32[128,2,3584]{2,1,0:T(2,128)} reshape(f32[256,3584]{1,0:T(8,128)} %gather_fusion.1) | data formatting | bytes 7340032 | tf_op jit(solution)/shard_map/reshape | solution.py:82
  465.1 7.5 %multiply_reduce_fusion = f32[128,3584]{1,0:T(8,128)S(1)} fusion(f32[128,2,3584]{2,1,0:T(2,128)} %reshape.167, f32[128,2]{1,0:T(8,128)S(1)} %copy.23), kind=kLoop, calls=%fused_computation.9 | loop fusion | flops 1376256 | bytes 5506048 | tf_op jit(solution)/shard_map/reduce_sum | solution.py:83
  473.8 67.6 %psum.7 = f32[16]{0:T(128)S(1)} all-reduce(f32[16]{0:T(128)S(1)} %convolution_bitcast_fusion), channel_id=1, replica_groups=mesh['group'=2,'expert'=16] {'expert'}, use_global_device_ids=true, to_apply=%region_9.10 | all-reduce | flops 16 | bytes 128 | tf_op jit(solution)/shard_map/psum | solution.py:93
  (55 shorter events, 5.5 us)
Async XLA Ops:
  129.8 4.8 collective-permute-start
  138.8 3.5 copy-start
  138.8 3.8 copy-start.1
  142.6 101.5 %collective-permute-start.1 = (bf16[16,40,3584]{2,1,0:T(8,128)(2,1)}, bf16[16,40,3584]{2,1,0:T(8,128)(2,1)}, u32[]{:S(2)}, u32[]{:S(2)}) collective-permute-start(bf16[16,40,3584]{2,1,0:T(8,128)(2,1)} %pad_maximum_fusion.1), channel_id=1, source_target_pairs={{0,2},{1,3},{2,0},{3,1},{4,6},{5,7},{6,4},{7,5},{8,10},{9,11},{10,... | collective-permute-start | bytes 13762568 | tf_op jit(solution)/shard_map/ppermute | solution.py:18
  249.3 4.3 copy-start.7
  250.1 3.5 copy-start.3
  275.2 5.1 copy-start.6
  275.2 5.3 copy-start.10
  275.2 169.2 %all-to-all-start.1 = ((bf16[16,80,3584]{2,1,0:T(8,128)(2,1)}), bf16[16,80,3584]{2,1,0:T(8,128)(2,1)}, u32[]{:S(2)}, u32[]{:S(2)}) async-start(bf16[16,80,3584]{2,1,0:T(8,128)(2,1)} %bitcast.49), calls=%async_computation.1 | async-start | bytes 18350080 | tf_op jit(solution)/shard_map/all_to_all | solution.py:77
  465.1 7.5 %copy-start.2 = (bf16[128,3584]{1,0:T(8,128)(2,1)S(1)}, bf16[128,3584]{1,0:T(8,128)(2,1)}, u32[]{:S(2)}) copy-start(bf16[128,3584]{1,0:T(8,128)(2,1)} %param.12) | copy-start | bytes 2752516
  465.1 7.8 %copy-start.4 = (bf16[128,3584]{1,0:T(8,128)(2,1)S(1)}, bf16[128,3584]{1,0:T(8,128)(2,1)}, u32[]{:S(2)}) copy-start(bf16[128,3584]{1,0:T(8,128)(2,1)} %param.20) | copy-start | bytes 2752516
  465.1 7.9 %copy-start.5 = (f32[3584]{0:T(1024)S(1)}, f32[3584]{0:T(1024)}, u32[]{:S(2)}) copy-start(f32[3584]{0:T(1024)} %param.14) | copy-start | bytes 43012
  472.6 0.9 copy-start.8
  472.6 0.9 copy-start.9
  541.5 0.7 copy-start.11
where the time goes:
time: 543 us; the launch traced here: 542 us
  waiting for transfers between devices  269 us (50%)
  blocking collectives  138 us (25%)
  local copies, waits for them, and re-layouts  71.6 us (13%)
  other arithmetic  34.4 us (6%)
  matrix products  21.8 us (4%)
  starting transfers between devices  6.18 us (1%)
    all_to_all x1, waiting for transfers between devices, per_device(): lax.all_to_all(partial_value, 'expert', split_axis=0, concat_axis=0, tile...  164 us
    ppermute x2, waiting for transfers between devices, partner(): return lax.ppermute(value, axis, pairs)  105 us
    all_to_all x1, blocking collectives, per_device(): lax.all_to_all(outgoing, 'expert', split_axis=0, concat_axis=0, tiled=True)  70.6 us
    psum x1, blocking collectives, per_device(): sequence_logps = lax.psum(local_sums, 'expert')  67.6 us
    scatter x1, local copies, waits for them, and re-layouts, per_device(): buffer = jnp.zeros((experts, capacity, width), jnp.bfloat16).at[flat_pick...  45.1 us
    dot_general x1, matrix products, per_device(): part = jnp.dot(hidden, down_weight, preferred_element_type=jnp.float32)  16.5 us
  transfers between devices with their start and end apart: 3, of which 3 were waited for; matrix products, arithmetic and copies ran while one was open for 0% of the time, Pallas kernels for 0%

commit v1 on v0

v1 whole, which is shorter than its diff:
```python
import functools

import jax
import jax.numpy as jnp
from jax import lax
from jax.experimental import pallas as pl
from jax.experimental.pallas import tpu as pltpu
from jax.sharding import PartitionSpec as P

FFE = 2048
HID_DEV = 512
TOPK = 2

EPS = 1e-06
BETA = 0.01

F32 = jnp.float32
BF16 = jnp.bfloat16
VMEM_LIMIT = 56 * 1024 * 1024


def swap(value, mask):
    pairs = [(source, source ^ mask) for source in range(lax.axis_size("expert"))]
    return lax.ppermute(value, "expert", pairs)


def iota(shape, dim):
    return lax.broadcasted_iota(jnp.int32, shape, dim)


def routing(own, picks, rows):
    tokens = picks.shape[1]
    expert = jnp.bitwise_xor(own, iota((rows, tokens), 0))
    hit = [picks[k : k + 1, :] == expert for k in range(TOPK)]
    member = hit[0] | hit[1]
    earlier = (iota((tokens, tokens), 0) < iota((tokens, tokens), 1)).astype(BF16)
    slot = jnp.dot(member.astype(F32).astype(BF16), earlier, preferred_element_type=F32)
    slot = jnp.where(member, slot.astype(jnp.int32), -1)
    return hit, slot


def pack_kernel(own_ref, tokens_ref, gain_ref, picks_ref, *out_refs):
    capacity = out_refs[0].shape[0]
    tokens = tokens_ref.shape[0]
    values = tokens_ref[...].astype(F32)
    scale = lax.rsqrt(jnp.mean(values * values, axis=-1, keepdims=True) + EPS)
    normed = (values * scale * gain_ref[...]).astype(BF16)
    _, slot = routing(own_ref[0], picks_ref[...], max(8, len(out_refs)))
    place = iota((capacity, tokens), 0)
    for k, out_ref in enumerate(out_refs):
        chosen = (slot[k : k + 1, :] == place).astype(F32).astype(BF16)
        out_ref[...] = jnp.dot(chosen, normed, preferred_element_type=F32).astype(BF16)


def pack(own, tokens, gain, picks, experts, capacity):
    rows, width = tokens.shape
    smem = pl.BlockSpec(memory_space=pltpu.SMEM)
    vmem = pl.BlockSpec(memory_space=pltpu.VMEM)
    return pl.pallas_call(
        pack_kernel,
        out_shape=[jax.ShapeDtypeStruct((capacity, width), BF16)] * experts,
        in_specs=[smem, vmem, vmem, vmem],
        out_specs=[vmem] * experts,
        compiler_params=pltpu.CompilerParams(vmem_limit_bytes=VMEM_LIMIT),
        cost_estimate=pl.CostEstimate(
            flops=2 * experts * capacity * rows * width,
            bytes_accessed=2 * width * (rows + experts * capacity),
            transcendentals=rows,
        ),
        name="pack",
    )(own, tokens, gain, picks)


def expert_kernel(a_ref, b_ref, c_ref, d_ref, gate_ref, up_ref, down_ref, own_ref, other_ref, rows, total):
    step = pl.program_id(0)
    capacity = a_ref.shape[0]

    @pl.when(step == 0)
    def _():
        for n, ref in enumerate((a_ref, b_ref, c_ref, d_ref)):
            rows[n * capacity : (n + 1) * capacity, :] = ref[...]

    gate = jnp.dot(rows[...], gate_ref[...], preferred_element_type=F32)
    up = jnp.dot(rows[...], up_ref[...], preferred_element_type=F32)
    hidden = (jax.nn.silu(gate) * up).astype(BF16)
    part = jnp.dot(hidden, down_ref[...], preferred_element_type=F32)

    @pl.when(step == 0)
    def _():
        total[...] = part

    @pl.when(step == 1)
    def _():
        whole = (total[...] + part).astype(BF16)
        own_ref[...] = whole[: 2 * capacity]
        other_ref[...] = whole[2 * capacity :]


def expert_block(blocks, gate_weight, up_weight, down_weight):
    capacity, width = blocks[0].shape
    hidden = gate_weight.shape[1]
    half = hidden // 2
    row_spec = pl.BlockSpec((capacity, width), lambda h: (0, 0))
    out_spec = pl.BlockSpec((2 * capacity, width), lambda h: (0, 0))
    return pl.pallas_call(
        expert_kernel,
        out_shape=[jax.ShapeDtypeStruct((2 * capacity, width), BF16)] * 2,
        grid=(2,),
        in_specs=[row_spec] * 4
        + [pl.BlockSpec((width, half), lambda h: (0, h))] * 2
        + [pl.BlockSpec((half, width), lambda h: (h, 0))],
        out_specs=[out_spec] * 2,
        scratch_shapes=[
            pltpu.VMEM((4 * capacity, width), BF16),
            pltpu.VMEM((4 * capacity, width), F32),
        ],
        compiler_params=pltpu.CompilerParams(vmem_limit_bytes=VMEM_LIMIT),
        cost_estimate=pl.CostEstimate(
            flops=2 * 3 * 4 * capacity * width * hidden,
            bytes_accessed=2 * width * (3 * hidden + 8 * capacity),
            transcendentals=4 * capacity * hidden,
        ),
        name="expert_block",
    )(*blocks, gate_weight, up_weight, down_weight)


def score_kernel(own_ref, tokens_ref, gain_ref, picks_ref, gates_ref, target_ref, rest_ref, seg_ref, *refs):
    *block_refs, out_ref, stacked, stream = refs
    capacity = block_refs[0].shape[0]
    tokens, width = tokens_ref.shape
    experts = len(block_refs)
    for k, ref in enumerate(block_refs):
        stacked[k * capacity : (k + 1) * capacity, :] = ref[...]
    hit, slot = routing(own_ref[0], picks_ref[...], max(8, experts))
    weight = sum(jnp.where(hit[k], gates_ref[k : k + 1, :], 0.0) for k in range(TOPK))
    place = iota((capacity, tokens), 0)
    parts = [
        jnp.where(slot[k : k + 1, :] == place, weight[k : k + 1, :], 0.0) for k in range(experts)
    ]
    spread = jnp.concatenate(parts, axis=0)
    coarse = spread.astype(BF16)
    fine = (spread - coarse.astype(F32)).astype(BF16)
    chunk = width // 7 if width % 7 == 0 else width
    over_rows = (((0,), (0,)), ((), ()))
    squares = jnp.zeros((tokens, 1), F32)
    for start in range(0, width, chunk):
        cols = slice(start, start + chunk)
        rows = stacked[:, cols]
        moe = lax.dot_general(coarse, rows, over_rows, preferred_element_type=F32)
        moe = moe + lax.dot_general(fine, rows, over_rows, preferred_element_type=F32)
        value = tokens_ref[:, cols].astype(F32) + moe
        stream[:, cols] = value
        squares = squares + jnp.sum(value * value, axis=-1, keepdims=True)
    scale = lax.rsqrt(squares / width + EPS)
    logit = jnp.zeros((tokens, 1), F32)
    for start in range(0, width, chunk):
        cols = slice(start, start + chunk)
        final = (stream[:, cols] * scale * gain_ref[:, cols]).astype(BF16).astype(F32)
        logit = logit + jnp.sum(final * target_ref[:, cols].astype(F32), axis=-1, keepdims=True)
    turn = iota((tokens, tokens), 0) == iota((tokens, tokens), 1)
    logit = jnp.sum(jnp.where(turn, logit, 0.0), axis=0, keepdims=True)
    gap = rest_ref[...] - logit
    token_logp = -(jnp.maximum(gap, 0.0) + jnp.log1p(jnp.exp(-jnp.abs(gap))))
    sequences = out_ref.shape[1]
    inside = iota((sequences, tokens), 0) == seg_ref[...]
    sums = jnp.sum(jnp.where(inside, token_logp, 0.0), axis=1, keepdims=True)
    turn = iota((sequences, sequences), 0) == iota((sequences, sequences), 1)
    out_ref[...] = jnp.sum(jnp.where(turn, sums, 0.0), axis=0, keepdims=True)


def score(own, tokens, gain, picks, gates, target, rest, seg, blocks, sequences):
    rows, width = tokens.shape
    capacity = blocks[0].shape[0]
    experts = len(blocks)
    smem = pl.BlockSpec(memory_space=pltpu.SMEM)
    vmem = pl.BlockSpec(memory_space=pltpu.VMEM)
    return pl.pallas_call(
        score_kernel,
        out_shape=jax.ShapeDtypeStruct((1, sequences), F32),
        in_specs=[smem] + [vmem] * (7 + experts),
        out_specs=vmem,
        scratch_shapes=[
            pltpu.VMEM((experts * capacity, width), BF16),
            pltpu.VMEM((rows, width), F32),
        ],
        compiler_params=pltpu.CompilerParams(vmem_limit_bytes=VMEM_LIMIT),
        cost_estimate=pl.CostEstimate(
            flops=4 * experts * capacity * rows * width,
            bytes_accessed=2 * width * (2 * rows + experts * capacity),
            transcendentals=rows,
        ),
        name="score",
    )(own, tokens, gain, picks, gates, target, rest, seg, *blocks)


def add(first, second):
    return (first.astype(F32) + second.astype(F32)).astype(BF16)


def per_device(
    tokens,
    norm_gain,
    final_gain,
    gate_weight,
    up_weight,
    down_weight,
    picks,
    gates,
    target_rows,
    rest_lse,
    segment_ids,
    ref_logps,
):
    tok_rows = tokens.shape[0]
    spread = FFE // HID_DEV
    devices = lax.axis_size("expert")
    experts = devices // spread
    capacity = (tok_rows * TOPK * 5 // (experts * 4) + 3) // 4 * 4
    capacity = (capacity + 15) // 16 * 16
    own = (lax.axis_index("expert") // spread).astype(jnp.int32).reshape(1)
    picks_t = picks.T
    core, side = 1, 2

    sent = pack(own, tokens, norm_gain[None, :], picks_t, experts, capacity)
    near = [sent[0]] + [swap(sent[k], k * spread) for k in range(1, experts)]
    back = []
    for k in range(experts):
        far = swap(near[k], side)
        blocks = [near[k], far, swap(near[k], core), swap(far, core)]
        own_part, other_part = expert_block(blocks, gate_weight, up_weight, down_weight)
        both = add(own_part, swap(other_part, core))
        total = add(both[:capacity], swap(both[capacity:], side))
        back.append(total if k == 0 else swap(total, k * spread))
    local = score(
        own,
        tokens,
        final_gain[None, :],
        picks_t,
        gates.T,
        target_rows,
        rest_lse[None, :],
        segment_ids[None, :],
        back,
        ref_logps.shape[0],
    )
    mask = 1
    while mask < devices:
        local = local + swap(local, mask)
        mask *= 2
    sequence_logps = local[0]
    margin = sequence_logps[0::2] - ref_logps[0::2] - (sequence_logps[1::2] - ref_logps[1::2])
    pair_loss = -jax.nn.log_sigmoid(BETA * margin)
    return (sequence_logps, pair_loss)


def solution(mesh):
    placed = (
        P(("group", "expert"), None),
        P(),
        P(),
        P(None, "expert"),
        P(None, "expert"),
        P("expert", None),
        P(("group", "expert"), None),
        P(("group", "expert"), None),
        P(("group", "expert"), None),
        P(("group", "expert")),
        P(("group", "expert")),
        P("group"),
    )
    return jax.shard_map(
        per_device, mesh=mesh, in_specs=placed, out_specs=(P("group"), P("group")), check_vma=False
    )
```

time: 543 us -> 222 us (0.41)
  blocking collectives: 138 us -> 0 us
  waiting for transfers between devices: 269 us -> 136 us
  local copies, waits for them, and re-layouts: 71.6 us -> 7.07 us
  Pallas kernels: 0 us -> 47.8 us
  other arithmetic: 34.4 us -> 3.63 us
  matrix products: 21.8 us -> 0 us
  starting transfers between devices: 6.18 us -> 25.7 us
    all_to_all x1 -> x0, waiting for transfers between devices: 164 us -> none  [per_device(): lax.all_to_all(partial_value, 'expert', split_axis=0, concat_axis=0, tile...]
    all_to_all x1 -> x0, blocking collectives: 70.6 us -> none  [per_device(): lax.all_to_all(outgoing, 'expert', split_axis=0, concat_axis=0, tiled=True)]
    psum x1 -> x0, blocking collectives: 67.6 us -> none  [per_device(): sequence_logps = lax.psum(local_sums, 'expert')]
    pallas_call x0 -> x6, Pallas kernels: none -> 47.8 us  [the longest x4 40 us: expert_block(): pl.pallas_call(expert_kernel, out_shape=[jax.ShapeDtypeStruct((2 * capaci...]
    scatter x1 -> x0, local copies, waits for them, and re-layouts: 45.1 us -> none  [per_device(): buffer = jnp.zeros((experts, capacity, width), jnp.bfloat16).at[flat_pick...]
    ppermute x2 -> x30, waiting for transfers between devices: 105 us -> 136 us  [swap(): return lax.ppermute(value, 'expert', pairs)]
    ppermute x2 -> x30, starting transfers between devices: 1.05 us -> 25.7 us  [swap(): return lax.ppermute(value, 'expert', pairs)]
    dot_general x3 -> x0, matrix products: 21.8 us -> none  [the longest x1 16.5 us: per_device(): part = jnp.dot(hidden, down_weight, preferred_element_type=jnp.float32)]
  transfers between devices with their start and end apart: 3 -> 30, of which waited for: 3 -> 12; matrix products, arithmetic and copies ran while one was open for 0% -> 2% of each run, Pallas kernels for 0% -> 18%
where the time goes in v1:
time: 222 us; the launch traced here: 221 us
  waiting for transfers between devices  136 us (61%)
  Pallas kernels  47.8 us (22%)
  starting transfers between devices  25.7 us (12%)
  local copies, waits for them, and re-layouts  7.07 us (3%)
  other arithmetic  3.63 us (2%)
    ppermute x30, waiting for transfers between devices, swap(): return lax.ppermute(value, 'expert', pairs)  136 us
    pallas_call x4, Pallas kernels, expert_block(): pl.pallas_call(expert_kernel, out_shape=[jax.ShapeDtypeStruct((2 * capaci...  40 us
    ppermute x30, starting transfers between devices, swap(): return lax.ppermute(value, 'expert', pairs)  25.7 us
    pallas_call x1, Pallas kernels, score(): pl.pallas_call(score_kernel, out_shape=jax.ShapeDtypeStruct((1, sequences...  4.64 us
    unnamed x50, local copies, waits for them, and re-layouts  4.6 us
  transfers between devices with their start and end apart: 30, of which 12 were waited for; matrix products, arithmetic and copies ran while one was open for 2% of the time, Pallas kernels for 18%

profile of v1, /device:TPU:0, one launch (start us, length us, event | category | flops | bytes accessed | tf_op | source)
XLA Modules:
  0.0 221.3 jit_solution(6843743541947961320)
XLA Ops:
  0.6 1.3 broadcast_in_dim.15.gain_ref
  2.0 3.2 %pack.1 = (bf16[80,3584]{1,0:T(8,128)(2,1)}, bf16[80,3584]{1,0:T(8,128)(2,1)}, bf16[80,3584]{1,0:T(8,128)(2,1)}, bf16[80,3584]{1,0:T(8,128)(2,1)}) custom-call(s32[1]{0:T(128)} %bitcast.own_ref, bf16[128,3584]{1,0:T(8,128)(2,1)} %tokens_ref.3, f32[1,3584]{1,0:T(1,128)} %broadcast_in_dim.15.gain_ref, s32[2,128]{1,0:T(2,128)} %bitcast.7), custom_call_target="tpu_custom_call" | custom-call | flops 293601280 | bytes 3211264 | tf_op jit(solution)/shard_map/pack/pallas_call | solution.py:59
  5.2 5.1 %collective-permute-start.19 = (bf16[80,3584]{1,0:T(8,128)(2,1)}, bf16[80,3584]{1,0:T(8,128)(2,1)S(1)}, u32[]{:S(2)}, u32[]{:S(2)}) collective-permute-start(bf16[80,3584]{1,0:T(8,128)(2,1)} %get-tuple-element.23), channel_id=1, source_target_pairs={{0,12},{1,13},{2,14},{3,15},{4,8},{5,9},{6,10},{7,11},{8,4},{9,5},... | collective-permute-start | bytes 1720328 | tf_op jit(solution)/shard_map/ppermute | solution.py:24
  10.2 1.5 collective-permute-start
  12.5 11.8 %collective-permute-done.19.a_ref = bf16[80,3584]{1,0:T(8,128)(2,1)S(1)} collective-permute-done((bf16[80,3584]{1,0:T(8,128)(2,1)}, bf16[80,3584]{1,0:T(8,128)(2,1)S(1)}, u32[]{:S(2)}, u32[]{:S(2)}) %collective-permute-start.19) | collective-permute-done | bytes 573472 | tf_op jit(solution)/shard_map/ppermute | solution.py:24
  24.4 1.7 collective-permute-start.20
  26.1 33.3 %collective-permute-done.12.a_ref = bf16[80,3584]{1,0:T(8,128)(2,1)S(1)} collective-permute-done((bf16[80,3584]{1,0:T(8,128)(2,1)}, bf16[80,3584]{1,0:T(8,128)(2,1)S(1)}, u32[]{:S(2)}, u32[]{:S(2)}) %collective-permute-start.12) | collective-permute-done | bytes 573472 | tf_op jit(solution)/shard_map/ppermute | solution.py:24
  59.4 1.5 collective-permute-start.13
  62.0 13.3 %collective-permute-done.13.b_ref = bf16[80,3584]{1,0:T(8,128)(2,1)S(1)} collective-permute-done((bf16[80,3584]{1,0:T(8,128)(2,1)S(1)}, bf16[80,3584]{1,0:T(8,128)(2,1)S(1)}, u32[]{:S(2)}, u32[]{:S(2)}) %collective-permute-start.13) | collective-permute-done | bytes 573472 | tf_op jit(solution)/shard_map/ppermute | solution.py:24
  76.2 10.0 %expert_block.4 = (bf16[160,3584]{1,0:T(8,128)(2,1)}, bf16[160,3584]{1,0:T(8,128)(2,1)}) custom-call(bf16[80,3584]{1,0:T(8,128)(2,1)} %get-tuple-element.14.a_ref, bf16[80,3584]{1,0:T(8,128)(2,1)} %copy-done.10, bf16[80,3584]{1,0:T(8,128)(2,1)} %copy-done.11, bf16[80,3584]{1,0:T(8,128)(2,1)} %copy-done.18, bf16[3584,512]{1,0:T(8,128)(2,1)} %gate_ref.7, ...), custom_call_target="tpu_custom_call" | custom-call | flops 3523215360 | bytes 15597568 | tf_op jit(solution)/shard_map/expert_block/pallas_call | solution.py:105
  88.4 10.0 %expert_block.7 = (bf16[160,3584]{1,0:T(8,128)(2,1)}, bf16[160,3584]{1,0:T(8,128)(2,1)}) custom-call(bf16[80,3584]{1,0:T(8,128)(2,1)} %copy-done.6, bf16[80,3584]{1,0:T(8,128)(2,1)} %copy-done.9, bf16[80,3584]{1,0:T(8,128)(2,1)} %copy-done.12, bf16[80,3584]{1,0:T(8,128)(2,1)} %copy-done.15, bf16[3584,512]{1,0:T(8,128)(2,1)} %gate_ref.7, ...), custom_call_target="tpu_custom_call" | custom-call | flops 3523215360 | bytes 15597568 | tf_op jit(solution)/shard_map/expert_block/pallas_call | solution.py:105
  100.1 10.0 %expert_block.6 = (bf16[160,3584]{1,0:T(8,128)(2,1)}, bf16[160,3584]{1,0:T(8,128)(2,1)}) custom-call(bf16[80,3584]{1,0:T(8,128)(2,1)} %copy-done.5, bf16[80,3584]{1,0:T(8,128)(2,1)} %copy-done.7, bf16[80,3584]{1,0:T(8,128)(2,1)} %copy-done.13, bf16[80,3584]{1,0:T(8,128)(2,1)} %copy-done.14, bf16[3584,512]{1,0:T(8,128)(2,1)} %gate_ref.7, ...), custom_call_target="tpu_custom_call" | custom-call | flops 3523215360 | bytes 15597568 | tf_op jit(solution)/shard_map/expert_block/pallas_call | solution.py:105
  112.1 10.0 %expert_block.5 = (bf16[160,3584]{1,0:T(8,128)(2,1)}, bf16[160,3584]{1,0:T(8,128)(2,1)}) custom-call(bf16[80,3584]{1,0:T(8,128)(2,1)} %copy-done.4, bf16[80,3584]{1,0:T(8,128)(2,1)} %copy-done.8, bf16[80,3584]{1,0:T(8,128)(2,1)} %copy-done.16, bf16[80,3584]{1,0:T(8,128)(2,1)} %copy-done.19, bf16[3584,512]{1,0:T(8,128)(2,1)} %gate_ref.7, ...), custom_call_target="tpu_custom_call" | custom-call | flops 3523215360 | bytes 15597568 | tf_op jit(solution)/shard_map/expert_block/pallas_call | solution.py:105
  122.6 1.6 collective-permute-start.4
  128.8 22.0 %collective-permute-done.24 = bf16[80,3584]{1,0:T(8,128)(2,1)S(1)} collective-permute-done((bf16[80,3584]{1,0:T(8,128)(2,1)S(1)}, bf16[80,3584]{1,0:T(8,128)(2,1)S(1)}, u32[]{:S(2)}, u32[]{:S(2)}) %collective-permute-start.24) | collective-permute-done | bytes 573472 | tf_op jit(solution)/shard_map/ppermute | solution.py:24
  150.9 2.5 %collective-permute-start.25 = (bf16[80,3584]{1,0:T(8,128)(2,1)S(1)}, bf16[80,3584]{1,0:T(8,128)(2,1)S(1)}, u32[]{:S(2)}, u32[]{:S(2)}) collective-permute-start(bf16[80,3584]{1,0:T(8,128)(2,1)S(1)} %add_convert_fusion.4), channel_id=1, source_target_pairs={{0,12},{1,13},{2,14},{3,15},{4,8},{5,9},{6,10},{7,11},{8,4},{9,5},... | collective-permute-start | bytes 1720328 | tf_op jit(solution)/shard_map/ppermute | solution.py:24
  153.4 9.6 %collective-permute-done.17 = bf16[80,3584]{1,0:T(8,128)(2,1)S(1)} collective-permute-done((bf16[80,3584]{1,0:T(8,128)(2,1)S(1)}, bf16[80,3584]{1,0:T(8,128)(2,1)S(1)}, u32[]{:S(2)}, u32[]{:S(2)}) %collective-permute-start.17) | collective-permute-done | bytes 573472 | tf_op jit(solution)/shard_map/ppermute | solution.py:24
  164.4 10.3 %collective-permute-done.10 = bf16[80,3584]{1,0:T(8,128)(2,1)S(1)} collective-permute-done((bf16[80,3584]{1,0:T(8,128)(2,1)S(1)}, bf16[80,3584]{1,0:T(8,128)(2,1)S(1)}, u32[]{:S(2)}, u32[]{:S(2)}) %collective-permute-start.10) | collective-permute-done | bytes 573472 | tf_op jit(solution)/shard_map/ppermute | solution.py:24
  175.9 25.3 %collective-permute-done.18.refs_2_ = bf16[80,3584]{1,0:T(8,128)(2,1)S(1)} collective-permute-done((bf16[80,3584]{1,0:T(8,128)(2,1)S(1)}, bf16[80,3584]{1,0:T(8,128)(2,1)S(1)}, u32[]{:S(2)}, u32[]{:S(2)}) %collective-permute-start.18) | collective-permute-done | bytes 573472 | tf_op jit(solution)/shard_map/ppermute | solution.py:24
  202.5 4.6 %score.1 = f32[1,16]{1,0:T(1,128)} custom-call(s32[1]{0:T(128)} %bitcast.own_ref, bf16[128,3584]{1,0:T(8,128)(2,1)} %tokens_ref.3, f32[1,3584]{1,0:T(1,128)} %broadcast_in_dim.12.gain_ref, s32[2,128]{1,0:T(2,128)} %bitcast.8, f32[2,128]{1,0:T(2,128)} %bitcast.9, bf16[128,3584]{1,0:T(8,128)(2,1)} %target_ref.1, f32[1,128]{1,0:T(1,128)} %bitcast.10, ...), custom_call_target="tpu_custom_call" | custom-call | flops 587202560 | bytes 4128768 | tf_op jit(solution)/shard_map/score/pallas_call | solution.py:177
  209.0 1.5 collective-permute-start.27
  210.6 2.0 collective-permute-done.27
  212.7 3.4 %collective-permute-done.28 = f32[1,16]{1,0:T(1,128)S(1)} collective-permute-done((f32[1,16]{1,0:T(1,128)S(1)}, f32[1,16]{1,0:T(1,128)S(1)}, u32[]{:S(2)}, u32[]{:S(2)}) %collective-permute-start.28) | collective-permute-done | bytes 96 | tf_op jit(solution)/shard_map/ppermute | solution.py:24
  217.2 3.3 %collective-permute-done.29 = f32[1,16]{1,0:T(1,128)S(1)} collective-permute-done((f32[1,16]{1,0:T(1,128)S(1)}, f32[1,16]{1,0:T(1,128)S(1)}, u32[]{:S(2)}, u32[]{:S(2)}) %collective-permute-start.29) | collective-permute-done | bytes 96 | tf_op jit(solution)/shard_map/ppermute | solution.py:24
  (115 shorter events, 21.3 us)
Async XLA Ops:
  5.2 19.2 %collective-permute-start.19 = (bf16[80,3584]{1,0:T(8,128)(2,1)}, bf16[80,3584]{1,0:T(8,128)(2,1)S(1)}, u32[]{:S(2)}, u32[]{:S(2)}) collective-permute-start(bf16[80,3584]{1,0:T(8,128)(2,1)} %get-tuple-element.23), channel_id=1, source_target_pairs={{0,12},{1,13},{2,14},{3,15},{4,8},{5,9},{6,10},{7,11},{8,4},{9,5},... | collective-permute-start | bytes 1720328 | tf_op jit(solution)/shard_map/ppermute | solution.py:24
  10.2 49.2 %collective-permute-start.12 = (bf16[80,3584]{1,0:T(8,128)(2,1)}, bf16[80,3584]{1,0:T(8,128)(2,1)S(1)}, u32[]{:S(2)}, u32[]{:S(2)}) collective-permute-start(bf16[80,3584]{1,0:T(8,128)(2,1)} %get-tuple-element.20), channel_id=1, source_target_pairs={{0,8},{1,9},{2,10},{3,11},{4,12},{5,13},{6,14},{7,15},{8,0},{9,1},... | collective-permute-start | bytes 1720328 | tf_op jit(solution)/shard_map/ppermute | solution.py:24
  10.2 50.7 %collective-permute-start = (bf16[80,3584]{1,0:T(8,128)(2,1)}, bf16[80,3584]{1,0:T(8,128)(2,1)S(1)}, u32[]{:S(2)}, u32[]{:S(2)}) collective-permute-start(bf16[80,3584]{1,0:T(8,128)(2,1)} %get-tuple-element.14.a_ref), channel_id=1, source_target_pairs={{0,2},{1,3},{2,0},{3,1},{4,6},{5,7},{6,4},{7,5},{8,10},{9,11},{10,... | collective-permute-start | bytes 1720328 | tf_op jit(solution)/shard_map/ppermute | solution.py:24
  11.8 49.2 %collective-permute-start.5 = (bf16[80,3584]{1,0:T(8,128)(2,1)}, bf16[80,3584]{1,0:T(8,128)(2,1)S(1)}, u32[]{:S(2)}, u32[]{:S(2)}) collective-permute-start(bf16[80,3584]{1,0:T(8,128)(2,1)} %get-tuple-element.17), channel_id=1, source_target_pairs={{0,4},{1,5},{2,6},{3,7},{4,0},{5,1},{6,2},{7,3},{8,12},{9,13},{10,... | collective-permute-start | bytes 1720328 | tf_op jit(solution)/shard_map/ppermute | solution.py:24
  12.5 49.0 %collective-permute-start.1 = (bf16[80,3584]{1,0:T(8,128)(2,1)}, bf16[80,3584]{1,0:T(8,128)(2,1)S(1)}, u32[]{:S(2)}, u32[]{:S(2)}) collective-permute-start(bf16[80,3584]{1,0:T(8,128)(2,1)} %get-tuple-element.14.a_ref), channel_id=1, source_target_pairs={{0,1},{1,0},{2,3},{3,2},{4,5},{5,4},{6,7},{7,6},{8,9},{9,8},{10,11... | collective-permute-start | bytes 1720328 | tf_op jit(solution)/shard_map/ppermute | solution.py:24
  24.4 37.6 %collective-permute-start.20 = (bf16[80,3584]{1,0:T(8,128)(2,1)S(1)}, bf16[80,3584]{1,0:T(8,128)(2,1)S(1)}, u32[]{:S(2)}, u32[]{:S(2)}) collective-permute-start(bf16[80,3584]{1,0:T(8,128)(2,1)S(1)} %collective-permute-done.19.a_ref), channel_id=1, source_target_pairs={{0,2},{1,3},{2,0},{3,1},{4,6},{5,7},{6,4},{7,5},{8,10},{9,11},{10,... | collective-permute-start | bytes 1720328 | tf_op jit(solution)/shard_map/ppermute | solution.py:24
  59.4 15.9 %collective-permute-start.13 = (bf16[80,3584]{1,0:T(8,128)(2,1)S(1)}, bf16[80,3584]{1,0:T(8,128)(2,1)S(1)}, u32[]{:S(2)}, u32[]{:S(2)}) collective-permute-start(bf16[80,3584]{1,0:T(8,128)(2,1)S(1)} %collective-permute-done.12.a_ref), channel_id=1, source_target_pairs={{0,2},{1,3},{2,0},{3,1},{4,6},{5,7},{6,4},{7,5},{8,10},{9,11},{10,... | collective-permute-start | bytes 1720328 | tf_op jit(solution)/shard_map/ppermute | solution.py:24
  61.0 25.2 %collective-permute-start.21 = (bf16[80,3584]{1,0:T(8,128)(2,1)S(1)}, bf16[80,3584]{1,0:T(8,128)(2,1)S(1)}, u32[]{:S(2)}, u32[]{:S(2)}) collective-permute-start(bf16[80,3584]{1,0:T(8,128)(2,1)S(1)} %collective-permute-done.19.a_ref), channel_id=1, source_target_pairs={{0,1},{1,0},{2,3},{3,2},{4,5},{5,4},{6,7},{7,6},{8,9},{9,8},{10,11... | collective-permute-start | bytes 1720328 | tf_op jit(solution)/shard_map/ppermute | solution.py:24
  61.5 25.9 %collective-permute-start.6 = (bf16[80,3584]{1,0:T(8,128)(2,1)S(1)}, bf16[80,3584]{1,0:T(8,128)(2,1)S(1)}, u32[]{:S(2)}, u32[]{:S(2)}) collective-permute-start(bf16[80,3584]{1,0:T(8,128)(2,1)S(1)} %collective-permute-done.5.a_ref), channel_id=1, source_target_pairs={{0,2},{1,3},{2,0},{3,1},{4,6},{5,7},{6,4},{7,5},{8,10},{9,11},{10,... | collective-permute-start | bytes 1720328 | tf_op jit(solution)/shard_map/ppermute | solution.py:24
  62.0 25.6 %collective-permute-start.22 = (bf16[80,3584]{1,0:T(8,128)(2,1)S(1)}, bf16[80,3584]{1,0:T(8,128)(2,1)S(1)}, u32[]{:S(2)}, u32[]{:S(2)}) collective-permute-start(bf16[80,3584]{1,0:T(8,128)(2,1)S(1)} %collective-permute-done.20.b_ref), channel_id=1, source_target_pairs={{0,1},{1,0},{2,3},{3,2},{4,5},{5,4},{6,7},{7,6},{8,9},{9,8},{10,11... | collective-permute-start | bytes 1720328 | tf_op jit(solution)/shard_map/ppermute | solution.py:24
  75.4 23.1 %collective-permute-start.14 = (bf16[80,3584]{1,0:T(8,128)(2,1)S(1)}, bf16[80,3584]{1,0:T(8,128)(2,1)S(1)}, u32[]{:S(2)}, u32[]{:S(2)}) collective-permute-start(bf16[80,3584]{1,0:T(8,128)(2,1)S(1)} %collective-permute-done.12.a_ref), channel_id=1, source_target_pairs={{0,1},{1,0},{2,3},{3,2},{4,5},{5,4},{6,7},{7,6},{8,9},{9,8},{10,11... | collective-permute-start | bytes 1720328 | tf_op jit(solution)/shard_map/ppermute | solution.py:24
  75.4 23.5 %collective-permute-start.15 = (bf16[80,3584]{1,0:T(8,128)(2,1)S(1)}, bf16[80,3584]{1,0:T(8,128)(2,1)S(1)}, u32[]{:S(2)}, u32[]{:S(2)}) collective-permute-start(bf16[80,3584]{1,0:T(8,128)(2,1)S(1)} %collective-permute-done.13.b_ref), channel_id=1, source_target_pairs={{0,1},{1,0},{2,3},{3,2},{4,5},{5,4},{6,7},{7,6},{8,9},{9,8},{10,11... | collective-permute-start | bytes 1720328 | tf_op jit(solution)/shard_map/ppermute | solution.py:24
  86.3 36.0 %collective-permute-start.3 = (bf16[160,3584]{1,0:T(8,128)(2,1)}, bf16[160,3584]{1,0:T(8,128)(2,1)S(1)}, u32[]{:S(2)}, u32[]{:S(2)}) collective-permute-start(bf16[160,3584]{1,0:T(8,128)(2,1)} %get-tuple-element.16), channel_id=1, source_target_pairs={{0,1},{1,0},{2,3},{3,2},{4,5},{5,4},{6,7},{7,6},{8,9},{9,8},{10,11... | collective-permute-start | bytes 3440648 | tf_op jit(solution)/shard_map/ppermute | solution.py:24
  87.4 23.1 %collective-permute-start.7 = (bf16[80,3584]{1,0:T(8,128)(2,1)S(1)}, bf16[80,3584]{1,0:T(8,128)(2,1)S(1)}, u32[]{:S(2)}, u32[]{:S(2)}) collective-permute-start(bf16[80,3584]{1,0:T(8,128)(2,1)S(1)} %collective-permute-done.5.a_ref), channel_id=1, source_target_pairs={{0,1},{1,0},{2,3},{3,2},{4,5},{5,4},{6,7},{7,6},{8,9},{9,8},{10,11... | collective-permute-start | bytes 1720328 | tf_op jit(solution)/shard_map/ppermute | solution.py:24
  87.6 22.8 %collective-permute-start.8 = (bf16[80,3584]{1,0:T(8,128)(2,1)S(1)}, bf16[80,3584]{1,0:T(8,128)(2,1)S(1)}, u32[]{:S(2)}, u32[]{:S(2)}) collective-permute-start(bf16[80,3584]{1,0:T(8,128)(2,1)S(1)} %collective-permute-done.6.b_ref), channel_id=1, source_target_pairs={{0,1},{1,0},{2,3},{3,2},{4,5},{5,4},{6,7},{7,6},{8,9},{9,8},{10,11... | collective-permute-start | bytes 1720328 | tf_op jit(solution)/shard_map/ppermute | solution.py:24
  98.5 25.7 %collective-permute-start.23 = (bf16[160,3584]{1,0:T(8,128)(2,1)}, bf16[160,3584]{1,0:T(8,128)(2,1)S(1)}, u32[]{:S(2)}, u32[]{:S(2)}) collective-permute-start(bf16[160,3584]{1,0:T(8,128)(2,1)} %get-tuple-element.25), channel_id=1, source_target_pairs={{0,1},{1,0},{2,3},{3,2},{4,5},{5,4},{6,7},{7,6},{8,9},{9,8},{10,11... | collective-permute-start | bytes 3440648 | tf_op jit(solution)/shard_map/ppermute | solution.py:24
  110.1 15.6 %collective-permute-start.16 = (bf16[160,3584]{1,0:T(8,128)(2,1)}, bf16[160,3584]{1,0:T(8,128)(2,1)S(1)}, u32[]{:S(2)}, u32[]{:S(2)}) collective-permute-start(bf16[160,3584]{1,0:T(8,128)(2,1)} %get-tuple-element.22), channel_id=1, source_target_pairs={{0,1},{1,0},{2,3},{3,2},{4,5},{5,4},{6,7},{7,6},{8,9},{9,8},{10,11... | collective-permute-start | bytes 3440648 | tf_op jit(solution)/shard_map/ppermute | solution.py:24
  122.6 52.4 %collective-permute-start.4 = (bf16[80,3584]{1,0:T(8,128)(2,1)S(1)}, bf16[80,3584]{1,0:T(8,128)(2,1)S(1)}, u32[]{:S(2)}, u32[]{:S(2)}) collective-permute-start(bf16[80,3584]{1,0:T(8,128)(2,1)S(1)} %slice.49), channel_id=1, source_target_pairs={{0,2},{1,3},{2,0},{3,1},{4,6},{5,7},{6,4},{7,5},{8,10},{9,11},{10,... | collective-permute-start | bytes 1720328 | tf_op jit(solution)/shard_map/ppermute | solution.py:24
  124.5 26.2 %collective-permute-start.24 = (bf16[80,3584]{1,0:T(8,128)(2,1)S(1)}, bf16[80,3584]{1,0:T(8,128)(2,1)S(1)}, u32[]{:S(2)}, u32[]{:S(2)}) collective-permute-start(bf16[80,3584]{1,0:T(8,128)(2,1)S(1)} %slice.55), channel_id=1, source_target_pairs={{0,2},{1,3},{2,0},{3,1},{4,6},{5,7},{6,4},{7,5},{8,10},{9,11},{10,... | collective-permute-start | bytes 1720328 | tf_op jit(solution)/shard_map/ppermute | solution.py:24
  126.0 37.0 %collective-permute-start.17 = (bf16[80,3584]{1,0:T(8,128)(2,1)S(1)}, bf16[80,3584]{1,0:T(8,128)(2,1)S(1)}, u32[]{:S(2)}, u32[]{:S(2)}) collective-permute-start(bf16[80,3584]{1,0:T(8,128)(2,1)S(1)} %slice.53), channel_id=1, source_target_pairs={{0,2},{1,3},{2,0},{3,1},{4,6},{5,7},{6,4},{7,5},{8,10},{9,11},{10,... | collective-permute-start | bytes 1720328 | tf_op jit(solution)/shard_map/ppermute | solution.py:24
  127.6 47.2 %collective-permute-start.10 = (bf16[80,3584]{1,0:T(8,128)(2,1)S(1)}, bf16[80,3584]{1,0:T(8,128)(2,1)S(1)}, u32[]{:S(2)}, u32[]{:S(2)}) collective-permute-start(bf16[80,3584]{1,0:T(8,128)(2,1)S(1)} %slice.51), channel_id=1, source_target_pairs={{0,2},{1,3},{2,0},{3,1},{4,6},{5,7},{6,4},{7,5},{8,10},{9,11},{10,... | collective-permute-start | bytes 1720328 | tf_op jit(solution)/shard_map/ppermute | solution.py:24
  150.9 25.1 %collective-permute-start.25 = (bf16[80,3584]{1,0:T(8,128)(2,1)S(1)}, bf16[80,3584]{1,0:T(8,128)(2,1)S(1)}, u32[]{:S(2)}, u32[]{:S(2)}) collective-permute-start(bf16[80,3584]{1,0:T(8,128)(2,1)S(1)} %add_convert_fusion.4), channel_id=1, source_target_pairs={{0,12},{1,13},{2,14},{3,15},{4,8},{5,9},{6,10},{7,11},{8,4},{9,5},... | collective-permute-start | bytes 1720328 | tf_op jit(solution)/shard_map/ppermute | solution.py:24
  163.2 38.0 %collective-permute-start.18 = (bf16[80,3584]{1,0:T(8,128)(2,1)S(1)}, bf16[80,3584]{1,0:T(8,128)(2,1)S(1)}, u32[]{:S(2)}, u32[]{:S(2)}) collective-permute-start(bf16[80,3584]{1,0:T(8,128)(2,1)S(1)} %add_convert_fusion.5), channel_id=1, source_target_pairs={{0,8},{1,9},{2,10},{3,11},{4,12},{5,13},{6,14},{7,15},{8,0},{9,1},... | collective-permute-start | bytes 1720328 | tf_op jit(solution)/shard_map/ppermute | solution.py:24
  174.9 26.8 %collective-permute-start.11 = (bf16[80,3584]{1,0:T(8,128)(2,1)S(1)}, bf16[80,3584]{1,0:T(8,128)(2,1)S(1)}, u32[]{:S(2)}, u32[]{:S(2)}) collective-permute-start(bf16[80,3584]{1,0:T(8,128)(2,1)S(1)} %add_convert_fusion.6), channel_id=1, source_target_pairs={{0,4},{1,5},{2,6},{3,7},{4,0},{5,1},{6,2},{7,3},{8,12},{9,13},{10,... | collective-permute-start | bytes 1720328 | tf_op jit(solution)/shard_map/ppermute | solution.py:24
  (31 other events, 359.0 us)

commit v2 on v1

--- a/solution.py
+++ b/solution.py
@@ -16,7 +16,7 @@
 
 F32 = jnp.float32
 BF16 = jnp.bfloat16
-VMEM_LIMIT = 56 * 1024 * 1024
+VMEM_LIMIT = 24 * 1024 * 1024
 
 
 def swap(value, mask):
@@ -71,49 +71,32 @@
     )(own, tokens, gain, picks)
 
 
-def expert_kernel(a_ref, b_ref, c_ref, d_ref, gate_ref, up_ref, down_ref, own_ref, other_ref, rows, total):
-    step = pl.program_id(0)
+def expert_kernel(a_ref, b_ref, c_ref, d_ref, gate_ref, up_ref, down_ref, own_ref, other_ref, rows):
     capacity = a_ref.shape[0]
-
-    @pl.when(step == 0)
-    def _():
-        for n, ref in enumerate((a_ref, b_ref, c_ref, d_ref)):
-            rows[n * capacity : (n + 1) * capacity, :] = ref[...]
-
+    for n, ref in enumerate((a_ref, b_ref, c_ref, d_ref)):
+        rows[n * capacity : (n + 1) * capacity, :] = ref[...]
     gate = jnp.dot(rows[...], gate_ref[...], preferred_element_type=F32)
     up = jnp.dot(rows[...], up_ref[...], preferred_element_type=F32)
     hidden = (jax.nn.silu(gate) * up).astype(BF16)
-    part = jnp.dot(hidden, down_ref[...], preferred_element_type=F32)
-
-    @pl.when(step == 0)
-    def _():
-        total[...] = part
-
-    @pl.when(step == 1)
-    def _():
-        whole = (total[...] + part).astype(BF16)
-        own_ref[...] = whole[: 2 * capacity]
-        other_ref[...] = whole[2 * capacity :]
+    width = down_ref.shape[1]
+    chunk = width // 7
+    for start in range(0, width, chunk):
+        cols = slice(start, start + chunk)
+        part = jnp.dot(hidden, down_ref[:, cols], preferred_element_type=F32).astype(BF16)
+        own_ref[:, cols] = part[: 2 * capacity]
+        other_ref[:, cols] = part[2 * capacity :]
 
 
 def expert_block(blocks, gate_weight, up_weight, down_weight):
     capacity, width = blocks[0].shape
     hidden = gate_weight.shape[1]
-    half = hidden // 2
-    row_spec = pl.BlockSpec((capacity, width), lambda h: (0, 0))
-    out_spec = pl.BlockSpec((2 * capacity, width), lambda h: (0, 0))
+    vmem = pl.BlockSpec(memory_space=pltpu.VMEM)
     return pl.pallas_call(
         expert_kernel,
         out_shape=[jax.ShapeDtypeStruct((2 * capacity, width), BF16)] * 2,
-        grid=(2,),
-        in_specs=[row_spec] * 4
-        + [pl.BlockSpec((width, half), lambda h: (0, h))] * 2
-        + [pl.BlockSpec((half, width), lambda h: (h, 0))],
-        out_specs=[out_spec] * 2,
-        scratch_shapes=[
-            pltpu.VMEM((4 * capacity, width), BF16),
-            pltpu.VMEM((4 * capacity, width), F32),
-        ],
+        in_specs=[vmem] * 7,
+        out_specs=[vmem] * 2,
+        scratch_shapes=[pltpu.VMEM((4 * capacity, width), BF16)],
         compiler_params=pltpu.CompilerParams(vmem_limit_bytes=VMEM_LIMIT),
         cost_estimate=pl.CostEstimate(
             flops=2 * 3 * 4 * capacity * width * hidden,
@@ -193,6 +176,10 @@
     )(own, tokens, gain, picks, gates, target, rest, seg, *blocks)
 
 
+def after(*values):
+    return lax.optimization_barrier(values)
+
+
 def add(first, second):
     return (first.astype(F32) + second.astype(F32)).astype(BF16)
 
@@ -222,12 +209,17 @@
     core, side = 1, 2
 
     sent = pack(own, tokens, norm_gain[None, :], picks_t, experts, capacity)
-    near = [sent[0]] + [swap(sent[k], k * spread) for k in range(1, experts)]
+    near = list(sent)
+    for k in range(1, min(3, experts)):
+        near[k] = swap(sent[k], k * spread)
     back = []
     for k in range(experts):
         far = swap(near[k], side)
         blocks = [near[k], far, swap(near[k], core), swap(far, core)]
         own_part, other_part = expert_block(blocks, gate_weight, up_weight, down_weight)
+        if k + 3 < experts:
+            near[k + 2], outgoing, own_part = after(near[k + 2], sent[k + 3], own_part)
+            near[k + 3] = swap(outgoing, (k + 3) * spread)
         both = add(own_part, swap(other_part, core))
         total = add(both[:capacity], swap(both[capacity:], side))
         back.append(total if k == 0 else swap(total, k * spread))

time: 222 us -> 194 us (0.87)
  Pallas kernels: 47.8 us -> 18.2 us
  starting transfers between devices: 25.7 us -> 46.9 us
  waiting for transfers between devices: 136 us -> 116 us
  local copies, waits for them, and re-layouts: 7.07 us -> 9.3 us
    pallas_call x4, Pallas kernels: 40 us -> 15.3 us  [expert_block(): pl.pallas_call(expert_kernel, out_shape=[jax.ShapeDtypeStruct((2 * capaci...]
    ppermute x30, starting transfers between devices: 25.7 us -> 46.9 us  [swap(): return lax.ppermute(value, 'expert', pairs)]
    ppermute x30, waiting for transfers between devices: 136 us -> 116 us  [swap(): return lax.ppermute(value, 'expert', pairs)]
    unnamed x50 -> x34, local copies, waits for them, and re-layouts: 4.6 us -> 8.03 us
    pallas_call x1, Pallas kernels: 4.64 us -> 1.93 us  [score(): pl.pallas_call(score_kernel, out_shape=jax.ShapeDtypeStruct((1, sequences...]
  transfers between devices with their start and end apart: 30 -> 30, of which waited for: 12 -> 15; matrix products, arithmetic and copies ran while one was open for 2% -> 1% of each run, Pallas kernels for 18% -> 8%
where the time goes in v2:
time: 194 us; the launch traced here: 193 us
  waiting for transfers between devices  116 us (60%)
  starting transfers between devices  46.9 us (24%)
  Pallas kernels  18.2 us (9%)
  local copies, waits for them, and re-layouts  9.3 us (5%)
  other arithmetic  2.27 us (1%)
    ppermute x30, waiting for transfers between devices, swap(): return lax.ppermute(value, 'expert', pairs)  116 us
    ppermute x30, starting transfers between devices, swap(): return lax.ppermute(value, 'expert', pairs)  46.9 us
    pallas_call x4, Pallas kernels, expert_block(): pl.pallas_call(expert_kernel, out_shape=[jax.ShapeDtypeStruct((2 * capaci...  15.3 us
    unnamed x34, local copies, waits for them, and re-layouts  8.03 us
  transfers between devices with their start and end apart: 30, of which 15 were waited for; matrix products, arithmetic and copies ran while one was open for 1% of the time, Pallas kernels for 8%

profile of v2, /device:TPU:0, one launch (start us, length us, event | category | flops | bytes accessed | tf_op | source)
XLA Modules:
  0.0 193.3 jit_solution(6154813357831930194)
XLA Ops:
  4.3 3.0 %collective-permute-start.1 = (bf16[80,3584]{1,0:T(8,128)(2,1)S(1)}, bf16[80,3584]{1,0:T(8,128)(2,1)S(1)}, u32[]{:S(2)}, u32[]{:S(2)}) collective-permute-start(bf16[80,3584]{1,0:T(8,128)(2,1)S(1)} %get-tuple-element.19.a_ref), channel_id=1, source_target_pairs={{0,2},{1,3},{2,0},{3,1},{4,6},{5,7},{6,4},{7,5},{8,10},{9,11},{10,... | collective-permute-start | bytes 1720328 | tf_op jit(solution)/shard_map/ppermute | solution.py:24
  8.9 11.4 %collective-permute-done.1.b_ref = bf16[80,3584]{1,0:T(8,128)(2,1)S(1)} collective-permute-done((bf16[80,3584]{1,0:T(8,128)(2,1)S(1)}, bf16[80,3584]{1,0:T(8,128)(2,1)S(1)}, u32[]{:S(2)}, u32[]{:S(2)}) %collective-permute-start.1) | collective-permute-done | bytes 573472 | tf_op jit(solution)/shard_map/ppermute | solution.py:24
  22.1 2.7 %collective-permute-start = (bf16[80,3584]{1,0:T(8,128)(2,1)S(1)}, bf16[80,3584]{1,0:T(8,128)(2,1)S(1)}, u32[]{:S(2)}, u32[]{:S(2)}) collective-permute-start(bf16[80,3584]{1,0:T(8,128)(2,1)S(1)} %get-tuple-element.17), channel_id=1, source_target_pairs={{0,8},{1,9},{2,10},{3,11},{4,12},{5,13},{6,14},{7,15},{8,0},{9,1},... | collective-permute-start | bytes 1720328 | tf_op jit(solution)/shard_map/ppermute | solution.py:24
  24.9 2.0 %copy-done = bf16[3584,512]{1,0:T(8,128)(2,1)S(1)} copy-done((bf16[3584,512]{1,0:T(8,128)(2,1)S(1)}, bf16[3584,512]{1,0:T(8,128)(2,1)}, u32[]{:S(2)}) %copy-start) | copy-done | bytes 3670040
  26.9 2.0 %copy-done.2 = bf16[3584,512]{1,0:T(8,128)(2,1)S(1)} copy-done((bf16[3584,512]{1,0:T(8,128)(2,1)S(1)}, bf16[3584,512]{1,0:T(8,128)(2,1)}, u32[]{:S(2)}) %copy-start.2) | copy-done | bytes 3670040
  28.9 2.0 %copy-done.4 = bf16[512,3584]{1,0:T(8,128)(2,1)S(1)} copy-done((bf16[512,3584]{1,0:T(8,128)(2,1)S(1)}, bf16[512,3584]{1,0:T(8,128)(2,1)}, u32[]{:S(2)}) %copy-start.4) | copy-done | bytes 3670040
  31.0 3.8 %expert_block.4 = (bf16[160,3584]{1,0:T(8,128)(2,1)S(1)}, bf16[160,3584]{1,0:T(8,128)(2,1)S(1)}) custom-call(bf16[80,3584]{1,0:T(8,128)(2,1)S(1)} %get-tuple-element.19.a_ref, bf16[80,3584]{1,0:T(8,128)(2,1)S(1)} %collective-permute-done.1.b_ref, bf16[80,3584]{1,0:T(8,128)(2,1)S(1)} %collective-permute-done.2.c_ref, ...), custom_call_target="tpu_custom_call" | custom-call | flops 3523215360 | bytes 15597568 | tf_op jit(solution)/shard_map/expert_block/pallas_call | solution.py:94
  35.7 14.6 %collective-permute-done.a_ref = bf16[80,3584]{1,0:T(8,128)(2,1)S(1)} collective-permute-done((bf16[80,3584]{1,0:T(8,128)(2,1)S(1)}, bf16[80,3584]{1,0:T(8,128)(2,1)S(1)}, u32[]{:S(2)}, u32[]{:S(2)}) %collective-permute-start) | collective-permute-done | bytes 573472 | tf_op jit(solution)/shard_map/ppermute | solution.py:24
  50.4 3.5 %collective-permute-start.19 = (bf16[80,3584]{1,0:T(8,128)(2,1)S(1)}, bf16[80,3584]{1,0:T(8,128)(2,1)S(1)}, u32[]{:S(2)}, u32[]{:S(2)}) collective-permute-start(bf16[80,3584]{1,0:T(8,128)(2,1)S(1)} %get-tuple-element.29), channel_id=1, source_target_pairs={{0,12},{1,13},{2,14},{3,15},{4,8},{5,9},{6,10},{7,11},{8,4},{9,5},... | collective-permute-start | bytes 1720328 | tf_op jit(solution)/shard_map/ppermute | solution.py:24
  54.4 3.8 %expert_block.5 = (bf16[160,3584]{1,0:T(8,128)(2,1)S(1)}, bf16[160,3584]{1,0:T(8,128)(2,1)S(1)}) custom-call(bf16[80,3584]{1,0:T(8,128)(2,1)S(1)} %collective-permute-done.6.a_ref, bf16[80,3584]{1,0:T(8,128)(2,1)S(1)} %collective-permute-done.7.b_ref, bf16[80,3584]{1,0:T(8,128)(2,1)S(1)} %collective-permute-done.8.c_ref, ...), custom_call_target="tpu_custom_call" | custom-call | flops 3523215360 | bytes 15597568 | tf_op jit(solution)/shard_map/expert_block/pallas_call | solution.py:94
  58.8 8.3 %collective-permute-done.19.a_ref = bf16[80,3584]{1,0:T(8,128)(2,1)S(1)} collective-permute-done((bf16[80,3584]{1,0:T(8,128)(2,1)S(1)}, bf16[80,3584]{1,0:T(8,128)(2,1)S(1)}, u32[]{:S(2)}, u32[]{:S(2)}) %collective-permute-start.19) | collective-permute-done | bytes 573472 | tf_op jit(solution)/shard_map/ppermute | solution.py:24
  69.4 11.7 %collective-permute-done.20.b_ref = bf16[80,3584]{1,0:T(8,128)(2,1)S(1)} collective-permute-done((bf16[80,3584]{1,0:T(8,128)(2,1)S(1)}, bf16[80,3584]{1,0:T(8,128)(2,1)S(1)}, u32[]{:S(2)}, u32[]{:S(2)}) %collective-permute-start.20) | collective-permute-done | bytes 573472 | tf_op jit(solution)/shard_map/ppermute | solution.py:24
  83.5 3.8 %expert_block.6 = (bf16[160,3584]{1,0:T(8,128)(2,1)S(1)}, bf16[160,3584]{1,0:T(8,128)(2,1)S(1)}) custom-call(bf16[80,3584]{1,0:T(8,128)(2,1)S(1)} %collective-permute-done.a_ref, bf16[80,3584]{1,0:T(8,128)(2,1)S(1)} %collective-permute-done.13.b_ref, bf16[80,3584]{1,0:T(8,128)(2,1)S(1)} %collective-permute-done.14.c_ref, ...), custom_call_target="tpu_custom_call" | custom-call | flops 3523215360 | bytes 15597568 | tf_op jit(solution)/shard_map/expert_block/pallas_call | solution.py:94
  87.6 4.0 %expert_block.7 = (bf16[160,3584]{1,0:T(8,128)(2,1)S(1)}, bf16[160,3584]{1,0:T(8,128)(2,1)S(1)}) custom-call(bf16[80,3584]{1,0:T(8,128)(2,1)S(1)} %collective-permute-done.19.a_ref, bf16[80,3584]{1,0:T(8,128)(2,1)S(1)} %collective-permute-done.20.b_ref, bf16[80,3584]{1,0:T(8,128)(2,1)S(1)} %collective-permute-done.21.c_ref, ...), custom_call_target="tpu_custom_call" | custom-call | flops 3523215360 | bytes 15597568 | tf_op jit(solution)/shard_map/expert_block/pallas_call | solution.py:94
  91.9 14.5 %collective-permute-done.11 = bf16[80,3584]{1,0:T(8,128)(2,1)S(1)} collective-permute-done((bf16[80,3584]{1,0:T(8,128)(2,1)S(1)}, bf16[80,3584]{1,0:T(8,128)(2,1)S(1)}, u32[]{:S(2)}, u32[]{:S(2)}) %collective-permute-start.11) | collective-permute-done | bytes 573472 | tf_op jit(solution)/shard_map/ppermute | solution.py:24
  106.6 11.3 %collective-permute-start.12 = (bf16[80,3584]{1,0:T(8,128)(2,1)S(1)}, bf16[80,3584]{1,0:T(8,128)(2,1)S(1)}, u32[]{:S(2)}, u32[]{:S(2)}) collective-permute-start(bf16[80,3584]{1,0:T(8,128)(2,1)S(1)} %add_convert_fusion.6), channel_id=1, source_target_pairs={{0,4},{1,5},{2,6},{3,7},{4,0},{5,1},{6,2},{7,3},{8,12},{9,13},{10,... | collective-permute-start | bytes 1720328 | tf_op jit(solution)/shard_map/ppermute | solution.py:24
  120.8 13.5 %collective-permute-done.17 = bf16[80,3584]{1,0:T(8,128)(2,1)S(1)} collective-permute-done((bf16[80,3584]{1,0:T(8,128)(2,1)S(1)}, bf16[80,3584]{1,0:T(8,128)(2,1)S(1)}, u32[]{:S(2)}, u32[]{:S(2)}) %collective-permute-start.17) | collective-permute-done | bytes 573472 | tf_op jit(solution)/shard_map/ppermute | solution.py:24
  134.8 7.7 %collective-permute-done.24 = bf16[80,3584]{1,0:T(8,128)(2,1)S(1)} collective-permute-done((bf16[80,3584]{1,0:T(8,128)(2,1)S(1)}, bf16[80,3584]{1,0:T(8,128)(2,1)S(1)}, u32[]{:S(2)}, u32[]{:S(2)}) %collective-permute-start.24) | collective-permute-done | bytes 573472 | tf_op jit(solution)/shard_map/ppermute | solution.py:24
  142.8 2.2 %collective-permute-start.25 = (bf16[80,3584]{1,0:T(8,128)(2,1)S(1)}, bf16[80,3584]{1,0:T(8,128)(2,1)S(1)}, u32[]{:S(2)}, u32[]{:S(2)}) collective-permute-start(bf16[80,3584]{1,0:T(8,128)(2,1)S(1)} %add_convert_fusion.4), channel_id=1, source_target_pairs={{0,12},{1,13},{2,14},{3,15},{4,8},{5,9},{6,10},{7,11},{8,4},{9,5},... | collective-permute-start | bytes 1720328 | tf_op jit(solution)/shard_map/ppermute | solution.py:24
  145.1 24.1 %collective-permute-done.18.refs_2_ = bf16[80,3584]{1,0:T(8,128)(2,1)S(1)} collective-permute-done((bf16[80,3584]{1,0:T(8,128)(2,1)S(1)}, bf16[80,3584]{1,0:T(8,128)(2,1)S(1)}, u32[]{:S(2)}, u32[]{:S(2)}) %collective-permute-start.18) | collective-permute-done | bytes 573472 | tf_op jit(solution)/shard_map/ppermute | solution.py:24
  169.3 1.9 %score.1 = f32[1,16]{1,0:T(1,128)S(1)} custom-call(s32[1]{0:T(128)} %bitcast.own_ref, bf16[128,3584]{1,0:T(8,128)(2,1)S(1)} %copy-done.7, f32[1,3584]{1,0:T(1,128)S(1)} %broadcast_in_dim.12.gain_ref, s32[2,128]{1,0:T(2,128)S(1)} %bitcast.8, f32[2,128]{1,0:T(2,128)S(1)} %bitcast.9, bf16[128,3584]{1,0:T(8,128)(2,1)S(1)} %copy-done.8, f32[1,128]{1,0:T(1,128)S(1)} %bitcast.10, ...), custom_call_target="tpu_custom_call" | custom-call | flops 587202560 | bytes 4128768 | tf_op jit(solution)/shard_map/score/pallas_call | solution.py:160
  172.9 3.0 %collective-permute-done.27 = f32[1,16]{1,0:T(1,128)S(1)} collective-permute-done((f32[1,16]{1,0:T(1,128)S(1)}, f32[1,16]{1,0:T(1,128)S(1)}, u32[]{:S(2)}, u32[]{:S(2)}) %collective-permute-start.27) | collective-permute-done | bytes 96 | tf_op jit(solution)/shard_map/ppermute | solution.py:24
  176.0 10.6 %collective-permute-start.28 = (f32[1,16]{1,0:T(1,128)S(1)}, f32[1,16]{1,0:T(1,128)S(1)}, u32[]{:S(2)}, u32[]{:S(2)}) collective-permute-start(f32[1,16]{1,0:T(1,128)S(1)} %add.51), channel_id=1, source_target_pairs={{0,4},{1,5},{2,6},{3,7},{4,0},{5,1},{6,2},{7,3},{8,12},{9,13},{10,... | collective-permute-start | bytes 200 | tf_op jit(solution)/shard_map/ppermute | solution.py:24
  188.0 3.0 %collective-permute-start.29 = (f32[1,16]{1,0:T(1,128)S(1)}, f32[1,16]{1,0:T(1,128)S(1)}, u32[]{:S(2)}, u32[]{:S(2)}) collective-permute-start(f32[1,16]{1,0:T(1,128)S(1)} %add.52), channel_id=1, source_target_pairs={{0,8},{1,9},{2,10},{3,11},{4,12},{5,13},{6,14},{7,15},{8,0},{9,1},... | collective-permute-start | bytes 200 | tf_op jit(solution)/shard_map/ppermute | solution.py:24
  (99 shorter events, 23.7 us)
Async XLA Ops:
  4.3 16.0 %collective-permute-start.1 = (bf16[80,3584]{1,0:T(8,128)(2,1)S(1)}, bf16[80,3584]{1,0:T(8,128)(2,1)S(1)}, u32[]{:S(2)}, u32[]{:S(2)}) collective-permute-start(bf16[80,3584]{1,0:T(8,128)(2,1)S(1)} %get-tuple-element.19.a_ref), channel_id=1, source_target_pairs={{0,2},{1,3},{2,0},{3,1},{4,6},{5,7},{6,4},{7,5},{8,10},{9,11},{10,... | collective-permute-start | bytes 1720328 | tf_op jit(solution)/shard_map/ppermute | solution.py:24
  7.3 14.4 %collective-permute-start.6 = (bf16[80,3584]{1,0:T(8,128)(2,1)S(1)}, bf16[80,3584]{1,0:T(8,128)(2,1)S(1)}, u32[]{:S(2)}, u32[]{:S(2)}) collective-permute-start(bf16[80,3584]{1,0:T(8,128)(2,1)S(1)} %get-tuple-element.23), channel_id=1, source_target_pairs={{0,4},{1,5},{2,6},{3,7},{4,0},{5,1},{6,2},{7,3},{8,12},{9,13},{10,... | collective-permute-start | bytes 1720328 | tf_op jit(solution)/shard_map/ppermute | solution.py:24
  8.9 16.0 %collective-permute-start.2 = (bf16[80,3584]{1,0:T(8,128)(2,1)S(1)}, bf16[80,3584]{1,0:T(8,128)(2,1)S(1)}, u32[]{:S(2)}, u32[]{:S(2)}) collective-permute-start(bf16[80,3584]{1,0:T(8,128)(2,1)S(1)} %get-tuple-element.19.a_ref), channel_id=1, source_target_pairs={{0,1},{1,0},{2,3},{3,2},{4,5},{5,4},{6,7},{7,6},{8,9},{9,8},{10,11... | collective-permute-start | bytes 1720328 | tf_op jit(solution)/shard_map/ppermute | solution.py:24
  21.8 13.9 %collective-permute-start.7 = (bf16[80,3584]{1,0:T(8,128)(2,1)S(1)}, bf16[80,3584]{1,0:T(8,128)(2,1)S(1)}, u32[]{:S(2)}, u32[]{:S(2)}) collective-permute-start(bf16[80,3584]{1,0:T(8,128)(2,1)S(1)} %collective-permute-done.6.a_ref), channel_id=1, source_target_pairs={{0,2},{1,3},{2,0},{3,1},{4,6},{5,7},{6,4},{7,5},{8,10},{9,11},{10,... | collective-permute-start | bytes 1720328 | tf_op jit(solution)/shard_map/ppermute | solution.py:24
  22.1 28.2 %collective-permute-start = (bf16[80,3584]{1,0:T(8,128)(2,1)S(1)}, bf16[80,3584]{1,0:T(8,128)(2,1)S(1)}, u32[]{:S(2)}, u32[]{:S(2)}) collective-permute-start(bf16[80,3584]{1,0:T(8,128)(2,1)S(1)} %get-tuple-element.17), channel_id=1, source_target_pairs={{0,8},{1,9},{2,10},{3,11},{4,12},{5,13},{6,14},{7,15},{8,0},{9,1},... | collective-permute-start | bytes 1720328 | tf_op jit(solution)/shard_map/ppermute | solution.py:24
  34.8 33.7 %collective-permute-start.4 = (bf16[160,3584]{1,0:T(8,128)(2,1)S(1)}, bf16[160,3584]{1,0:T(8,128)(2,1)S(1)}, u32[]{:S(2)}, u32[]{:S(2)}) collective-permute-start(bf16[160,3584]{1,0:T(8,128)(2,1)S(1)} %get-tuple-element.22), channel_id=1, source_target_pairs={{0,1},{1,0},{2,3},{3,2},{4,5},{5,4},{6,7},{7,6},{8,9},{9,8},{10,11... | collective-permute-start | bytes 3440648 | tf_op jit(solution)/shard_map/ppermute | solution.py:24
  34.8 19.5 %collective-permute-start.8 = (bf16[80,3584]{1,0:T(8,128)(2,1)S(1)}, bf16[80,3584]{1,0:T(8,128)(2,1)S(1)}, u32[]{:S(2)}, u32[]{:S(2)}) collective-permute-start(bf16[80,3584]{1,0:T(8,128)(2,1)S(1)} %collective-permute-done.6.a_ref), channel_id=1, source_target_pairs={{0,1},{1,0},{2,3},{3,2},{4,5},{5,4},{6,7},{7,6},{8,9},{9,8},{10,11... | collective-permute-start | bytes 1720328 | tf_op jit(solution)/shard_map/ppermute | solution.py:24
  35.7 18.6 %collective-permute-start.9 = (bf16[80,3584]{1,0:T(8,128)(2,1)S(1)}, bf16[80,3584]{1,0:T(8,128)(2,1)S(1)}, u32[]{:S(2)}, u32[]{:S(2)}) collective-permute-start(bf16[80,3584]{1,0:T(8,128)(2,1)S(1)} %collective-permute-done.7.b_ref), channel_id=1, source_target_pairs={{0,1},{1,0},{2,3},{3,2},{4,5},{5,4},{6,7},{7,6},{8,9},{9,8},{10,11... | collective-permute-start | bytes 1720328 | tf_op jit(solution)/shard_map/ppermute | solution.py:24
  50.4 16.8 %collective-permute-start.19 = (bf16[80,3584]{1,0:T(8,128)(2,1)S(1)}, bf16[80,3584]{1,0:T(8,128)(2,1)S(1)}, u32[]{:S(2)}, u32[]{:S(2)}) collective-permute-start(bf16[80,3584]{1,0:T(8,128)(2,1)S(1)} %get-tuple-element.29), channel_id=1, source_target_pairs={{0,12},{1,13},{2,14},{3,15},{4,8},{5,9},{6,10},{7,11},{8,4},{9,5},... | collective-permute-start | bytes 1720328 | tf_op jit(solution)/shard_map/ppermute | solution.py:24
  53.8 14.6 %collective-permute-start.13 = (bf16[80,3584]{1,0:T(8,128)(2,1)S(1)}, bf16[80,3584]{1,0:T(8,128)(2,1)S(1)}, u32[]{:S(2)}, u32[]{:S(2)}) collective-permute-start(bf16[80,3584]{1,0:T(8,128)(2,1)S(1)} %collective-permute-done.a_ref), channel_id=1, source_target_pairs={{0,2},{1,3},{2,0},{3,1},{4,6},{5,7},{6,4},{7,5},{8,10},{9,11},{10,... | collective-permute-start | bytes 1720328 | tf_op jit(solution)/shard_map/ppermute | solution.py:24
  58.2 23.4 %collective-permute-start.10 = (bf16[160,3584]{1,0:T(8,128)(2,1)S(1)}, bf16[160,3584]{1,0:T(8,128)(2,1)S(1)}, u32[]{:S(2)}, u32[]{:S(2)}) collective-permute-start(bf16[160,3584]{1,0:T(8,128)(2,1)S(1)} %get-tuple-element.25), channel_id=1, source_target_pairs={{0,1},{1,0},{2,3},{3,2},{4,5},{5,4},{6,7},{7,6},{8,9},{9,8},{10,11... | collective-permute-start | bytes 3440648 | tf_op jit(solution)/shard_map/ppermute | solution.py:24
  58.3 23.7 %collective-permute-start.14 = (bf16[80,3584]{1,0:T(8,128)(2,1)S(1)}, bf16[80,3584]{1,0:T(8,128)(2,1)S(1)}, u32[]{:S(2)}, u32[]{:S(2)}) collective-permute-start(bf16[80,3584]{1,0:T(8,128)(2,1)S(1)} %collective-permute-done.a_ref), channel_id=1, source_target_pairs={{0,1},{1,0},{2,3},{3,2},{4,5},{5,4},{6,7},{7,6},{8,9},{9,8},{10,11... | collective-permute-start | bytes 1720328 | tf_op jit(solution)/shard_map/ppermute | solution.py:24
  67.1 14.0 %collective-permute-start.20 = (bf16[80,3584]{1,0:T(8,128)(2,1)S(1)}, bf16[80,3584]{1,0:T(8,128)(2,1)S(1)}, u32[]{:S(2)}, u32[]{:S(2)}) collective-permute-start(bf16[80,3584]{1,0:T(8,128)(2,1)S(1)} %collective-permute-done.19.a_ref), channel_id=1, source_target_pairs={{0,2},{1,3},{2,0},{3,1},{4,6},{5,7},{6,4},{7,5},{8,10},{9,11},{10,... | collective-permute-start | bytes 1720328 | tf_op jit(solution)/shard_map/ppermute | solution.py:24
  68.5 19.1 %collective-permute-start.21 = (bf16[80,3584]{1,0:T(8,128)(2,1)S(1)}, bf16[80,3584]{1,0:T(8,128)(2,1)S(1)}, u32[]{:S(2)}, u32[]{:S(2)}) collective-permute-start(bf16[80,3584]{1,0:T(8,128)(2,1)S(1)} %collective-permute-done.19.a_ref), channel_id=1, source_target_pairs={{0,1},{1,0},{2,3},{3,2},{4,5},{5,4},{6,7},{7,6},{8,9},{9,8},{10,11... | collective-permute-start | bytes 1720328 | tf_op jit(solution)/shard_map/ppermute | solution.py:24
  68.5 15.0 %collective-permute-start.15 = (bf16[80,3584]{1,0:T(8,128)(2,1)S(1)}, bf16[80,3584]{1,0:T(8,128)(2,1)S(1)}, u32[]{:S(2)}, u32[]{:S(2)}) collective-permute-start(bf16[80,3584]{1,0:T(8,128)(2,1)S(1)} %collective-permute-done.13.b_ref), channel_id=1, source_target_pairs={{0,1},{1,0},{2,3},{3,2},{4,5},{5,4},{6,7},{7,6},{8,9},{9,8},{10,11... | collective-permute-start | bytes 1720328 | tf_op jit(solution)/shard_map/ppermute | solution.py:24
  81.1 63.9 %collective-permute-start.5 = (bf16[80,3584]{1,0:T(8,128)(2,1)S(1)}, bf16[80,3584]{1,0:T(8,128)(2,1)S(1)}, u32[]{:S(2)}, u32[]{:S(2)}) collective-permute-start(bf16[80,3584]{1,0:T(8,128)(2,1)S(1)} %slice.49), channel_id=1, source_target_pairs={{0,2},{1,3},{2,0},{3,1},{4,6},{5,7},{6,4},{7,5},{8,10},{9,11},{10,... | collective-permute-start | bytes 1720328 | tf_op jit(solution)/shard_map/ppermute | solution.py:24
  81.9 24.5 %collective-permute-start.11 = (bf16[80,3584]{1,0:T(8,128)(2,1)S(1)}, bf16[80,3584]{1,0:T(8,128)(2,1)S(1)}, u32[]{:S(2)}, u32[]{:S(2)}) collective-permute-start(bf16[80,3584]{1,0:T(8,128)(2,1)S(1)} %slice.51), channel_id=1, source_target_pairs={{0,2},{1,3},{2,0},{3,1},{4,6},{5,7},{6,4},{7,5},{8,10},{9,11},{10,... | collective-permute-start | bytes 1720328 | tf_op jit(solution)/shard_map/ppermute | solution.py:24
  87.3 30.6 %collective-permute-start.16 = (bf16[160,3584]{1,0:T(8,128)(2,1)S(1)}, bf16[160,3584]{1,0:T(8,128)(2,1)S(1)}, u32[]{:S(2)}, u32[]{:S(2)}) collective-permute-start(bf16[160,3584]{1,0:T(8,128)(2,1)S(1)} %get-tuple-element.28), channel_id=1, source_target_pairs={{0,1},{1,0},{2,3},{3,2},{4,5},{5,4},{6,7},{7,6},{8,9},{9,8},{10,11... | collective-permute-start | bytes 3440648 | tf_op jit(solution)/shard_map/ppermute | solution.py:24
  91.6 27.3 %collective-permute-start.23 = (bf16[160,3584]{1,0:T(8,128)(2,1)S(1)}, bf16[160,3584]{1,0:T(8,128)(2,1)S(1)}, u32[]{:S(2)}, u32[]{:S(2)}) collective-permute-start(bf16[160,3584]{1,0:T(8,128)(2,1)S(1)} %get-tuple-element.31), channel_id=1, source_target_pairs={{0,1},{1,0},{2,3},{3,2},{4,5},{5,4},{6,7},{7,6},{8,9},{9,8},{10,11... | collective-permute-start | bytes 3440648 | tf_op jit(solution)/shard_map/ppermute | solution.py:24
  106.6 38.6 %collective-permute-start.12 = (bf16[80,3584]{1,0:T(8,128)(2,1)S(1)}, bf16[80,3584]{1,0:T(8,128)(2,1)S(1)}, u32[]{:S(2)}, u32[]{:S(2)}) collective-permute-start(bf16[80,3584]{1,0:T(8,128)(2,1)S(1)} %add_convert_fusion.6), channel_id=1, source_target_pairs={{0,4},{1,5},{2,6},{3,7},{4,0},{5,1},{6,2},{7,3},{8,12},{9,13},{10,... | collective-permute-start | bytes 1720328 | tf_op jit(solution)/shard_map/ppermute | solution.py:24
  118.3 16.0 %collective-permute-start.17 = (bf16[80,3584]{1,0:T(8,128)(2,1)S(1)}, bf16[80,3584]{1,0:T(8,128)(2,1)S(1)}, u32[]{:S(2)}, u32[]{:S(2)}) collective-permute-start(bf16[80,3584]{1,0:T(8,128)(2,1)S(1)} %slice.53), channel_id=1, source_target_pairs={{0,2},{1,3},{2,0},{3,1},{4,6},{5,7},{6,4},{7,5},{8,10},{9,11},{10,... | collective-permute-start | bytes 1720328 | tf_op jit(solution)/shard_map/ppermute | solution.py:24
  119.2 23.4 %collective-permute-start.24 = (bf16[80,3584]{1,0:T(8,128)(2,1)S(1)}, bf16[80,3584]{1,0:T(8,128)(2,1)S(1)}, u32[]{:S(2)}, u32[]{:S(2)}) collective-permute-start(bf16[80,3584]{1,0:T(8,128)(2,1)S(1)} %slice.55), channel_id=1, source_target_pairs={{0,2},{1,3},{2,0},{3,1},{4,6},{5,7},{6,4},{7,5},{8,10},{9,11},{10,... | collective-permute-start | bytes 1720328 | tf_op jit(solution)/shard_map/ppermute | solution.py:24
  134.4 34.9 %collective-permute-start.18 = (bf16[80,3584]{1,0:T(8,128)(2,1)S(1)}, bf16[80,3584]{1,0:T(8,128)(2,1)S(1)}, u32[]{:S(2)}, u32[]{:S(2)}) collective-permute-start(bf16[80,3584]{1,0:T(8,128)(2,1)S(1)} %add_convert_fusion.5), channel_id=1, source_target_pairs={{0,8},{1,9},{2,10},{3,11},{4,12},{5,13},{6,14},{7,15},{8,0},{9,1},... | collective-permute-start | bytes 1720328 | tf_op jit(solution)/shard_map/ppermute | solution.py:24
  142.8 26.5 %collective-permute-start.25 = (bf16[80,3584]{1,0:T(8,128)(2,1)S(1)}, bf16[80,3584]{1,0:T(8,128)(2,1)S(1)}, u32[]{:S(2)}, u32[]{:S(2)}) collective-permute-start(bf16[80,3584]{1,0:T(8,128)(2,1)S(1)} %add_convert_fusion.4), channel_id=1, source_target_pairs={{0,12},{1,13},{2,14},{3,15},{4,8},{5,9},{6,10},{7,11},{8,4},{9,5},... | collective-permute-start | bytes 1720328 | tf_op jit(solution)/shard_map/ppermute | solution.py:24
  (23 other events, 295.2 us)

commit v3 on v2

v3 whole, which is shorter than its diff:
```python
import functools

import jax
import jax.numpy as jnp
from jax import lax
from jax.experimental import pallas as pl
from jax.experimental.pallas import tpu as pltpu
from jax.sharding import PartitionSpec as P

FFE = 2048
HID_DEV = 512
TOPK = 2

PIECE = 16

EPS = 1e-06
BETA = 0.01

F32 = jnp.float32
BF16 = jnp.bfloat16
VMEM_LIMIT = 20 * 1024 * 1024
COST = pl.CostEstimate(flops=1024, bytes_accessed=1024, transcendentals=0)


def swap(value, mask):
    pairs = [(source, source ^ mask) for source in range(lax.axis_size("expert"))]
    return lax.ppermute(value, "expert", pairs)


def iota(shape, dim):
    return lax.broadcasted_iota(jnp.int32, shape, dim)


def routing(own, picks, rows):
    tokens = picks.shape[1]
    expert = jnp.bitwise_xor(own, iota((rows, tokens), 0))
    hit = [picks[k : k + 1, :] == expert for k in range(TOPK)]
    member = hit[0] | hit[1]
    earlier = (iota((tokens, tokens), 0) < iota((tokens, tokens), 1)).astype(BF16)
    slot = jnp.dot(member.astype(F32).astype(BF16), earlier, preferred_element_type=F32)
    slot = jnp.where(member, slot.astype(jnp.int32), -1)
    return hit, slot


def pack_kernel(chunks, own_ref, tokens_ref, gain_ref, picks_ref, *out_refs):
    tokens = tokens_ref.shape[0]
    values = tokens_ref[...].astype(F32)
    scale = lax.rsqrt(jnp.mean(values * values, axis=-1, keepdims=True) + EPS)
    normed = (values * scale * gain_ref[...]).astype(BF16)
    _, slot = routing(own_ref[0], picks_ref[...], max(8, 1 + max(k for k, _, _ in chunks)))
    for (k, first, count), out_ref in zip(chunks, out_refs):
        place = first + iota((count, tokens), 0)
        chosen = (slot[k : k + 1, :] == place).astype(F32).astype(BF16)
        out_ref[...] = jnp.dot(chosen, normed, preferred_element_type=F32).astype(BF16)


def pack(own, tokens, gain, picks, chunks):
    rows, width = tokens.shape
    smem = pl.BlockSpec(memory_space=pltpu.SMEM)
    vmem = pl.BlockSpec(memory_space=pltpu.VMEM)
    return pl.pallas_call(
        functools.partial(pack_kernel, chunks),
        out_shape=[jax.ShapeDtypeStruct((count, width), BF16) for _, _, count in chunks],
        in_specs=[smem, vmem, vmem, vmem],
        out_specs=[vmem] * len(chunks),
        compiler_params=pltpu.CompilerParams(vmem_limit_bytes=VMEM_LIMIT),
        cost_estimate=COST,
        name="pack",
    )(own, tokens, gain, picks)


def expert_kernel(blocks, gate_ref, up_ref, down_ref, *refs):
    block_refs, out_refs, rows = refs[:blocks], refs[blocks:-1], refs[-1]
    first = 0
    for ref in block_refs:
        rows[first : first + ref.shape[0], :] = ref[...]
        first += ref.shape[0]
    gate = jnp.dot(rows[...], gate_ref[...], preferred_element_type=F32)
    up = jnp.dot(rows[...], up_ref[...], preferred_element_type=F32)
    hidden = (jax.nn.silu(gate) * up).astype(BF16)
    width = down_ref.shape[1]
    chunk = width // 7 if width % 7 == 0 else width
    for start in range(0, width, chunk):
        cols = slice(start, start + chunk)
        part = jnp.dot(hidden, down_ref[:, cols], preferred_element_type=F32).astype(BF16)
        first = 0
        for out_ref in out_refs:
            out_ref[:, cols] = part[first : first + out_ref.shape[0]]
            first += out_ref.shape[0]


def expert_block(blocks, gate_weight, up_weight, down_weight):
    count, width = blocks[0].shape
    outs = [count] * 3 + [PIECE] * (count // PIECE)
    vmem = pl.BlockSpec(memory_space=pltpu.VMEM)
    return pl.pallas_call(
        functools.partial(expert_kernel, len(blocks)),
        out_shape=[jax.ShapeDtypeStruct((rows, width), BF16) for rows in outs],
        in_specs=[vmem] * (3 + len(blocks)),
        out_specs=[vmem] * len(outs),
        scratch_shapes=[pltpu.VMEM((4 * count, width), BF16)],
        compiler_params=pltpu.CompilerParams(vmem_limit_bytes=VMEM_LIMIT),
        cost_estimate=COST,
        name="expert_block",
    )(gate_weight, up_weight, down_weight, *blocks)


def score_kernel(capacity, own_ref, tokens_ref, gain_ref, picks_ref, gates_ref, target_ref, rest_ref, seg_ref, *refs):
    *block_refs, out_ref, stacked, stream = refs
    tokens, width = tokens_ref.shape
    experts = stacked.shape[0] // capacity
    first = 0
    for ref in block_refs:
        stacked[first : first + ref.shape[0], :] = ref[...]
        first += ref.shape[0]
    hit, slot = routing(own_ref[0], picks_ref[...], max(8, experts))
    weight = sum(jnp.where(hit[k], gates_ref[k : k + 1, :], 0.0) for k in range(TOPK))
    place = iota((capacity, tokens), 0)
    parts = [
        jnp.where(slot[k : k + 1, :] == place, weight[k : k + 1, :], 0.0) for k in range(experts)
    ]
    spread = jnp.concatenate(parts, axis=0)
    coarse = spread.astype(BF16)
    fine = (spread - coarse.astype(F32)).astype(BF16)
    chunk = width // 7 if width % 7 == 0 else width
    over_rows = (((0,), (0,)), ((), ()))
    squares = jnp.zeros((tokens, 1), F32)
    for start in range(0, width, chunk):
        cols = slice(start, start + chunk)
        rows = stacked[:, cols]
        moe = lax.dot_general(coarse, rows, over_rows, preferred_element_type=F32)
        moe = moe + lax.dot_general(fine, rows, over_rows, preferred_element_type=F32)
        value = tokens_ref[:, cols].astype(F32) + moe
        stream[:, cols] = value
        squares = squares + jnp.sum(value * value, axis=-1, keepdims=True)
    scale = lax.rsqrt(squares / width + EPS)
    logit = jnp.zeros((tokens, 1), F32)
    for start in range(0, width, chunk):
        cols = slice(start, start + chunk)
        final = (stream[:, cols] * scale * gain_ref[:, cols]).astype(BF16).astype(F32)
        logit = logit + jnp.sum(final * target_ref[:, cols].astype(F32), axis=-1, keepdims=True)
    turn = iota((tokens, tokens), 0) == iota((tokens, tokens), 1)
    logit = jnp.sum(jnp.where(turn, logit, 0.0), axis=0, keepdims=True)
    gap = rest_ref[...] - logit
    token_logp = -(jnp.maximum(gap, 0.0) + jnp.log1p(jnp.exp(-jnp.abs(gap))))
    sequences = out_ref.shape[1]
    inside = iota((sequences, tokens), 0) == seg_ref[...]
    sums = jnp.sum(jnp.where(inside, token_logp, 0.0), axis=1, keepdims=True)
    turn = iota((sequences, sequences), 0) == iota((sequences, sequences), 1)
    out_ref[...] = jnp.sum(jnp.where(turn, sums, 0.0), axis=0, keepdims=True)


def score(own, tokens, gain, picks, gates, target, rest, seg, blocks, capacity, sequences):
    rows, width = tokens.shape
    slots = sum(block.shape[0] for block in blocks)
    smem = pl.BlockSpec(memory_space=pltpu.SMEM)
    vmem = pl.BlockSpec(memory_space=pltpu.VMEM)
    return pl.pallas_call(
        functools.partial(score_kernel, capacity),
        out_shape=jax.ShapeDtypeStruct((1, sequences), F32),
        in_specs=[smem] + [vmem] * (7 + len(blocks)),
        out_specs=vmem,
        scratch_shapes=[
            pltpu.VMEM((slots, width), BF16),
            pltpu.VMEM((rows, width), F32),
        ],
        compiler_params=pltpu.CompilerParams(vmem_limit_bytes=VMEM_LIMIT),
        cost_estimate=COST,
        name="score",
    )(own, tokens, gain, picks, gates, target, rest, seg, *blocks)


class Order:
    def __init__(self, token):
        self.token = token

    def mark(self, *values):
        *values, self.token = lax.optimization_barrier((*values, self.token))
        return values

    def mark_one(self, value):
        return self.mark(value)[0]

    def late(self, value):
        return lax.optimization_barrier((value, self.token))[0]


def cut_kernel(whole_ref, *refs):
    for n, ref in enumerate(refs):
        ref[...] = whole_ref[n * PIECE : (n + 1) * PIECE, :]


def cut(whole):
    rows, width = whole.shape
    vmem = pl.BlockSpec(memory_space=pltpu.VMEM)
    return pl.pallas_call(
        cut_kernel,
        out_shape=[jax.ShapeDtypeStruct((PIECE, width), BF16)] * (rows // PIECE),
        in_specs=[vmem],
        out_specs=[vmem] * (rows // PIECE),
        compiler_params=pltpu.CompilerParams(vmem_limit_bytes=VMEM_LIMIT),
        cost_estimate=COST,
        name="cut",
    )(whole)


def total_kernel(*refs):
    *refs, out_ref = refs
    out_ref[...] = sum(ref[...].astype(F32) for ref in refs).astype(BF16)


def joined_kernel(whole_ref, *refs):
    *refs, out_ref = refs
    for n, ref in enumerate(refs):
        rows = slice(n * PIECE, (n + 1) * PIECE)
        out_ref[rows, :] = (whole_ref[rows, :].astype(F32) + ref[...].astype(F32)).astype(BF16)


def total(*values, kernel=total_kernel):
    vmem = pl.BlockSpec(memory_space=pltpu.VMEM)
    return pl.pallas_call(
        kernel,
        out_shape=jax.ShapeDtypeStruct(values[0].shape, BF16),
        in_specs=[vmem] * len(values),
        out_specs=vmem,
        compiler_params=pltpu.CompilerParams(vmem_limit_bytes=VMEM_LIMIT),
        cost_estimate=COST,
        name="total",
    )(*values)


def per_device(
    tokens,
    norm_gain,
    final_gain,
    gate_weight,
    up_weight,
    down_weight,
    picks,
    gates,
    target_rows,
    rest_lse,
    segment_ids,
    ref_logps,
):
    tok_rows = tokens.shape[0]
    spread = FFE // HID_DEV
    devices = lax.axis_size("expert")
    experts = devices // spread
    capacity = (tok_rows * TOPK * 5 // (experts * 4) + 3) // 4 * 4
    capacity = (capacity + 15) // 16 * 16
    own = (lax.axis_index("expert") // spread).astype(jnp.int32).reshape(1)
    picks_t = picks.T
    core, side = 1, 2
    weights = (gate_weight, up_weight, down_weight)

    half = (capacity // 2 + 15) // 16 * 16 if capacity >= 64 else capacity
    cuts = [(first, min(half, capacity - first)) for first in range(0, capacity, half)]
    chunks = [(k, 0, capacity) for k in range(min(2, experts))]
    near_count = len(chunks)
    chunks += [(k, first, count) for k in range(2, experts) for first, count in cuts]
    travelling = list(range(near_count, len(chunks)))
    sent = pack(own, tokens, norm_gain[None, :], picks_t, tuple(chunks))
    order = Order(own)
    near, far, beside, across = list(sent), {}, {}, {}
    mine, theirs, other_mine, other_theirs, back = {}, {}, {}, {}, {}

    def leave(n):
        near[n] = swap(order.late(near[n]), chunks[n][0] * spread)

    def arrive(n):
        near[n] = order.mark_one(near[n])

    def share(n):
        far[n], beside[n] = swap(order.late(near[n]), side), swap(order.late(near[n]), core)

    def meet(n):
        far[n] = order.mark_one(far[n])
        pieces = order.mark(*cut(far[n])) if n in travelling else [far[n]]
        across[n] = [swap(piece, core) for piece in pieces]

    def work(n):
        rows = [order.late(rows) for rows in (near[n], far[n], beside[n], *across[n])]
        mine[n], theirs[n], other, *pieces = order.mark(*expert_block(rows, *weights))
        other_theirs[n] = [swap(piece, core) for piece in pieces]
        other_mine[n] = swap(other, core)

    def half_way(n):
        pieces = order.mark(*other_theirs[n])
        theirs[n] = order.mark_one(total(theirs[n], *pieces, kernel=joined_kernel))

    def cross(n):
        theirs[n] = swap(order.late(theirs[n]), side)

    def home(n):
        back[n] = order.mark_one(total(mine[n], other_mine[n], order.mark_one(theirs[n])))

    def leave_back(n):
        back[n] = swap(order.late(back[n]), chunks[n][0] * spread)

    def arrive_back(n):
        back[n] = order.mark_one(back[n])

    far_count = len(travelling)
    begin_back = max(far_count, 4)
    steps = begin_back + far_count

    def at(step):
        return travelling[step] if 0 <= step < far_count else None

    for step in range(steps):
        out, shared, worked, crossing, back_now = (
            at(step), at(step - 1), at(step - 2), at(step - 3), at(step - begin_back)
        )
        if out is not None:
            leave(out)
        if back_now is not None:
            leave_back(back_now)
        if shared is not None:
            share(shared)
        if step == 0:
            share(0)
            leave(1)
            meet(0)
        if worked is not None:
            work(worked)
        if shared is not None:
            meet(shared)
        if worked is not None:
            half_way(worked)
            cross(worked)
        if crossing is not None:
            home(crossing)
        if step == 1:
            arrive(1)
            share(1)
        if step == 2:
            meet(1)
        if step == 3:
            work(0)
        if step == 4:
            work(1)
        if step == steps - 3:
            half_way(1)
            cross(1)
        if step == steps - 2:
            half_way(0)
            cross(0)
            home(1)
            leave_back(1)
        if step == steps - 1:
            home(0)
        if out is not None:
            arrive(out)
        if back_now is not None:
            arrive_back(back_now)
    blocks = [back[n] for n in range(len(chunks))]
    local = score(
        own,
        tokens,
        final_gain[None, :],
        picks_t,
        gates.T,
        target_rows,
        rest_lse[None, :],
        segment_ids[None, :],
        blocks,
        capacity,
        ref_logps.shape[0],
    )
    mask = 1
    while mask < devices:
        local = local + swap(local, mask)
        mask *= 2
    sequence_logps = local[0]
    margin = sequence_logps[0::2] - ref_logps[0::2] - (sequence_logps[1::2] - ref_logps[1::2])
    pair_loss = -jax.nn.log_sigmoid(BETA * margin)
    return (sequence_logps, pair_loss)


def solution(mesh):
    placed = (
        P(("group", "expert"), None),
        P(),
        P(),
        P(None, "expert"),
        P(None, "expert"),
        P("expert", None),
        P(("group", "expert"), None),
        P(("group", "expert"), None),
        P(("group", "expert"), None),
        P(("group", "expert")),
        P(("group", "expert")),
        P("group"),
    )
    return jax.shard_map(
        per_device, mesh=mesh, in_specs=placed, out_specs=(P("group"), P("group")), check_vma=False
    )
```

time: 194 us -> 186 us (0.959)
  waiting for transfers between devices: 116 us -> 109 us
  Pallas kernels: 18.2 us -> 20.4 us
    ppermute x30 -> x70, waiting for transfers between devices: 116 us -> 109 us  [swap(): return lax.ppermute(value, 'expert', pairs)]
    pallas_call x6 -> x24, Pallas kernels: 18.2 us -> 20.4 us  [the longest x6 15.8 us: expert_block(): pl.pallas_call(functools.partial(expert_kernel, len(blocks)), out_shape=[...]
    ppermute x30 -> x70, starting transfers between devices: 46.9 us -> 45.5 us  [swap(): return lax.ppermute(value, 'expert', pairs)]
    unnamed x34 -> x30, local copies, waits for them, and re-layouts: 8.03 us -> 8.02 us
  transfers between devices with their start and end apart: 30 -> 70, of which waited for: 15 -> 28; matrix products, arithmetic and copies ran while one was open for 1% -> 0% of each run, Pallas kernels for 8% -> 9%
where the time goes in v3:
time: 186 us
  waiting for transfers between devices  109 us (59%)
  starting transfers between devices  45.5 us (24%)
  Pallas kernels  20.4 us (11%)
  local copies, waits for them, and re-layouts  9.14 us (5%)
    ppermute x70, waiting for transfers between devices, swap(): return lax.ppermute(value, 'expert', pairs)  109 us
    ppermute x70, starting transfers between devices, swap(): return lax.ppermute(value, 'expert', pairs)  45.5 us
    pallas_call x6, Pallas kernels, expert_block(): pl.pallas_call(functools.partial(expert_kernel, len(blocks)), out_shape=[...  15.8 us
    unnamed x30, local copies, waits for them, and re-layouts  8.02 us
  transfers between devices with their start and end apart: 70, of which 28 were waited for; matrix products, arithmetic and copies ran while one was open for 0% of the time, Pallas kernels for 9%

profile of v3, /device:TPU:0, one launch (start us, length us, event | category | flops | bytes accessed | tf_op | source)
XLA Modules:
  0.0 186.1 jit_solution(2643764820577568402)
XLA Ops:
  4.5 3.0 %collective-permute-start.1 = (bf16[80,3584]{1,0:T(8,128)(2,1)S(1)}, bf16[80,3584]{1,0:T(8,128)(2,1)S(1)}, u32[]{:S(2)}, u32[]{:S(2)}) collective-permute-start(bf16[80,3584]{1,0:T(8,128)(2,1)S(1)} %get-tuple-element.341.refs_0_), channel_id=1, source_target_pairs={{0,2},{1,3},{2,0},{3,1},{4,6},{5,7},{6,4},{7,5},{8,10},{9,11},{10,... | collective-permute-start | bytes 1720328 | tf_op jit(solution)/shard_map/ppermute | solution.py:27
  7.5 2.6 %collective-permute-start = (bf16[48,3584]{1,0:T(8,128)(2,1)S(1)}, bf16[48,3584]{1,0:T(8,128)(2,1)S(1)}, u32[]{:S(2)}, u32[]{:S(2)}) collective-permute-start(bf16[48,3584]{1,0:T(8,128)(2,1)S(1)} %get-tuple-element.255), channel_id=1, source_target_pairs={{0,8},{1,9},{2,10},{3,11},{4,12},{5,13},{6,14},{7,15},{8,0},{9,1},... | collective-permute-start | bytes 1032200 | tf_op jit(solution)/shard_map/ppermute | solution.py:27
  11.7 8.8 %collective-permute-done.1.refs_1_ = bf16[80,3584]{1,0:T(8,128)(2,1)S(1)} collective-permute-done((bf16[80,3584]{1,0:T(8,128)(2,1)S(1)}, bf16[80,3584]{1,0:T(8,128)(2,1)S(1)}, u32[]{:S(2)}, u32[]{:S(2)}) %collective-permute-start.1) | collective-permute-done | bytes 573472 | tf_op jit(solution)/shard_map/ppermute | solution.py:27
  20.5 4.9 %collective-permute-done.refs_0_ = bf16[48,3584]{1,0:T(8,128)(2,1)S(1)} collective-permute-done((bf16[48,3584]{1,0:T(8,128)(2,1)S(1)}, bf16[48,3584]{1,0:T(8,128)(2,1)S(1)}, u32[]{:S(2)}, u32[]{:S(2)}) %collective-permute-start) | collective-permute-done | bytes 344096 | tf_op jit(solution)/shard_map/ppermute | solution.py:27
  25.8 8.4 %collective-permute-done.4.whole_ref.refs_1_ = bf16[48,3584]{1,0:T(8,128)(2,1)S(1)} collective-permute-done((bf16[48,3584]{1,0:T(8,128)(2,1)S(1)}, bf16[48,3584]{1,0:T(8,128)(2,1)S(1)}, u32[]{:S(2)}, u32[]{:S(2)}) %collective-permute-start.4) | collective-permute-done | bytes 344096 | tf_op jit(solution)/shard_map/ppermute | solution.py:27
  34.9 4.8 %collective-permute-done.2.refs_0_ = bf16[32,3584]{1,0:T(8,128)(2,1)S(1)} collective-permute-done((bf16[32,3584]{1,0:T(8,128)(2,1)S(1)}, bf16[32,3584]{1,0:T(8,128)(2,1)S(1)}, u32[]{:S(2)}, u32[]{:S(2)}) %collective-permute-start.2) | collective-permute-done | bytes 229408 | tf_op jit(solution)/shard_map/ppermute | solution.py:27
  50.8 3.0 %collective-permute-start.15 = (bf16[48,3584]{1,0:T(8,128)(2,1)S(1)}, bf16[48,3584]{1,0:T(8,128)(2,1)S(1)}, u32[]{:S(2)}, u32[]{:S(2)}) collective-permute-start(bf16[48,3584]{1,0:T(8,128)(2,1)S(1)} %get-tuple-element.306), channel_id=1, source_target_pairs={{0,12},{1,13},{2,14},{3,15},{4,8},{5,9},{6,10},{7,11},{8,4},{9,5},... | collective-permute-start | bytes 1032200 | tf_op jit(solution)/shard_map/ppermute | solution.py:27
  53.8 5.4 %collective-permute-done.13.whole_ref.refs_1_ = bf16[32,3584]{1,0:T(8,128)(2,1)S(1)} collective-permute-done((bf16[32,3584]{1,0:T(8,128)(2,1)S(1)}, bf16[32,3584]{1,0:T(8,128)(2,1)S(1)}, u32[]{:S(2)}, u32[]{:S(2)}) %collective-permute-start.13) | collective-permute-done | bytes 229408 | tf_op jit(solution)/shard_map/ppermute | solution.py:27
  68.5 5.3 %collective-permute-done.14.refs_2_ = bf16[48,3584]{1,0:T(8,128)(2,1)S(1)} collective-permute-done((bf16[48,3584]{1,0:T(8,128)(2,1)S(1)}, bf16[48,3584]{1,0:T(8,128)(2,1)S(1)}, u32[]{:S(2)}, u32[]{:S(2)}) %collective-permute-start.14) | collective-permute-done | bytes 344096 | tf_op jit(solution)/shard_map/ppermute | solution.py:27
  73.8 3.0 %collective-permute-start.31 = (bf16[32,3584]{1,0:T(8,128)(2,1)S(1)}, bf16[32,3584]{1,0:T(8,128)(2,1)S(1)}, u32[]{:S(2)}, u32[]{:S(2)}) collective-permute-start(bf16[32,3584]{1,0:T(8,128)(2,1)S(1)} %get-tuple-element.363), channel_id=1, source_target_pairs={{0,12},{1,13},{2,14},{3,15},{4,8},{5,9},{6,10},{7,11},{8,4},{9,5},... | collective-permute-start | bytes 688136 | tf_op jit(solution)/shard_map/ppermute | solution.py:27
  76.7 3.1 %collective-permute-done.22.whole_ref.refs_1_ = bf16[48,3584]{1,0:T(8,128)(2,1)S(1)} collective-permute-done((bf16[48,3584]{1,0:T(8,128)(2,1)S(1)}, bf16[48,3584]{1,0:T(8,128)(2,1)S(1)}, u32[]{:S(2)}, u32[]{:S(2)}) %collective-permute-start.22) | collective-permute-done | bytes 344096 | tf_op jit(solution)/shard_map/ppermute | solution.py:27
  82.0 3.8 %expert_block.8 = (bf16[80,3584]{1,0:T(8,128)(2,1)S(1)}, bf16[80,3584]{1,0:T(8,128)(2,1)S(1)}, bf16[80,3584]{1,0:T(8,128)(2,1)S(1)}, bf16[16,3584]{1,0:T(8,128)(...) custom-call(bf16[3584,512]{1,0:T(8,128)(2,1)S(1)} %copy-done.1, ...), custom_call_target="tpu_custom_call" | custom-call | flops 1024 | bytes 1024 | tf_op jit(solution)/shard_map/expert_block/pallas_call | solution.py:96
  87.9 2.4 %expert_block.9 = (bf16[48,3584]{1,0:T(8,128)(2,1)S(1)}, bf16[48,3584]{1,0:T(8,128)(2,1)S(1)}, bf16[48,3584]{1,0:T(8,128)(2,1)S(1)}, bf16[16,3584]{1,0:T(8,128)(...) custom-call(bf16[3584,512]{1,0:T(8,128)(2,1)S(1)} %copy-done.1, bf16[3584,512]{1,0:T(8,128)(2,1)S(1)} %copy-done.2, ...), custom_call_target="tpu_custom_call" | custom-call | flops 1024 | bytes 1024 | tf_op jit(solution)/shard_map/expert_block/pallas_call | solution.py:96
  90.9 4.6 %collective-permute-start.32 = (bf16[48,3584]{1,0:T(8,128)(2,1)S(1)}, bf16[48,3584]{1,0:T(8,128)(2,1)S(1)}, u32[]{:S(2)}, u32[]{:S(2)}) collective-permute-start(bf16[48,3584]{1,0:T(8,128)(2,1)S(1)} %total.14), channel_id=1, source_target_pairs={{0,8},{1,9},{2,10},{3,11},{4,12},{5,13},{6,14},{7,15},{8,0},{9,1},... | collective-permute-start | bytes 1032200 | tf_op jit(solution)/shard_map/ppermute | solution.py:27
  98.6 4.9 %collective-permute-done.34.refs_2_ = bf16[32,3584]{1,0:T(8,128)(2,1)S(1)} collective-permute-done((bf16[32,3584]{1,0:T(8,128)(2,1)S(1)}, bf16[32,3584]{1,0:T(8,128)(2,1)S(1)}, u32[]{:S(2)}, u32[]{:S(2)}) %collective-permute-start.34) | collective-permute-done | bytes 229408 | tf_op jit(solution)/shard_map/ppermute | solution.py:27
  104.6 6.8 %collective-permute-done.32.refs_2_ = bf16[48,3584]{1,0:T(8,128)(2,1)S(1)} collective-permute-done((bf16[48,3584]{1,0:T(8,128)(2,1)S(1)}, bf16[48,3584]{1,0:T(8,128)(2,1)S(1)}, u32[]{:S(2)}, u32[]{:S(2)}) %collective-permute-start.32) | collective-permute-done | bytes 344096 | tf_op jit(solution)/shard_map/ppermute | solution.py:27
  111.5 3.8 %expert_block.10 = (bf16[80,3584]{1,0:T(8,128)(2,1)S(1)}, bf16[80,3584]{1,0:T(8,128)(2,1)S(1)}, bf16[80,3584]{1,0:T(8,128)(2,1)S(1)}, bf16[16,3584]{1,0:T(8,128)...) custom-call(bf16[3584,512]{1,0:T(8,128)(2,1)S(1)} %copy-done.1, ...), custom_call_target="tpu_custom_call" | custom-call | flops 1024 | bytes 1024 | tf_op jit(solution)/shard_map/expert_block/pallas_call | solution.py:96
  125.0 10.7 %collective-permute-done.52.refs_3_ = bf16[32,3584]{1,0:T(8,128)(2,1)S(1)} collective-permute-done((bf16[32,3584]{1,0:T(8,128)(2,1)S(1)}, bf16[32,3584]{1,0:T(8,128)(2,1)S(1)}, u32[]{:S(2)}, u32[]{:S(2)}) %collective-permute-start.52) | collective-permute-done | bytes 229408 | tf_op jit(solution)/shard_map/ppermute | solution.py:27
  136.3 4.6 %collective-permute-done.51.refs_2_ = bf16[32,3584]{1,0:T(8,128)(2,1)S(1)} collective-permute-done((bf16[32,3584]{1,0:T(8,128)(2,1)S(1)}, bf16[32,3584]{1,0:T(8,128)(2,1)S(1)}, u32[]{:S(2)}, u32[]{:S(2)}) %collective-permute-start.51) | collective-permute-done | bytes 229408 | tf_op jit(solution)/shard_map/ppermute | solution.py:27
  145.4 8.9 %collective-permute-done.61.refs_4_ = bf16[48,3584]{1,0:T(8,128)(2,1)S(1)} collective-permute-done((bf16[48,3584]{1,0:T(8,128)(2,1)S(1)}, bf16[48,3584]{1,0:T(8,128)(2,1)S(1)}, u32[]{:S(2)}, u32[]{:S(2)}) %collective-permute-start.61) | collective-permute-done | bytes 344096 | tf_op jit(solution)/shard_map/ppermute | solution.py:27
  159.0 11.7 %collective-permute-done.65.refs_5_ = bf16[32,3584]{1,0:T(8,128)(2,1)S(1)} collective-permute-done((bf16[32,3584]{1,0:T(8,128)(2,1)S(1)}, bf16[32,3584]{1,0:T(8,128)(2,1)S(1)}, u32[]{:S(2)}, u32[]{:S(2)}) %collective-permute-start.65) | collective-permute-done | bytes 229408 | tf_op jit(solution)/shard_map/ppermute | solution.py:27
  174.7 2.6 %collective-permute-done.67 = f32[1,16]{1,0:T(1,128)S(1)} collective-permute-done((f32[1,16]{1,0:T(1,128)S(1)}, f32[1,16]{1,0:T(1,128)S(1)}, u32[]{:S(2)}, u32[]{:S(2)}) %collective-permute-start.67) | collective-permute-done | bytes 96 | tf_op jit(solution)/shard_map/ppermute | solution.py:27
  177.5 3.4 %collective-permute-done.68 = f32[1,16]{1,0:T(1,128)S(1)} collective-permute-done((f32[1,16]{1,0:T(1,128)S(1)}, f32[1,16]{1,0:T(1,128)S(1)}, u32[]{:S(2)}, u32[]{:S(2)}) %collective-permute-start.68) | collective-permute-done | bytes 96 | tf_op jit(solution)/shard_map/ppermute | solution.py:27
  181.9 3.5 %collective-permute-done.69 = f32[1,16]{1,0:T(1,128)S(1)} collective-permute-done((f32[1,16]{1,0:T(1,128)S(1)}, f32[1,16]{1,0:T(1,128)S(1)}, u32[]{:S(2)}, u32[]{:S(2)}) %collective-permute-start.69) | collective-permute-done | bytes 96 | tf_op jit(solution)/shard_map/ppermute | solution.py:27
  (181 shorter events, 61.0 us)
Async XLA Ops:
  4.5 16.0 %collective-permute-start.1 = (bf16[80,3584]{1,0:T(8,128)(2,1)S(1)}, bf16[80,3584]{1,0:T(8,128)(2,1)S(1)}, u32[]{:S(2)}, u32[]{:S(2)}) collective-permute-start(bf16[80,3584]{1,0:T(8,128)(2,1)S(1)} %get-tuple-element.341.refs_0_), channel_id=1, source_target_pairs={{0,2},{1,3},{2,0},{3,1},{4,6},{5,7},{6,4},{7,5},{8,10},{9,11},{10,... | collective-permute-start | bytes 1720328 | tf_op jit(solution)/shard_map/ppermute | solution.py:27
  7.5 17.9 %collective-permute-start = (bf16[48,3584]{1,0:T(8,128)(2,1)S(1)}, bf16[48,3584]{1,0:T(8,128)(2,1)S(1)}, u32[]{:S(2)}, u32[]{:S(2)}) collective-permute-start(bf16[48,3584]{1,0:T(8,128)(2,1)S(1)} %get-tuple-element.255), channel_id=1, source_target_pairs={{0,8},{1,9},{2,10},{3,11},{4,12},{5,13},{6,14},{7,15},{8,0},{9,1},... | collective-permute-start | bytes 1032200 | tf_op jit(solution)/shard_map/ppermute | solution.py:27
  10.1 24.8 %collective-permute-start.3 = (bf16[80,3584]{1,0:T(8,128)(2,1)S(1)}, bf16[80,3584]{1,0:T(8,128)(2,1)S(1)}, u32[]{:S(2)}, u32[]{:S(2)}) collective-permute-start(bf16[80,3584]{1,0:T(8,128)(2,1)S(1)} %get-tuple-element.263), channel_id=1, source_target_pairs={{0,4},{1,5},{2,6},{3,7},{4,0},{5,1},{6,2},{7,3},{8,12},{9,13},{10,... | collective-permute-start | bytes 1720328 | tf_op jit(solution)/shard_map/ppermute | solution.py:27
  25.8 15.4 %collective-permute-start.5 = (bf16[48,3584]{1,0:T(8,128)(2,1)S(1)}, bf16[48,3584]{1,0:T(8,128)(2,1)S(1)}, u32[]{:S(2)}, u32[]{:S(2)}) collective-permute-start(bf16[48,3584]{1,0:T(8,128)(2,1)S(1)} %collective-permute-done.refs_0_), channel_id=1, source_target_pairs={{0,1},{1,0},{2,3},{3,2},{4,5},{5,4},{6,7},{7,6},{8,9},{9,8},{10,11... | collective-permute-start | bytes 1032200 | tf_op jit(solution)/shard_map/ppermute | solution.py:27
  25.8 13.9 %collective-permute-start.2 = (bf16[32,3584]{1,0:T(8,128)(2,1)S(1)}, bf16[32,3584]{1,0:T(8,128)(2,1)S(1)}, u32[]{:S(2)}, u32[]{:S(2)}) collective-permute-start(bf16[32,3584]{1,0:T(8,128)(2,1)S(1)} %get-tuple-element.261), channel_id=1, source_target_pairs={{0,8},{1,9},{2,10},{3,11},{4,12},{5,13},{6,14},{7,15},{8,0},{9,1},... | collective-permute-start | bytes 688136 | tf_op jit(solution)/shard_map/ppermute | solution.py:27
  39.7 24.6 %collective-permute-start.16 = (bf16[80,3584]{1,0:T(8,128)(2,1)S(1)}, bf16[80,3584]{1,0:T(8,128)(2,1)S(1)}, u32[]{:S(2)}, u32[]{:S(2)}) collective-permute-start(bf16[80,3584]{1,0:T(8,128)(2,1)S(1)} %collective-permute-done.3.refs_0_), channel_id=1, source_target_pairs={{0,2},{1,3},{2,0},{3,1},{4,6},{5,7},{6,4},{7,5},{8,10},{9,11},{10,... | collective-permute-start | bytes 1720328 | tf_op jit(solution)/shard_map/ppermute | solution.py:27
  41.2 18.0 %collective-permute-start.13 = (bf16[32,3584]{1,0:T(8,128)(2,1)S(1)}, bf16[32,3584]{1,0:T(8,128)(2,1)S(1)}, u32[]{:S(2)}, u32[]{:S(2)}) collective-permute-start(bf16[32,3584]{1,0:T(8,128)(2,1)S(1)} %collective-permute-done.2.refs_0_), channel_id=1, source_target_pairs={{0,2},{1,3},{2,0},{3,1},{4,6},{5,7},{6,4},{7,5},{8,10},{9,11},{10,... | collective-permute-start | bytes 688136 | tf_op jit(solution)/shard_map/ppermute | solution.py:27
  64.3 17.2 %collective-permute-start.23 = (bf16[80,3584]{1,0:T(8,128)(2,1)S(1)}, bf16[80,3584]{1,0:T(8,128)(2,1)S(1)}, u32[]{:S(2)}, u32[]{:S(2)}) collective-permute-start(bf16[80,3584]{1,0:T(8,128)(2,1)S(1)} %get-tuple-element.341.refs_0_), channel_id=1, source_target_pairs={{0,1},{1,0},{2,3},{3,2},{4,5},{5,4},{6,7},{7,6},{8,9},{9,8},{10,11... | collective-permute-start | bytes 1720328 | tf_op jit(solution)/shard_map/ppermute | solution.py:27
  65.7 14.2 %collective-permute-start.22 = (bf16[48,3584]{1,0:T(8,128)(2,1)S(1)}, bf16[48,3584]{1,0:T(8,128)(2,1)S(1)}, u32[]{:S(2)}, u32[]{:S(2)}) collective-permute-start(bf16[48,3584]{1,0:T(8,128)(2,1)S(1)} %collective-permute-done.15.refs_0_), channel_id=1, source_target_pairs={{0,2},{1,3},{2,0},{3,1},{4,6},{5,7},{6,4},{7,5},{8,10},{9,11},{10,... | collective-permute-start | bytes 1032200 | tf_op jit(solution)/shard_map/ppermute | solution.py:27
  68.0 22.9 %collective-permute-start.43 = (bf16[80,3584]{1,0:T(8,128)(2,1)S(1)}, bf16[80,3584]{1,0:T(8,128)(2,1)S(1)}, u32[]{:S(2)}, u32[]{:S(2)}) collective-permute-start(bf16[80,3584]{1,0:T(8,128)(2,1)S(1)} %collective-permute-done.3.refs_0_), channel_id=1, source_target_pairs={{0,1},{1,0},{2,3},{3,2},{4,5},{5,4},{6,7},{7,6},{8,9},{9,8},{10,11... | collective-permute-start | bytes 1720328 | tf_op jit(solution)/shard_map/ppermute | solution.py:27
  81.5 23.0 %collective-permute-start.44 = (bf16[80,3584]{1,0:T(8,128)(2,1)S(1)}, bf16[80,3584]{1,0:T(8,128)(2,1)S(1)}, u32[]{:S(2)}, u32[]{:S(2)}) collective-permute-start(bf16[80,3584]{1,0:T(8,128)(2,1)S(1)} %collective-permute-done.16.refs_1_), channel_id=1, source_target_pairs={{0,1},{1,0},{2,3},{3,2},{4,5},{5,4},{6,7},{7,6},{8,9},{9,8},{10,11... | collective-permute-start | bytes 1720328 | tf_op jit(solution)/shard_map/ppermute | solution.py:27
  90.9 20.5 %collective-permute-start.32 = (bf16[48,3584]{1,0:T(8,128)(2,1)S(1)}, bf16[48,3584]{1,0:T(8,128)(2,1)S(1)}, u32[]{:S(2)}, u32[]{:S(2)}) collective-permute-start(bf16[48,3584]{1,0:T(8,128)(2,1)S(1)} %total.14), channel_id=1, source_target_pairs={{0,8},{1,9},{2,10},{3,11},{4,12},{5,13},{6,14},{7,15},{8,0},{9,1},... | collective-permute-start | bytes 1032200 | tf_op jit(solution)/shard_map/ppermute | solution.py:27
  98.0 17.3 %collective-permute-start.45 = (bf16[32,3584]{1,0:T(8,128)(2,1)S(1)}, bf16[32,3584]{1,0:T(8,128)(2,1)S(1)}, u32[]{:S(2)}, u32[]{:S(2)}) collective-permute-start(bf16[32,3584]{1,0:T(8,128)(2,1)S(1)} %collective-permute-done.31.refs_0_), channel_id=1, source_target_pairs={{0,1},{1,0},{2,3},{3,2},{4,5},{5,4},{6,7},{7,6},{8,9},{9,8},{10,11... | collective-permute-start | bytes 688136 | tf_op jit(solution)/shard_map/ppermute | solution.py:27
  98.1 20.0 %collective-permute-start.58 = (bf16[48,3584]{1,0:T(8,128)(2,1)S(1)}, bf16[48,3584]{1,0:T(8,128)(2,1)S(1)}, u32[]{:S(2)}, u32[]{:S(2)}) collective-permute-start(bf16[48,3584]{1,0:T(8,128)(2,1)S(1)} %get-tuple-element.451), channel_id=1, source_target_pairs={{0,1},{1,0},{2,3},{3,2},{4,5},{5,4},{6,7},{7,6},{8,9},{9,8},{10,11... | collective-permute-start | bytes 1032200 | tf_op jit(solution)/shard_map/ppermute | solution.py:27
  103.5 15.6 %collective-permute-start.59 = (bf16[48,3584]{1,0:T(8,128)(2,1)S(1)}, bf16[48,3584]{1,0:T(8,128)(2,1)S(1)}, u32[]{:S(2)}, u32[]{:S(2)}) collective-permute-start(bf16[48,3584]{1,0:T(8,128)(2,1)S(1)} %total.15), channel_id=1, source_target_pairs={{0,2},{1,3},{2,0},{3,1},{4,6},{5,7},{6,4},{7,5},{8,10},{9,11},{10,... | collective-permute-start | bytes 1032200 | tf_op jit(solution)/shard_map/ppermute | solution.py:27
  120.6 24.4 %collective-permute-start.63 = (bf16[80,3584]{1,0:T(8,128)(2,1)S(1)}, bf16[80,3584]{1,0:T(8,128)(2,1)S(1)}, u32[]{:S(2)}, u32[]{:S(2)}) collective-permute-start(bf16[80,3584]{1,0:T(8,128)(2,1)S(1)} %total.19), channel_id=1, source_target_pairs={{0,2},{1,3},{2,0},{3,1},{4,6},{5,7},{6,4},{7,5},{8,10},{9,11},{10,... | collective-permute-start | bytes 1720328 | tf_op jit(solution)/shard_map/ppermute | solution.py:27
  121.6 23.5 %collective-permute-start.62 = (bf16[80,3584]{1,0:T(8,128)(2,1)S(1)}, bf16[80,3584]{1,0:T(8,128)(2,1)S(1)}, u32[]{:S(2)}, u32[]{:S(2)}) collective-permute-start(bf16[80,3584]{1,0:T(8,128)(2,1)S(1)} %get-tuple-element.478), channel_id=1, source_target_pairs={{0,1},{1,0},{2,3},{3,2},{4,5},{5,4},{6,7},{7,6},{8,9},{9,8},{10,11... | collective-permute-start | bytes 1720328 | tf_op jit(solution)/shard_map/ppermute | solution.py:27
  122.2 13.5 %collective-permute-start.52 = (bf16[32,3584]{1,0:T(8,128)(2,1)S(1)}, bf16[32,3584]{1,0:T(8,128)(2,1)S(1)}, u32[]{:S(2)}, u32[]{:S(2)}) collective-permute-start(bf16[32,3584]{1,0:T(8,128)(2,1)S(1)} %total.16), channel_id=1, source_target_pairs={{0,8},{1,9},{2,10},{3,11},{4,12},{5,13},{6,14},{7,15},{8,0},{9,1},... | collective-permute-start | bytes 688136 | tf_op jit(solution)/shard_map/ppermute | solution.py:27
  123.9 16.9 %collective-permute-start.51 = (bf16[32,3584]{1,0:T(8,128)(2,1)S(1)}, bf16[32,3584]{1,0:T(8,128)(2,1)S(1)}, u32[]{:S(2)}, u32[]{:S(2)}) collective-permute-start(bf16[32,3584]{1,0:T(8,128)(2,1)S(1)} %total.17), channel_id=1, source_target_pairs={{0,2},{1,3},{2,0},{3,1},{4,6},{5,7},{6,4},{7,5},{8,10},{9,11},{10,... | collective-permute-start | bytes 688136 | tf_op jit(solution)/shard_map/ppermute | solution.py:27
  141.0 17.8 %collective-permute-start.25 = (bf16[80,3584]{1,0:T(8,128)(2,1)S(1)}, bf16[80,3584]{1,0:T(8,128)(2,1)S(1)}, u32[]{:S(2)}, u32[]{:S(2)}) collective-permute-start(bf16[80,3584]{1,0:T(8,128)(2,1)S(1)} %get-tuple-element.355), channel_id=1, source_target_pairs={{0,1},{1,0},{2,3},{3,2},{4,5},{5,4},{6,7},{7,6},{8,9},{9,8},{10,11... | collective-permute-start | bytes 1720328 | tf_op jit(solution)/shard_map/ppermute | solution.py:27
  141.5 12.8 %collective-permute-start.61 = (bf16[48,3584]{1,0:T(8,128)(2,1)S(1)}, bf16[48,3584]{1,0:T(8,128)(2,1)S(1)}, u32[]{:S(2)}, u32[]{:S(2)}) collective-permute-start(bf16[48,3584]{1,0:T(8,128)(2,1)S(1)} %total.18), channel_id=1, source_target_pairs={{0,12},{1,13},{2,14},{3,15},{4,8},{5,9},{6,10},{7,11},{8,4},{9,5},... | collective-permute-start | bytes 1032200 | tf_op jit(solution)/shard_map/ppermute | solution.py:27
  144.0 14.8 %collective-permute-start.60 = (bf16[80,3584]{1,0:T(8,128)(2,1)S(1)}, bf16[80,3584]{1,0:T(8,128)(2,1)S(1)}, u32[]{:S(2)}, u32[]{:S(2)}) collective-permute-start(bf16[80,3584]{1,0:T(8,128)(2,1)S(1)} %total.21), channel_id=1, source_target_pairs={{0,2},{1,3},{2,0},{3,1},{4,6},{5,7},{6,4},{7,5},{8,10},{9,11},{10,... | collective-permute-start | bytes 1720328 | tf_op jit(solution)/shard_map/ppermute | solution.py:27
  145.3 25.4 %collective-permute-start.64 = (bf16[80,3584]{1,0:T(8,128)(2,1)S(1)}, bf16[80,3584]{1,0:T(8,128)(2,1)S(1)}, u32[]{:S(2)}, u32[]{:S(2)}) collective-permute-start(bf16[80,3584]{1,0:T(8,128)(2,1)S(1)} %total.22), channel_id=1, source_target_pairs={{0,4},{1,5},{2,6},{3,7},{4,0},{5,1},{6,2},{7,3},{8,12},{9,13},{10,... | collective-permute-start | bytes 1720328 | tf_op jit(solution)/shard_map/ppermute | solution.py:27
  154.3 16.3 %collective-permute-start.65 = (bf16[32,3584]{1,0:T(8,128)(2,1)S(1)}, bf16[32,3584]{1,0:T(8,128)(2,1)S(1)}, u32[]{:S(2)}, u32[]{:S(2)}) collective-permute-start(bf16[32,3584]{1,0:T(8,128)(2,1)S(1)} %total.20), channel_id=1, source_target_pairs={{0,12},{1,13},{2,14},{3,15},{4,8},{5,9},{6,10},{7,11},{8,4},{9,5},... | collective-permute-start | bytes 688136 | tf_op jit(solution)/shard_map/ppermute | solution.py:27
  (61 other events, 632.6 us)

commit v4 on v3

--- a/solution.py
+++ b/solution.py
@@ -10,8 +10,6 @@
 FFE = 2048
 HID_DEV = 512
 TOPK = 2
-
-PIECE = 16
 
 EPS = 1e-06
 BETA = 0.01
@@ -69,40 +67,42 @@
     )(own, tokens, gain, picks)
 
 
-def expert_kernel(blocks, gate_ref, up_ref, down_ref, *refs):
-    block_refs, out_refs, rows = refs[:blocks], refs[blocks:-1], refs[-1]
-    first = 0
-    for ref in block_refs:
-        rows[first : first + ref.shape[0], :] = ref[...]
-        first += ref.shape[0]
-    gate = jnp.dot(rows[...], gate_ref[...], preferred_element_type=F32)
-    up = jnp.dot(rows[...], up_ref[...], preferred_element_type=F32)
-    hidden = (jax.nn.silu(gate) * up).astype(BF16)
-    width = down_ref.shape[1]
+def expert_kernel(near_ref, far_ref, *refs):
+    weight_refs, (mine_ref, theirs_ref, rows) = refs[:-3], refs[-3:]
+    count = near_ref.shape[0]
+    rows[:count, :] = near_ref[...]
+    rows[count:, :] = far_ref[...]
+    halves = [weight_refs[n : n + 3] for n in range(0, len(weight_refs), 3)]
+    hidden = []
+    for gate_ref, up_ref, _ in halves:
+        gate = jnp.dot(rows[...], gate_ref[...], preferred_element_type=F32)
+        up = jnp.dot(rows[...], up_ref[...], preferred_element_type=F32)
+        hidden.append((jax.nn.silu(gate) * up).astype(BF16))
+    width = near_ref.shape[1]
     chunk = width // 7 if width % 7 == 0 else width
     for start in range(0, width, chunk):
         cols = slice(start, start + chunk)
-        part = jnp.dot(hidden, down_ref[:, cols], preferred_element_type=F32).astype(BF16)
-        first = 0
-        for out_ref in out_refs:
-            out_ref[:, cols] = part[first : first + out_ref.shape[0]]
-            first += out_ref.shape[0]
-
-
-def expert_block(blocks, gate_weight, up_weight, down_weight):
-    count, width = blocks[0].shape
-    outs = [count] * 3 + [PIECE] * (count // PIECE)
-    vmem = pl.BlockSpec(memory_space=pltpu.VMEM)
-    return pl.pallas_call(
-        functools.partial(expert_kernel, len(blocks)),
-        out_shape=[jax.ShapeDtypeStruct((rows, width), BF16) for rows in outs],
-        in_specs=[vmem] * (3 + len(blocks)),
-        out_specs=[vmem] * len(outs),
-        scratch_shapes=[pltpu.VMEM((4 * count, width), BF16)],
+        part = sum(
+            jnp.dot(value, down_ref[:, cols], preferred_element_type=F32)
+            for value, (_, _, down_ref) in zip(hidden, halves)
+        ).astype(BF16)
+        mine_ref[:, cols] = part[:count]
+        theirs_ref[:, cols] = part[count:]
+
+
+def expert_block(near, far, weights):
+    count, width = near.shape
+    vmem = pl.BlockSpec(memory_space=pltpu.VMEM)
+    return pl.pallas_call(
+        expert_kernel,
+        out_shape=[jax.ShapeDtypeStruct((count, width), BF16)] * 2,
+        in_specs=[vmem] * (2 + len(weights)),
+        out_specs=[vmem] * 2,
+        scratch_shapes=[pltpu.VMEM((2 * count, width), BF16)],
         compiler_params=pltpu.CompilerParams(vmem_limit_bytes=VMEM_LIMIT),
         cost_estimate=COST,
         name="expert_block",
-    )(gate_weight, up_weight, down_weight, *blocks)
+    )(near, far, *weights)
 
 
 def score_kernel(capacity, own_ref, tokens_ref, gain_ref, picks_ref, gates_ref, target_ref, rest_ref, seg_ref, *refs):
@@ -185,23 +185,23 @@
         return lax.optimization_barrier((value, self.token))[0]
 
 
-def cut_kernel(whole_ref, *refs):
-    for n, ref in enumerate(refs):
-        ref[...] = whole_ref[n * PIECE : (n + 1) * PIECE, :]
-
-
-def cut(whole):
-    rows, width = whole.shape
-    vmem = pl.BlockSpec(memory_space=pltpu.VMEM)
-    return pl.pallas_call(
-        cut_kernel,
-        out_shape=[jax.ShapeDtypeStruct((PIECE, width), BF16)] * (rows // PIECE),
-        in_specs=[vmem],
-        out_specs=[vmem] * (rows // PIECE),
-        compiler_params=pltpu.CompilerParams(vmem_limit_bytes=VMEM_LIMIT),
-        cost_estimate=COST,
-        name="cut",
-    )(whole)
+def hold_kernel(own_ref, *refs):
+    *_, out_ref = refs
+    out_ref[0] = own_ref[0]
+
+
+def hold(own, arrays):
+    smem = pl.BlockSpec(memory_space=pltpu.SMEM)
+    vmem = pl.BlockSpec(memory_space=pltpu.VMEM)
+    return pl.pallas_call(
+        hold_kernel,
+        out_shape=jax.ShapeDtypeStruct((1,), jnp.int32),
+        in_specs=[smem] + [vmem] * len(arrays),
+        out_specs=smem,
+        compiler_params=pltpu.CompilerParams(vmem_limit_bytes=VMEM_LIMIT),
+        cost_estimate=COST,
+        name="hold",
+    )(own, *arrays)
 
 
 def total_kernel(*refs):
@@ -209,17 +209,10 @@
     out_ref[...] = sum(ref[...].astype(F32) for ref in refs).astype(BF16)
 
 
-def joined_kernel(whole_ref, *refs):
-    *refs, out_ref = refs
-    for n, ref in enumerate(refs):
-        rows = slice(n * PIECE, (n + 1) * PIECE)
-        out_ref[rows, :] = (whole_ref[rows, :].astype(F32) + ref[...].astype(F32)).astype(BF16)
-
-
-def total(*values, kernel=total_kernel):
-    vmem = pl.BlockSpec(memory_space=pltpu.VMEM)
-    return pl.pallas_call(
-        kernel,
+def total(*values):
+    vmem = pl.BlockSpec(memory_space=pltpu.VMEM)
+    return pl.pallas_call(
+        total_kernel,
         out_shape=jax.ShapeDtypeStruct(values[0].shape, BF16),
         in_specs=[vmem] * len(values),
         out_specs=vmem,
@@ -252,18 +245,17 @@
     own = (lax.axis_index("expert") // spread).astype(jnp.int32).reshape(1)
     picks_t = picks.T
     core, side = 1, 2
-    weights = (gate_weight, up_weight, down_weight)
-
-    half = (capacity // 2 + 15) // 16 * 16 if capacity >= 64 else capacity
-    cuts = [(first, min(half, capacity - first)) for first in range(0, capacity, half)]
+    weights = [gate_weight, up_weight, down_weight]
+    weights += [swap(weight, core) for weight in weights]
+
+    half = capacity // 2 // 16 * 16 if capacity >= 64 else capacity
+    cuts = [(0, half), (half, capacity - half)] if half < capacity else [(0, capacity)]
     chunks = [(k, 0, capacity) for k in range(min(2, experts))]
-    near_count = len(chunks)
+    travelling = len(chunks)
     chunks += [(k, first, count) for k in range(2, experts) for first, count in cuts]
-    travelling = list(range(near_count, len(chunks)))
     sent = pack(own, tokens, norm_gain[None, :], picks_t, tuple(chunks))
     order = Order(own)
-    near, far, beside, across = list(sent), {}, {}, {}
-    mine, theirs, other_mine, other_theirs, back = {}, {}, {}, {}, {}
+    near, far, mine, theirs, back = list(sent), {}, {}, {}, {}
 
     def leave(n):
         near[n] = swap(order.late(near[n]), chunks[n][0] * spread)
@@ -272,28 +264,17 @@
         near[n] = order.mark_one(near[n])
 
     def share(n):
-        far[n], beside[n] = swap(order.late(near[n]), side), swap(order.late(near[n]), core)
+        far[n] = swap(order.late(near[n]), side)
 
     def meet(n):
         far[n] = order.mark_one(far[n])
-        pieces = order.mark(*cut(far[n])) if n in travelling else [far[n]]
-        across[n] = [swap(piece, core) for piece in pieces]
 
     def work(n):
-        rows = [order.late(rows) for rows in (near[n], far[n], beside[n], *across[n])]
-        mine[n], theirs[n], other, *pieces = order.mark(*expert_block(rows, *weights))
-        other_theirs[n] = [swap(piece, core) for piece in pieces]
-        other_mine[n] = swap(other, core)
-
-    def half_way(n):
-        pieces = order.mark(*other_theirs[n])
-        theirs[n] = order.mark_one(total(theirs[n], *pieces, kernel=joined_kernel))
-
-    def cross(n):
-        theirs[n] = swap(order.late(theirs[n]), side)
+        mine[n], part = order.mark(*expert_block(order.late(near[n]), order.late(far[n]), weights))
+        theirs[n] = swap(part, side)
 
     def home(n):
-        back[n] = order.mark_one(total(mine[n], other_mine[n], order.mark_one(theirs[n])))
+        back[n] = order.mark_one(total(mine[n], order.mark_one(theirs[n])))
 
     def leave_back(n):
         back[n] = swap(order.late(back[n]), chunks[n][0] * spread)
@@ -301,59 +282,50 @@
     def arrive_back(n):
         back[n] = order.mark_one(back[n])
 
-    far_count = len(travelling)
-    begin_back = max(far_count, 4)
-    steps = begin_back + far_count
-
-    def at(step):
-        return travelling[step] if 0 <= step < far_count else None
-
+    count = len(chunks) - travelling
+    begin_back = max(count, 4)
+    steps = max(begin_back + count, 8)
     for step in range(steps):
-        out, shared, worked, crossing, back_now = (
-            at(step), at(step - 1), at(step - 2), at(step - 3), at(step - begin_back)
+        out, shared, worked, crossing, coming = (
+            travelling + step - late if 0 <= step - late < count else None
+            for late in (0, 1, 2, 3, begin_back)
         )
         if out is not None:
             leave(out)
-        if back_now is not None:
-            leave_back(back_now)
+        if coming is not None:
+            leave_back(coming)
+        if step == 0:
+            share(0)
+            own = order.mark_one(hold(order.late(own), weights[:3]))
+        if step == 1:
+            meet(0)
         if shared is not None:
             share(shared)
-        if step == 0:
-            share(0)
-            leave(1)
-            meet(0)
         if worked is not None:
             work(worked)
+        if step == 2 and experts > 1:
+            arrive(1)
+            share(1)
+        if step == steps - 4 and experts > 1:
+            meet(1)
+            work(1)
         if shared is not None:
             meet(shared)
-        if worked is not None:
-            half_way(worked)
-            cross(worked)
         if crossing is not None:
             home(crossing)
-        if step == 1:
-            arrive(1)
-            share(1)
-        if step == 2:
-            meet(1)
-        if step == 3:
+        if step == 1 and experts > 1:
+            leave(1)
+        if step == steps - 3:
+            if experts > 1:
+                home(1)
+                leave_back(1)
             work(0)
-        if step == 4:
-            work(1)
-        if step == steps - 3:
-            half_way(1)
-            cross(1)
-        if step == steps - 2:
-            half_way(0)
-            cross(0)
-            home(1)
-            leave_back(1)
         if step == steps - 1:
             home(0)
         if out is not None:
             arrive(out)
-        if back_now is not None:
-            arrive_back(back_now)
+        if coming is not None:
+            arrive_back(coming)
     blocks = [back[n] for n in range(len(chunks))]
     local = score(
         own,

time: 186 us -> 171 us (0.919)
  waiting for transfers between devices: 109 us -> 62.7 us
  Pallas kernels: 20.4 us -> 53.4 us
    ppermute x70 -> x29, waiting for transfers between devices: 109 us -> 62.7 us  [swap(): return lax.ppermute(value, 'expert', pairs)]
    pallas_call x22 -> x13, Pallas kernels: 17.2 us -> 49.6 us  [the longest x6 48.5 us: expert_block(): pl.pallas_call(expert_kernel, out_shape=[jax.ShapeDtypeStruct((count, wid...]
    ppermute x70 -> x29, starting transfers between devices: 45.5 us -> 43.9 us  [swap(): return lax.ppermute(value, 'expert', pairs)]
    unnamed x30 -> x34, local copies, waits for them, and re-layouts: 8.02 us -> 8.03 us
  transfers between devices with their start and end apart: 70 -> 29, of which waited for: 28 -> 15; matrix products, arithmetic and copies ran while one was open for 0% -> 1% of each run, Pallas kernels for 9% -> 30%
where the time goes in v4:
time: 171 us
  waiting for transfers between devices  62.7 us (37%)
  Pallas kernels  53.4 us (31%)
  starting transfers between devices  43.9 us (26%)
  local copies, waits for them, and re-layouts  9.15 us (5%)
    ppermute x29, waiting for transfers between devices, swap(): return lax.ppermute(value, 'expert', pairs)  62.7 us
    pallas_call x6, Pallas kernels, expert_block(): pl.pallas_call(expert_kernel, out_shape=[jax.ShapeDtypeStruct((count, wid...  48.5 us
    ppermute x29, starting transfers between devices, swap(): return lax.ppermute(value, 'expert', pairs)  43.9 us
    unnamed x34, local copies, waits for them, and re-layouts  8.03 us
  transfers between devices with their start and end apart: 29, of which 15 were waited for; matrix products, arithmetic and copies ran while one was open for 1% of the time, Pallas kernels for 30%

profile of v4, /device:TPU:0, one launch (start us, length us, event | category | flops | bytes accessed | tf_op | source)
XLA Modules:
  0.0 170.6 jit_solution(3491106529533680805)
XLA Ops:
  5.5 2.7 %collective-permute-start.1 = (bf16[80,3584]{1,0:T(8,128)(2,1)S(1)}, bf16[80,3584]{1,0:T(8,128)(2,1)S(1)}, u32[]{:S(2)}, u32[]{:S(2)}) collective-permute-start(bf16[80,3584]{1,0:T(8,128)(2,1)S(1)} %get-tuple-element.202.near_ref), channel_id=1, source_target_pairs={{0,2},{1,3},{2,0},{3,1},{4,6},{5,7},{6,4},{7,5},{8,10},{9,11},{10,... | collective-permute-start | bytes 1720328 | tf_op jit(solution)/shard_map/ppermute | solution.py:25
  8.1 2.6 %collective-permute-start = (bf16[32,3584]{1,0:T(8,128)(2,1)S(1)}, bf16[32,3584]{1,0:T(8,128)(2,1)S(1)}, u32[]{:S(2)}, u32[]{:S(2)}) collective-permute-start(bf16[32,3584]{1,0:T(8,128)(2,1)S(1)} %get-tuple-element.123), channel_id=1, source_target_pairs={{0,8},{1,9},{2,10},{3,11},{4,12},{5,13},{6,14},{7,15},{8,0},{9,1},... | collective-permute-start | bytes 688136 | tf_op jit(solution)/shard_map/ppermute | solution.py:25
  17.4 4.2 %collective-permute-done.near_ref = bf16[32,3584]{1,0:T(8,128)(2,1)S(1)} collective-permute-done((bf16[32,3584]{1,0:T(8,128)(2,1)S(1)}, bf16[32,3584]{1,0:T(8,128)(2,1)S(1)}, u32[]{:S(2)}, u32[]{:S(2)}) %collective-permute-start) | collective-permute-done | bytes 229408 | tf_op jit(solution)/shard_map/ppermute | solution.py:25
  23.5 2.6 %collective-permute-start.4 = (bf16[48,3584]{1,0:T(8,128)(2,1)S(1)}, bf16[48,3584]{1,0:T(8,128)(2,1)S(1)}, u32[]{:S(2)}, u32[]{:S(2)}) collective-permute-start(bf16[48,3584]{1,0:T(8,128)(2,1)S(1)} %get-tuple-element.133), channel_id=1, source_target_pairs={{0,8},{1,9},{2,10},{3,11},{4,12},{5,13},{6,14},{7,15},{8,0},{9,1},... | collective-permute-start | bytes 1032200 | tf_op jit(solution)/shard_map/ppermute | solution.py:25
  26.1 3.0 %collective-permute-done.2.far_ref = bf16[32,3584]{1,0:T(8,128)(2,1)S(1)} collective-permute-done((bf16[32,3584]{1,0:T(8,128)(2,1)S(1)}, bf16[32,3584]{1,0:T(8,128)(2,1)S(1)}, u32[]{:S(2)}, u32[]{:S(2)}) %collective-permute-start.2) | collective-permute-done | bytes 229408 | tf_op jit(solution)/shard_map/ppermute | solution.py:25
  30.7 10.5 %collective-permute-done.4.near_ref = bf16[48,3584]{1,0:T(8,128)(2,1)S(1)} collective-permute-done((bf16[48,3584]{1,0:T(8,128)(2,1)S(1)}, bf16[48,3584]{1,0:T(8,128)(2,1)S(1)}, u32[]{:S(2)}, u32[]{:S(2)}) %collective-permute-start.4) | collective-permute-done | bytes 344096 | tf_op jit(solution)/shard_map/ppermute | solution.py:25
  41.7 3.5 %collective-permute-start.9 = (bf16[32,3584]{1,0:T(8,128)(2,1)S(1)}, bf16[32,3584]{1,0:T(8,128)(2,1)S(1)}, u32[]{:S(2)}, u32[]{:S(2)}) collective-permute-start(bf16[32,3584]{1,0:T(8,128)(2,1)S(1)} %get-tuple-element.143), channel_id=1, source_target_pairs={{0,12},{1,13},{2,14},{3,15},{4,8},{5,9},{6,10},{7,11},{8,4},{9,5},... | collective-permute-start | bytes 688136 | tf_op jit(solution)/shard_map/ppermute | solution.py:25
  45.2 8.2 %expert_block.6 = (bf16[32,3584]{1,0:T(8,128)(2,1)S(1)}, bf16[32,3584]{1,0:T(8,128)(2,1)S(1)}) custom-call(bf16[32,3584]{1,0:T(8,128)(2,1)S(1)} %collective-permute-done.near_ref, bf16[32,3584]{1,0:T(8,128)(2,1)S(1)} %collective-permute-done.2.far_ref, bf16[3584,512]{1,0:T(8,128)(2,1)S(1)} %copy-done.1, bf16[3584,512]{1,0:T(8,128)(2,1)S(1)} %copy-done.3, ...), custom_call_target="tpu_custom_call" | custom-call | flops 1024 | bytes 1024 | tf_op jit(solution)/shard_map/expert_block/pallas_call | solution.py:96
  55.4 4.7 %collective-permute-start.11 = (bf16[48,3584]{1,0:T(8,128)(2,1)S(1)}, bf16[48,3584]{1,0:T(8,128)(2,1)S(1)}, u32[]{:S(2)}, u32[]{:S(2)}) collective-permute-start(bf16[48,3584]{1,0:T(8,128)(2,1)S(1)} %get-tuple-element.150), channel_id=1, source_target_pairs={{0,12},{1,13},{2,14},{3,15},{4,8},{5,9},{6,10},{7,11},{8,4},{9,5},... | collective-permute-start | bytes 1032200 | tf_op jit(solution)/shard_map/ppermute | solution.py:25
  62.1 7.9 %expert_block.7 = (bf16[48,3584]{1,0:T(8,128)(2,1)S(1)}, bf16[48,3584]{1,0:T(8,128)(2,1)S(1)}) custom-call(bf16[48,3584]{1,0:T(8,128)(2,1)S(1)} %collective-permute-done.4.near_ref, bf16[48,3584]{1,0:T(8,128)(2,1)S(1)} %collective-permute-done.10.far_ref, bf16[3584,512]{1,0:T(8,128)(2,1)S(1)} %copy-done.1, bf16[3584,512]{1,0:T(8,128)(2,1)S(1)} %copy-done.3, ...), custom_call_target="tpu_custom_call" | custom-call | flops 1024 | bytes 1024 | tf_op jit(solution)/shard_map/expert_block/pallas_call | solution.py:96
  70.0 4.9 %collective-permute-done.13.far_ref = bf16[32,3584]{1,0:T(8,128)(2,1)S(1)} collective-permute-done((bf16[32,3584]{1,0:T(8,128)(2,1)S(1)}, bf16[32,3584]{1,0:T(8,128)(2,1)S(1)}, u32[]{:S(2)}, u32[]{:S(2)}) %collective-permute-start.13) | collective-permute-done | bytes 229408 | tf_op jit(solution)/shard_map/ppermute | solution.py:25
  74.9 2.7 %collective-permute-done.12.refs_1_ = bf16[32,3584]{1,0:T(8,128)(2,1)S(1)} collective-permute-done((bf16[32,3584]{1,0:T(8,128)(2,1)S(1)}, bf16[32,3584]{1,0:T(8,128)(2,1)S(1)}, u32[]{:S(2)}, u32[]{:S(2)}) %collective-permute-start.12) | collective-permute-done | bytes 229408 | tf_op jit(solution)/shard_map/ppermute | solution.py:25
  79.8 8.2 %expert_block.8 = (bf16[32,3584]{1,0:T(8,128)(2,1)S(1)}, bf16[32,3584]{1,0:T(8,128)(2,1)S(1)}) custom-call(bf16[32,3584]{1,0:T(8,128)(2,1)S(1)} %collective-permute-done.9.near_ref, bf16[32,3584]{1,0:T(8,128)(2,1)S(1)} %collective-permute-done.13.far_ref, bf16[3584,512]{1,0:T(8,128)(2,1)S(1)} %copy-done.1, bf16[3584,512]{1,0:T(8,128)(2,1)S(1)} %copy-done.3, ...), custom_call_target="tpu_custom_call" | custom-call | flops 1024 | bytes 1024 | tf_op jit(solution)/shard_map/expert_block/pallas_call | solution.py:96
  88.0 8.2 %expert_block.9 = (bf16[80,3584]{1,0:T(8,128)(2,1)S(1)}, bf16[80,3584]{1,0:T(8,128)(2,1)S(1)}) custom-call(bf16[80,3584]{1,0:T(8,128)(2,1)S(1)} %collective-permute-done.3.near_ref, bf16[80,3584]{1,0:T(8,128)(2,1)S(1)} %collective-permute-done.8.far_ref, bf16[3584,512]{1,0:T(8,128)(2,1)S(1)} %copy-done.1, bf16[3584,512]{1,0:T(8,128)(2,1)S(1)} %copy-done.3, ...), custom_call_target="tpu_custom_call" | custom-call | flops 1024 | bytes 1024 | tf_op jit(solution)/shard_map/expert_block/pallas_call | solution.py:96
  100.3 8.1 %collective-permute-done.16.refs_2_ = bf16[32,3584]{1,0:T(8,128)(2,1)S(1)} collective-permute-done((bf16[32,3584]{1,0:T(8,128)(2,1)S(1)}, bf16[32,3584]{1,0:T(8,128)(2,1)S(1)}, u32[]{:S(2)}, u32[]{:S(2)}) %collective-permute-start.16) | collective-permute-done | bytes 229408 | tf_op jit(solution)/shard_map/ppermute | solution.py:25
  108.7 7.9 %expert_block.10 = (bf16[48,3584]{1,0:T(8,128)(2,1)S(1)}, bf16[48,3584]{1,0:T(8,128)(2,1)S(1)}) custom-call(bf16[48,3584]{1,0:T(8,128)(2,1)S(1)} %collective-permute-done.11.near_ref, bf16[48,3584]{1,0:T(8,128)(2,1)S(1)} %collective-permute-done.18.far_ref, bf16[3584,512]{1,0:T(8,128)(2,1)S(1)} %copy-done.1, bf16[3584,512]{1,0:T(8,128)(2,1)S(1)} %copy-done.3, ...), custom_call_target="tpu_custom_call" | custom-call | flops 1024 | bytes 1024 | tf_op jit(solution)/shard_map/expert_block/pallas_call | solution.py:96
  118.7 8.1 %expert_block.11 = (bf16[80,3584]{1,0:T(8,128)(2,1)S(1)}, bf16[80,3584]{1,0:T(8,128)(2,1)S(1)}) custom-call(bf16[80,3584]{1,0:T(8,128)(2,1)S(1)} %get-tuple-element.202.near_ref, bf16[80,3584]{1,0:T(8,128)(2,1)S(1)} %collective-permute-done.1.far_ref, bf16[3584,512]{1,0:T(8,128)(2,1)S(1)} %copy-done.1, bf16[3584,512]{1,0:T(8,128)(2,1)S(1)} %copy-done.3, ...), custom_call_target="tpu_custom_call" | custom-call | flops 1024 | bytes 1024 | tf_op jit(solution)/shard_map/expert_block/pallas_call | solution.py:96
  126.8 3.0 %collective-permute-start.21 = (bf16[32,3584]{1,0:T(8,128)(2,1)S(1)}, bf16[32,3584]{1,0:T(8,128)(2,1)S(1)}, u32[]{:S(2)}, u32[]{:S(2)}) collective-permute-start(bf16[32,3584]{1,0:T(8,128)(2,1)S(1)} %total.8), channel_id=1, source_target_pairs={{0,12},{1,13},{2,14},{3,15},{4,8},{5,9},{6,10},{7,11},{8,4},{9,5},... | collective-permute-start | bytes 688136 | tf_op jit(solution)/shard_map/ppermute | solution.py:25
  130.9 6.3 %collective-permute-done.21.refs_4_ = bf16[32,3584]{1,0:T(8,128)(2,1)S(1)} collective-permute-done((bf16[32,3584]{1,0:T(8,128)(2,1)S(1)}, bf16[32,3584]{1,0:T(8,128)(2,1)S(1)}, u32[]{:S(2)}, u32[]{:S(2)}) %collective-permute-start.21) | collective-permute-done | bytes 229408 | tf_op jit(solution)/shard_map/ppermute | solution.py:25
  137.2 2.9 %collective-permute-start.24 = (bf16[48,3584]{1,0:T(8,128)(2,1)S(1)}, bf16[48,3584]{1,0:T(8,128)(2,1)S(1)}, u32[]{:S(2)}, u32[]{:S(2)}) collective-permute-start(bf16[48,3584]{1,0:T(8,128)(2,1)S(1)} %total.10), channel_id=1, source_target_pairs={{0,12},{1,13},{2,14},{3,15},{4,8},{5,9},{6,10},{7,11},{8,4},{9,5},... | collective-permute-start | bytes 1032200 | tf_op jit(solution)/shard_map/ppermute | solution.py:25
  142.3 12.0 %collective-permute-done.24.refs_5_ = bf16[48,3584]{1,0:T(8,128)(2,1)S(1)} collective-permute-done((bf16[48,3584]{1,0:T(8,128)(2,1)S(1)}, bf16[48,3584]{1,0:T(8,128)(2,1)S(1)}, u32[]{:S(2)}, u32[]{:S(2)}) %collective-permute-start.24) | collective-permute-done | bytes 344096 | tf_op jit(solution)/shard_map/ppermute | solution.py:25
  154.4 2.6 %score.1 = f32[1,16]{1,0:T(1,128)S(1)} custom-call(s32[1]{0:T(128)} %hold.1.own_ref, bf16[128,3584]{1,0:T(8,128)(2,1)S(1)} %copy-done.7, f32[1,3584]{1,0:T(1,128)S(1)} %broadcast_in_dim.12.gain_ref, s32[2,128]{1,0:T(2,128)S(1)} %bitcast.8, f32[2,128]{1,0:T(2,128)S(1)} %bitcast.9, bf16[128,3584]{1,0:T(8,128)(2,1)S(1)} %copy-done.8, f32[1,128]{1,0:T(1,128)S(1)} %bitcast.10, ...), custom_call_target="tpu_custom_call" | custom-call | flops 1024 | bytes 1024 | tf_op jit(solution)/shard_map/score/pallas_call | solution.py:158
  158.6 3.0 %collective-permute-done.26 = f32[1,16]{1,0:T(1,128)S(1)} collective-permute-done((f32[1,16]{1,0:T(1,128)S(1)}, f32[1,16]{1,0:T(1,128)S(1)}, u32[]{:S(2)}, u32[]{:S(2)}) %collective-permute-start.26) | collective-permute-done | bytes 96 | tf_op jit(solution)/shard_map/ppermute | solution.py:25
  167.3 2.6 %collective-permute-done.28 = f32[1,16]{1,0:T(1,128)S(1)} collective-permute-done((f32[1,16]{1,0:T(1,128)S(1)}, f32[1,16]{1,0:T(1,128)S(1)}, u32[]{:S(2)}, u32[]{:S(2)}) %collective-permute-start.28) | collective-permute-done | bytes 96 | tf_op jit(solution)/shard_map/ppermute | solution.py:25
  (94 shorter events, 39.2 us)
Async XLA Ops:
  0.6 41.0 %collective-permute-start.5 = (bf16[3584,512]{1,0:T(8,128)(2,1)}, bf16[3584,512]{1,0:T(8,128)(2,1)}, u32[]{:S(2)}, u32[]{:S(2)}) collective-permute-start(bf16[3584,512]{1,0:T(8,128)(2,1)} %refs_0_.13), channel_id=1, source_target_pairs={{0,1},{1,0},{2,3},{3,2},{4,5},{5,4},{6,7},{7,6},{8,9},{9,8},{10,11... | collective-permute-start | bytes 11010056 | tf_op jit(solution)/shard_map/ppermute | solution.py:25
  1.1 44.0 %collective-permute-start.6 = (bf16[3584,512]{1,0:T(8,128)(2,1)}, bf16[3584,512]{1,0:T(8,128)(2,1)}, u32[]{:S(2)}, u32[]{:S(2)}) collective-permute-start(bf16[3584,512]{1,0:T(8,128)(2,1)} %refs_1_.13), channel_id=1, source_target_pairs={{0,1},{1,0},{2,3},{3,2},{4,5},{5,4},{6,7},{7,6},{8,9},{9,8},{10,11... | collective-permute-start | bytes 11010056 | tf_op jit(solution)/shard_map/ppermute | solution.py:25
  1.2 44.0 %collective-permute-start.7 = (bf16[512,3584]{1,0:T(8,128)(2,1)}, bf16[512,3584]{1,0:T(8,128)(2,1)}, u32[]{:S(2)}, u32[]{:S(2)}) collective-permute-start(bf16[512,3584]{1,0:T(8,128)(2,1)} %refs_2_.13), channel_id=1, source_target_pairs={{0,1},{1,0},{2,3},{3,2},{4,5},{5,4},{6,7},{7,6},{8,9},{9,8},{10,11... | collective-permute-start | bytes 11010056 | tf_op jit(solution)/shard_map/ppermute | solution.py:25
  5.5 16.2 %collective-permute-start.1 = (bf16[80,3584]{1,0:T(8,128)(2,1)S(1)}, bf16[80,3584]{1,0:T(8,128)(2,1)S(1)}, u32[]{:S(2)}, u32[]{:S(2)}) collective-permute-start(bf16[80,3584]{1,0:T(8,128)(2,1)S(1)} %get-tuple-element.202.near_ref), channel_id=1, source_target_pairs={{0,2},{1,3},{2,0},{3,1},{4,6},{5,7},{6,4},{7,5},{8,10},{9,11},{10,... | collective-permute-start | bytes 1720328 | tf_op jit(solution)/shard_map/ppermute | solution.py:25
  8.1 13.5 %collective-permute-start = (bf16[32,3584]{1,0:T(8,128)(2,1)S(1)}, bf16[32,3584]{1,0:T(8,128)(2,1)S(1)}, u32[]{:S(2)}, u32[]{:S(2)}) collective-permute-start(bf16[32,3584]{1,0:T(8,128)(2,1)S(1)} %get-tuple-element.123), channel_id=1, source_target_pairs={{0,8},{1,9},{2,10},{3,11},{4,12},{5,13},{6,14},{7,15},{8,0},{9,1},... | collective-permute-start | bytes 688136 | tf_op jit(solution)/shard_map/ppermute | solution.py:25
  23.5 17.7 %collective-permute-start.4 = (bf16[48,3584]{1,0:T(8,128)(2,1)S(1)}, bf16[48,3584]{1,0:T(8,128)(2,1)S(1)}, u32[]{:S(2)}, u32[]{:S(2)}) collective-permute-start(bf16[48,3584]{1,0:T(8,128)(2,1)S(1)} %get-tuple-element.133), channel_id=1, source_target_pairs={{0,8},{1,9},{2,10},{3,11},{4,12},{5,13},{6,14},{7,15},{8,0},{9,1},... | collective-permute-start | bytes 1032200 | tf_op jit(solution)/shard_map/ppermute | solution.py:25
  29.1 25.0 %collective-permute-start.3 = (bf16[80,3584]{1,0:T(8,128)(2,1)S(1)}, bf16[80,3584]{1,0:T(8,128)(2,1)S(1)}, u32[]{:S(2)}, u32[]{:S(2)}) collective-permute-start(bf16[80,3584]{1,0:T(8,128)(2,1)S(1)} %get-tuple-element.131), channel_id=1, source_target_pairs={{0,4},{1,5},{2,6},{3,7},{4,0},{5,1},{6,2},{7,3},{8,12},{9,13},{10,... | collective-permute-start | bytes 1720328 | tf_op jit(solution)/shard_map/ppermute | solution.py:25
  41.2 14.2 %collective-permute-start.10 = (bf16[48,3584]{1,0:T(8,128)(2,1)S(1)}, bf16[48,3584]{1,0:T(8,128)(2,1)S(1)}, u32[]{:S(2)}, u32[]{:S(2)}) collective-permute-start(bf16[48,3584]{1,0:T(8,128)(2,1)S(1)} %collective-permute-done.4.near_ref), channel_id=1, source_target_pairs={{0,2},{1,3},{2,0},{3,1},{4,6},{5,7},{6,4},{7,5},{8,10},{9,11},{10,... | collective-permute-start | bytes 1032200 | tf_op jit(solution)/shard_map/ppermute | solution.py:25
  41.7 13.7 %collective-permute-start.9 = (bf16[32,3584]{1,0:T(8,128)(2,1)S(1)}, bf16[32,3584]{1,0:T(8,128)(2,1)S(1)}, u32[]{:S(2)}, u32[]{:S(2)}) collective-permute-start(bf16[32,3584]{1,0:T(8,128)(2,1)S(1)} %get-tuple-element.143), channel_id=1, source_target_pairs={{0,12},{1,13},{2,14},{3,15},{4,8},{5,9},{6,10},{7,11},{8,4},{9,5},... | collective-permute-start | bytes 688136 | tf_op jit(solution)/shard_map/ppermute | solution.py:25
  54.1 33.9 %collective-permute-start.8 = (bf16[80,3584]{1,0:T(8,128)(2,1)S(1)}, bf16[80,3584]{1,0:T(8,128)(2,1)S(1)}, u32[]{:S(2)}, u32[]{:S(2)}) collective-permute-start(bf16[80,3584]{1,0:T(8,128)(2,1)S(1)} %collective-permute-done.3.near_ref), channel_id=1, source_target_pairs={{0,2},{1,3},{2,0},{3,1},{4,6},{5,7},{6,4},{7,5},{8,10},{9,11},{10,... | collective-permute-start | bytes 1720328 | tf_op jit(solution)/shard_map/ppermute | solution.py:25
  55.4 22.3 %collective-permute-start.11 = (bf16[48,3584]{1,0:T(8,128)(2,1)S(1)}, bf16[48,3584]{1,0:T(8,128)(2,1)S(1)}, u32[]{:S(2)}, u32[]{:S(2)}) collective-permute-start(bf16[48,3584]{1,0:T(8,128)(2,1)S(1)} %get-tuple-element.150), channel_id=1, source_target_pairs={{0,12},{1,13},{2,14},{3,15},{4,8},{5,9},{6,10},{7,11},{8,4},{9,5},... | collective-permute-start | bytes 1032200 | tf_op jit(solution)/shard_map/ppermute | solution.py:25
  60.1 14.8 %collective-permute-start.13 = (bf16[32,3584]{1,0:T(8,128)(2,1)S(1)}, bf16[32,3584]{1,0:T(8,128)(2,1)S(1)}, u32[]{:S(2)}, u32[]{:S(2)}) collective-permute-start(bf16[32,3584]{1,0:T(8,128)(2,1)S(1)} %collective-permute-done.9.near_ref), channel_id=1, source_target_pairs={{0,2},{1,3},{2,0},{3,1},{4,6},{5,7},{6,4},{7,5},{8,10},{9,11},{10,... | collective-permute-start | bytes 688136 | tf_op jit(solution)/shard_map/ppermute | solution.py:25
  60.6 17.0 %collective-permute-start.12 = (bf16[32,3584]{1,0:T(8,128)(2,1)S(1)}, bf16[32,3584]{1,0:T(8,128)(2,1)S(1)}, u32[]{:S(2)}, u32[]{:S(2)}) collective-permute-start(bf16[32,3584]{1,0:T(8,128)(2,1)S(1)} %get-tuple-element.152), channel_id=1, source_target_pairs={{0,2},{1,3},{2,0},{3,1},{4,6},{5,7},{6,4},{7,5},{8,10},{9,11},{10,... | collective-permute-start | bytes 688136 | tf_op jit(solution)/shard_map/ppermute | solution.py:25
  77.7 22.5 %collective-permute-start.18 = (bf16[48,3584]{1,0:T(8,128)(2,1)S(1)}, bf16[48,3584]{1,0:T(8,128)(2,1)S(1)}, u32[]{:S(2)}, u32[]{:S(2)}) collective-permute-start(bf16[48,3584]{1,0:T(8,128)(2,1)S(1)} %collective-permute-done.11.near_ref), channel_id=1, source_target_pairs={{0,2},{1,3},{2,0},{3,1},{4,6},{5,7},{6,4},{7,5},{8,10},{9,11},{10,... | collective-permute-start | bytes 1032200 | tf_op jit(solution)/shard_map/ppermute | solution.py:25
  79.2 20.9 %collective-permute-start.17 = (bf16[48,3584]{1,0:T(8,128)(2,1)S(1)}, bf16[48,3584]{1,0:T(8,128)(2,1)S(1)}, u32[]{:S(2)}, u32[]{:S(2)}) collective-permute-start(bf16[48,3584]{1,0:T(8,128)(2,1)S(1)} %get-tuple-element.183), channel_id=1, source_target_pairs={{0,2},{1,3},{2,0},{3,1},{4,6},{5,7},{6,4},{7,5},{8,10},{9,11},{10,... | collective-permute-start | bytes 1032200 | tf_op jit(solution)/shard_map/ppermute | solution.py:25
  96.2 22.2 %collective-permute-start.14 = (bf16[80,3584]{1,0:T(8,128)(2,1)S(1)}, bf16[80,3584]{1,0:T(8,128)(2,1)S(1)}, u32[]{:S(2)}, u32[]{:S(2)}) collective-permute-start(bf16[80,3584]{1,0:T(8,128)(2,1)S(1)} %get-tuple-element.176), channel_id=1, source_target_pairs={{0,2},{1,3},{2,0},{3,1},{4,6},{5,7},{6,4},{7,5},{8,10},{9,11},{10,... | collective-permute-start | bytes 1720328 | tf_op jit(solution)/shard_map/ppermute | solution.py:25
  97.8 10.6 %collective-permute-start.16 = (bf16[32,3584]{1,0:T(8,128)(2,1)S(1)}, bf16[32,3584]{1,0:T(8,128)(2,1)S(1)}, u32[]{:S(2)}, u32[]{:S(2)}) collective-permute-start(bf16[32,3584]{1,0:T(8,128)(2,1)S(1)} %total.6), channel_id=1, source_target_pairs={{0,8},{1,9},{2,10},{3,11},{4,12},{5,13},{6,14},{7,15},{8,0},{9,1},... | collective-permute-start | bytes 688136 | tf_op jit(solution)/shard_map/ppermute | solution.py:25
  108.4 18.5 %collective-permute-start.20 = (bf16[48,3584]{1,0:T(8,128)(2,1)S(1)}, bf16[48,3584]{1,0:T(8,128)(2,1)S(1)}, u32[]{:S(2)}, u32[]{:S(2)}) collective-permute-start(bf16[48,3584]{1,0:T(8,128)(2,1)S(1)} %total.7), channel_id=1, source_target_pairs={{0,8},{1,9},{2,10},{3,11},{4,12},{5,13},{6,14},{7,15},{8,0},{9,1},... | collective-permute-start | bytes 1032200 | tf_op jit(solution)/shard_map/ppermute | solution.py:25
  108.4 10.0 %collective-permute-start.15 = (bf16[32,3584]{1,0:T(8,128)(2,1)S(1)}, bf16[32,3584]{1,0:T(8,128)(2,1)S(1)}, u32[]{:S(2)}, u32[]{:S(2)}) collective-permute-start(bf16[32,3584]{1,0:T(8,128)(2,1)S(1)} %get-tuple-element.178), channel_id=1, source_target_pairs={{0,2},{1,3},{2,0},{3,1},{4,6},{5,7},{6,4},{7,5},{8,10},{9,11},{10,... | collective-permute-start | bytes 688136 | tf_op jit(solution)/shard_map/ppermute | solution.py:25
  116.6 14.2 %collective-permute-start.22 = (bf16[48,3584]{1,0:T(8,128)(2,1)S(1)}, bf16[48,3584]{1,0:T(8,128)(2,1)S(1)}, u32[]{:S(2)}, u32[]{:S(2)}) collective-permute-start(bf16[48,3584]{1,0:T(8,128)(2,1)S(1)} %get-tuple-element.216), channel_id=1, source_target_pairs={{0,2},{1,3},{2,0},{3,1},{4,6},{5,7},{6,4},{7,5},{8,10},{9,11},{10,... | collective-permute-start | bytes 1032200 | tf_op jit(solution)/shard_map/ppermute | solution.py:25
  126.8 10.4 %collective-permute-start.21 = (bf16[32,3584]{1,0:T(8,128)(2,1)S(1)}, bf16[32,3584]{1,0:T(8,128)(2,1)S(1)}, u32[]{:S(2)}, u32[]{:S(2)}) collective-permute-start(bf16[32,3584]{1,0:T(8,128)(2,1)S(1)} %total.8), channel_id=1, source_target_pairs={{0,12},{1,13},{2,14},{3,15},{4,8},{5,9},{6,10},{7,11},{8,4},{9,5},... | collective-permute-start | bytes 688136 | tf_op jit(solution)/shard_map/ppermute | solution.py:25
  129.8 12.3 %collective-permute-start.19 = (bf16[80,3584]{1,0:T(8,128)(2,1)S(1)}, bf16[80,3584]{1,0:T(8,128)(2,1)S(1)}, u32[]{:S(2)}, u32[]{:S(2)}) collective-permute-start(bf16[80,3584]{1,0:T(8,128)(2,1)S(1)} %get-tuple-element.208), channel_id=1, source_target_pairs={{0,2},{1,3},{2,0},{3,1},{4,6},{5,7},{6,4},{7,5},{8,10},{9,11},{10,... | collective-permute-start | bytes 1720328 | tf_op jit(solution)/shard_map/ppermute | solution.py:25
  130.2 24.1 %collective-permute-start.23 = (bf16[80,3584]{1,0:T(8,128)(2,1)S(1)}, bf16[80,3584]{1,0:T(8,128)(2,1)S(1)}, u32[]{:S(2)}, u32[]{:S(2)}) collective-permute-start(bf16[80,3584]{1,0:T(8,128)(2,1)S(1)} %total.9), channel_id=1, source_target_pairs={{0,4},{1,5},{2,6},{3,7},{4,0},{5,1},{6,2},{7,3},{8,12},{9,13},{10,... | collective-permute-start | bytes 1720328 | tf_op jit(solution)/shard_map/ppermute | solution.py:25
  137.2 17.1 %collective-permute-start.24 = (bf16[48,3584]{1,0:T(8,128)(2,1)S(1)}, bf16[48,3584]{1,0:T(8,128)(2,1)S(1)}, u32[]{:S(2)}, u32[]{:S(2)}) collective-permute-start(bf16[48,3584]{1,0:T(8,128)(2,1)S(1)} %total.10), channel_id=1, source_target_pairs={{0,12},{1,13},{2,14},{3,15},{4,8},{5,9},{6,10},{7,11},{8,4},{9,5},... | collective-permute-start | bytes 1032200 | tf_op jit(solution)/shard_map/ppermute | solution.py:25
  (22 other events, 387.1 us)

commit v5 on v4

--- a/solution.py
+++ b/solution.py
@@ -16,7 +16,7 @@
 
 F32 = jnp.float32
 BF16 = jnp.bfloat16
-VMEM_LIMIT = 20 * 1024 * 1024
+VMEM_LIMIT = 10 * 1024 * 1024
 COST = pl.CostEstimate(flops=1024, bytes_accessed=1024, transcendentals=0)
 
 
@@ -40,7 +40,20 @@
     return hit, slot
 
 
-def pack_kernel(chunks, own_ref, tokens_ref, gain_ref, picks_ref, *out_refs):
+def pack_kernel(
+    chunks, own_ref, tokens_ref, gain_ref, picks_ref, gate_ref, up_ref, down_ref, *refs
+):
+    *out_refs, weights_ref, arrived = refs
+    width, hidden = gate_ref.shape
+    sources = [gate_ref, up_ref]
+    sources += [down_ref.at[:, pl.ds(first, hidden)] for first in range(0, width, hidden)]
+    copies, first = [], 0
+    for n, source in enumerate(sources):
+        there = weights_ref.at[pl.ds(first, source.shape[0]), :]
+        copies.append(pltpu.make_async_copy(source, there, arrived.at[n]))
+        first += source.shape[0]
+    for copy in copies:
+        copy.start()
     tokens = tokens_ref.shape[0]
     values = tokens_ref[...].astype(F32)
     scale = lax.rsqrt(jnp.mean(values * values, axis=-1, keepdims=True) + EPS)
@@ -50,59 +63,66 @@
         place = first + iota((count, tokens), 0)
         chosen = (slot[k : k + 1, :] == place).astype(F32).astype(BF16)
         out_ref[...] = jnp.dot(chosen, normed, preferred_element_type=F32).astype(BF16)
-
-
-def pack(own, tokens, gain, picks, chunks):
-    rows, width = tokens.shape
+    for copy in copies:
+        copy.wait()
+
+
+def pack(own, tokens, gain, picks, weights, chunks):
+    width, hidden = weights[0].shape
     smem = pl.BlockSpec(memory_space=pltpu.SMEM)
     vmem = pl.BlockSpec(memory_space=pltpu.VMEM)
+    anywhere = pl.BlockSpec(memory_space=pltpu.HBM)
+    shapes = [(count, width) for _, _, count in chunks] + [(3 * width, hidden)]
     return pl.pallas_call(
         functools.partial(pack_kernel, chunks),
-        out_shape=[jax.ShapeDtypeStruct((count, width), BF16) for _, _, count in chunks],
-        in_specs=[smem, vmem, vmem, vmem],
-        out_specs=[vmem] * len(chunks),
+        out_shape=[jax.ShapeDtypeStruct(shape, BF16) for shape in shapes],
+        in_specs=[smem, vmem, vmem, vmem] + [anywhere] * 3,
+        out_specs=[vmem] * len(shapes),
+        scratch_shapes=[pltpu.SemaphoreType.DMA((2 + width // hidden,))],
         compiler_params=pltpu.CompilerParams(vmem_limit_bytes=VMEM_LIMIT),
         cost_estimate=COST,
         name="pack",
-    )(own, tokens, gain, picks)
-
-
-def expert_kernel(near_ref, far_ref, *refs):
-    weight_refs, (mine_ref, theirs_ref, rows) = refs[:-3], refs[-3:]
-    count = near_ref.shape[0]
-    rows[:count, :] = near_ref[...]
-    rows[count:, :] = far_ref[...]
-    halves = [weight_refs[n : n + 3] for n in range(0, len(weight_refs), 3)]
+    )(own, tokens, gain, picks, *(pltpu.with_memory_space_constraint(w, pltpu.HBM) for w in weights))
+
+
+def expert_kernel(blocks, slices, *refs):
+    block_refs, weight_refs = refs[:blocks], refs[blocks : blocks + slices]
+    out_refs, rows = refs[blocks + slices : -1], refs[-1]
+    first = 0
+    for ref in block_refs:
+        rows[first : first + ref.shape[0], :] = ref[...]
+        first += ref.shape[0]
+    width = rows.shape[1]
+    size = weight_refs[0].shape[1]
     hidden = []
-    for gate_ref, up_ref, _ in halves:
-        gate = jnp.dot(rows[...], gate_ref[...], preferred_element_type=F32)
-        up = jnp.dot(rows[...], up_ref[...], preferred_element_type=F32)
+    for ref in weight_refs:
+        gate = jnp.dot(rows[...], ref[:width, :], preferred_element_type=F32)
+        up = jnp.dot(rows[...], ref[width : 2 * width, :], preferred_element_type=F32)
         hidden.append((jax.nn.silu(gate) * up).astype(BF16))
-    width = near_ref.shape[1]
-    chunk = width // 7 if width % 7 == 0 else width
-    for start in range(0, width, chunk):
-        cols = slice(start, start + chunk)
+    for start in range(0, width, size):
         part = sum(
-            jnp.dot(value, down_ref[:, cols], preferred_element_type=F32)
-            for value, (_, _, down_ref) in zip(hidden, halves)
+            jnp.dot(value, ref[pl.ds(2 * width + start, size), :], preferred_element_type=F32)
+            for value, ref in zip(hidden, weight_refs)
         ).astype(BF16)
-        mine_ref[:, cols] = part[:count]
-        theirs_ref[:, cols] = part[count:]
-
-
-def expert_block(near, far, weights):
-    count, width = near.shape
-    vmem = pl.BlockSpec(memory_space=pltpu.VMEM)
-    return pl.pallas_call(
-        expert_kernel,
-        out_shape=[jax.ShapeDtypeStruct((count, width), BF16)] * 2,
-        in_specs=[vmem] * (2 + len(weights)),
-        out_specs=[vmem] * 2,
-        scratch_shapes=[pltpu.VMEM((2 * count, width), BF16)],
+        first = 0
+        for ref in out_refs:
+            ref[:, start : start + size] = part[first : first + ref.shape[0]]
+            first += ref.shape[0]
+
+
+def expert_block(blocks, weights, outs):
+    width = blocks[0].shape[1]
+    vmem = pl.BlockSpec(memory_space=pltpu.VMEM)
+    return pl.pallas_call(
+        functools.partial(expert_kernel, len(blocks), len(weights)),
+        out_shape=[jax.ShapeDtypeStruct((rows, width), BF16) for rows in outs],
+        in_specs=[vmem] * (len(blocks) + len(weights)),
+        out_specs=[vmem] * len(outs),
+        scratch_shapes=[pltpu.VMEM((sum(outs), width), BF16)],
         compiler_params=pltpu.CompilerParams(vmem_limit_bytes=VMEM_LIMIT),
         cost_estimate=COST,
         name="expert_block",
-    )(near, far, *weights)
+    )(*blocks, *weights)
 
 
 def score_kernel(capacity, own_ref, tokens_ref, gain_ref, picks_ref, gates_ref, target_ref, rest_ref, seg_ref, *refs):
@@ -185,41 +205,46 @@
         return lax.optimization_barrier((value, self.token))[0]
 
 
-def hold_kernel(own_ref, *refs):
-    *_, out_ref = refs
-    out_ref[0] = own_ref[0]
-
-
-def hold(own, arrays):
-    smem = pl.BlockSpec(memory_space=pltpu.SMEM)
-    vmem = pl.BlockSpec(memory_space=pltpu.VMEM)
-    return pl.pallas_call(
-        hold_kernel,
-        out_shape=jax.ShapeDtypeStruct((1,), jnp.int32),
-        in_specs=[smem] + [vmem] * len(arrays),
-        out_specs=smem,
-        compiler_params=pltpu.CompilerParams(vmem_limit_bytes=VMEM_LIMIT),
-        cost_estimate=COST,
-        name="hold",
-    )(own, *arrays)
-
-
-def total_kernel(*refs):
+def cut_kernel(whole_ref, *refs):
+    first = 0
+    for ref in refs:
+        ref[...] = whole_ref[first : first + ref.shape[0], :]
+        first += ref.shape[0]
+
+
+def cut(whole, pieces):
+    vmem = pl.BlockSpec(memory_space=pltpu.VMEM)
+    return pl.pallas_call(
+        cut_kernel,
+        out_shape=[jax.ShapeDtypeStruct((count, whole.shape[1]), BF16) for _, count in pieces],
+        in_specs=[vmem],
+        out_specs=[vmem] * len(pieces),
+        compiler_params=pltpu.CompilerParams(vmem_limit_bytes=VMEM_LIMIT),
+        cost_estimate=COST,
+        name="cut",
+    )(whole)
+
+
+def total_kernel(whole_ref, *refs):
     *refs, out_ref = refs
-    out_ref[...] = sum(ref[...].astype(F32) for ref in refs).astype(BF16)
-
-
-def total(*values):
+    first = 0
+    for ref in refs:
+        rows = slice(first, first + ref.shape[0])
+        out_ref[rows, :] = (whole_ref[rows, :].astype(F32) + ref[...].astype(F32)).astype(BF16)
+        first += ref.shape[0]
+
+
+def total(whole, pieces):
     vmem = pl.BlockSpec(memory_space=pltpu.VMEM)
     return pl.pallas_call(
         total_kernel,
-        out_shape=jax.ShapeDtypeStruct(values[0].shape, BF16),
-        in_specs=[vmem] * len(values),
+        out_shape=jax.ShapeDtypeStruct(whole.shape, BF16),
+        in_specs=[vmem] * (1 + len(pieces)),
         out_specs=vmem,
         compiler_params=pltpu.CompilerParams(vmem_limit_bytes=VMEM_LIMIT),
         cost_estimate=COST,
         name="total",
-    )(*values)
+    )(whole, *pieces)
 
 
 def per_device(
@@ -245,88 +270,88 @@
     own = (lax.axis_index("expert") // spread).astype(jnp.int32).reshape(1)
     picks_t = picks.T
     core, side = 1, 2
-    weights = [gate_weight, up_weight, down_weight]
-    weights += [swap(weight, core) for weight in weights]
-
-    half = capacity // 2 // 16 * 16 if capacity >= 64 else capacity
-    cuts = [(0, half), (half, capacity - half)] if half < capacity else [(0, capacity)]
-    chunks = [(k, 0, capacity) for k in range(min(2, experts))]
-    travelling = len(chunks)
-    chunks += [(k, first, count) for k in range(2, experts) for first, count in cuts]
-    sent = pack(own, tokens, norm_gain[None, :], picks_t, tuple(chunks))
+    cut_at = capacity * 5 // 8 // 16 * 16
+    pieces = [(0, cut_at), (cut_at, capacity - cut_at)] if cut_at else [(0, capacity)]
+    counts = [count for _, count in pieces]
+    chunks = [(0, 0, capacity)] + [(1, first, count) for first, count in pieces]
+    chunks += [(k, 0, capacity) for k in range(2, experts)]
+    packed = pack(own, tokens, norm_gain[None, :], picks_t, (gate_weight, up_weight, down_weight), tuple(chunks))
+    near = {0: packed[:1], 1: packed[1 : 1 + len(pieces)]}
+    near.update((k, [packed[k - 1 + len(pieces)]]) for k in range(2, experts))
+    weights = [packed[-1], swap(packed[-1], core)]
     order = Order(own)
-    near, far, mine, theirs, back = list(sent), {}, {}, {}, {}
-
-    def leave(n):
-        near[n] = swap(order.late(near[n]), chunks[n][0] * spread)
-
-    def arrive(n):
-        near[n] = order.mark_one(near[n])
-
-    def share(n):
-        far[n] = swap(order.late(near[n]), side)
-
-    def meet(n):
-        far[n] = order.mark_one(far[n])
-
-    def work(n):
-        mine[n], part = order.mark(*expert_block(order.late(near[n]), order.late(far[n]), weights))
-        theirs[n] = swap(part, side)
-
-    def home(n):
-        back[n] = order.mark_one(total(mine[n], order.mark_one(theirs[n])))
-
-    def leave_back(n):
-        back[n] = swap(order.late(back[n]), chunks[n][0] * spread)
-
-    def arrive_back(n):
-        back[n] = order.mark_one(back[n])
-
-    count = len(chunks) - travelling
-    begin_back = max(count, 4)
-    steps = max(begin_back + count, 8)
-    for step in range(steps):
-        out, shared, worked, crossing, coming = (
-            travelling + step - late if 0 <= step - late < count else None
-            for late in (0, 1, 2, 3, begin_back)
-        )
-        if out is not None:
-            leave(out)
-        if coming is not None:
-            leave_back(coming)
-        if step == 0:
-            share(0)
-            own = order.mark_one(hold(order.late(own), weights[:3]))
-        if step == 1:
-            meet(0)
-        if shared is not None:
-            share(shared)
-        if worked is not None:
-            work(worked)
-        if step == 2 and experts > 1:
-            arrive(1)
-            share(1)
-        if step == steps - 4 and experts > 1:
-            meet(1)
+    far, mine, theirs, back = {}, {}, {}, {}
+
+    def leave(k):
+        near[k] = [swap(order.late(rows), k * spread) for rows in near[k]]
+
+    def arrive(k):
+        near[k] = order.mark(*near[k])
+
+    def share(k):
+        rows = near[k] if k < 2 else order.mark(*cut(near[k][0], pieces))
+        far[k] = [swap(order.late(piece), side) for piece in rows]
+
+    def meet(k):
+        far[k] = order.mark(*far[k])
+
+    def work(k):
+        rows = [order.late(rows) for rows in (*near[k], *far[k])]
+        own_counts = [count for count in (counts if k == 1 else [capacity])]
+        parts = order.mark(*expert_block(rows, weights, own_counts + counts))
+        mine[k], theirs[k] = parts[: len(own_counts)], parts[len(own_counts) :]
+
+    def cross(k):
+        theirs[k] = [swap(order.late(piece), side) for piece in theirs[k]]
+
+    def home(k):
+        other = order.mark(*theirs[k])
+        if k == 1:
+            back[k] = order.mark(*(total(rows, [piece]) for rows, piece in zip(mine[k], other)))
+        else:
+            back[k] = order.mark(total(mine[k][0], other))
+
+    def leave_back(k):
+        back[k] = [swap(order.late(rows), k * spread) for rows in back[k]]
+
+    def arrive_back(k):
+        back[k] = order.mark(*back[k])
+
+    share(0)
+    leave(1)
+    leave(2)
+    meet(0)
+    arrive(1)
+    share(1)
+    meet(1)
+    arrive(2)
+    for k in range(3, experts + 1):
+        share(k - 1)
+        if k < experts:
+            leave(k)
+        if k > 3:
+            home(k - 2)
+            leave_back(k - 2)
+        meet(k - 1)
+        work(k - 1)
+        cross(k - 1)
+        if k == 3:
+            work(0)
             work(1)
-        if shared is not None:
-            meet(shared)
-        if crossing is not None:
-            home(crossing)
-        if step == 1 and experts > 1:
-            leave(1)
-        if step == steps - 3:
-            if experts > 1:
-                home(1)
-                leave_back(1)
-            work(0)
-        if step == steps - 1:
-            home(0)
-        if out is not None:
-            arrive(out)
-        if coming is not None:
-            arrive_back(coming)
-    blocks = [back[n] for n in range(len(chunks))]
+        if k < experts:
+            arrive(k)
+        if k > 3:
+            arrive_back(k - 2)
+    home(experts - 1)
+    cross(1)
+    leave_back(experts - 1)
+    home(1)
+    leave_back(1)
+    cross(0)
+    home(0)
+    arrive_back(experts - 1)
+    arrive_back(1)
+    blocks = [rows for k in range(experts) for rows in back[k]]
     local = score(
         own,
         tokens,

time: 171 us -> 153 us (0.89)
  waiting for transfers between devices: 62.7 us -> 96.7 us
  Pallas kernels: 53.4 us -> 22.8 us
  starting transfers between devices: 43.9 us -> 29.3 us
  local copies, waits for them, and re-layouts: 9.15 us -> 3.03 us
    ppermute x29 -> x28, waiting for transfers between devices: 62.7 us -> 96.7 us  [swap(): return lax.ppermute(value, 'expert', pairs)]
    pallas_call x13 -> x11, Pallas kernels: 49.6 us -> 16.1 us  [the longest x4 15.5 us: expert_block(): pl.pallas_call(functools.partial(expert_kernel, len(blocks), len(weights)...]
    ppermute x29 -> x28, starting transfers between devices: 43.9 us -> 29.3 us  [swap(): return lax.ppermute(value, 'expert', pairs)]
    unnamed x34 -> x22, local copies, waits for them, and re-layouts: 8.03 us -> 1.91 us
    pallas_call x1, Pallas kernels: 1.21 us -> 4.74 us  [pack(): pl.pallas_call(functools.partial(pack_kernel, chunks), out_shape=[jax.Sha...]
  transfers between devices with their start and end apart: 29 -> 28, of which waited for: 15 -> 15; matrix products, arithmetic and copies ran while one was open for 1% -> 0% of each run, Pallas kernels for 30% -> 10%
where the time goes in v5:
time: 153 us
  waiting for transfers between devices  96.7 us (63%)
  starting transfers between devices  29.3 us (19%)
  Pallas kernels  22.8 us (15%)
  local copies, waits for them, and re-layouts  3.03 us (2%)
    ppermute x28, waiting for transfers between devices, swap(): return lax.ppermute(value, 'expert', pairs)  96.7 us
    ppermute x28, starting transfers between devices, swap(): return lax.ppermute(value, 'expert', pairs)  29.3 us
    pallas_call x4, Pallas kernels, expert_block(): pl.pallas_call(functools.partial(expert_kernel, len(blocks), len(weights)...  15.5 us
    pallas_call x1, Pallas kernels, pack(): pl.pallas_call(functools.partial(pack_kernel, chunks), out_shape=[jax.Sha...  4.74 us
  transfers between devices with their start and end apart: 28, of which 15 were waited for; matrix products, arithmetic and copies ran while one was open for 0% of the time, Pallas kernels for 10%

profile of v5, /device:TPU:0, one launch (start us, length us, event | category | flops | bytes accessed | tf_op | source)
XLA Modules:
  0.0 153.2 jit_solution(9586883717754696325)
XLA Ops:
  3.3 4.7 %pack.1 = (bf16[80,3584]{1,0:T(8,128)(2,1)S(1)}, bf16[48,3584]{1,0:T(8,128)(2,1)S(1)}, bf16[32,3584]{1,0:T(8,128)(2,1)S(1)}, bf16[80,3584]{1,0:T(8,128)(2,1)S(1)...) custom-call(s32[1]{0:T(128)} %bitcast.own_ref, bf16[128,3584]{1,0:T(8,128)(2,1)S(1)} %copy-done, ...), custom_call_target="tpu_custom_call" | custom-call | flops 1024 | bytes 1024 | tf_op jit(solution)/shard_map/pack/pallas_call | solution.py:76
  8.5 2.6 %collective-permute-start.3 = (bf16[80,3584]{1,0:T(8,128)(2,1)S(1)}, bf16[80,3584]{1,0:T(8,128)(2,1)S(1)}, u32[]{:S(2)}, u32[]{:S(2)}) collective-permute-start(bf16[80,3584]{1,0:T(8,128)(2,1)S(1)} %get-tuple-element.158.refs_0_), channel_id=1, source_target_pairs={{0,2},{1,3},{2,0},{3,1},{4,6},{5,7},{6,4},{7,5},{8,10},{9,11},{10,... | collective-permute-start | bytes 1720328 | tf_op jit(solution)/shard_map/ppermute | solution.py:25
  13.1 2.6 %collective-permute-start = (bf16[80,3584]{1,0:T(8,128)(2,1)S(1)}, bf16[80,3584]{1,0:T(8,128)(2,1)S(1)}, u32[]{:S(2)}, u32[]{:S(2)}) collective-permute-start(bf16[80,3584]{1,0:T(8,128)(2,1)S(1)} %get-tuple-element.125), channel_id=1, source_target_pairs={{0,8},{1,9},{2,10},{3,11},{4,12},{5,13},{6,14},{7,15},{8,0},{9,1},... | collective-permute-start | bytes 1720328 | tf_op jit(solution)/shard_map/ppermute | solution.py:25
  15.7 9.0 %collective-permute-done.3.refs_1_ = bf16[80,3584]{1,0:T(8,128)(2,1)S(1)} collective-permute-done((bf16[80,3584]{1,0:T(8,128)(2,1)S(1)}, bf16[80,3584]{1,0:T(8,128)(2,1)S(1)}, u32[]{:S(2)}, u32[]{:S(2)}) %collective-permute-start.3) | collective-permute-done | bytes 573472 | tf_op jit(solution)/shard_map/ppermute | solution.py:25
  24.7 13.5 %collective-permute-done.2.refs_1_ = bf16[32,3584]{1,0:T(8,128)(2,1)S(1)} collective-permute-done((bf16[32,3584]{1,0:T(8,128)(2,1)S(1)}, bf16[32,3584]{1,0:T(8,128)(2,1)S(1)}, u32[]{:S(2)}, u32[]{:S(2)}) %collective-permute-start.2) | collective-permute-done | bytes 229408 | tf_op jit(solution)/shard_map/ppermute | solution.py:25
  38.6 1.6 %collective-permute-start.5 = (bf16[32,3584]{1,0:T(8,128)(2,1)S(1)}, bf16[32,3584]{1,0:T(8,128)(2,1)S(1)}, u32[]{:S(2)}, u32[]{:S(2)}) collective-permute-start(bf16[32,3584]{1,0:T(8,128)(2,1)S(1)} %collective-permute-done.2.refs_1_), channel_id=1, source_target_pairs={{0,2},{1,3},{2,0},{3,1},{4,6},{5,7},{6,4},{7,5},{8,10},{9,11},{10,... | collective-permute-start | bytes 688136 | tf_op jit(solution)/shard_map/ppermute | solution.py:25
  40.2 12.2 %collective-permute-done.5.refs_3_ = bf16[32,3584]{1,0:T(8,128)(2,1)S(1)} collective-permute-done((bf16[32,3584]{1,0:T(8,128)(2,1)S(1)}, bf16[32,3584]{1,0:T(8,128)(2,1)S(1)}, u32[]{:S(2)}, u32[]{:S(2)}) %collective-permute-start.5) | collective-permute-done | bytes 229408 | tf_op jit(solution)/shard_map/ppermute | solution.py:25
  55.9 9.9 %collective-permute-done.7.refs_2_ = bf16[32,3584]{1,0:T(8,128)(2,1)S(1)} collective-permute-done((bf16[32,3584]{1,0:T(8,128)(2,1)S(1)}, bf16[32,3584]{1,0:T(8,128)(2,1)S(1)}, u32[]{:S(2)}, u32[]{:S(2)}) %collective-permute-start.7) | collective-permute-done | bytes 229408 | tf_op jit(solution)/shard_map/ppermute | solution.py:25
  65.8 3.8 %expert_block.4 = (bf16[80,3584]{1,0:T(8,128)(2,1)S(1)}, bf16[48,3584]{1,0:T(8,128)(2,1)S(1)}, bf16[32,3584]{1,0:T(8,128)(2,1)S(1)}) custom-call(bf16[80,3584]{1,0:T(8,128)(2,1)S(1)} %collective-permute-done.whole_ref.refs_0_, bf16[48,3584]{1,0:T(8,128)(2,1)S(1)} %collective-permute-done.6.refs_1_, bf16[32,3584]{1,0:T(8,128)(2,1)S(1)} %collective-permute-done.7.refs_2_, ...), custom_call_target="tpu_custom_call" | custom-call | flops 1024 | bytes 1024 | tf_op jit(solution)/shard_map/expert_block/pallas_call | solution.py:116
  71.7 3.8 %expert_block.5 = (bf16[80,3584]{1,0:T(8,128)(2,1)S(1)}, bf16[48,3584]{1,0:T(8,128)(2,1)S(1)}, bf16[32,3584]{1,0:T(8,128)(2,1)S(1)}) custom-call(bf16[80,3584]{1,0:T(8,128)(2,1)S(1)} %get-tuple-element.158.refs_0_, bf16[80,3584]{1,0:T(8,128)(2,1)S(1)} %collective-permute-done.3.refs_1_, bf16[10752,512]{1,0:T(8,128)(2,1)S(1)} %get-tuple-element.153.refs_3_.refs_2_.refs_4_, ...), custom_call_target="tpu_custom_call" | custom-call | flops 1024 | bytes 1024 | tf_op jit(solution)/shard_map/expert_block/pallas_call | solution.py:116
  75.5 3.8 %expert_block.6 = (bf16[48,3584]{1,0:T(8,128)(2,1)S(1)}, bf16[32,3584]{1,0:T(8,128)(2,1)S(1)}, bf16[48,3584]{1,0:T(8,128)(2,1)S(1)}, bf16[32,3584]{1,0:T(8,128)(2,1)S(1)}) custom-call(bf16[48,3584]{1,0:T(8,128)(2,1)S(1)} %collective-permute-done.1.refs_0_, bf16[32,3584]{1,0:T(8,128)(2,1)S(1)} %collective-permute-done.2.refs_1_, ...), custom_call_target="tpu_custom_call" | custom-call | flops 1024 | bytes 1024 | tf_op jit(solution)/shard_map/expert_block/pallas_call | solution.py:116
  81.5 3.5 %collective-permute-done.13.refs_1_ = bf16[32,3584]{1,0:T(8,128)(2,1)S(1)} collective-permute-done((bf16[32,3584]{1,0:T(8,128)(2,1)S(1)}, bf16[32,3584]{1,0:T(8,128)(2,1)S(1)}, u32[]{:S(2)}, u32[]{:S(2)}) %collective-permute-start.13) | collective-permute-done | bytes 229408 | tf_op jit(solution)/shard_map/ppermute | solution.py:25
  85.3 9.1 %collective-permute-done.11.refs_2_ = bf16[32,3584]{1,0:T(8,128)(2,1)S(1)} collective-permute-done((bf16[32,3584]{1,0:T(8,128)(2,1)S(1)}, bf16[32,3584]{1,0:T(8,128)(2,1)S(1)}, u32[]{:S(2)}, u32[]{:S(2)}) %collective-permute-start.11) | collective-permute-done | bytes 229408 | tf_op jit(solution)/shard_map/ppermute | solution.py:25
  94.4 4.0 %expert_block.7 = (bf16[80,3584]{1,0:T(8,128)(2,1)S(1)}, bf16[48,3584]{1,0:T(8,128)(2,1)S(1)}, bf16[32,3584]{1,0:T(8,128)(2,1)S(1)}) custom-call(bf16[80,3584]{1,0:T(8,128)(2,1)S(1)} %collective-permute-done.9.whole_ref.refs_0_, bf16[48,3584]{1,0:T(8,128)(2,1)S(1)} %collective-permute-done.10.refs_1_, bf16[32,3584]{1,0:T(8,128)(2,1)S(1)} %collective-permute-done.11.refs_2_, ...), custom_call_target="tpu_custom_call" | custom-call | flops 1024 | bytes 1024 | tf_op jit(solution)/shard_map/expert_block/pallas_call | solution.py:116
  100.6 5.3 %collective-permute-done.16.refs_3_ = bf16[80,3584]{1,0:T(8,128)(2,1)S(1)} collective-permute-done((bf16[80,3584]{1,0:T(8,128)(2,1)S(1)}, bf16[80,3584]{1,0:T(8,128)(2,1)S(1)}, u32[]{:S(2)}, u32[]{:S(2)}) %collective-permute-start.16) | collective-permute-done | bytes 573472 | tf_op jit(solution)/shard_map/ppermute | solution.py:25
  105.9 5.6 %collective-permute-done.15.refs_1_ = bf16[32,3584]{1,0:T(8,128)(2,1)S(1)} collective-permute-done((bf16[32,3584]{1,0:T(8,128)(2,1)S(1)}, bf16[32,3584]{1,0:T(8,128)(2,1)S(1)}, u32[]{:S(2)}, u32[]{:S(2)}) %collective-permute-start.15) | collective-permute-done | bytes 229408 | tf_op jit(solution)/shard_map/ppermute | solution.py:25
  115.0 9.5 %collective-permute-done.18.refs_0_ = bf16[32,3584]{1,0:T(8,128)(2,1)S(1)} collective-permute-done((bf16[32,3584]{1,0:T(8,128)(2,1)S(1)}, bf16[32,3584]{1,0:T(8,128)(2,1)S(1)}, u32[]{:S(2)}, u32[]{:S(2)}) %collective-permute-start.18) | collective-permute-done | bytes 229408 | tf_op jit(solution)/shard_map/ppermute | solution.py:25
  126.1 1.9 %collective-permute-start.22 = (bf16[32,3584]{1,0:T(8,128)(2,1)S(1)}, bf16[32,3584]{1,0:T(8,128)(2,1)S(1)}, u32[]{:S(2)}, u32[]{:S(2)}) collective-permute-start(bf16[32,3584]{1,0:T(8,128)(2,1)S(1)} %total.8), channel_id=1, source_target_pairs={{0,4},{1,5},{2,6},{3,7},{4,0},{5,1},{6,2},{7,3},{8,12},{9,13},{10,... | collective-permute-start | bytes 688136 | tf_op jit(solution)/shard_map/ppermute | solution.py:25
  129.7 7.9 %collective-permute-done.22.refs_2_ = bf16[32,3584]{1,0:T(8,128)(2,1)S(1)} collective-permute-done((bf16[32,3584]{1,0:T(8,128)(2,1)S(1)}, bf16[32,3584]{1,0:T(8,128)(2,1)S(1)}, u32[]{:S(2)}, u32[]{:S(2)}) %collective-permute-start.22) | collective-permute-done | bytes 229408 | tf_op jit(solution)/shard_map/ppermute | solution.py:25
  137.9 1.9 %score.1 = f32[1,16]{1,0:T(1,128)S(1)} custom-call(s32[1]{0:T(128)} %bitcast.own_ref, bf16[128,3584]{1,0:T(8,128)(2,1)S(1)} %copy-done.1, f32[1,3584]{1,0:T(1,128)S(1)} %broadcast_in_dim.12.gain_ref, s32[2,128]{1,0:T(2,128)S(1)} %bitcast.8, f32[2,128]{1,0:T(2,128)S(1)} %bitcast.9, bf16[128,3584]{1,0:T(8,128)(2,1)S(1)} %copy-done.2, f32[1,128]{1,0:T(1,128)S(1)} %bitcast.10, ...), custom_call_target="tpu_custom_call" | custom-call | flops 1024 | bytes 1024 | tf_op jit(solution)/shard_map/score/pallas_call | solution.py:178
  140.9 1.8 %collective-permute-start.25 = (f32[1,16]{1,0:T(1,128)S(1)}, f32[1,16]{1,0:T(1,128)S(1)}, u32[]{:S(2)}, u32[]{:S(2)}) collective-permute-start(f32[1,16]{1,0:T(1,128)S(1)} %add.18), channel_id=1, source_target_pairs={{0,2},{1,3},{2,0},{3,1},{4,6},{5,7},{6,4},{7,5},{8,10},{9,11},{10,... | collective-permute-start | bytes 200 | tf_op jit(solution)/shard_map/ppermute | solution.py:25
  142.7 1.8 %collective-permute-done.25 = f32[1,16]{1,0:T(1,128)S(1)} collective-permute-done((f32[1,16]{1,0:T(1,128)S(1)}, f32[1,16]{1,0:T(1,128)S(1)}, u32[]{:S(2)}, u32[]{:S(2)}) %collective-permute-start.25) | collective-permute-done | bytes 96 | tf_op jit(solution)/shard_map/ppermute | solution.py:25
  144.6 3.4 %collective-permute-done.26 = f32[1,16]{1,0:T(1,128)S(1)} collective-permute-done((f32[1,16]{1,0:T(1,128)S(1)}, f32[1,16]{1,0:T(1,128)S(1)}, u32[]{:S(2)}, u32[]{:S(2)}) %collective-permute-start.26) | collective-permute-done | bytes 96 | tf_op jit(solution)/shard_map/ppermute | solution.py:25
  148.5 3.9 %collective-permute-done.27 = f32[1,16]{1,0:T(1,128)S(1)} collective-permute-done((f32[1,16]{1,0:T(1,128)S(1)}, f32[1,16]{1,0:T(1,128)S(1)}, u32[]{:S(2)}, u32[]{:S(2)}) %collective-permute-start.27) | collective-permute-done | bytes 96 | tf_op jit(solution)/shard_map/ppermute | solution.py:25
  (78 shorter events, 25.0 us)
Async XLA Ops:
  8.0 57.8 %collective-permute-start.8 = (bf16[10752,512]{1,0:T(8,128)(2,1)S(1)}, bf16[10752,512]{1,0:T(8,128)(2,1)S(1)}, u32[]{:S(2)}, u32[]{:S(2)}) collective-permute-start(bf16[10752,512]{1,0:T(8,128)(2,1)S(1)} %get-tuple-element.153.refs_3_.refs_2_.refs_4_), channel_id=1, source_target_pairs={{0,1},{1,0},{2,3},{3,2},{4,5},{5,4},{6,7},{7,6},{8,9},{9,8},{10,11... | collective-permute-start | bytes 33030152 | tf_op jit(solution)/shard_map/ppermute | solution.py:25
  8.5 16.2 %collective-permute-start.3 = (bf16[80,3584]{1,0:T(8,128)(2,1)S(1)}, bf16[80,3584]{1,0:T(8,128)(2,1)S(1)}, u32[]{:S(2)}, u32[]{:S(2)}) collective-permute-start(bf16[80,3584]{1,0:T(8,128)(2,1)S(1)} %get-tuple-element.158.refs_0_), channel_id=1, source_target_pairs={{0,2},{1,3},{2,0},{3,1},{4,6},{5,7},{6,4},{7,5},{8,10},{9,11},{10,... | collective-permute-start | bytes 1720328 | tf_op jit(solution)/shard_map/ppermute | solution.py:25
  11.1 27.1 %collective-permute-start.1 = (bf16[48,3584]{1,0:T(8,128)(2,1)S(1)}, bf16[48,3584]{1,0:T(8,128)(2,1)S(1)}, u32[]{:S(2)}, u32[]{:S(2)}) collective-permute-start(bf16[48,3584]{1,0:T(8,128)(2,1)S(1)} %get-tuple-element.127), channel_id=1, source_target_pairs={{0,4},{1,5},{2,6},{3,7},{4,0},{5,1},{6,2},{7,3},{8,12},{9,13},{10,... | collective-permute-start | bytes 1032200 | tf_op jit(solution)/shard_map/ppermute | solution.py:25
  12.7 25.5 %collective-permute-start.2 = (bf16[32,3584]{1,0:T(8,128)(2,1)S(1)}, bf16[32,3584]{1,0:T(8,128)(2,1)S(1)}, u32[]{:S(2)}, u32[]{:S(2)}) collective-permute-start(bf16[32,3584]{1,0:T(8,128)(2,1)S(1)} %get-tuple-element.129), channel_id=1, source_target_pairs={{0,4},{1,5},{2,6},{3,7},{4,0},{5,1},{6,2},{7,3},{8,12},{9,13},{10,... | collective-permute-start | bytes 688136 | tf_op jit(solution)/shard_map/ppermute | solution.py:25
  13.1 39.3 %collective-permute-start = (bf16[80,3584]{1,0:T(8,128)(2,1)S(1)}, bf16[80,3584]{1,0:T(8,128)(2,1)S(1)}, u32[]{:S(2)}, u32[]{:S(2)}) collective-permute-start(bf16[80,3584]{1,0:T(8,128)(2,1)S(1)} %get-tuple-element.125), channel_id=1, source_target_pairs={{0,8},{1,9},{2,10},{3,11},{4,12},{5,13},{6,14},{7,15},{8,0},{9,1},... | collective-permute-start | bytes 1720328 | tf_op jit(solution)/shard_map/ppermute | solution.py:25
  38.2 14.2 %collective-permute-start.4 = (bf16[48,3584]{1,0:T(8,128)(2,1)S(1)}, bf16[48,3584]{1,0:T(8,128)(2,1)S(1)}, u32[]{:S(2)}, u32[]{:S(2)}) collective-permute-start(bf16[48,3584]{1,0:T(8,128)(2,1)S(1)} %collective-permute-done.1.refs_0_), channel_id=1, source_target_pairs={{0,2},{1,3},{2,0},{3,1},{4,6},{5,7},{6,4},{7,5},{8,10},{9,11},{10,... | collective-permute-start | bytes 1032200 | tf_op jit(solution)/shard_map/ppermute | solution.py:25
  38.6 13.8 %collective-permute-start.5 = (bf16[32,3584]{1,0:T(8,128)(2,1)S(1)}, bf16[32,3584]{1,0:T(8,128)(2,1)S(1)}, u32[]{:S(2)}, u32[]{:S(2)}) collective-permute-start(bf16[32,3584]{1,0:T(8,128)(2,1)S(1)} %collective-permute-done.2.refs_1_), channel_id=1, source_target_pairs={{0,2},{1,3},{2,0},{3,1},{4,6},{5,7},{6,4},{7,5},{8,10},{9,11},{10,... | collective-permute-start | bytes 688136 | tf_op jit(solution)/shard_map/ppermute | solution.py:25
  52.4 13.4 %collective-permute-start.6 = (bf16[48,3584]{1,0:T(8,128)(2,1)S(1)}, bf16[48,3584]{1,0:T(8,128)(2,1)S(1)}, u32[]{:S(2)}, u32[]{:S(2)}) collective-permute-start(bf16[48,3584]{1,0:T(8,128)(2,1)S(1)} %get-tuple-element.144), channel_id=1, source_target_pairs={{0,2},{1,3},{2,0},{3,1},{4,6},{5,7},{6,4},{7,5},{8,10},{9,11},{10,... | collective-permute-start | bytes 1032200 | tf_op jit(solution)/shard_map/ppermute | solution.py:25
  53.2 26.2 %collective-permute-start.9 = (bf16[80,3584]{1,0:T(8,128)(2,1)S(1)}, bf16[80,3584]{1,0:T(8,128)(2,1)S(1)}, u32[]{:S(2)}, u32[]{:S(2)}) collective-permute-start(bf16[80,3584]{1,0:T(8,128)(2,1)S(1)} %get-tuple-element.180), channel_id=1, source_target_pairs={{0,12},{1,13},{2,14},{3,15},{4,8},{5,9},{6,10},{7,11},{8,4},{9,5},... | collective-permute-start | bytes 1720328 | tf_op jit(solution)/shard_map/ppermute | solution.py:25
  54.4 11.4 %collective-permute-start.7 = (bf16[32,3584]{1,0:T(8,128)(2,1)S(1)}, bf16[32,3584]{1,0:T(8,128)(2,1)S(1)}, u32[]{:S(2)}, u32[]{:S(2)}) collective-permute-start(bf16[32,3584]{1,0:T(8,128)(2,1)S(1)} %get-tuple-element.146), channel_id=1, source_target_pairs={{0,2},{1,3},{2,0},{3,1},{4,6},{5,7},{6,4},{7,5},{8,10},{9,11},{10,... | collective-permute-start | bytes 688136 | tf_op jit(solution)/shard_map/ppermute | solution.py:25
  69.6 15.4 %collective-permute-start.12 = (bf16[48,3584]{1,0:T(8,128)(2,1)S(1)}, bf16[48,3584]{1,0:T(8,128)(2,1)S(1)}, u32[]{:S(2)}, u32[]{:S(2)}) collective-permute-start(bf16[48,3584]{1,0:T(8,128)(2,1)S(1)} %get-tuple-element.193), channel_id=1, source_target_pairs={{0,2},{1,3},{2,0},{3,1},{4,6},{5,7},{6,4},{7,5},{8,10},{9,11},{10,... | collective-permute-start | bytes 1032200 | tf_op jit(solution)/shard_map/ppermute | solution.py:25
  70.7 14.3 %collective-permute-start.13 = (bf16[32,3584]{1,0:T(8,128)(2,1)S(1)}, bf16[32,3584]{1,0:T(8,128)(2,1)S(1)}, u32[]{:S(2)}, u32[]{:S(2)}) collective-permute-start(bf16[32,3584]{1,0:T(8,128)(2,1)S(1)} %get-tuple-element.195), channel_id=1, source_target_pairs={{0,2},{1,3},{2,0},{3,1},{4,6},{5,7},{6,4},{7,5},{8,10},{9,11},{10,... | collective-permute-start | bytes 688136 | tf_op jit(solution)/shard_map/ppermute | solution.py:25
  79.4 14.9 %collective-permute-start.10 = (bf16[48,3584]{1,0:T(8,128)(2,1)S(1)}, bf16[48,3584]{1,0:T(8,128)(2,1)S(1)}, u32[]{:S(2)}, u32[]{:S(2)}) collective-permute-start(bf16[48,3584]{1,0:T(8,128)(2,1)S(1)} %get-tuple-element.188), channel_id=1, source_target_pairs={{0,2},{1,3},{2,0},{3,1},{4,6},{5,7},{6,4},{7,5},{8,10},{9,11},{10,... | collective-permute-start | bytes 1032200 | tf_op jit(solution)/shard_map/ppermute | solution.py:25
  80.5 13.8 %collective-permute-start.11 = (bf16[32,3584]{1,0:T(8,128)(2,1)S(1)}, bf16[32,3584]{1,0:T(8,128)(2,1)S(1)}, u32[]{:S(2)}, u32[]{:S(2)}) collective-permute-start(bf16[32,3584]{1,0:T(8,128)(2,1)S(1)} %get-tuple-element.190), channel_id=1, source_target_pairs={{0,2},{1,3},{2,0},{3,1},{4,6},{5,7},{6,4},{7,5},{8,10},{9,11},{10,... | collective-permute-start | bytes 688136 | tf_op jit(solution)/shard_map/ppermute | solution.py:25
  85.2 20.7 %collective-permute-start.16 = (bf16[80,3584]{1,0:T(8,128)(2,1)S(1)}, bf16[80,3584]{1,0:T(8,128)(2,1)S(1)}, u32[]{:S(2)}, u32[]{:S(2)}) collective-permute-start(bf16[80,3584]{1,0:T(8,128)(2,1)S(1)} %total.5), channel_id=1, source_target_pairs={{0,8},{1,9},{2,10},{3,11},{4,12},{5,13},{6,14},{7,15},{8,0},{9,1},... | collective-permute-start | bytes 1720328 | tf_op jit(solution)/shard_map/ppermute | solution.py:25
  98.5 13.0 %collective-permute-start.14 = (bf16[48,3584]{1,0:T(8,128)(2,1)S(1)}, bf16[48,3584]{1,0:T(8,128)(2,1)S(1)}, u32[]{:S(2)}, u32[]{:S(2)}) collective-permute-start(bf16[48,3584]{1,0:T(8,128)(2,1)S(1)} %get-tuple-element.212), channel_id=1, source_target_pairs={{0,2},{1,3},{2,0},{3,1},{4,6},{5,7},{6,4},{7,5},{8,10},{9,11},{10,... | collective-permute-start | bytes 1032200 | tf_op jit(solution)/shard_map/ppermute | solution.py:25
  99.9 11.6 %collective-permute-start.15 = (bf16[32,3584]{1,0:T(8,128)(2,1)S(1)}, bf16[32,3584]{1,0:T(8,128)(2,1)S(1)}, u32[]{:S(2)}, u32[]{:S(2)}) collective-permute-start(bf16[32,3584]{1,0:T(8,128)(2,1)S(1)} %get-tuple-element.214), channel_id=1, source_target_pairs={{0,2},{1,3},{2,0},{3,1},{4,6},{5,7},{6,4},{7,5},{8,10},{9,11},{10,... | collective-permute-start | bytes 688136 | tf_op jit(solution)/shard_map/ppermute | solution.py:25
  111.6 12.9 %collective-permute-start.17 = (bf16[48,3584]{1,0:T(8,128)(2,1)S(1)}, bf16[48,3584]{1,0:T(8,128)(2,1)S(1)}, u32[]{:S(2)}, u32[]{:S(2)}) collective-permute-start(bf16[48,3584]{1,0:T(8,128)(2,1)S(1)} %get-tuple-element.221), channel_id=1, source_target_pairs={{0,2},{1,3},{2,0},{3,1},{4,6},{5,7},{6,4},{7,5},{8,10},{9,11},{10,... | collective-permute-start | bytes 1032200 | tf_op jit(solution)/shard_map/ppermute | solution.py:25
  113.0 11.5 %collective-permute-start.18 = (bf16[32,3584]{1,0:T(8,128)(2,1)S(1)}, bf16[32,3584]{1,0:T(8,128)(2,1)S(1)}, u32[]{:S(2)}, u32[]{:S(2)}) collective-permute-start(bf16[32,3584]{1,0:T(8,128)(2,1)S(1)} %get-tuple-element.223), channel_id=1, source_target_pairs={{0,2},{1,3},{2,0},{3,1},{4,6},{5,7},{6,4},{7,5},{8,10},{9,11},{10,... | collective-permute-start | bytes 688136 | tf_op jit(solution)/shard_map/ppermute | solution.py:25
  113.7 16.0 %collective-permute-start.23 = (bf16[80,3584]{1,0:T(8,128)(2,1)S(1)}, bf16[80,3584]{1,0:T(8,128)(2,1)S(1)}, u32[]{:S(2)}, u32[]{:S(2)}) collective-permute-start(bf16[80,3584]{1,0:T(8,128)(2,1)S(1)} %total.6), channel_id=1, source_target_pairs={{0,12},{1,13},{2,14},{3,15},{4,8},{5,9},{6,10},{7,11},{8,4},{9,5},... | collective-permute-start | bytes 1720328 | tf_op jit(solution)/shard_map/ppermute | solution.py:25
  124.7 13.0 %collective-permute-start.21 = (bf16[48,3584]{1,0:T(8,128)(2,1)S(1)}, bf16[48,3584]{1,0:T(8,128)(2,1)S(1)}, u32[]{:S(2)}, u32[]{:S(2)}) collective-permute-start(bf16[48,3584]{1,0:T(8,128)(2,1)S(1)} %total.7), channel_id=1, source_target_pairs={{0,4},{1,5},{2,6},{3,7},{4,0},{5,1},{6,2},{7,3},{8,12},{9,13},{10,... | collective-permute-start | bytes 1032200 | tf_op jit(solution)/shard_map/ppermute | solution.py:25
  124.8 12.9 %collective-permute-start.19 = (bf16[48,3584]{1,0:T(8,128)(2,1)S(1)}, bf16[48,3584]{1,0:T(8,128)(2,1)S(1)}, u32[]{:S(2)}, u32[]{:S(2)}) collective-permute-start(bf16[48,3584]{1,0:T(8,128)(2,1)S(1)} %get-tuple-element.229), channel_id=1, source_target_pairs={{0,2},{1,3},{2,0},{3,1},{4,6},{5,7},{6,4},{7,5},{8,10},{9,11},{10,... | collective-permute-start | bytes 1032200 | tf_op jit(solution)/shard_map/ppermute | solution.py:25
  126.1 11.5 %collective-permute-start.22 = (bf16[32,3584]{1,0:T(8,128)(2,1)S(1)}, bf16[32,3584]{1,0:T(8,128)(2,1)S(1)}, u32[]{:S(2)}, u32[]{:S(2)}) collective-permute-start(bf16[32,3584]{1,0:T(8,128)(2,1)S(1)} %total.8), channel_id=1, source_target_pairs={{0,4},{1,5},{2,6},{3,7},{4,0},{5,1},{6,2},{7,3},{8,12},{9,13},{10,... | collective-permute-start | bytes 688136 | tf_op jit(solution)/shard_map/ppermute | solution.py:25
  128.1 9.6 %collective-permute-start.20 = (bf16[32,3584]{1,0:T(8,128)(2,1)S(1)}, bf16[32,3584]{1,0:T(8,128)(2,1)S(1)}, u32[]{:S(2)}, u32[]{:S(2)}) collective-permute-start(bf16[32,3584]{1,0:T(8,128)(2,1)S(1)} %get-tuple-element.231), channel_id=1, source_target_pairs={{0,2},{1,3},{2,0},{3,1},{4,6},{5,7},{6,4},{7,5},{8,10},{9,11},{10,... | collective-permute-start | bytes 688136 | tf_op jit(solution)/shard_map/ppermute | solution.py:25
  (15 other events, 328.3 us)

commit v6 on v5

--- a/solution.py
+++ b/solution.py
@@ -40,58 +40,62 @@
     return hit, slot
 
 
-def pack_kernel(
-    chunks, own_ref, tokens_ref, gain_ref, picks_ref, gate_ref, up_ref, down_ref, *refs
-):
-    *out_refs, weights_ref, arrived = refs
-    width, hidden = gate_ref.shape
-    sources = [gate_ref, up_ref]
-    sources += [down_ref.at[:, pl.ds(first, hidden)] for first in range(0, width, hidden)]
-    copies, first = [], 0
-    for n, source in enumerate(sources):
-        there = weights_ref.at[pl.ds(first, source.shape[0]), :]
-        copies.append(pltpu.make_async_copy(source, there, arrived.at[n]))
+def pack_kernel(own_ref, tokens_hbm, gain_ref, picks_hbm, gate_hbm, up_hbm, down_hbm, *refs):
+    *out_refs, weights_ref, tokens_ref, picks_ref, arrived = refs
+    width, hidden = gate_hbm.shape
+    moves = [(tokens_hbm, tokens_ref), (picks_hbm, picks_ref)]
+    sources = [gate_hbm, up_hbm]
+    sources += [down_hbm.at[:, pl.ds(first, hidden)] for first in range(0, width, hidden)]
+    first = 0
+    for source in sources:
+        moves.append((source, weights_ref.at[pl.ds(first, source.shape[0]), :]))
         first += source.shape[0]
+    copies = [pltpu.make_async_copy(*move, arrived.at[n]) for n, move in enumerate(moves)]
     for copy in copies:
         copy.start()
+    copies[0].wait()
+    copies[1].wait()
     tokens = tokens_ref.shape[0]
     values = tokens_ref[...].astype(F32)
     scale = lax.rsqrt(jnp.mean(values * values, axis=-1, keepdims=True) + EPS)
     normed = (values * scale * gain_ref[...]).astype(BF16)
-    _, slot = routing(own_ref[0], picks_ref[...], max(8, 1 + max(k for k, _, _ in chunks)))
-    for (k, first, count), out_ref in zip(chunks, out_refs):
-        place = first + iota((count, tokens), 0)
+    _, slot = routing(own_ref[0], picks_ref[...], max(8, len(out_refs)))
+    for k, out_ref in enumerate(out_refs):
+        place = iota((out_ref.shape[0], tokens), 0)
         chosen = (slot[k : k + 1, :] == place).astype(F32).astype(BF16)
         out_ref[...] = jnp.dot(chosen, normed, preferred_element_type=F32).astype(BF16)
-    for copy in copies:
+    for copy in copies[2:]:
         copy.wait()
 
 
-def pack(own, tokens, gain, picks, weights, chunks):
+def pack(own, tokens, gain, picks, weights, experts, capacity):
     width, hidden = weights[0].shape
     smem = pl.BlockSpec(memory_space=pltpu.SMEM)
     vmem = pl.BlockSpec(memory_space=pltpu.VMEM)
-    anywhere = pl.BlockSpec(memory_space=pltpu.HBM)
-    shapes = [(count, width) for _, _, count in chunks] + [(3 * width, hidden)]
-    return pl.pallas_call(
-        functools.partial(pack_kernel, chunks),
+    hbm = pl.BlockSpec(memory_space=pltpu.HBM)
+    shapes = [(capacity, width)] * experts + [(3 * width, hidden)]
+    there = [pltpu.with_memory_space_constraint(array, pltpu.HBM) for array in (tokens, picks, *weights)]
+    return pl.pallas_call(
+        pack_kernel,
         out_shape=[jax.ShapeDtypeStruct(shape, BF16) for shape in shapes],
-        in_specs=[smem, vmem, vmem, vmem] + [anywhere] * 3,
+        in_specs=[smem, hbm, vmem, hbm] + [hbm] * 3,
         out_specs=[vmem] * len(shapes),
-        scratch_shapes=[pltpu.SemaphoreType.DMA((2 + width // hidden,))],
+        scratch_shapes=[
+            pltpu.VMEM(tokens.shape, BF16),
+            pltpu.VMEM(picks.shape, jnp.int32),
+            pltpu.SemaphoreType.DMA((4 + width // hidden,)),
+        ],
         compiler_params=pltpu.CompilerParams(vmem_limit_bytes=VMEM_LIMIT),
         cost_estimate=COST,
         name="pack",
-    )(own, tokens, gain, picks, *(pltpu.with_memory_space_constraint(w, pltpu.HBM) for w in weights))
-
-
-def expert_kernel(blocks, slices, *refs):
-    block_refs, weight_refs = refs[:blocks], refs[blocks : blocks + slices]
-    out_refs, rows = refs[blocks + slices : -1], refs[-1]
-    first = 0
-    for ref in block_refs:
-        rows[first : first + ref.shape[0], :] = ref[...]
-        first += ref.shape[0]
+    )(own, there[0], gain, *there[1:])
+
+
+def expert_kernel(first, near_ref, far_ref, *refs):
+    *weight_refs, mine_ref, theirs_ref, rows = refs
+    count = far_ref.shape[0]
+    rows[:count, :] = near_ref[first : first + count, :]
+    rows[count:, :] = far_ref[...]
     width = rows.shape[1]
     size = weight_refs[0].shape[1]
     hidden = []
@@ -104,25 +108,23 @@
             jnp.dot(value, ref[pl.ds(2 * width + start, size), :], preferred_element_type=F32)
             for value, ref in zip(hidden, weight_refs)
         ).astype(BF16)
-        first = 0
-        for ref in out_refs:
-            ref[:, start : start + size] = part[first : first + ref.shape[0]]
-            first += ref.shape[0]
-
-
-def expert_block(blocks, weights, outs):
-    width = blocks[0].shape[1]
-    vmem = pl.BlockSpec(memory_space=pltpu.VMEM)
-    return pl.pallas_call(
-        functools.partial(expert_kernel, len(blocks), len(weights)),
-        out_shape=[jax.ShapeDtypeStruct((rows, width), BF16) for rows in outs],
-        in_specs=[vmem] * (len(blocks) + len(weights)),
-        out_specs=[vmem] * len(outs),
-        scratch_shapes=[pltpu.VMEM((sum(outs), width), BF16)],
+        mine_ref[:, start : start + size] = part[:count]
+        theirs_ref[:, start : start + size] = part[count:]
+
+
+def expert_block(near, first, far, weights):
+    count, width = far.shape
+    vmem = pl.BlockSpec(memory_space=pltpu.VMEM)
+    return pl.pallas_call(
+        functools.partial(expert_kernel, first),
+        out_shape=[jax.ShapeDtypeStruct((count, width), BF16)] * 2,
+        in_specs=[vmem] * (2 + len(weights)),
+        out_specs=[vmem] * 2,
+        scratch_shapes=[pltpu.VMEM((2 * count, width), BF16)],
         compiler_params=pltpu.CompilerParams(vmem_limit_bytes=VMEM_LIMIT),
         cost_estimate=COST,
         name="expert_block",
-    )(*blocks, *weights)
+    )(near, far, *weights)
 
 
 def score_kernel(capacity, own_ref, tokens_ref, gain_ref, picks_ref, gates_ref, target_ref, rest_ref, seg_ref, *refs):
@@ -225,26 +227,31 @@
     )(whole)
 
 
-def total_kernel(whole_ref, *refs):
+def total_kernel(count, *refs):
     *refs, out_ref = refs
-    first = 0
-    for ref in refs:
-        rows = slice(first, first + ref.shape[0])
-        out_ref[rows, :] = (whole_ref[rows, :].astype(F32) + ref[...].astype(F32)).astype(BF16)
-        first += ref.shape[0]
-
-
-def total(whole, pieces):
-    vmem = pl.BlockSpec(memory_space=pltpu.VMEM)
-    return pl.pallas_call(
-        total_kernel,
-        out_shape=jax.ShapeDtypeStruct(whole.shape, BF16),
-        in_specs=[vmem] * (1 + len(pieces)),
+    for side in (refs[:count], refs[count:]):
+        first = 0
+        for ref in side:
+            rows = slice(first, first + ref.shape[0])
+            if side[0] is refs[0]:
+                out_ref[rows, :] = ref[...]
+            else:
+                out_ref[rows, :] = (out_ref[rows, :].astype(F32) + ref[...].astype(F32)).astype(BF16)
+            first += ref.shape[0]
+
+
+def total(ours, others):
+    rows = sum(piece.shape[0] for piece in ours)
+    vmem = pl.BlockSpec(memory_space=pltpu.VMEM)
+    return pl.pallas_call(
+        functools.partial(total_kernel, len(ours)),
+        out_shape=jax.ShapeDtypeStruct((rows, ours[0].shape[1]), BF16),
+        in_specs=[vmem] * (len(ours) + len(others)),
         out_specs=vmem,
         compiler_params=pltpu.CompilerParams(vmem_limit_bytes=VMEM_LIMIT),
         cost_estimate=COST,
         name="total",
-    )(whole, *pieces)
+    )(*ours, *others)
 
 
 def per_device(
@@ -272,86 +279,79 @@
     core, side = 1, 2
     cut_at = capacity * 5 // 8 // 16 * 16
     pieces = [(0, cut_at), (cut_at, capacity - cut_at)] if cut_at else [(0, capacity)]
-    counts = [count for _, count in pieces]
-    chunks = [(0, 0, capacity)] + [(1, first, count) for first, count in pieces]
-    chunks += [(k, 0, capacity) for k in range(2, experts)]
-    packed = pack(own, tokens, norm_gain[None, :], picks_t, (gate_weight, up_weight, down_weight), tuple(chunks))
-    near = {0: packed[:1], 1: packed[1 : 1 + len(pieces)]}
-    near.update((k, [packed[k - 1 + len(pieces)]]) for k in range(2, experts))
-    weights = [packed[-1], swap(packed[-1], core)]
+    weights = (gate_weight, up_weight, down_weight)
+    *near, staged = pack(own, tokens, norm_gain[None, :], picks_t, weights, experts, capacity)
+    weights = [staged, swap(staged, core)]
     order = Order(own)
     far, mine, theirs, back = {}, {}, {}, {}
 
     def leave(k):
-        near[k] = [swap(order.late(rows), k * spread) for rows in near[k]]
+        near[k] = swap(order.late(near[k]), k * spread)
 
     def arrive(k):
-        near[k] = order.mark(*near[k])
+        near[k] = order.mark_one(near[k])
 
     def share(k):
-        rows = near[k] if k < 2 else order.mark(*cut(near[k][0], pieces))
-        far[k] = [swap(order.late(piece), side) for piece in rows]
-
-    def meet(k):
-        far[k] = order.mark(*far[k])
+        far[k] = [swap(order.late(piece), side) for piece in order.mark(*cut(near[k], pieces))]
 
     def work(k):
-        rows = [order.late(rows) for rows in (*near[k], *far[k])]
-        own_counts = [count for count in (counts if k == 1 else [capacity])]
-        parts = order.mark(*expert_block(rows, weights, own_counts + counts))
-        mine[k], theirs[k] = parts[: len(own_counts)], parts[len(own_counts) :]
-
-    def cross(k):
-        theirs[k] = [swap(order.late(piece), side) for piece in theirs[k]]
+        mine[k], theirs[k] = [], []
+        for (first, _), piece in zip(pieces, far[k]):
+            there = order.mark_one(piece)
+            part, other = order.mark(*expert_block(order.late(near[k]), first, there, weights))
+            mine[k].append(part)
+            theirs[k].append(swap(other, side))
+
+    def work_whole(k):
+        rows = (order.late(near[k]), 0, order.late(far[k]))
+        mine[k], theirs[k] = order.mark(*expert_block(*rows, weights))
 
     def home(k):
-        other = order.mark(*theirs[k])
-        if k == 1:
-            back[k] = order.mark(*(total(rows, [piece]) for rows, piece in zip(mine[k], other)))
-        else:
-            back[k] = order.mark(total(mine[k][0], other))
+        theirs[k] = order.mark(*theirs[k])
+        back[k] = order.mark_one(total(mine[k], theirs[k]))
 
     def leave_back(k):
-        back[k] = [swap(order.late(rows), k * spread) for rows in back[k]]
+        back[k] = swap(order.late(back[k]), k * spread)
 
     def arrive_back(k):
-        back[k] = order.mark(*back[k])
-
-    share(0)
+        back[k] = order.mark_one(back[k])
+
+    far[0], far[1] = swap(near[0], side), swap(near[1], side)
     leave(1)
     leave(2)
-    meet(0)
-    arrive(1)
-    share(1)
-    meet(1)
-    arrive(2)
+    far[0], far[1], near[1], near[2] = order.mark(far[0], far[1], near[1], near[2])
     for k in range(3, experts + 1):
         share(k - 1)
         if k < experts:
             leave(k)
+        if k == 3:
+            far[1] = swap(order.late(far[1]), spread)
         if k > 3:
             home(k - 2)
             leave_back(k - 2)
-        meet(k - 1)
+        if k == experts:
+            work_whole(1)
+            theirs[1] = swap(theirs[1], spread)
         work(k - 1)
-        cross(k - 1)
         if k == 3:
-            work(0)
-            work(1)
+            work_whole(0)
         if k < experts:
             arrive(k)
+        if k == 3:
+            far[1] = order.mark_one(far[1])
         if k > 3:
             arrive_back(k - 2)
     home(experts - 1)
-    cross(1)
     leave_back(experts - 1)
+    mine[1] = [swap(order.late(mine[1]), spread)]
+    mine[0], theirs[0] = [mine[0]], [swap(order.late(theirs[0]), side)]
+    theirs[1] = order.mark(*cut(order.mark_one(theirs[1]), pieces))
+    theirs[1] = [swap(order.late(piece), side) for piece in theirs[1]]
+    home(0)
+    mine[1] = order.mark(*mine[1])
     home(1)
-    leave_back(1)
-    cross(0)
-    home(0)
     arrive_back(experts - 1)
-    arrive_back(1)
-    blocks = [rows for k in range(experts) for rows in back[k]]
+    blocks = [back[k] for k in range(experts)]
     local = score(
         own,
         tokens,

time: 153 us -> 147 us (0.961)
  Pallas kernels: 22.8 us -> 30.9 us
  waiting for transfers between devices: 96.7 us -> 89.4 us
  starting transfers between devices: 29.3 us -> 24.2 us
  local copies, waits for them, and re-layouts: 3.03 us -> 1.17 us
    pallas_call x10 -> x11, Pallas kernels: 20.8 us -> 28.9 us  [the longest x6 23.3 us: expert_block(): pl.pallas_call(functools.partial(expert_kernel, first), out_shape=[jax.Sh...]
    ppermute x28 -> x26, waiting for transfers between devices: 96.7 us -> 89.4 us  [swap(): return lax.ppermute(value, 'expert', pairs)]
    ppermute x28 -> x26, starting transfers between devices: 29.3 us -> 24.2 us  [swap(): return lax.ppermute(value, 'expert', pairs)]
    unnamed x22 -> x18, local copies, waits for them, and re-layouts: 1.91 us -> 0.05 us
  transfers between devices with their start and end apart: 28 -> 26, of which waited for: 15 -> 14; matrix products, arithmetic and copies ran while one was open for 0% -> 0% of each run, Pallas kernels for 10% -> 17%
where the time goes in v6:
time: 147 us
  waiting for transfers between devices  89.4 us (61%)
  Pallas kernels  30.9 us (21%)
  starting transfers between devices  24.2 us (16%)
    ppermute x26, waiting for transfers between devices, swap(): return lax.ppermute(value, 'expert', pairs)  89.4 us
    ppermute x26, starting transfers between devices, swap(): return lax.ppermute(value, 'expert', pairs)  24.2 us
    pallas_call x6, Pallas kernels, expert_block(): pl.pallas_call(functools.partial(expert_kernel, first), out_shape=[jax.Sh...  23.3 us
    pallas_call x1, Pallas kernels, pack(): pl.pallas_call(pack_kernel, out_shape=[jax.ShapeDtypeStruct(shape, BF16)...  4.5 us
  transfers between devices with their start and end apart: 26, of which 14 were waited for; matrix products, arithmetic and copies ran while one was open for 0% of the time, Pallas kernels for 17%

profile of v6, /device:TPU:0, one launch (start us, length us, event | category | flops | bytes accessed | tf_op | source)
XLA Modules:
  0.0 147.1 jit_solution(91947855452760556)
XLA Ops:
  1.4 4.5 %pack.1 = (bf16[80,3584]{1,0:T(8,128)(2,1)S(1)}, bf16[80,3584]{1,0:T(8,128)(2,1)S(1)}, bf16[80,3584]{1,0:T(8,128)(2,1)S(1)}, bf16[80,3584]{1,0:T(8,128)(2,1)S(1)}, bf16[10752,512]{1,0:T(8,128)(2,1)S(1)}) custom-call(s32[1]{0:T(128)} %bitcast.own_ref, bf16[128,3584]{1,0:T(8,128)(2,1)} %tokens_ref.1, f32[1,3584]{1,0:T(1,128)S(1)} %broadcast_in_dim.15.gain_ref, ...), custom_call_target="tpu_custom_call" | custom-call | flops 1024 | bytes 1024 | tf_op jit(solution)/shard_map/pack/pallas_call | solution.py:78
  6.4 2.6 %collective-permute-start.2 = (bf16[80,3584]{1,0:T(8,128)(2,1)S(1)}, bf16[80,3584]{1,0:T(8,128)(2,1)S(1)}, u32[]{:S(2)}, u32[]{:S(2)}) collective-permute-start(bf16[80,3584]{1,0:T(8,128)(2,1)S(1)} %get-tuple-element.110), channel_id=1, source_target_pairs={{0,4},{1,5},{2,6},{3,7},{4,0},{5,1},{6,2},{7,3},{8,12},{9,13},{10,... | collective-permute-start | bytes 1720328 | tf_op jit(solution)/shard_map/ppermute | solution.py:25
  9.1 2.6 %collective-permute-start.3 = (bf16[80,3584]{1,0:T(8,128)(2,1)S(1)}, bf16[80,3584]{1,0:T(8,128)(2,1)S(1)}, u32[]{:S(2)}, u32[]{:S(2)}) collective-permute-start(bf16[80,3584]{1,0:T(8,128)(2,1)S(1)} %get-tuple-element.112), channel_id=1, source_target_pairs={{0,8},{1,9},{2,10},{3,11},{4,12},{5,13},{6,14},{7,15},{8,0},{9,1},... | collective-permute-start | bytes 1720328 | tf_op jit(solution)/shard_map/ppermute | solution.py:25
  13.7 21.1 %collective-permute-done.2.near_ref = bf16[80,3584]{1,0:T(8,128)(2,1)S(1)} collective-permute-done((bf16[80,3584]{1,0:T(8,128)(2,1)S(1)}, bf16[80,3584]{1,0:T(8,128)(2,1)S(1)}, u32[]{:S(2)}, u32[]{:S(2)}) %collective-permute-start.2) | collective-permute-done | bytes 573472 | tf_op jit(solution)/shard_map/ppermute | solution.py:25
  34.8 2.5 %collective-permute-done.3.whole_ref.near_ref = bf16[80,3584]{1,0:T(8,128)(2,1)S(1)} collective-permute-done((bf16[80,3584]{1,0:T(8,128)(2,1)S(1)}, bf16[80,3584]{1,0:T(8,128)(2,1)S(1)}, u32[]{:S(2)}, u32[]{:S(2)}) %collective-permute-start.3) | collective-permute-done | bytes 573472 | tf_op jit(solution)/shard_map/ppermute | solution.py:25
  42.0 9.0 %collective-permute-done.5.far_ref = bf16[48,3584]{1,0:T(8,128)(2,1)S(1)} collective-permute-done((bf16[48,3584]{1,0:T(8,128)(2,1)S(1)}, bf16[48,3584]{1,0:T(8,128)(2,1)S(1)}, u32[]{:S(2)}, u32[]{:S(2)}) %collective-permute-start.5) | collective-permute-done | bytes 344096 | tf_op jit(solution)/shard_map/ppermute | solution.py:25
  50.9 3.7 %expert_block.6 = (bf16[48,3584]{1,0:T(8,128)(2,1)S(1)}, bf16[48,3584]{1,0:T(8,128)(2,1)S(1)}) custom-call(bf16[80,3584]{1,0:T(8,128)(2,1)S(1)} %collective-permute-done.3.whole_ref.near_ref, bf16[48,3584]{1,0:T(8,128)(2,1)S(1)} %collective-permute-done.5.far_ref, bf16[10752,512]{1,0:T(8,128)(2,1)S(1)} %get-tuple-element.125.refs_0_, ...), custom_call_target="tpu_custom_call" | custom-call | flops 1024 | bytes 1024 | tf_op jit(solution)/shard_map/expert_block/pallas_call | solution.py:118
  54.7 1.6 %collective-permute-start.10 = (bf16[48,3584]{1,0:T(8,128)(2,1)S(1)}, bf16[48,3584]{1,0:T(8,128)(2,1)S(1)}, u32[]{:S(2)}, u32[]{:S(2)}) collective-permute-start(bf16[48,3584]{1,0:T(8,128)(2,1)S(1)} %get-tuple-element.158), channel_id=1, source_target_pairs={{0,2},{1,3},{2,0},{3,1},{4,6},{5,7},{6,4},{7,5},{8,10},{9,11},{10,... | collective-permute-start | bytes 1032200 | tf_op jit(solution)/shard_map/ppermute | solution.py:25
  56.3 4.0 %expert_block.7 = (bf16[32,3584]{1,0:T(8,128)(2,1)S(1)}, bf16[32,3584]{1,0:T(8,128)(2,1)S(1)}) custom-call(bf16[80,3584]{1,0:T(8,128)(2,1)S(1)} %collective-permute-done.3.whole_ref.near_ref, bf16[32,3584]{1,0:T(8,128)(2,1)S(1)} %collective-permute-done.4.far_ref, bf16[10752,512]{1,0:T(8,128)(2,1)S(1)} %get-tuple-element.125.refs_0_, ...), custom_call_target="tpu_custom_call" | custom-call | flops 1024 | bytes 1024 | tf_op jit(solution)/shard_map/expert_block/pallas_call | solution.py:118
  60.8 3.8 %expert_block.8 = (bf16[80,3584]{1,0:T(8,128)(2,1)S(1)}, bf16[80,3584]{1,0:T(8,128)(2,1)S(1)}) custom-call(bf16[80,3584]{1,0:T(8,128)(2,1)S(1)} %get-tuple-element.135.near_ref, bf16[80,3584]{1,0:T(8,128)(2,1)S(1)} %collective-permute-done.far_ref, bf16[10752,512]{1,0:T(8,128)(2,1)S(1)} %get-tuple-element.125.refs_0_, ...), custom_call_target="tpu_custom_call" | custom-call | flops 1024 | bytes 1024 | tf_op jit(solution)/shard_map/expert_block/pallas_call | solution.py:118
  64.7 2.2 %collective-permute-done.8.far_ref = bf16[80,3584]{1,0:T(8,128)(2,1)S(1)} collective-permute-done((bf16[80,3584]{1,0:T(8,128)(2,1)S(1)}, bf16[80,3584]{1,0:T(8,128)(2,1)S(1)}, u32[]{:S(2)}, u32[]{:S(2)}) %collective-permute-start.8) | collective-permute-done | bytes 573472 | tf_op jit(solution)/shard_map/ppermute | solution.py:25
  69.8 4.0 %expert_block.9 = (bf16[80,3584]{1,0:T(8,128)(2,1)S(1)}, bf16[80,3584]{1,0:T(8,128)(2,1)S(1)}) custom-call(bf16[80,3584]{1,0:T(8,128)(2,1)S(1)} %collective-permute-done.2.near_ref, bf16[80,3584]{1,0:T(8,128)(2,1)S(1)} %collective-permute-done.8.far_ref, bf16[10752,512]{1,0:T(8,128)(2,1)S(1)} %get-tuple-element.125.refs_0_, ...), custom_call_target="tpu_custom_call" | custom-call | flops 1024 | bytes 1024 | tf_op jit(solution)/shard_map/expert_block/pallas_call | solution.py:118
  73.9 4.0 %collective-permute-done.9.far_ref = bf16[48,3584]{1,0:T(8,128)(2,1)S(1)} collective-permute-done((bf16[48,3584]{1,0:T(8,128)(2,1)S(1)}, bf16[48,3584]{1,0:T(8,128)(2,1)S(1)}, u32[]{:S(2)}, u32[]{:S(2)}) %collective-permute-start.9) | collective-permute-done | bytes 344096 | tf_op jit(solution)/shard_map/ppermute | solution.py:25
  77.8 3.7 %expert_block.10 = (bf16[48,3584]{1,0:T(8,128)(2,1)S(1)}, bf16[48,3584]{1,0:T(8,128)(2,1)S(1)}) custom-call(bf16[80,3584]{1,0:T(8,128)(2,1)S(1)} %collective-permute-done.7.whole_ref.near_ref, bf16[48,3584]{1,0:T(8,128)(2,1)S(1)} %collective-permute-done.9.far_ref, bf16[10752,512]{1,0:T(8,128)(2,1)S(1)} %get-tuple-element.125.refs_0_, ...), custom_call_target="tpu_custom_call" | custom-call | flops 1024 | bytes 1024 | tf_op jit(solution)/shard_map/expert_block/pallas_call | solution.py:118
  82.9 4.0 %expert_block.11 = (bf16[32,3584]{1,0:T(8,128)(2,1)S(1)}, bf16[32,3584]{1,0:T(8,128)(2,1)S(1)}) custom-call(bf16[80,3584]{1,0:T(8,128)(2,1)S(1)} %collective-permute-done.7.whole_ref.near_ref, bf16[32,3584]{1,0:T(8,128)(2,1)S(1)} %collective-permute-done.12.far_ref, bf16[10752,512]{1,0:T(8,128)(2,1)S(1)} %get-tuple-element.125.refs_0_, ...), custom_call_target="tpu_custom_call" | custom-call | flops 1024 | bytes 1024 | tf_op jit(solution)/shard_map/expert_block/pallas_call | solution.py:118
  87.9 7.6 %collective-permute-done.15.refs_2_ = bf16[80,3584]{1,0:T(8,128)(2,1)S(1)} collective-permute-done((bf16[80,3584]{1,0:T(8,128)(2,1)S(1)}, bf16[80,3584]{1,0:T(8,128)(2,1)S(1)}, u32[]{:S(2)}, u32[]{:S(2)}) %collective-permute-start.15) | collective-permute-done | bytes 573472 | tf_op jit(solution)/shard_map/ppermute | solution.py:25
  97.2 2.6 %collective-permute-start.21 = (bf16[80,3584]{1,0:T(8,128)(2,1)S(1)}, bf16[80,3584]{1,0:T(8,128)(2,1)S(1)}, u32[]{:S(2)}, u32[]{:S(2)}) collective-permute-start(bf16[80,3584]{1,0:T(8,128)(2,1)S(1)} %total.5), channel_id=1, source_target_pairs={{0,12},{1,13},{2,14},{3,15},{4,8},{5,9},{6,10},{7,11},{8,4},{9,5},... | collective-permute-start | bytes 1720328 | tf_op jit(solution)/shard_map/ppermute | solution.py:25
  99.8 8.0 %collective-permute-done.17.whole_ref = bf16[80,3584]{1,0:T(8,128)(2,1)S(1)} collective-permute-done((bf16[80,3584]{1,0:T(8,128)(2,1)S(1)}, bf16[80,3584]{1,0:T(8,128)(2,1)S(1)}, u32[]{:S(2)}, u32[]{:S(2)}) %collective-permute-start.17) | collective-permute-done | bytes 573472 | tf_op jit(solution)/shard_map/ppermute | solution.py:25
  110.0 13.0 %collective-permute-done.20.refs_2_ = bf16[32,3584]{1,0:T(8,128)(2,1)S(1)} collective-permute-done((bf16[32,3584]{1,0:T(8,128)(2,1)S(1)}, bf16[32,3584]{1,0:T(8,128)(2,1)S(1)}, u32[]{:S(2)}, u32[]{:S(2)}) %collective-permute-start.20) | collective-permute-done | bytes 229408 | tf_op jit(solution)/shard_map/ppermute | solution.py:25
  123.3 8.2 %collective-permute-done.18.refs_0_ = bf16[80,3584]{1,0:T(8,128)(2,1)S(1)} collective-permute-done((bf16[80,3584]{1,0:T(8,128)(2,1)S(1)}, bf16[80,3584]{1,0:T(8,128)(2,1)S(1)}, u32[]{:S(2)}, u32[]{:S(2)}) %collective-permute-start.18) | collective-permute-done | bytes 573472 | tf_op jit(solution)/shard_map/ppermute | solution.py:25
  131.8 1.9 %score.1 = f32[1,16]{1,0:T(1,128)S(1)} custom-call(s32[1]{0:T(128)} %bitcast.own_ref, bf16[128,3584]{1,0:T(8,128)(2,1)S(1)} %copy-done, f32[1,3584]{1,0:T(1,128)S(1)} %broadcast_in_dim.12.gain_ref, s32[2,128]{1,0:T(2,128)S(1)} %bitcast.8, f32[2,128]{1,0:T(2,128)S(1)} %bitcast.9, bf16[128,3584]{1,0:T(8,128)(2,1)S(1)} %copy-done.1, f32[1,128]{1,0:T(1,128)S(1)} %bitcast.10, ...), custom_call_target="tpu_custom_call" | custom-call | flops 1024 | bytes 1024 | tf_op jit(solution)/shard_map/score/pallas_call | solution.py:180
  134.9 3.5 %collective-permute-done.23 = f32[1,16]{1,0:T(1,128)S(1)} collective-permute-done((f32[1,16]{1,0:T(1,128)S(1)}, f32[1,16]{1,0:T(1,128)S(1)}, u32[]{:S(2)}, u32[]{:S(2)}) %collective-permute-start.23) | collective-permute-done | bytes 96 | tf_op jit(solution)/shard_map/ppermute | solution.py:25
  138.5 3.4 %collective-permute-done.24 = f32[1,16]{1,0:T(1,128)S(1)} collective-permute-done((f32[1,16]{1,0:T(1,128)S(1)}, f32[1,16]{1,0:T(1,128)S(1)}, u32[]{:S(2)}, u32[]{:S(2)}) %collective-permute-start.24) | collective-permute-done | bytes 96 | tf_op jit(solution)/shard_map/ppermute | solution.py:25
  142.1 4.3 %collective-permute-done.25 = f32[1,16]{1,0:T(1,128)S(1)} collective-permute-done((f32[1,16]{1,0:T(1,128)S(1)}, f32[1,16]{1,0:T(1,128)S(1)}, u32[]{:S(2)}, u32[]{:S(2)}) %collective-permute-start.25) | collective-permute-done | bytes 96 | tf_op jit(solution)/shard_map/ppermute | solution.py:25
  (72 shorter events, 20.3 us)
Async XLA Ops:
  5.9 45.0 %collective-permute-start.6 = (bf16[10752,512]{1,0:T(8,128)(2,1)S(1)}, bf16[10752,512]{1,0:T(8,128)(2,1)S(1)}, u32[]{:S(2)}, u32[]{:S(2)}) collective-permute-start(bf16[10752,512]{1,0:T(8,128)(2,1)S(1)} %get-tuple-element.125.refs_0_), channel_id=1, source_target_pairs={{0,1},{1,0},{2,3},{3,2},{4,5},{5,4},{6,7},{7,6},{8,9},{9,8},{10,11... | collective-permute-start | bytes 33030152 | tf_op jit(solution)/shard_map/ppermute | solution.py:25
  6.4 28.4 %collective-permute-start.2 = (bf16[80,3584]{1,0:T(8,128)(2,1)S(1)}, bf16[80,3584]{1,0:T(8,128)(2,1)S(1)}, u32[]{:S(2)}, u32[]{:S(2)}) collective-permute-start(bf16[80,3584]{1,0:T(8,128)(2,1)S(1)} %get-tuple-element.110), channel_id=1, source_target_pairs={{0,4},{1,5},{2,6},{3,7},{4,0},{5,1},{6,2},{7,3},{8,12},{9,13},{10,... | collective-permute-start | bytes 1720328 | tf_op jit(solution)/shard_map/ppermute | solution.py:25
  9.1 28.3 %collective-permute-start.3 = (bf16[80,3584]{1,0:T(8,128)(2,1)S(1)}, bf16[80,3584]{1,0:T(8,128)(2,1)S(1)}, u32[]{:S(2)}, u32[]{:S(2)}) collective-permute-start(bf16[80,3584]{1,0:T(8,128)(2,1)S(1)} %get-tuple-element.112), channel_id=1, source_target_pairs={{0,8},{1,9},{2,10},{3,11},{4,12},{5,13},{6,14},{7,15},{8,0},{9,1},... | collective-permute-start | bytes 1720328 | tf_op jit(solution)/shard_map/ppermute | solution.py:25
  11.7 25.7 %collective-permute-start = (bf16[80,3584]{1,0:T(8,128)(2,1)S(1)}, bf16[80,3584]{1,0:T(8,128)(2,1)S(1)}, u32[]{:S(2)}, u32[]{:S(2)}) collective-permute-start(bf16[80,3584]{1,0:T(8,128)(2,1)S(1)} %get-tuple-element.135.near_ref), channel_id=1, source_target_pairs={{0,2},{1,3},{2,0},{3,1},{4,6},{5,7},{6,4},{7,5},{8,10},{9,11},{10,... | collective-permute-start | bytes 1720328 | tf_op jit(solution)/shard_map/ppermute | solution.py:25
  13.2 25.5 %collective-permute-start.1 = (bf16[80,3584]{1,0:T(8,128)(2,1)S(1)}, bf16[80,3584]{1,0:T(8,128)(2,1)S(1)}, u32[]{:S(2)}, u32[]{:S(2)}) collective-permute-start(bf16[80,3584]{1,0:T(8,128)(2,1)S(1)} %get-tuple-element.110), channel_id=1, source_target_pairs={{0,2},{1,3},{2,0},{3,1},{4,6},{5,7},{6,4},{7,5},{8,10},{9,11},{10,... | collective-permute-start | bytes 1720328 | tf_op jit(solution)/shard_map/ppermute | solution.py:25
  38.8 25.9 %collective-permute-start.7 = (bf16[80,3584]{1,0:T(8,128)(2,1)S(1)}, bf16[80,3584]{1,0:T(8,128)(2,1)S(1)}, u32[]{:S(2)}, u32[]{:S(2)}) collective-permute-start(bf16[80,3584]{1,0:T(8,128)(2,1)S(1)} %get-tuple-element.143), channel_id=1, source_target_pairs={{0,12},{1,13},{2,14},{3,15},{4,8},{5,9},{6,10},{7,11},{8,4},{9,5},... | collective-permute-start | bytes 1720328 | tf_op jit(solution)/shard_map/ppermute | solution.py:25
  39.9 11.0 %collective-permute-start.5 = (bf16[48,3584]{1,0:T(8,128)(2,1)S(1)}, bf16[48,3584]{1,0:T(8,128)(2,1)S(1)}, u32[]{:S(2)}, u32[]{:S(2)}) collective-permute-start(bf16[48,3584]{1,0:T(8,128)(2,1)S(1)} %get-tuple-element.121), channel_id=1, source_target_pairs={{0,2},{1,3},{2,0},{3,1},{4,6},{5,7},{6,4},{7,5},{8,10},{9,11},{10,... | collective-permute-start | bytes 1032200 | tf_op jit(solution)/shard_map/ppermute | solution.py:25
  41.5 25.5 %collective-permute-start.8 = (bf16[80,3584]{1,0:T(8,128)(2,1)S(1)}, bf16[80,3584]{1,0:T(8,128)(2,1)S(1)}, u32[]{:S(2)}, u32[]{:S(2)}) collective-permute-start(bf16[80,3584]{1,0:T(8,128)(2,1)S(1)} %collective-permute-done.1), channel_id=1, source_target_pairs={{0,4},{1,5},{2,6},{3,7},{4,0},{5,1},{6,2},{7,3},{8,12},{9,13},{10,... | collective-permute-start | bytes 1720328 | tf_op jit(solution)/shard_map/ppermute | solution.py:25
  41.5 14.8 %collective-permute-start.4 = (bf16[32,3584]{1,0:T(8,128)(2,1)S(1)}, bf16[32,3584]{1,0:T(8,128)(2,1)S(1)}, u32[]{:S(2)}, u32[]{:S(2)}) collective-permute-start(bf16[32,3584]{1,0:T(8,128)(2,1)S(1)} %get-tuple-element.119), channel_id=1, source_target_pairs={{0,2},{1,3},{2,0},{3,1},{4,6},{5,7},{6,4},{7,5},{8,10},{9,11},{10,... | collective-permute-start | bytes 688136 | tf_op jit(solution)/shard_map/ppermute | solution.py:25
  54.7 13.2 %collective-permute-start.10 = (bf16[48,3584]{1,0:T(8,128)(2,1)S(1)}, bf16[48,3584]{1,0:T(8,128)(2,1)S(1)}, u32[]{:S(2)}, u32[]{:S(2)}) collective-permute-start(bf16[48,3584]{1,0:T(8,128)(2,1)S(1)} %get-tuple-element.158), channel_id=1, source_target_pairs={{0,2},{1,3},{2,0},{3,1},{4,6},{5,7},{6,4},{7,5},{8,10},{9,11},{10,... | collective-permute-start | bytes 1032200 | tf_op jit(solution)/shard_map/ppermute | solution.py:25
  60.2 7.7 %collective-permute-start.11 = (bf16[32,3584]{1,0:T(8,128)(2,1)S(1)}, bf16[32,3584]{1,0:T(8,128)(2,1)S(1)}, u32[]{:S(2)}, u32[]{:S(2)}) collective-permute-start(bf16[32,3584]{1,0:T(8,128)(2,1)S(1)} %get-tuple-element.159), channel_id=1, source_target_pairs={{0,2},{1,3},{2,0},{3,1},{4,6},{5,7},{6,4},{7,5},{8,10},{9,11},{10,... | collective-permute-start | bytes 688136 | tf_op jit(solution)/shard_map/ppermute | solution.py:25
  66.9 10.9 %collective-permute-start.9 = (bf16[48,3584]{1,0:T(8,128)(2,1)S(1)}, bf16[48,3584]{1,0:T(8,128)(2,1)S(1)}, u32[]{:S(2)}, u32[]{:S(2)}) collective-permute-start(bf16[48,3584]{1,0:T(8,128)(2,1)S(1)} %get-tuple-element.154), channel_id=1, source_target_pairs={{0,2},{1,3},{2,0},{3,1},{4,6},{5,7},{6,4},{7,5},{8,10},{9,11},{10,... | collective-permute-start | bytes 1032200 | tf_op jit(solution)/shard_map/ppermute | solution.py:25
  68.2 27.3 %collective-permute-start.15 = (bf16[80,3584]{1,0:T(8,128)(2,1)S(1)}, bf16[80,3584]{1,0:T(8,128)(2,1)S(1)}, u32[]{:S(2)}, u32[]{:S(2)}) collective-permute-start(bf16[80,3584]{1,0:T(8,128)(2,1)S(1)} %total.4), channel_id=1, source_target_pairs={{0,8},{1,9},{2,10},{3,11},{4,12},{5,13},{6,14},{7,15},{8,0},{9,1},... | collective-permute-start | bytes 1720328 | tf_op jit(solution)/shard_map/ppermute | solution.py:25
  69.3 13.6 %collective-permute-start.12 = (bf16[32,3584]{1,0:T(8,128)(2,1)S(1)}, bf16[32,3584]{1,0:T(8,128)(2,1)S(1)}, u32[]{:S(2)}, u32[]{:S(2)}) collective-permute-start(bf16[32,3584]{1,0:T(8,128)(2,1)S(1)} %get-tuple-element.177), channel_id=1, source_target_pairs={{0,2},{1,3},{2,0},{3,1},{4,6},{5,7},{6,4},{7,5},{8,10},{9,11},{10,... | collective-permute-start | bytes 688136 | tf_op jit(solution)/shard_map/ppermute | solution.py:25
  81.6 26.3 %collective-permute-start.17 = (bf16[80,3584]{1,0:T(8,128)(2,1)S(1)}, bf16[80,3584]{1,0:T(8,128)(2,1)S(1)}, u32[]{:S(2)}, u32[]{:S(2)}) collective-permute-start(bf16[80,3584]{1,0:T(8,128)(2,1)S(1)} %get-tuple-element.195), channel_id=1, source_target_pairs={{0,4},{1,5},{2,6},{3,7},{4,0},{5,1},{6,2},{7,3},{8,12},{9,13},{10,... | collective-permute-start | bytes 1720328 | tf_op jit(solution)/shard_map/ppermute | solution.py:25
  81.7 13.8 %collective-permute-start.13 = (bf16[48,3584]{1,0:T(8,128)(2,1)S(1)}, bf16[48,3584]{1,0:T(8,128)(2,1)S(1)}, u32[]{:S(2)}, u32[]{:S(2)}) collective-permute-start(bf16[48,3584]{1,0:T(8,128)(2,1)S(1)} %get-tuple-element.185), channel_id=1, source_target_pairs={{0,2},{1,3},{2,0},{3,1},{4,6},{5,7},{6,4},{7,5},{8,10},{9,11},{10,... | collective-permute-start | bytes 1032200 | tf_op jit(solution)/shard_map/ppermute | solution.py:25
  86.9 8.6 %collective-permute-start.14 = (bf16[32,3584]{1,0:T(8,128)(2,1)S(1)}, bf16[32,3584]{1,0:T(8,128)(2,1)S(1)}, u32[]{:S(2)}, u32[]{:S(2)}) collective-permute-start(bf16[32,3584]{1,0:T(8,128)(2,1)S(1)} %get-tuple-element.186), channel_id=1, source_target_pairs={{0,2},{1,3},{2,0},{3,1},{4,6},{5,7},{6,4},{7,5},{8,10},{9,11},{10,... | collective-permute-start | bytes 688136 | tf_op jit(solution)/shard_map/ppermute | solution.py:25
  95.8 27.2 %collective-permute-start.16 = (bf16[80,3584]{1,0:T(8,128)(2,1)S(1)}, bf16[80,3584]{1,0:T(8,128)(2,1)S(1)}, u32[]{:S(2)}, u32[]{:S(2)}) collective-permute-start(bf16[80,3584]{1,0:T(8,128)(2,1)S(1)} %get-tuple-element.194), channel_id=1, source_target_pairs={{0,2},{1,3},{2,0},{3,1},{4,6},{5,7},{6,4},{7,5},{8,10},{9,11},{10,... | collective-permute-start | bytes 1720328 | tf_op jit(solution)/shard_map/ppermute | solution.py:25
  96.5 34.9 %collective-permute-start.18 = (bf16[80,3584]{1,0:T(8,128)(2,1)S(1)}, bf16[80,3584]{1,0:T(8,128)(2,1)S(1)}, u32[]{:S(2)}, u32[]{:S(2)}) collective-permute-start(bf16[80,3584]{1,0:T(8,128)(2,1)S(1)} %get-tuple-element.203), channel_id=1, source_target_pairs={{0,4},{1,5},{2,6},{3,7},{4,0},{5,1},{6,2},{7,3},{8,12},{9,13},{10,... | collective-permute-start | bytes 1720328 | tf_op jit(solution)/shard_map/ppermute | solution.py:25
  97.2 34.5 %collective-permute-start.21 = (bf16[80,3584]{1,0:T(8,128)(2,1)S(1)}, bf16[80,3584]{1,0:T(8,128)(2,1)S(1)}, u32[]{:S(2)}, u32[]{:S(2)}) collective-permute-start(bf16[80,3584]{1,0:T(8,128)(2,1)S(1)} %total.5), channel_id=1, source_target_pairs={{0,12},{1,13},{2,14},{3,15},{4,8},{5,9},{6,10},{7,11},{8,4},{9,5},... | collective-permute-start | bytes 1720328 | tf_op jit(solution)/shard_map/ppermute | solution.py:25
  107.9 15.1 %collective-permute-start.19 = (bf16[48,3584]{1,0:T(8,128)(2,1)S(1)}, bf16[48,3584]{1,0:T(8,128)(2,1)S(1)}, u32[]{:S(2)}, u32[]{:S(2)}) collective-permute-start(bf16[48,3584]{1,0:T(8,128)(2,1)S(1)} %get-tuple-element.205), channel_id=1, source_target_pairs={{0,2},{1,3},{2,0},{3,1},{4,6},{5,7},{6,4},{7,5},{8,10},{9,11},{10,... | collective-permute-start | bytes 1032200 | tf_op jit(solution)/shard_map/ppermute | solution.py:25
  108.6 14.3 %collective-permute-start.20 = (bf16[32,3584]{1,0:T(8,128)(2,1)S(1)}, bf16[32,3584]{1,0:T(8,128)(2,1)S(1)}, u32[]{:S(2)}, u32[]{:S(2)}) collective-permute-start(bf16[32,3584]{1,0:T(8,128)(2,1)S(1)} %get-tuple-element.207), channel_id=1, source_target_pairs={{0,2},{1,3},{2,0},{3,1},{4,6},{5,7},{6,4},{7,5},{8,10},{9,11},{10,... | collective-permute-start | bytes 688136 | tf_op jit(solution)/shard_map/ppermute | solution.py:25
  134.9 3.5 %collective-permute-start.23 = (f32[1,16]{1,0:T(1,128)S(1)}, f32[1,16]{1,0:T(1,128)S(1)}, u32[]{:S(2)}, u32[]{:S(2)}) collective-permute-start(f32[1,16]{1,0:T(1,128)S(1)} %add.18), channel_id=1, source_target_pairs={{0,2},{1,3},{2,0},{3,1},{4,6},{5,7},{6,4},{7,5},{8,10},{9,11},{10,... | collective-permute-start | bytes 200 | tf_op jit(solution)/shard_map/ppermute | solution.py:25
  142.0 4.4 %collective-permute-start.25 = (f32[1,16]{1,0:T(1,128)S(1)}, f32[1,16]{1,0:T(1,128)S(1)}, u32[]{:S(2)}, u32[]{:S(2)}) collective-permute-start(f32[1,16]{1,0:T(1,128)S(1)} %add.20), channel_id=1, source_target_pairs={{0,8},{1,9},{2,10},{3,11},{4,12},{5,13},{6,14},{7,15},{8,0},{9,1},... | collective-permute-start | bytes 200 | tf_op jit(solution)/shard_map/ppermute | solution.py:25
  (11 other events, 331.6 us)

commit v7 on v6

--- a/solution.py
+++ b/solution.py
@@ -319,7 +319,11 @@
     far[0], far[1] = swap(near[0], side), swap(near[1], side)
     leave(1)
     leave(2)
-    far[0], far[1], near[1], near[2] = order.mark(far[0], far[1], near[1], near[2])
+    far[0], weights[1] = order.mark(far[0], weights[1])
+    work_whole(0)
+    arrive(2)
+    arrive(1)
+    far[1] = order.mark_one(far[1])
     for k in range(3, experts + 1):
         share(k - 1)
         if k < experts:
@@ -331,26 +335,24 @@
             leave_back(k - 2)
         if k == experts:
             work_whole(1)
-            theirs[1] = swap(theirs[1], spread)
+            theirs[1] = [swap(piece, spread) for piece in order.mark(*cut(theirs[1], pieces))]
         work(k - 1)
-        if k == 3:
-            work_whole(0)
         if k < experts:
             arrive(k)
         if k == 3:
             far[1] = order.mark_one(far[1])
         if k > 3:
             arrive_back(k - 2)
+    theirs[1] = order.mark(*theirs[1])
     home(experts - 1)
     leave_back(experts - 1)
     mine[1] = [swap(order.late(mine[1]), spread)]
     mine[0], theirs[0] = [mine[0]], [swap(order.late(theirs[0]), side)]
-    theirs[1] = order.mark(*cut(order.mark_one(theirs[1]), pieces))
     theirs[1] = [swap(order.late(piece), side) for piece in theirs[1]]
+    arrive_back(experts - 1)
     home(0)
     mine[1] = order.mark(*mine[1])
     home(1)
-    arrive_back(experts - 1)
     blocks = [back[k] for k in range(experts)]
     local = score(
         own,

time: 147 us -> 144 us (0.980)
  waiting for transfers between devices: 89.4 us -> 78.5 us
  starting transfers between devices: 24.2 us -> 31.6 us
    ppermute x26 -> x27, waiting for transfers between devices: 89.4 us -> 78.5 us  [swap(): return lax.ppermute(value, 'expert', pairs)]
    ppermute x26 -> x27, starting transfers between devices: 24.2 us -> 31.6 us  [swap(): return lax.ppermute(value, 'expert', pairs)]
  transfers between devices with their start and end apart: 26 -> 27, of which waited for: 14 -> 14; matrix products, arithmetic and copies ran while one was open for 0% -> 0% of each run, Pallas kernels for 17% -> 17%
where the time goes in v7:
time: 144 us
  waiting for transfers between devices  78.5 us (55%)
  starting transfers between devices  31.6 us (22%)
  Pallas kernels  30.9 us (21%)
    ppermute x27, waiting for transfers between devices, swap(): return lax.ppermute(value, 'expert', pairs)  78.5 us
    ppermute x27, starting transfers between devices, swap(): return lax.ppermute(value, 'expert', pairs)  31.6 us
    pallas_call x6, Pallas kernels, expert_block(): pl.pallas_call(functools.partial(expert_kernel, first), out_shape=[jax.Sh...  23.3 us
    pallas_call x1, Pallas kernels, pack(): pl.pallas_call(pack_kernel, out_shape=[jax.ShapeDtypeStruct(shape, BF16)...  4.5 us
  transfers between devices with their start and end apart: 27, of which 14 were waited for; matrix products, arithmetic and copies ran while one was open for 0% of the time, Pallas kernels for 17%

profile of v7, /device:TPU:0, one launch (start us, length us, event | category | flops | bytes accessed | tf_op | source)
XLA Modules:
  0.0 143.7 jit_solution(776412136209340922)
XLA Ops:
  1.4 4.5 %pack.1 = (bf16[80,3584]{1,0:T(8,128)(2,1)S(1)}, bf16[80,3584]{1,0:T(8,128)(2,1)S(1)}, bf16[80,3584]{1,0:T(8,128)(2,1)S(1)}, bf16[80,3584]{1,0:T(8,128)(2,1)S(1)}, bf16[10752,512]{1,0:T(8,128)(2,1)S(1)}) custom-call(s32[1]{0:T(128)} %bitcast.own_ref, bf16[128,3584]{1,0:T(8,128)(2,1)} %tokens_ref.1, f32[1,3584]{1,0:T(1,128)S(1)} %broadcast_in_dim.15.gain_ref, ...), custom_call_target="tpu_custom_call" | custom-call | flops 1024 | bytes 1024 | tf_op jit(solution)/shard_map/pack/pallas_call | solution.py:78
  6.4 2.6 %collective-permute-start = (bf16[80,3584]{1,0:T(8,128)(2,1)S(1)}, bf16[80,3584]{1,0:T(8,128)(2,1)S(1)}, u32[]{:S(2)}, u32[]{:S(2)}) collective-permute-start(bf16[80,3584]{1,0:T(8,128)(2,1)S(1)} %get-tuple-element.116.near_ref), channel_id=1, source_target_pairs={{0,2},{1,3},{2,0},{3,1},{4,6},{5,7},{6,4},{7,5},{8,10},{9,11},{10,... | collective-permute-start | bytes 1720328 | tf_op jit(solution)/shard_map/ppermute | solution.py:25
  9.0 2.6 %collective-permute-start.2 = (bf16[80,3584]{1,0:T(8,128)(2,1)S(1)}, bf16[80,3584]{1,0:T(8,128)(2,1)S(1)}, u32[]{:S(2)}, u32[]{:S(2)}) collective-permute-start(bf16[80,3584]{1,0:T(8,128)(2,1)S(1)} %get-tuple-element.126), channel_id=1, source_target_pairs={{0,8},{1,9},{2,10},{3,11},{4,12},{5,13},{6,14},{7,15},{8,0},{9,1},... | collective-permute-start | bytes 1720328 | tf_op jit(solution)/shard_map/ppermute | solution.py:25
  13.7 9.2 %collective-permute-done.far_ref = bf16[80,3584]{1,0:T(8,128)(2,1)S(1)} collective-permute-done((bf16[80,3584]{1,0:T(8,128)(2,1)S(1)}, bf16[80,3584]{1,0:T(8,128)(2,1)S(1)}, u32[]{:S(2)}, u32[]{:S(2)}) %collective-permute-start) | collective-permute-done | bytes 573472 | tf_op jit(solution)/shard_map/ppermute | solution.py:25
  23.0 3.8 %expert_block.6 = (bf16[80,3584]{1,0:T(8,128)(2,1)S(1)}, bf16[80,3584]{1,0:T(8,128)(2,1)S(1)}) custom-call(bf16[80,3584]{1,0:T(8,128)(2,1)S(1)} %get-tuple-element.116.near_ref, bf16[80,3584]{1,0:T(8,128)(2,1)S(1)} %collective-permute-done.far_ref, bf16[10752,512]{1,0:T(8,128)(2,1)S(1)} %get-tuple-element.114.refs_0_, ...), custom_call_target="tpu_custom_call" | custom-call | flops 1024 | bytes 1024 | tf_op jit(solution)/shard_map/expert_block/pallas_call | solution.py:118
  26.8 10.6 %collective-permute-done.2.whole_ref.near_ref = bf16[80,3584]{1,0:T(8,128)(2,1)S(1)} collective-permute-done((bf16[80,3584]{1,0:T(8,128)(2,1)S(1)}, bf16[80,3584]{1,0:T(8,128)(2,1)S(1)}, u32[]{:S(2)}, u32[]{:S(2)}) %collective-permute-start.2) | collective-permute-done | bytes 573472 | tf_op jit(solution)/shard_map/ppermute | solution.py:25
  38.1 3.3 %collective-permute-start.5 = (bf16[80,3584]{1,0:T(8,128)(2,1)S(1)}, bf16[80,3584]{1,0:T(8,128)(2,1)S(1)}, u32[]{:S(2)}, u32[]{:S(2)}) collective-permute-start(bf16[80,3584]{1,0:T(8,128)(2,1)S(1)} %get-tuple-element.137), channel_id=1, source_target_pairs={{0,12},{1,13},{2,14},{3,15},{4,8},{5,9},{6,10},{7,11},{8,4},{9,5},... | collective-permute-start | bytes 1720328 | tf_op jit(solution)/shard_map/ppermute | solution.py:25
  42.9 5.8 %collective-permute-done.7.far_ref = bf16[48,3584]{1,0:T(8,128)(2,1)S(1)} collective-permute-done((bf16[48,3584]{1,0:T(8,128)(2,1)S(1)}, bf16[48,3584]{1,0:T(8,128)(2,1)S(1)}, u32[]{:S(2)}, u32[]{:S(2)}) %collective-permute-start.7) | collective-permute-done | bytes 344096 | tf_op jit(solution)/shard_map/ppermute | solution.py:25
  48.7 3.7 %expert_block.7 = (bf16[48,3584]{1,0:T(8,128)(2,1)S(1)}, bf16[48,3584]{1,0:T(8,128)(2,1)S(1)}) custom-call(bf16[80,3584]{1,0:T(8,128)(2,1)S(1)} %collective-permute-done.2.whole_ref.near_ref, bf16[48,3584]{1,0:T(8,128)(2,1)S(1)} %collective-permute-done.7.far_ref, bf16[10752,512]{1,0:T(8,128)(2,1)S(1)} %get-tuple-element.114.refs_0_, ...), custom_call_target="tpu_custom_call" | custom-call | flops 1024 | bytes 1024 | tf_op jit(solution)/shard_map/expert_block/pallas_call | solution.py:118
  52.9 4.0 %expert_block.8 = (bf16[32,3584]{1,0:T(8,128)(2,1)S(1)}, bf16[32,3584]{1,0:T(8,128)(2,1)S(1)}) custom-call(bf16[80,3584]{1,0:T(8,128)(2,1)S(1)} %collective-permute-done.2.whole_ref.near_ref, bf16[32,3584]{1,0:T(8,128)(2,1)S(1)} %collective-permute-done.6.far_ref, bf16[10752,512]{1,0:T(8,128)(2,1)S(1)} %get-tuple-element.114.refs_0_, ...), custom_call_target="tpu_custom_call" | custom-call | flops 1024 | bytes 1024 | tf_op jit(solution)/shard_map/expert_block/pallas_call | solution.py:118
  58.6 8.1 %collective-permute-done.8.far_ref = bf16[80,3584]{1,0:T(8,128)(2,1)S(1)} collective-permute-done((bf16[80,3584]{1,0:T(8,128)(2,1)S(1)}, bf16[80,3584]{1,0:T(8,128)(2,1)S(1)}, u32[]{:S(2)}, u32[]{:S(2)}) %collective-permute-start.8) | collective-permute-done | bytes 573472 | tf_op jit(solution)/shard_map/ppermute | solution.py:25
  69.6 4.0 %expert_block.9 = (bf16[80,3584]{1,0:T(8,128)(2,1)S(1)}, bf16[80,3584]{1,0:T(8,128)(2,1)S(1)}) custom-call(bf16[80,3584]{1,0:T(8,128)(2,1)S(1)} %collective-permute-done.4.near_ref, bf16[80,3584]{1,0:T(8,128)(2,1)S(1)} %collective-permute-done.8.far_ref, bf16[10752,512]{1,0:T(8,128)(2,1)S(1)} %get-tuple-element.114.refs_0_, ...), custom_call_target="tpu_custom_call" | custom-call | flops 1024 | bytes 1024 | tf_op jit(solution)/shard_map/expert_block/pallas_call | solution.py:118
  75.4 2.2 %collective-permute-done.9.far_ref = bf16[48,3584]{1,0:T(8,128)(2,1)S(1)} collective-permute-done((bf16[48,3584]{1,0:T(8,128)(2,1)S(1)}, bf16[48,3584]{1,0:T(8,128)(2,1)S(1)}, u32[]{:S(2)}, u32[]{:S(2)}) %collective-permute-start.9) | collective-permute-done | bytes 344096 | tf_op jit(solution)/shard_map/ppermute | solution.py:25
  77.6 3.7 %expert_block.10 = (bf16[48,3584]{1,0:T(8,128)(2,1)S(1)}, bf16[48,3584]{1,0:T(8,128)(2,1)S(1)}) custom-call(bf16[80,3584]{1,0:T(8,128)(2,1)S(1)} %collective-permute-done.5.whole_ref.near_ref, bf16[48,3584]{1,0:T(8,128)(2,1)S(1)} %collective-permute-done.9.far_ref, bf16[10752,512]{1,0:T(8,128)(2,1)S(1)} %get-tuple-element.114.refs_0_, ...), custom_call_target="tpu_custom_call" | custom-call | flops 1024 | bytes 1024 | tf_op jit(solution)/shard_map/expert_block/pallas_call | solution.py:118
  82.9 1.8 %collective-permute-start.16 = (bf16[32,3584]{1,0:T(8,128)(2,1)S(1)}, bf16[32,3584]{1,0:T(8,128)(2,1)S(1)}, u32[]{:S(2)}, u32[]{:S(2)}) collective-permute-start(bf16[32,3584]{1,0:T(8,128)(2,1)S(1)} %get-tuple-element.201), channel_id=1, source_target_pairs={{0,4},{1,5},{2,6},{3,7},{4,0},{5,1},{6,2},{7,3},{8,12},{9,13},{10,... | collective-permute-start | bytes 688136 | tf_op jit(solution)/shard_map/ppermute | solution.py:25
  84.7 4.0 %expert_block.11 = (bf16[32,3584]{1,0:T(8,128)(2,1)S(1)}, bf16[32,3584]{1,0:T(8,128)(2,1)S(1)}) custom-call(bf16[80,3584]{1,0:T(8,128)(2,1)S(1)} %collective-permute-done.5.whole_ref.near_ref, bf16[32,3584]{1,0:T(8,128)(2,1)S(1)} %collective-permute-done.12.far_ref, bf16[10752,512]{1,0:T(8,128)(2,1)S(1)} %get-tuple-element.114.refs_0_, ...), custom_call_target="tpu_custom_call" | custom-call | flops 1024 | bytes 1024 | tf_op jit(solution)/shard_map/expert_block/pallas_call | solution.py:118
  89.3 7.1 %collective-permute-done.17.refs_2_ = bf16[80,3584]{1,0:T(8,128)(2,1)S(1)} collective-permute-done((bf16[80,3584]{1,0:T(8,128)(2,1)S(1)}, bf16[80,3584]{1,0:T(8,128)(2,1)S(1)}, u32[]{:S(2)}, u32[]{:S(2)}) %collective-permute-start.17) | collective-permute-done | bytes 573472 | tf_op jit(solution)/shard_map/ppermute | solution.py:25
  96.4 3.3 %collective-permute-done.16 = bf16[32,3584]{1,0:T(8,128)(2,1)S(1)} collective-permute-done((bf16[32,3584]{1,0:T(8,128)(2,1)S(1)}, bf16[32,3584]{1,0:T(8,128)(2,1)S(1)}, u32[]{:S(2)}, u32[]{:S(2)}) %collective-permute-start.16) | collective-permute-done | bytes 229408 | tf_op jit(solution)/shard_map/ppermute | solution.py:25
  100.1 1.8 %collective-permute-start.22 = (bf16[80,3584]{1,0:T(8,128)(2,1)S(1)}, bf16[80,3584]{1,0:T(8,128)(2,1)S(1)}, u32[]{:S(2)}, u32[]{:S(2)}) collective-permute-start(bf16[80,3584]{1,0:T(8,128)(2,1)S(1)} %total.5), channel_id=1, source_target_pairs={{0,12},{1,13},{2,14},{3,15},{4,8},{5,9},{6,10},{7,11},{8,4},{9,5},... | collective-permute-start | bytes 1720328 | tf_op jit(solution)/shard_map/ppermute | solution.py:25
  105.5 22.2 %collective-permute-done.21.refs_2_ = bf16[32,3584]{1,0:T(8,128)(2,1)S(1)} collective-permute-done((bf16[32,3584]{1,0:T(8,128)(2,1)S(1)}, bf16[32,3584]{1,0:T(8,128)(2,1)S(1)}, u32[]{:S(2)}, u32[]{:S(2)}) %collective-permute-start.21) | collective-permute-done | bytes 229408 | tf_op jit(solution)/shard_map/ppermute | solution.py:25
  128.4 1.9 %score.1 = f32[1,16]{1,0:T(1,128)S(1)} custom-call(s32[1]{0:T(128)} %bitcast.own_ref, bf16[128,3584]{1,0:T(8,128)(2,1)S(1)} %copy-done, f32[1,3584]{1,0:T(1,128)S(1)} %broadcast_in_dim.12.gain_ref, s32[2,128]{1,0:T(2,128)S(1)} %bitcast.8, f32[2,128]{1,0:T(2,128)S(1)} %bitcast.9, bf16[128,3584]{1,0:T(8,128)(2,1)S(1)} %copy-done.1, f32[1,128]{1,0:T(1,128)S(1)} %bitcast.10, ...), custom_call_target="tpu_custom_call" | custom-call | flops 1024 | bytes 1024 | tf_op jit(solution)/shard_map/score/pallas_call | solution.py:180
  132.0 3.0 %collective-permute-done.24 = f32[1,16]{1,0:T(1,128)S(1)} collective-permute-done((f32[1,16]{1,0:T(1,128)S(1)}, f32[1,16]{1,0:T(1,128)S(1)}, u32[]{:S(2)}, u32[]{:S(2)}) %collective-permute-start.24) | collective-permute-done | bytes 96 | tf_op jit(solution)/shard_map/ppermute | solution.py:25
  135.9 2.7 %collective-permute-done.25 = f32[1,16]{1,0:T(1,128)S(1)} collective-permute-done((f32[1,16]{1,0:T(1,128)S(1)}, f32[1,16]{1,0:T(1,128)S(1)}, u32[]{:S(2)}, u32[]{:S(2)}) %collective-permute-start.25) | collective-permute-done | bytes 96 | tf_op jit(solution)/shard_map/ppermute | solution.py:25
  140.0 2.9 %collective-permute-done.26 = f32[1,16]{1,0:T(1,128)S(1)} collective-permute-done((f32[1,16]{1,0:T(1,128)S(1)}, f32[1,16]{1,0:T(1,128)S(1)}, u32[]{:S(2)}, u32[]{:S(2)}) %collective-permute-start.26) | collective-permute-done | bytes 96 | tf_op jit(solution)/shard_map/ppermute | solution.py:25
  (74 shorter events, 24.0 us)
Async XLA Ops:
  5.9 17.1 %collective-permute-start.1 = (bf16[10752,512]{1,0:T(8,128)(2,1)S(1)}, bf16[10752,512]{1,0:T(8,128)(2,1)S(1)}, u32[]{:S(2)}, u32[]{:S(2)}) collective-permute-start(bf16[10752,512]{1,0:T(8,128)(2,1)S(1)} %get-tuple-element.114.refs_0_), channel_id=1, source_target_pairs={{0,1},{1,0},{2,3},{3,2},{4,5},{5,4},{6,7},{7,6},{8,9},{9,8},{10,11... | collective-permute-start | bytes 33030152 | tf_op jit(solution)/shard_map/ppermute | solution.py:25
  6.4 16.4 %collective-permute-start = (bf16[80,3584]{1,0:T(8,128)(2,1)S(1)}, bf16[80,3584]{1,0:T(8,128)(2,1)S(1)}, u32[]{:S(2)}, u32[]{:S(2)}) collective-permute-start(bf16[80,3584]{1,0:T(8,128)(2,1)S(1)} %get-tuple-element.116.near_ref), channel_id=1, source_target_pairs={{0,2},{1,3},{2,0},{3,1},{4,6},{5,7},{6,4},{7,5},{8,10},{9,11},{10,... | collective-permute-start | bytes 1720328 | tf_op jit(solution)/shard_map/ppermute | solution.py:25
  9.0 28.3 %collective-permute-start.2 = (bf16[80,3584]{1,0:T(8,128)(2,1)S(1)}, bf16[80,3584]{1,0:T(8,128)(2,1)S(1)}, u32[]{:S(2)}, u32[]{:S(2)}) collective-permute-start(bf16[80,3584]{1,0:T(8,128)(2,1)S(1)} %get-tuple-element.126), channel_id=1, source_target_pairs={{0,8},{1,9},{2,10},{3,11},{4,12},{5,13},{6,14},{7,15},{8,0},{9,1},... | collective-permute-start | bytes 1720328 | tf_op jit(solution)/shard_map/ppermute | solution.py:25
  11.6 25.9 %collective-permute-start.4 = (bf16[80,3584]{1,0:T(8,128)(2,1)S(1)}, bf16[80,3584]{1,0:T(8,128)(2,1)S(1)}, u32[]{:S(2)}, u32[]{:S(2)}) collective-permute-start(bf16[80,3584]{1,0:T(8,128)(2,1)S(1)} %get-tuple-element.132), channel_id=1, source_target_pairs={{0,4},{1,5},{2,6},{3,7},{4,0},{5,1},{6,2},{7,3},{8,12},{9,13},{10,... | collective-permute-start | bytes 1720328 | tf_op jit(solution)/shard_map/ppermute | solution.py:25
  13.2 24.4 %collective-permute-start.3 = (bf16[80,3584]{1,0:T(8,128)(2,1)S(1)}, bf16[80,3584]{1,0:T(8,128)(2,1)S(1)}, u32[]{:S(2)}, u32[]{:S(2)}) collective-permute-start(bf16[80,3584]{1,0:T(8,128)(2,1)S(1)} %get-tuple-element.132), channel_id=1, source_target_pairs={{0,2},{1,3},{2,0},{3,1},{4,6},{5,7},{6,4},{7,5},{8,10},{9,11},{10,... | collective-permute-start | bytes 1720328 | tf_op jit(solution)/shard_map/ppermute | solution.py:25
  37.6 11.1 %collective-permute-start.7 = (bf16[48,3584]{1,0:T(8,128)(2,1)S(1)}, bf16[48,3584]{1,0:T(8,128)(2,1)S(1)}, u32[]{:S(2)}, u32[]{:S(2)}) collective-permute-start(bf16[48,3584]{1,0:T(8,128)(2,1)S(1)} %get-tuple-element.141), channel_id=1, source_target_pairs={{0,2},{1,3},{2,0},{3,1},{4,6},{5,7},{6,4},{7,5},{8,10},{9,11},{10,... | collective-permute-start | bytes 1032200 | tf_op jit(solution)/shard_map/ppermute | solution.py:25
  38.1 20.4 %collective-permute-start.5 = (bf16[80,3584]{1,0:T(8,128)(2,1)S(1)}, bf16[80,3584]{1,0:T(8,128)(2,1)S(1)}, u32[]{:S(2)}, u32[]{:S(2)}) collective-permute-start(bf16[80,3584]{1,0:T(8,128)(2,1)S(1)} %get-tuple-element.137), channel_id=1, source_target_pairs={{0,12},{1,13},{2,14},{3,15},{4,8},{5,9},{6,10},{7,11},{8,4},{9,5},... | collective-permute-start | bytes 1720328 | tf_op jit(solution)/shard_map/ppermute | solution.py:25
  41.4 25.3 %collective-permute-start.8 = (bf16[80,3584]{1,0:T(8,128)(2,1)S(1)}, bf16[80,3584]{1,0:T(8,128)(2,1)S(1)}, u32[]{:S(2)}, u32[]{:S(2)}) collective-permute-start(bf16[80,3584]{1,0:T(8,128)(2,1)S(1)} %collective-permute-done.3), channel_id=1, source_target_pairs={{0,4},{1,5},{2,6},{3,7},{4,0},{5,1},{6,2},{7,3},{8,12},{9,13},{10,... | collective-permute-start | bytes 1720328 | tf_op jit(solution)/shard_map/ppermute | solution.py:25
  41.4 11.5 %collective-permute-start.6 = (bf16[32,3584]{1,0:T(8,128)(2,1)S(1)}, bf16[32,3584]{1,0:T(8,128)(2,1)S(1)}, u32[]{:S(2)}, u32[]{:S(2)}) collective-permute-start(bf16[32,3584]{1,0:T(8,128)(2,1)S(1)} %get-tuple-element.139), channel_id=1, source_target_pairs={{0,2},{1,3},{2,0},{3,1},{4,6},{5,7},{6,4},{7,5},{8,10},{9,11},{10,... | collective-permute-start | bytes 688136 | tf_op jit(solution)/shard_map/ppermute | solution.py:25
  52.4 15.8 %collective-permute-start.10 = (bf16[48,3584]{1,0:T(8,128)(2,1)S(1)}, bf16[48,3584]{1,0:T(8,128)(2,1)S(1)}, u32[]{:S(2)}, u32[]{:S(2)}) collective-permute-start(bf16[48,3584]{1,0:T(8,128)(2,1)S(1)} %get-tuple-element.167), channel_id=1, source_target_pairs={{0,2},{1,3},{2,0},{3,1},{4,6},{5,7},{6,4},{7,5},{8,10},{9,11},{10,... | collective-permute-start | bytes 1032200 | tf_op jit(solution)/shard_map/ppermute | solution.py:25
  56.9 11.3 %collective-permute-start.11 = (bf16[32,3584]{1,0:T(8,128)(2,1)S(1)}, bf16[32,3584]{1,0:T(8,128)(2,1)S(1)}, u32[]{:S(2)}, u32[]{:S(2)}) collective-permute-start(bf16[32,3584]{1,0:T(8,128)(2,1)S(1)} %get-tuple-element.168), channel_id=1, source_target_pairs={{0,2},{1,3},{2,0},{3,1},{4,6},{5,7},{6,4},{7,5},{8,10},{9,11},{10,... | collective-permute-start | bytes 688136 | tf_op jit(solution)/shard_map/ppermute | solution.py:25
  66.6 10.9 %collective-permute-start.9 = (bf16[48,3584]{1,0:T(8,128)(2,1)S(1)}, bf16[48,3584]{1,0:T(8,128)(2,1)S(1)}, u32[]{:S(2)}, u32[]{:S(2)}) collective-permute-start(bf16[48,3584]{1,0:T(8,128)(2,1)S(1)} %get-tuple-element.163), channel_id=1, source_target_pairs={{0,2},{1,3},{2,0},{3,1},{4,6},{5,7},{6,4},{7,5},{8,10},{9,11},{10,... | collective-permute-start | bytes 1032200 | tf_op jit(solution)/shard_map/ppermute | solution.py:25
  68.4 28.0 %collective-permute-start.17 = (bf16[80,3584]{1,0:T(8,128)(2,1)S(1)}, bf16[80,3584]{1,0:T(8,128)(2,1)S(1)}, u32[]{:S(2)}, u32[]{:S(2)}) collective-permute-start(bf16[80,3584]{1,0:T(8,128)(2,1)S(1)} %total.4), channel_id=1, source_target_pairs={{0,8},{1,9},{2,10},{3,11},{4,12},{5,13},{6,14},{7,15},{8,0},{9,1},... | collective-permute-start | bytes 1720328 | tf_op jit(solution)/shard_map/ppermute | solution.py:25
  69.1 15.6 %collective-permute-start.12 = (bf16[32,3584]{1,0:T(8,128)(2,1)S(1)}, bf16[32,3584]{1,0:T(8,128)(2,1)S(1)}, u32[]{:S(2)}, u32[]{:S(2)}) collective-permute-start(bf16[32,3584]{1,0:T(8,128)(2,1)S(1)} %get-tuple-element.190), channel_id=1, source_target_pairs={{0,2},{1,3},{2,0},{3,1},{4,6},{5,7},{6,4},{7,5},{8,10},{9,11},{10,... | collective-permute-start | bytes 688136 | tf_op jit(solution)/shard_map/ppermute | solution.py:25
  73.6 26.1 %collective-permute-start.15 = (bf16[48,3584]{1,0:T(8,128)(2,1)S(1)}, bf16[48,3584]{1,0:T(8,128)(2,1)S(1)}, u32[]{:S(2)}, u32[]{:S(2)}) collective-permute-start(bf16[48,3584]{1,0:T(8,128)(2,1)S(1)} %get-tuple-element.200), channel_id=1, source_target_pairs={{0,4},{1,5},{2,6},{3,7},{4,0},{5,1},{6,2},{7,3},{8,12},{9,13},{10,... | collective-permute-start | bytes 1032200 | tf_op jit(solution)/shard_map/ppermute | solution.py:25
  81.3 18.4 %collective-permute-start.13 = (bf16[48,3584]{1,0:T(8,128)(2,1)S(1)}, bf16[48,3584]{1,0:T(8,128)(2,1)S(1)}, u32[]{:S(2)}, u32[]{:S(2)}) collective-permute-start(bf16[48,3584]{1,0:T(8,128)(2,1)S(1)} %get-tuple-element.198), channel_id=1, source_target_pairs={{0,2},{1,3},{2,0},{3,1},{4,6},{5,7},{6,4},{7,5},{8,10},{9,11},{10,... | collective-permute-start | bytes 1032200 | tf_op jit(solution)/shard_map/ppermute | solution.py:25
  82.9 16.8 %collective-permute-start.16 = (bf16[32,3584]{1,0:T(8,128)(2,1)S(1)}, bf16[32,3584]{1,0:T(8,128)(2,1)S(1)}, u32[]{:S(2)}, u32[]{:S(2)}) collective-permute-start(bf16[32,3584]{1,0:T(8,128)(2,1)S(1)} %get-tuple-element.201), channel_id=1, source_target_pairs={{0,4},{1,5},{2,6},{3,7},{4,0},{5,1},{6,2},{7,3},{8,12},{9,13},{10,... | collective-permute-start | bytes 688136 | tf_op jit(solution)/shard_map/ppermute | solution.py:25
  88.7 11.0 %collective-permute-start.14 = (bf16[32,3584]{1,0:T(8,128)(2,1)S(1)}, bf16[32,3584]{1,0:T(8,128)(2,1)S(1)}, u32[]{:S(2)}, u32[]{:S(2)}) collective-permute-start(bf16[32,3584]{1,0:T(8,128)(2,1)S(1)} %get-tuple-element.199), channel_id=1, source_target_pairs={{0,2},{1,3},{2,0},{3,1},{4,6},{5,7},{6,4},{7,5},{8,10},{9,11},{10,... | collective-permute-start | bytes 688136 | tf_op jit(solution)/shard_map/ppermute | solution.py:25
  100.0 27.7 %collective-permute-start.19 = (bf16[80,3584]{1,0:T(8,128)(2,1)S(1)}, bf16[80,3584]{1,0:T(8,128)(2,1)S(1)}, u32[]{:S(2)}, u32[]{:S(2)}) collective-permute-start(bf16[80,3584]{1,0:T(8,128)(2,1)S(1)} %get-tuple-element.212), channel_id=1, source_target_pairs={{0,4},{1,5},{2,6},{3,7},{4,0},{5,1},{6,2},{7,3},{8,12},{9,13},{10,... | collective-permute-start | bytes 1720328 | tf_op jit(solution)/shard_map/ppermute | solution.py:25
  100.1 27.9 %collective-permute-start.22 = (bf16[80,3584]{1,0:T(8,128)(2,1)S(1)}, bf16[80,3584]{1,0:T(8,128)(2,1)S(1)}, u32[]{:S(2)}, u32[]{:S(2)}) collective-permute-start(bf16[80,3584]{1,0:T(8,128)(2,1)S(1)} %total.5), channel_id=1, source_target_pairs={{0,12},{1,13},{2,14},{3,15},{4,8},{5,9},{6,10},{7,11},{8,4},{9,5},... | collective-permute-start | bytes 1720328 | tf_op jit(solution)/shard_map/ppermute | solution.py:25
  101.9 26.1 %collective-permute-start.18 = (bf16[80,3584]{1,0:T(8,128)(2,1)S(1)}, bf16[80,3584]{1,0:T(8,128)(2,1)S(1)}, u32[]{:S(2)}, u32[]{:S(2)}) collective-permute-start(bf16[80,3584]{1,0:T(8,128)(2,1)S(1)} %get-tuple-element.210), channel_id=1, source_target_pairs={{0,2},{1,3},{2,0},{3,1},{4,6},{5,7},{6,4},{7,5},{8,10},{9,11},{10,... | collective-permute-start | bytes 1720328 | tf_op jit(solution)/shard_map/ppermute | solution.py:25
  103.4 24.3 %collective-permute-start.20 = (bf16[48,3584]{1,0:T(8,128)(2,1)S(1)}, bf16[48,3584]{1,0:T(8,128)(2,1)S(1)}, u32[]{:S(2)}, u32[]{:S(2)}) collective-permute-start(bf16[48,3584]{1,0:T(8,128)(2,1)S(1)} %collective-permute-done.15), channel_id=1, source_target_pairs={{0,2},{1,3},{2,0},{3,1},{4,6},{5,7},{6,4},{7,5},{8,10},{9,11},{10,... | collective-permute-start | bytes 1032200 | tf_op jit(solution)/shard_map/ppermute | solution.py:25
  103.9 23.8 %collective-permute-start.21 = (bf16[32,3584]{1,0:T(8,128)(2,1)S(1)}, bf16[32,3584]{1,0:T(8,128)(2,1)S(1)}, u32[]{:S(2)}, u32[]{:S(2)}) collective-permute-start(bf16[32,3584]{1,0:T(8,128)(2,1)S(1)} %collective-permute-done.16), channel_id=1, source_target_pairs={{0,2},{1,3},{2,0},{3,1},{4,6},{5,7},{6,4},{7,5},{8,10},{9,11},{10,... | collective-permute-start | bytes 688136 | tf_op jit(solution)/shard_map/ppermute | solution.py:25
  138.5 4.4 %collective-permute-start.26 = (f32[1,16]{1,0:T(1,128)S(1)}, f32[1,16]{1,0:T(1,128)S(1)}, u32[]{:S(2)}, u32[]{:S(2)}) collective-permute-start(f32[1,16]{1,0:T(1,128)S(1)} %add.20), channel_id=1, source_target_pairs={{0,8},{1,9},{2,10},{3,11},{4,12},{5,13},{6,14},{7,15},{8,0},{9,1},... | collective-permute-start | bytes 200 | tf_op jit(solution)/shard_map/ppermute | solution.py:25
  (12 other events, 301.3 us)

commit v8 on v7

--- a/solution.py
+++ b/solution.py
@@ -169,17 +169,18 @@
     inside = iota((sequences, tokens), 0) == seg_ref[...]
     sums = jnp.sum(jnp.where(inside, token_logp, 0.0), axis=1, keepdims=True)
     turn = iota((sequences, sequences), 0) == iota((sequences, sequences), 1)
-    out_ref[...] = jnp.sum(jnp.where(turn, sums, 0.0), axis=0, keepdims=True)
-
-
-def score(own, tokens, gain, picks, gates, target, rest, seg, blocks, capacity, sequences):
+    sums = jnp.sum(jnp.where(turn, sums, 0.0), axis=0, keepdims=True)
+    out_ref[...] = jnp.broadcast_to(sums, out_ref.shape)
+
+
+def score(own, tokens, gain, picks, gates, target, rest, seg, blocks, capacity, outs):
     rows, width = tokens.shape
     slots = sum(block.shape[0] for block in blocks)
     smem = pl.BlockSpec(memory_space=pltpu.SMEM)
     vmem = pl.BlockSpec(memory_space=pltpu.VMEM)
     return pl.pallas_call(
         functools.partial(score_kernel, capacity),
-        out_shape=jax.ShapeDtypeStruct((1, sequences), F32),
+        out_shape=jax.ShapeDtypeStruct(outs, F32),
         in_specs=[smem] + [vmem] * (7 + len(blocks)),
         out_specs=vmem,
         scratch_shapes=[
@@ -298,6 +299,8 @@
         mine[k], theirs[k] = [], []
         for (first, _), piece in zip(pieces, far[k]):
             there = order.mark_one(piece)
+            if first == 0 and k == 2:
+                theirs[0] = order.mark(*theirs[0])
             part, other = order.mark(*expert_block(order.late(near[k]), first, there, weights))
             mine[k].append(part)
             theirs[k].append(swap(other, side))
@@ -321,6 +324,8 @@
     leave(2)
     far[0], weights[1] = order.mark(far[0], weights[1])
     work_whole(0)
+    theirs[0] = [swap(theirs[0], side)]
+    mine[0] = [mine[0]]
     arrive(2)
     arrive(1)
     far[1] = order.mark_one(far[1])
@@ -334,20 +339,18 @@
             home(k - 2)
             leave_back(k - 2)
         if k == experts:
+            far[1] = order.mark_one(far[1])
             work_whole(1)
             theirs[1] = [swap(piece, spread) for piece in order.mark(*cut(theirs[1], pieces))]
         work(k - 1)
         if k < experts:
             arrive(k)
-        if k == 3:
-            far[1] = order.mark_one(far[1])
         if k > 3:
             arrive_back(k - 2)
     theirs[1] = order.mark(*theirs[1])
     home(experts - 1)
     leave_back(experts - 1)
     mine[1] = [swap(order.late(mine[1]), spread)]
-    mine[0], theirs[0] = [mine[0]], [swap(order.late(theirs[0]), side)]
     theirs[1] = [swap(order.late(piece), side) for piece in theirs[1]]
     arrive_back(experts - 1)
     home(0)
@@ -365,13 +368,10 @@
         segment_ids[None, :],
         blocks,
         capacity,
-        ref_logps.shape[0],
+        (devices, ref_logps.shape[0]),
     )
-    mask = 1
-    while mask < devices:
-        local = local + swap(local, mask)
-        mask *= 2
-    sequence_logps = local[0]
+    gathered = lax.all_to_all(local, "expert", split_axis=0, concat_axis=0, tiled=True)
+    sequence_logps = jnp.sum(gathered, axis=0)
     margin = sequence_logps[0::2] - ref_logps[0::2] - (sequence_logps[1::2] - ref_logps[1::2])
     pair_loss = -jax.nn.log_sigmoid(BETA * margin)
     return (sequence_logps, pair_loss)

time: 144 us -> 147 us (1.021)
  starting transfers between devices: 31.6 us -> 39 us
  waiting for transfers between devices: 78.5 us -> 73.3 us
    ppermute x27 -> x23, waiting for transfers between devices: 78.5 us -> 67.1 us  [swap(): return lax.ppermute(value, 'expert', pairs)]
    all_to_all x0 -> x1, waiting for transfers between devices: none -> 6.21 us  [per_device(): lax.all_to_all(local, 'expert', split_axis=0, concat_axis=0, tiled=True)]
    all_to_all x0 -> x1, starting transfers between devices: none -> 4.39 us  [per_device(): lax.all_to_all(local, 'expert', split_axis=0, concat_axis=0, tiled=True)]
    ppermute x27 -> x23, starting transfers between devices: 31.6 us -> 34.6 us  [swap(): return lax.ppermute(value, 'expert', pairs)]
  transfers between devices with their start and end apart: 27 -> 24, of which waited for: 14 -> 11; matrix products, arithmetic and copies ran while one was open for 0% -> 0% of each run, Pallas kernels for 17% -> 16%
where the time goes in v8:
time: 147 us; the launch traced here: 146 us
  waiting for transfers between devices  73.3 us (50%)
  starting transfers between devices  39 us (27%)
  Pallas kernels  31.5 us (21%)
    ppermute x23, waiting for transfers between devices, swap(): return lax.ppermute(value, 'expert', pairs)  67.1 us
    ppermute x23, starting transfers between devices, swap(): return lax.ppermute(value, 'expert', pairs)  34.6 us
    pallas_call x6, Pallas kernels, expert_block(): pl.pallas_call(functools.partial(expert_kernel, first), out_shape=[jax.Sh...  23.2 us
    all_to_all x1, waiting for transfers between devices, per_device(): lax.all_to_all(local, 'expert', split_axis=0, concat_axis=0, tiled=True)  6.21 us
    pallas_call x1, Pallas kernels, pack(): pl.pallas_call(pack_kernel, out_shape=[jax.ShapeDtypeStruct(shape, BF16)...  4.5 us
    all_to_all x1, starting transfers between devices, per_device(): lax.all_to_all(local, 'expert', split_axis=0, concat_axis=0, tiled=True)  4.39 us
  transfers between devices with their start and end apart: 24, of which 11 were waited for; matrix products, arithmetic and copies ran while one was open for 0% of the time, Pallas kernels for 16%

profile of v8, /device:TPU:0, one launch (start us, length us, event | category | flops | bytes accessed | tf_op | source)
XLA Modules:
  0.0 146.5 jit_solution(9682850937026769566)
XLA Ops:
  1.4 4.5 %pack.1 = (bf16[80,3584]{1,0:T(8,128)(2,1)S(1)}, bf16[80,3584]{1,0:T(8,128)(2,1)S(1)}, bf16[80,3584]{1,0:T(8,128)(2,1)S(1)}, bf16[80,3584]{1,0:T(8,128)(2,1)S(1)}, bf16[10752,512]{1,0:T(8,128)(2,1)S(1)}) custom-call(s32[1]{0:T(128)} %bitcast.own_ref, bf16[128,3584]{1,0:T(8,128)(2,1)} %tokens_ref.1, f32[1,3584]{1,0:T(1,128)S(1)} %broadcast_in_dim.15.gain_ref, ...), custom_call_target="tpu_custom_call" | custom-call | flops 1024 | bytes 1024 | tf_op jit(solution)/shard_map/pack/pallas_call | solution.py:78
  6.4 2.6 %collective-permute-start = (bf16[80,3584]{1,0:T(8,128)(2,1)S(1)}, bf16[80,3584]{1,0:T(8,128)(2,1)S(1)}, u32[]{:S(2)}, u32[]{:S(2)}) collective-permute-start(bf16[80,3584]{1,0:T(8,128)(2,1)S(1)} %get-tuple-element.117.near_ref), channel_id=1, source_target_pairs={{0,2},{1,3},{2,0},{3,1},{4,6},{5,7},{6,4},{7,5},{8,10},{9,11},{10,... | collective-permute-start | bytes 1720328 | tf_op jit(solution)/shard_map/ppermute | solution.py:25
  9.0 2.6 %collective-permute-start.3 = (bf16[80,3584]{1,0:T(8,128)(2,1)S(1)}, bf16[80,3584]{1,0:T(8,128)(2,1)S(1)}, u32[]{:S(2)}, u32[]{:S(2)}) collective-permute-start(bf16[80,3584]{1,0:T(8,128)(2,1)S(1)} %get-tuple-element.126), channel_id=1, source_target_pairs={{0,8},{1,9},{2,10},{3,11},{4,12},{5,13},{6,14},{7,15},{8,0},{9,1},... | collective-permute-start | bytes 1720328 | tf_op jit(solution)/shard_map/ppermute | solution.py:25
  13.7 9.2 %collective-permute-done.far_ref = bf16[80,3584]{1,0:T(8,128)(2,1)S(1)} collective-permute-done((bf16[80,3584]{1,0:T(8,128)(2,1)S(1)}, bf16[80,3584]{1,0:T(8,128)(2,1)S(1)}, u32[]{:S(2)}, u32[]{:S(2)}) %collective-permute-start) | collective-permute-done | bytes 573472 | tf_op jit(solution)/shard_map/ppermute | solution.py:25
  23.0 3.8 %expert_block.6 = (bf16[80,3584]{1,0:T(8,128)(2,1)S(1)}, bf16[80,3584]{1,0:T(8,128)(2,1)S(1)}) custom-call(bf16[80,3584]{1,0:T(8,128)(2,1)S(1)} %get-tuple-element.117.near_ref, bf16[80,3584]{1,0:T(8,128)(2,1)S(1)} %collective-permute-done.far_ref, bf16[10752,512]{1,0:T(8,128)(2,1)S(1)} %get-tuple-element.115.refs_0_, ...), custom_call_target="tpu_custom_call" | custom-call | flops 1024 | bytes 1024 | tf_op jit(solution)/shard_map/expert_block/pallas_call | solution.py:118
  26.8 2.9 %collective-permute-start.2 = (bf16[80,3584]{1,0:T(8,128)(2,1)S(1)}, bf16[80,3584]{1,0:T(8,128)(2,1)S(1)}, u32[]{:S(2)}, u32[]{:S(2)}) collective-permute-start(bf16[80,3584]{1,0:T(8,128)(2,1)S(1)} %get-tuple-element.124), channel_id=1, source_target_pairs={{0,2},{1,3},{2,0},{3,1},{4,6},{5,7},{6,4},{7,5},{8,10},{9,11},{10,... | collective-permute-start | bytes 1720328 | tf_op jit(solution)/shard_map/ppermute | solution.py:25
  29.7 7.6 %collective-permute-done.3.whole_ref.near_ref = bf16[80,3584]{1,0:T(8,128)(2,1)S(1)} collective-permute-done((bf16[80,3584]{1,0:T(8,128)(2,1)S(1)}, bf16[80,3584]{1,0:T(8,128)(2,1)S(1)}, u32[]{:S(2)}, u32[]{:S(2)}) %collective-permute-start.3) | collective-permute-done | bytes 573472 | tf_op jit(solution)/shard_map/ppermute | solution.py:25
  38.0 3.4 %collective-permute-start.11 = (bf16[80,3584]{1,0:T(8,128)(2,1)S(1)}, bf16[80,3584]{1,0:T(8,128)(2,1)S(1)}, u32[]{:S(2)}, u32[]{:S(2)}) collective-permute-start(bf16[80,3584]{1,0:T(8,128)(2,1)S(1)} %get-tuple-element.162), channel_id=1, source_target_pairs={{0,12},{1,13},{2,14},{3,15},{4,8},{5,9},{6,10},{7,11},{8,4},{9,5},... | collective-permute-start | bytes 1720328 | tf_op jit(solution)/shard_map/ppermute | solution.py:25
  42.9 11.9 %collective-permute-done.6.far_ref = bf16[48,3584]{1,0:T(8,128)(2,1)S(1)} collective-permute-done((bf16[48,3584]{1,0:T(8,128)(2,1)S(1)}, bf16[48,3584]{1,0:T(8,128)(2,1)S(1)}, u32[]{:S(2)}, u32[]{:S(2)}) %collective-permute-start.6) | collective-permute-done | bytes 344096 | tf_op jit(solution)/shard_map/ppermute | solution.py:25
  54.8 3.7 %expert_block.7 = (bf16[48,3584]{1,0:T(8,128)(2,1)S(1)}, bf16[48,3584]{1,0:T(8,128)(2,1)S(1)}) custom-call(bf16[80,3584]{1,0:T(8,128)(2,1)S(1)} %collective-permute-done.3.whole_ref.near_ref, bf16[48,3584]{1,0:T(8,128)(2,1)S(1)} %collective-permute-done.6.far_ref, bf16[10752,512]{1,0:T(8,128)(2,1)S(1)} %get-tuple-element.115.refs_0_, ...), custom_call_target="tpu_custom_call" | custom-call | flops 1024 | bytes 1024 | tf_op jit(solution)/shard_map/expert_block/pallas_call | solution.py:118
  60.5 4.0 %expert_block.8 = (bf16[32,3584]{1,0:T(8,128)(2,1)S(1)}, bf16[32,3584]{1,0:T(8,128)(2,1)S(1)}) custom-call(bf16[80,3584]{1,0:T(8,128)(2,1)S(1)} %collective-permute-done.3.whole_ref.near_ref, bf16[32,3584]{1,0:T(8,128)(2,1)S(1)} %collective-permute-done.8.far_ref, bf16[10752,512]{1,0:T(8,128)(2,1)S(1)} %get-tuple-element.115.refs_0_, ...), custom_call_target="tpu_custom_call" | custom-call | flops 1024 | bytes 1024 | tf_op jit(solution)/shard_map/expert_block/pallas_call | solution.py:118
  66.7 7.7 %collective-permute-done.10.refs_3_ = bf16[32,3584]{1,0:T(8,128)(2,1)S(1)} collective-permute-done((bf16[32,3584]{1,0:T(8,128)(2,1)S(1)}, bf16[32,3584]{1,0:T(8,128)(2,1)S(1)}, u32[]{:S(2)}, u32[]{:S(2)}) %collective-permute-start.10) | collective-permute-done | bytes 229408 | tf_op jit(solution)/shard_map/ppermute | solution.py:25
  74.7 3.1 %collective-permute-start.18 = (bf16[80,3584]{1,0:T(8,128)(2,1)S(1)}, bf16[80,3584]{1,0:T(8,128)(2,1)S(1)}, u32[]{:S(2)}, u32[]{:S(2)}) collective-permute-start(bf16[80,3584]{1,0:T(8,128)(2,1)S(1)} %total.5), channel_id=1, source_target_pairs={{0,8},{1,9},{2,10},{3,11},{4,12},{5,13},{6,14},{7,15},{8,0},{9,1},... | collective-permute-start | bytes 1720328 | tf_op jit(solution)/shard_map/ppermute | solution.py:25
  79.4 4.0 %expert_block.9 = (bf16[80,3584]{1,0:T(8,128)(2,1)S(1)}, bf16[80,3584]{1,0:T(8,128)(2,1)S(1)}) custom-call(bf16[80,3584]{1,0:T(8,128)(2,1)S(1)} %collective-permute-done.5.near_ref, bf16[80,3584]{1,0:T(8,128)(2,1)S(1)} %collective-permute-done.7.far_ref, bf16[10752,512]{1,0:T(8,128)(2,1)S(1)} %get-tuple-element.115.refs_0_, ...), custom_call_target="tpu_custom_call" | custom-call | flops 1024 | bytes 1024 | tf_op jit(solution)/shard_map/expert_block/pallas_call | solution.py:118
  85.1 3.7 %expert_block.10 = (bf16[48,3584]{1,0:T(8,128)(2,1)S(1)}, bf16[48,3584]{1,0:T(8,128)(2,1)S(1)}) custom-call(bf16[80,3584]{1,0:T(8,128)(2,1)S(1)} %collective-permute-done.11.whole_ref.near_ref, bf16[48,3584]{1,0:T(8,128)(2,1)S(1)} %collective-permute-done.12.far_ref, bf16[10752,512]{1,0:T(8,128)(2,1)S(1)} %get-tuple-element.115.refs_0_, ...), custom_call_target="tpu_custom_call" | custom-call | flops 1024 | bytes 1024 | tf_op jit(solution)/shard_map/expert_block/pallas_call | solution.py:118
  89.9 4.0 %expert_block.11 = (bf16[32,3584]{1,0:T(8,128)(2,1)S(1)}, bf16[32,3584]{1,0:T(8,128)(2,1)S(1)}) custom-call(bf16[80,3584]{1,0:T(8,128)(2,1)S(1)} %collective-permute-done.11.whole_ref.near_ref, bf16[32,3584]{1,0:T(8,128)(2,1)S(1)} %collective-permute-done.13.far_ref, bf16[10752,512]{1,0:T(8,128)(2,1)S(1)} %get-tuple-element.115.refs_0_, ...), custom_call_target="tpu_custom_call" | custom-call | flops 1024 | bytes 1024 | tf_op jit(solution)/shard_map/expert_block/pallas_call | solution.py:118
  95.5 4.8 %collective-permute-done.18.refs_2_ = bf16[80,3584]{1,0:T(8,128)(2,1)S(1)} collective-permute-done((bf16[80,3584]{1,0:T(8,128)(2,1)S(1)}, bf16[80,3584]{1,0:T(8,128)(2,1)S(1)}, u32[]{:S(2)}, u32[]{:S(2)}) %collective-permute-start.18) | collective-permute-done | bytes 573472 | tf_op jit(solution)/shard_map/ppermute | solution.py:25
  100.3 5.9 %collective-permute-done.17 = bf16[32,3584]{1,0:T(8,128)(2,1)S(1)} collective-permute-done((bf16[32,3584]{1,0:T(8,128)(2,1)S(1)}, bf16[32,3584]{1,0:T(8,128)(2,1)S(1)}, u32[]{:S(2)}, u32[]{:S(2)}) %collective-permute-start.17) | collective-permute-done | bytes 229408 | tf_op jit(solution)/shard_map/ppermute | solution.py:25
  106.6 3.3 %collective-permute-start.22 = (bf16[80,3584]{1,0:T(8,128)(2,1)S(1)}, bf16[80,3584]{1,0:T(8,128)(2,1)S(1)}, u32[]{:S(2)}, u32[]{:S(2)}) collective-permute-start(bf16[80,3584]{1,0:T(8,128)(2,1)S(1)} %total.6), channel_id=1, source_target_pairs={{0,12},{1,13},{2,14},{3,15},{4,8},{5,9},{6,10},{7,11},{8,4},{9,5},... | collective-permute-start | bytes 1720328 | tf_op jit(solution)/shard_map/ppermute | solution.py:25
  112.3 9.2 %collective-permute-done.21.refs_2_ = bf16[32,3584]{1,0:T(8,128)(2,1)S(1)} collective-permute-done((bf16[32,3584]{1,0:T(8,128)(2,1)S(1)}, bf16[32,3584]{1,0:T(8,128)(2,1)S(1)}, u32[]{:S(2)}, u32[]{:S(2)}) %collective-permute-start.21) | collective-permute-done | bytes 229408 | tf_op jit(solution)/shard_map/ppermute | solution.py:25
  121.7 10.6 %collective-permute-done.22.refs_3_ = bf16[80,3584]{1,0:T(8,128)(2,1)S(1)} collective-permute-done((bf16[80,3584]{1,0:T(8,128)(2,1)S(1)}, bf16[80,3584]{1,0:T(8,128)(2,1)S(1)}, u32[]{:S(2)}, u32[]{:S(2)}) %collective-permute-start.22) | collective-permute-done | bytes 573472 | tf_op jit(solution)/shard_map/ppermute | solution.py:25
  132.3 2.5 %score.1 = f32[16,16]{1,0:T(8,128)} custom-call(s32[1]{0:T(128)} %bitcast.own_ref, bf16[128,3584]{1,0:T(8,128)(2,1)S(1)} %copy-done, f32[1,3584]{1,0:T(1,128)S(1)} %broadcast_in_dim.12.gain_ref, s32[2,128]{1,0:T(2,128)S(1)} %bitcast.9, f32[2,128]{1,0:T(2,128)S(1)} %bitcast.10, bf16[128,3584]{1,0:T(8,128)(2,1)S(1)} %copy-done.1, f32[1,128]{1,0:T(1,128)S(1)} %bitcast.11, ...), custom_call_target="tpu_custom_call" | custom-call | flops 1024 | bytes 1024 | tf_op jit(solution)/shard_map/score/pallas_call | solution.py:181
  134.9 4.4 %all-to-all-start = ((f32[16,1,16]{2,1,0:T(1,128)}), f32[16,1,16]{2,1,0:T(1,128)S(1)}, u32[]{:S(2)}, u32[]{:S(2)}) async-start(f32[16,1,16]{2,1,0:T(1,128)} %bitcast.6), calls=%async_computation | async-start | bytes 16384 | tf_op jit(solution)/shard_map/all_to_all | solution.py:373
  139.5 6.2 %all-to-all-done = f32[16,1,16]{2,1,0:T(1,128)S(1)} async-done(((f32[16,1,16]{2,1,0:T(1,128)}), f32[16,1,16]{2,1,0:T(1,128)S(1)}, u32[]{:S(2)}, u32[]{:S(2)}) %all-to-all-start) | async-done | bytes 1056 | tf_op jit(solution)/shard_map/all_to_all | solution.py:373
  (65 shorter events, 19.9 us)
Async XLA Ops:
  5.9 17.1 %collective-permute-start.1 = (bf16[10752,512]{1,0:T(8,128)(2,1)S(1)}, bf16[10752,512]{1,0:T(8,128)(2,1)S(1)}, u32[]{:S(2)}, u32[]{:S(2)}) collective-permute-start(bf16[10752,512]{1,0:T(8,128)(2,1)S(1)} %get-tuple-element.115.refs_0_), channel_id=1, source_target_pairs={{0,1},{1,0},{2,3},{3,2},{4,5},{5,4},{6,7},{7,6},{8,9},{9,8},{10,11... | collective-permute-start | bytes 33030152 | tf_op jit(solution)/shard_map/ppermute | solution.py:25
  6.4 16.4 %collective-permute-start = (bf16[80,3584]{1,0:T(8,128)(2,1)S(1)}, bf16[80,3584]{1,0:T(8,128)(2,1)S(1)}, u32[]{:S(2)}, u32[]{:S(2)}) collective-permute-start(bf16[80,3584]{1,0:T(8,128)(2,1)S(1)} %get-tuple-element.117.near_ref), channel_id=1, source_target_pairs={{0,2},{1,3},{2,0},{3,1},{4,6},{5,7},{6,4},{7,5},{8,10},{9,11},{10,... | collective-permute-start | bytes 1720328 | tf_op jit(solution)/shard_map/ppermute | solution.py:25
  9.0 28.3 %collective-permute-start.3 = (bf16[80,3584]{1,0:T(8,128)(2,1)S(1)}, bf16[80,3584]{1,0:T(8,128)(2,1)S(1)}, u32[]{:S(2)}, u32[]{:S(2)}) collective-permute-start(bf16[80,3584]{1,0:T(8,128)(2,1)S(1)} %get-tuple-element.126), channel_id=1, source_target_pairs={{0,8},{1,9},{2,10},{3,11},{4,12},{5,13},{6,14},{7,15},{8,0},{9,1},... | collective-permute-start | bytes 1720328 | tf_op jit(solution)/shard_map/ppermute | solution.py:25
  11.6 25.9 %collective-permute-start.5 = (bf16[80,3584]{1,0:T(8,128)(2,1)S(1)}, bf16[80,3584]{1,0:T(8,128)(2,1)S(1)}, u32[]{:S(2)}, u32[]{:S(2)}) collective-permute-start(bf16[80,3584]{1,0:T(8,128)(2,1)S(1)} %get-tuple-element.132), channel_id=1, source_target_pairs={{0,4},{1,5},{2,6},{3,7},{4,0},{5,1},{6,2},{7,3},{8,12},{9,13},{10,... | collective-permute-start | bytes 1720328 | tf_op jit(solution)/shard_map/ppermute | solution.py:25
  13.2 24.4 %collective-permute-start.4 = (bf16[80,3584]{1,0:T(8,128)(2,1)S(1)}, bf16[80,3584]{1,0:T(8,128)(2,1)S(1)}, u32[]{:S(2)}, u32[]{:S(2)}) collective-permute-start(bf16[80,3584]{1,0:T(8,128)(2,1)S(1)} %get-tuple-element.132), channel_id=1, source_target_pairs={{0,2},{1,3},{2,0},{3,1},{4,6},{5,7},{6,4},{7,5},{8,10},{9,11},{10,... | collective-permute-start | bytes 1720328 | tf_op jit(solution)/shard_map/ppermute | solution.py:25
  26.8 28.0 %collective-permute-start.2 = (bf16[80,3584]{1,0:T(8,128)(2,1)S(1)}, bf16[80,3584]{1,0:T(8,128)(2,1)S(1)}, u32[]{:S(2)}, u32[]{:S(2)}) collective-permute-start(bf16[80,3584]{1,0:T(8,128)(2,1)S(1)} %get-tuple-element.124), channel_id=1, source_target_pairs={{0,2},{1,3},{2,0},{3,1},{4,6},{5,7},{6,4},{7,5},{8,10},{9,11},{10,... | collective-permute-start | bytes 1720328 | tf_op jit(solution)/shard_map/ppermute | solution.py:25
  37.5 17.2 %collective-permute-start.6 = (bf16[48,3584]{1,0:T(8,128)(2,1)S(1)}, bf16[48,3584]{1,0:T(8,128)(2,1)S(1)}, u32[]{:S(2)}, u32[]{:S(2)}) collective-permute-start(bf16[48,3584]{1,0:T(8,128)(2,1)S(1)} %get-tuple-element.138), channel_id=1, source_target_pairs={{0,2},{1,3},{2,0},{3,1},{4,6},{5,7},{6,4},{7,5},{8,10},{9,11},{10,... | collective-permute-start | bytes 1032200 | tf_op jit(solution)/shard_map/ppermute | solution.py:25
  38.0 27.3 %collective-permute-start.11 = (bf16[80,3584]{1,0:T(8,128)(2,1)S(1)}, bf16[80,3584]{1,0:T(8,128)(2,1)S(1)}, u32[]{:S(2)}, u32[]{:S(2)}) collective-permute-start(bf16[80,3584]{1,0:T(8,128)(2,1)S(1)} %get-tuple-element.162), channel_id=1, source_target_pairs={{0,12},{1,13},{2,14},{3,15},{4,8},{5,9},{6,10},{7,11},{8,4},{9,5},... | collective-permute-start | bytes 1720328 | tf_op jit(solution)/shard_map/ppermute | solution.py:25
  41.4 19.2 %collective-permute-start.8 = (bf16[32,3584]{1,0:T(8,128)(2,1)S(1)}, bf16[32,3584]{1,0:T(8,128)(2,1)S(1)}, u32[]{:S(2)}, u32[]{:S(2)}) collective-permute-start(bf16[32,3584]{1,0:T(8,128)(2,1)S(1)} %get-tuple-element.151), channel_id=1, source_target_pairs={{0,2},{1,3},{2,0},{3,1},{4,6},{5,7},{6,4},{7,5},{8,10},{9,11},{10,... | collective-permute-start | bytes 688136 | tf_op jit(solution)/shard_map/ppermute | solution.py:25
  42.9 36.5 %collective-permute-start.7 = (bf16[80,3584]{1,0:T(8,128)(2,1)S(1)}, bf16[80,3584]{1,0:T(8,128)(2,1)S(1)}, u32[]{:S(2)}, u32[]{:S(2)}) collective-permute-start(bf16[80,3584]{1,0:T(8,128)(2,1)S(1)} %collective-permute-done.4), channel_id=1, source_target_pairs={{0,4},{1,5},{2,6},{3,7},{4,0},{5,1},{6,2},{7,3},{8,12},{9,13},{10,... | collective-permute-start | bytes 1720328 | tf_op jit(solution)/shard_map/ppermute | solution.py:25
  58.5 16.0 %collective-permute-start.9 = (bf16[48,3584]{1,0:T(8,128)(2,1)S(1)}, bf16[48,3584]{1,0:T(8,128)(2,1)S(1)}, u32[]{:S(2)}, u32[]{:S(2)}) collective-permute-start(bf16[48,3584]{1,0:T(8,128)(2,1)S(1)} %get-tuple-element.159), channel_id=1, source_target_pairs={{0,2},{1,3},{2,0},{3,1},{4,6},{5,7},{6,4},{7,5},{8,10},{9,11},{10,... | collective-permute-start | bytes 1032200 | tf_op jit(solution)/shard_map/ppermute | solution.py:25
  64.5 9.9 %collective-permute-start.10 = (bf16[32,3584]{1,0:T(8,128)(2,1)S(1)}, bf16[32,3584]{1,0:T(8,128)(2,1)S(1)}, u32[]{:S(2)}, u32[]{:S(2)}) collective-permute-start(bf16[32,3584]{1,0:T(8,128)(2,1)S(1)} %get-tuple-element.160), channel_id=1, source_target_pairs={{0,2},{1,3},{2,0},{3,1},{4,6},{5,7},{6,4},{7,5},{8,10},{9,11},{10,... | collective-permute-start | bytes 688136 | tf_op jit(solution)/shard_map/ppermute | solution.py:25
  65.3 18.2 %collective-permute-start.12 = (bf16[48,3584]{1,0:T(8,128)(2,1)S(1)}, bf16[48,3584]{1,0:T(8,128)(2,1)S(1)}, u32[]{:S(2)}, u32[]{:S(2)}) collective-permute-start(bf16[48,3584]{1,0:T(8,128)(2,1)S(1)} %get-tuple-element.180), channel_id=1, source_target_pairs={{0,2},{1,3},{2,0},{3,1},{4,6},{5,7},{6,4},{7,5},{8,10},{9,11},{10,... | collective-permute-start | bytes 1032200 | tf_op jit(solution)/shard_map/ppermute | solution.py:25
  74.7 25.6 %collective-permute-start.18 = (bf16[80,3584]{1,0:T(8,128)(2,1)S(1)}, bf16[80,3584]{1,0:T(8,128)(2,1)S(1)}, u32[]{:S(2)}, u32[]{:S(2)}) collective-permute-start(bf16[80,3584]{1,0:T(8,128)(2,1)S(1)} %total.5), channel_id=1, source_target_pairs={{0,8},{1,9},{2,10},{3,11},{4,12},{5,13},{6,14},{7,15},{8,0},{9,1},... | collective-permute-start | bytes 1720328 | tf_op jit(solution)/shard_map/ppermute | solution.py:25
  77.9 11.6 %collective-permute-start.13 = (bf16[32,3584]{1,0:T(8,128)(2,1)S(1)}, bf16[32,3584]{1,0:T(8,128)(2,1)S(1)}, u32[]{:S(2)}, u32[]{:S(2)}) collective-permute-start(bf16[32,3584]{1,0:T(8,128)(2,1)S(1)} %get-tuple-element.193), channel_id=1, source_target_pairs={{0,2},{1,3},{2,0},{3,1},{4,6},{5,7},{6,4},{7,5},{8,10},{9,11},{10,... | collective-permute-start | bytes 688136 | tf_op jit(solution)/shard_map/ppermute | solution.py:25
  83.5 22.7 %collective-permute-start.16 = (bf16[48,3584]{1,0:T(8,128)(2,1)S(1)}, bf16[48,3584]{1,0:T(8,128)(2,1)S(1)}, u32[]{:S(2)}, u32[]{:S(2)}) collective-permute-start(bf16[48,3584]{1,0:T(8,128)(2,1)S(1)} %get-tuple-element.203), channel_id=1, source_target_pairs={{0,4},{1,5},{2,6},{3,7},{4,0},{5,1},{6,2},{7,3},{8,12},{9,13},{10,... | collective-permute-start | bytes 1032200 | tf_op jit(solution)/shard_map/ppermute | solution.py:25
  88.8 17.4 %collective-permute-start.14 = (bf16[48,3584]{1,0:T(8,128)(2,1)S(1)}, bf16[48,3584]{1,0:T(8,128)(2,1)S(1)}, u32[]{:S(2)}, u32[]{:S(2)}) collective-permute-start(bf16[48,3584]{1,0:T(8,128)(2,1)S(1)} %get-tuple-element.201), channel_id=1, source_target_pairs={{0,2},{1,3},{2,0},{3,1},{4,6},{5,7},{6,4},{7,5},{8,10},{9,11},{10,... | collective-permute-start | bytes 1032200 | tf_op jit(solution)/shard_map/ppermute | solution.py:25
  89.4 16.8 %collective-permute-start.17 = (bf16[32,3584]{1,0:T(8,128)(2,1)S(1)}, bf16[32,3584]{1,0:T(8,128)(2,1)S(1)}, u32[]{:S(2)}, u32[]{:S(2)}) collective-permute-start(bf16[32,3584]{1,0:T(8,128)(2,1)S(1)} %get-tuple-element.204), channel_id=1, source_target_pairs={{0,4},{1,5},{2,6},{3,7},{4,0},{5,1},{6,2},{7,3},{8,12},{9,13},{10,... | collective-permute-start | bytes 688136 | tf_op jit(solution)/shard_map/ppermute | solution.py:25
  93.9 12.3 %collective-permute-start.15 = (bf16[32,3584]{1,0:T(8,128)(2,1)S(1)}, bf16[32,3584]{1,0:T(8,128)(2,1)S(1)}, u32[]{:S(2)}, u32[]{:S(2)}) collective-permute-start(bf16[32,3584]{1,0:T(8,128)(2,1)S(1)} %get-tuple-element.202), channel_id=1, source_target_pairs={{0,2},{1,3},{2,0},{3,1},{4,6},{5,7},{6,4},{7,5},{8,10},{9,11},{10,... | collective-permute-start | bytes 688136 | tf_op jit(solution)/shard_map/ppermute | solution.py:25
  106.5 14.9 %collective-permute-start.19 = (bf16[80,3584]{1,0:T(8,128)(2,1)S(1)}, bf16[80,3584]{1,0:T(8,128)(2,1)S(1)}, u32[]{:S(2)}, u32[]{:S(2)}) collective-permute-start(bf16[80,3584]{1,0:T(8,128)(2,1)S(1)} %get-tuple-element.213), channel_id=1, source_target_pairs={{0,4},{1,5},{2,6},{3,7},{4,0},{5,1},{6,2},{7,3},{8,12},{9,13},{10,... | collective-permute-start | bytes 1720328 | tf_op jit(solution)/shard_map/ppermute | solution.py:25
  106.6 25.7 %collective-permute-start.22 = (bf16[80,3584]{1,0:T(8,128)(2,1)S(1)}, bf16[80,3584]{1,0:T(8,128)(2,1)S(1)}, u32[]{:S(2)}, u32[]{:S(2)}) collective-permute-start(bf16[80,3584]{1,0:T(8,128)(2,1)S(1)} %total.6), channel_id=1, source_target_pairs={{0,12},{1,13},{2,14},{3,15},{4,8},{5,9},{6,10},{7,11},{8,4},{9,5},... | collective-permute-start | bytes 1720328 | tf_op jit(solution)/shard_map/ppermute | solution.py:25
  109.9 11.5 %collective-permute-start.20 = (bf16[48,3584]{1,0:T(8,128)(2,1)S(1)}, bf16[48,3584]{1,0:T(8,128)(2,1)S(1)}, u32[]{:S(2)}, u32[]{:S(2)}) collective-permute-start(bf16[48,3584]{1,0:T(8,128)(2,1)S(1)} %collective-permute-done.16), channel_id=1, source_target_pairs={{0,2},{1,3},{2,0},{3,1},{4,6},{5,7},{6,4},{7,5},{8,10},{9,11},{10,... | collective-permute-start | bytes 1032200 | tf_op jit(solution)/shard_map/ppermute | solution.py:25
  111.4 10.0 %collective-permute-start.21 = (bf16[32,3584]{1,0:T(8,128)(2,1)S(1)}, bf16[32,3584]{1,0:T(8,128)(2,1)S(1)}, u32[]{:S(2)}, u32[]{:S(2)}) collective-permute-start(bf16[32,3584]{1,0:T(8,128)(2,1)S(1)} %collective-permute-done.17), channel_id=1, source_target_pairs={{0,2},{1,3},{2,0},{3,1},{4,6},{5,7},{6,4},{7,5},{8,10},{9,11},{10,... | collective-permute-start | bytes 688136 | tf_op jit(solution)/shard_map/ppermute | solution.py:25
  134.9 10.8 %all-to-all-start = ((f32[16,1,16]{2,1,0:T(1,128)}), f32[16,1,16]{2,1,0:T(1,128)S(1)}, u32[]{:S(2)}, u32[]{:S(2)}) async-start(f32[16,1,16]{2,1,0:T(1,128)} %bitcast.6), calls=%async_computation | async-start | bytes 16384 | tf_op jit(solution)/shard_map/all_to_all | solution.py:373
  (9 other events, 281.7 us)

commit v9 on v8

--- a/solution.py
+++ b/solution.py
@@ -40,7 +40,7 @@
     return hit, slot
 
 
-def pack_kernel(own_ref, tokens_hbm, gain_ref, picks_hbm, gate_hbm, up_hbm, down_hbm, *refs):
+def pack_kernel(chunks, own_ref, tokens_hbm, gain_ref, picks_hbm, gate_hbm, up_hbm, down_hbm, *refs):
     *out_refs, weights_ref, tokens_ref, picks_ref, arrived = refs
     width, hidden = gate_hbm.shape
     moves = [(tokens_hbm, tokens_ref), (picks_hbm, picks_ref)]
@@ -59,24 +59,24 @@
     values = tokens_ref[...].astype(F32)
     scale = lax.rsqrt(jnp.mean(values * values, axis=-1, keepdims=True) + EPS)
     normed = (values * scale * gain_ref[...]).astype(BF16)
-    _, slot = routing(own_ref[0], picks_ref[...], max(8, len(out_refs)))
-    for k, out_ref in enumerate(out_refs):
-        place = iota((out_ref.shape[0], tokens), 0)
+    _, slot = routing(own_ref[0], picks_ref[...], max(8, 1 + chunks[-1][0]))
+    for (k, first, count), out_ref in zip(chunks, out_refs):
+        place = first + iota((count, tokens), 0)
         chosen = (slot[k : k + 1, :] == place).astype(F32).astype(BF16)
         out_ref[...] = jnp.dot(chosen, normed, preferred_element_type=F32).astype(BF16)
     for copy in copies[2:]:
         copy.wait()
 
 
-def pack(own, tokens, gain, picks, weights, experts, capacity):
+def pack(own, tokens, gain, picks, weights, chunks):
     width, hidden = weights[0].shape
     smem = pl.BlockSpec(memory_space=pltpu.SMEM)
     vmem = pl.BlockSpec(memory_space=pltpu.VMEM)
     hbm = pl.BlockSpec(memory_space=pltpu.HBM)
-    shapes = [(capacity, width)] * experts + [(3 * width, hidden)]
+    shapes = [(count, width) for _, _, count in chunks] + [(3 * width, hidden)]
     there = [pltpu.with_memory_space_constraint(array, pltpu.HBM) for array in (tokens, picks, *weights)]
     return pl.pallas_call(
-        pack_kernel,
+        functools.partial(pack_kernel, chunks),
         out_shape=[jax.ShapeDtypeStruct(shape, BF16) for shape in shapes],
         in_specs=[smem, hbm, vmem, hbm] + [hbm] * 3,
         out_specs=[vmem] * len(shapes),
@@ -91,10 +91,10 @@
     )(own, there[0], gain, *there[1:])
 
 
-def expert_kernel(first, near_ref, far_ref, *refs):
+def expert_kernel(near_ref, far_ref, *refs):
     *weight_refs, mine_ref, theirs_ref, rows = refs
     count = far_ref.shape[0]
-    rows[:count, :] = near_ref[first : first + count, :]
+    rows[:count, :] = near_ref[...]
     rows[count:, :] = far_ref[...]
     width = rows.shape[1]
     size = weight_refs[0].shape[1]
@@ -112,11 +112,11 @@
         theirs_ref[:, start : start + size] = part[count:]
 
 
-def expert_block(near, first, far, weights):
+def expert_block(near, far, weights):
     count, width = far.shape
     vmem = pl.BlockSpec(memory_space=pltpu.VMEM)
     return pl.pallas_call(
-        functools.partial(expert_kernel, first),
+        expert_kernel,
         out_shape=[jax.ShapeDtypeStruct((count, width), BF16)] * 2,
         in_specs=[vmem] * (2 + len(weights)),
         out_specs=[vmem] * 2,
@@ -280,38 +280,36 @@
     core, side = 1, 2
     cut_at = capacity * 5 // 8 // 16 * 16
     pieces = [(0, cut_at), (cut_at, capacity - cut_at)] if cut_at else [(0, capacity)]
+    chunks = [(0, 0, capacity), (1, 0, capacity)]
+    chunks += [(k, first, count) for k in range(2, experts) for first, count in pieces]
+    travel = [(k, i) for k in range(2, experts) for i in range(len(pieces))]
     weights = (gate_weight, up_weight, down_weight)
-    *near, staged = pack(own, tokens, norm_gain[None, :], picks_t, weights, experts, capacity)
+    *packed, staged = pack(own, tokens, norm_gain[None, :], picks_t, weights, tuple(chunks))
+    near = dict(zip([0, 1, *travel], packed))
     weights = [staged, swap(staged, core)]
     order = Order(own)
     far, mine, theirs, back = {}, {}, {}, {}
 
-    def leave(k):
-        near[k] = swap(order.late(near[k]), k * spread)
-
-    def arrive(k):
-        near[k] = order.mark_one(near[k])
-
-    def share(k):
-        far[k] = [swap(order.late(piece), side) for piece in order.mark(*cut(near[k], pieces))]
-
-    def work(k):
-        mine[k], theirs[k] = [], []
-        for (first, _), piece in zip(pieces, far[k]):
-            there = order.mark_one(piece)
-            if first == 0 and k == 2:
-                theirs[0] = order.mark(*theirs[0])
-            part, other = order.mark(*expert_block(order.late(near[k]), first, there, weights))
-            mine[k].append(part)
-            theirs[k].append(swap(other, side))
-
-    def work_whole(k):
-        rows = (order.late(near[k]), 0, order.late(far[k]))
-        mine[k], theirs[k] = order.mark(*expert_block(*rows, weights))
-
-    def home(k):
-        theirs[k] = order.mark(*theirs[k])
-        back[k] = order.mark_one(total(mine[k], theirs[k]))
+    def leave(piece):
+        near[piece] = swap(order.late(near[piece]), piece[0] * spread)
+
+    def arrive(piece):
+        near[piece] = order.mark_one(near[piece])
+
+    def share(piece):
+        far[piece] = swap(order.late(near[piece]), side)
+
+    def work(piece):
+        there = order.mark_one(far[piece])
+        rows = (order.late(near[piece]), there)
+        mine[piece], theirs[piece] = order.mark(*expert_block(*rows, weights))
+
+    def cross(piece):
+        theirs[piece] = swap(theirs[piece], side)
+
+    def home(k, parts):
+        others = order.mark(*(theirs[part] for part in parts))
+        back[k] = order.mark_one(total([mine[part] for part in parts], others))
 
     def leave_back(k):
         back[k] = swap(order.late(back[k]), k * spread)
@@ -319,43 +317,50 @@
     def arrive_back(k):
         back[k] = order.mark_one(back[k])
 
+    def parts_of(k):
+        return [(k, i) for i in range(len(pieces))]
+
     far[0], far[1] = swap(near[0], side), swap(near[1], side)
-    leave(1)
-    leave(2)
-    far[0], weights[1] = order.mark(far[0], weights[1])
-    work_whole(0)
-    theirs[0] = [swap(theirs[0], side)]
-    mine[0] = [mine[0]]
-    arrive(2)
-    arrive(1)
-    far[1] = order.mark_one(far[1])
-    for k in range(3, experts + 1):
-        share(k - 1)
-        if k < experts:
-            leave(k)
-        if k == 3:
+    near[1] = swap(near[1], spread)
+    leave(travel[0])
+    far[0] = order.mark_one(far[0])
+    for n, piece in enumerate(travel):
+        k, i = piece
+        arrive(piece)
+        if n + 1 < len(travel):
+            leave(travel[n + 1])
+        if k > 2 and i == len(pieces) - 1:
+            if k > 3:
+                arrive_back(k - 2)
+            leave_back(k - 1)
+        share(piece)
+        if n == 0:
+            weights[1] = order.mark_one(weights[1])
+            work(0)
+        if n == 1:
             far[1] = swap(order.late(far[1]), spread)
-        if k > 3:
-            home(k - 2)
-            leave_back(k - 2)
-        if k == experts:
+        if k > 2 and i == 0:
+            home(k - 1, parts_of(k - 1))
+        if n == len(travel) - 1:
+            work(1)
+            theirs[1] = [swap(part, spread) for part in order.mark(*cut(theirs[1], pieces))]
+        work(piece)
+        cross(piece)
+        if n == 0:
+            far[1], near[1] = order.mark(far[1], near[1])
+        if n == len(travel) - 2:
             far[1] = order.mark_one(far[1])
-            work_whole(1)
-            theirs[1] = [swap(piece, spread) for piece in order.mark(*cut(theirs[1], pieces))]
-        work(k - 1)
-        if k < experts:
-            arrive(k)
-        if k > 3:
-            arrive_back(k - 2)
-    theirs[1] = order.mark(*theirs[1])
-    home(experts - 1)
+    home(experts - 1, parts_of(experts - 1))
+    arrive_back(experts - 2)
     leave_back(experts - 1)
-    mine[1] = [swap(order.late(mine[1]), spread)]
-    theirs[1] = [swap(order.late(piece), side) for piece in theirs[1]]
+    theirs[0] = swap(order.late(theirs[0]), side)
+    mine[1] = swap(order.late(mine[1]), spread)
+    theirs[1] = [swap(part, side) for part in order.mark(*theirs[1])]
     arrive_back(experts - 1)
-    home(0)
-    mine[1] = order.mark(*mine[1])
-    home(1)
+    home(0, [0])
+    mine[1] = order.mark_one(mine[1])
+    others = order.mark(*theirs[1])
+    back[1] = total([mine[1]], others)
     blocks = [back[k] for k in range(experts)]
     local = score(
         own,

time: 147 us -> 156 us (1.061)
  waiting for transfers between devices: 73.3 us -> 86.8 us
  starting transfers between devices: 39 us -> 34.9 us
    ppermute x23 -> x25, waiting for transfers between devices: 67.1 us -> 80.6 us  [swap(): return lax.ppermute(value, 'expert', pairs)]
    ppermute x23 -> x25, starting transfers between devices: 34.6 us -> 31.1 us  [swap(): return lax.ppermute(value, 'expert', pairs)]
  transfers between devices with their start and end apart: 24 -> 26, of which waited for: 11 -> 13; matrix products, arithmetic and copies ran while one was open for 0% -> 0% of each run, Pallas kernels for 16% -> 16%
where the time goes in v9:
time: 156 us
  waiting for transfers between devices  86.8 us (56%)
  starting transfers between devices  34.9 us (22%)
  Pallas kernels  31.5 us (20%)
    ppermute x25, waiting for transfers between devices, swap(): return lax.ppermute(value, 'expert', pairs)  80.6 us
    ppermute x25, starting transfers between devices, swap(): return lax.ppermute(value, 'expert', pairs)  31.1 us
    pallas_call x6, Pallas kernels, expert_block(): pl.pallas_call(expert_kernel, out_shape=[jax.ShapeDtypeStruct((count, wid...  23.3 us
    all_to_all x1, waiting for transfers between devices, per_device(): lax.all_to_all(local, 'expert', split_axis=0, concat_axis=0, tiled=True)  6.21 us
    pallas_call x1, Pallas kernels, pack(): pl.pallas_call(functools.partial(pack_kernel, chunks), out_shape=[jax.Sha...  4.5 us
    all_to_all x1, starting transfers between devices, per_device(): lax.all_to_all(local, 'expert', split_axis=0, concat_axis=0, tiled=True)  3.81 us
  transfers between devices with their start and end apart: 26, of which 13 were waited for; matrix products, arithmetic and copies ran while one was open for 0% of the time, Pallas kernels for 16%

profile of v9, /device:TPU:0, one launch (start us, length us, event | category | flops | bytes accessed | tf_op | source)
XLA Modules:
  0.0 155.9 jit_solution(8438202099218877065)
XLA Ops:
  1.4 4.5 %pack.1 = (bf16[80,3584]{1,0:T(8,128)(2,1)S(1)}, bf16[80,3584]{1,0:T(8,128)(2,1)S(1)}, bf16[48,3584]{1,0:T(8,128)(2,1)S(1)}, bf16[32,3584]{1,0:T(8,128)(2,1)S(1)...) custom-call(s32[1]{0:T(128)} %bitcast.own_ref, ...), custom_call_target="tpu_custom_call" | custom-call | flops 1024 | bytes 1024 | tf_op jit(solution)/shard_map/pack/pallas_call | solution.py:78
  6.4 2.6 %collective-permute-start = (bf16[80,3584]{1,0:T(8,128)(2,1)S(1)}, bf16[80,3584]{1,0:T(8,128)(2,1)S(1)}, u32[]{:S(2)}, u32[]{:S(2)}) collective-permute-start(bf16[80,3584]{1,0:T(8,128)(2,1)S(1)} %get-tuple-element.117.near_ref), channel_id=1, source_target_pairs={{0,2},{1,3},{2,0},{3,1},{4,6},{5,7},{6,4},{7,5},{8,10},{9,11},{10,... | collective-permute-start | bytes 1720328 | tf_op jit(solution)/shard_map/ppermute | solution.py:25
  9.0 2.6 %collective-permute-start.2 = (bf16[48,3584]{1,0:T(8,128)(2,1)S(1)}, bf16[48,3584]{1,0:T(8,128)(2,1)S(1)}, u32[]{:S(2)}, u32[]{:S(2)}) collective-permute-start(bf16[48,3584]{1,0:T(8,128)(2,1)S(1)} %get-tuple-element.112), channel_id=1, source_target_pairs={{0,8},{1,9},{2,10},{3,11},{4,12},{5,13},{6,14},{7,15},{8,0},{9,1},... | collective-permute-start | bytes 1032200 | tf_op jit(solution)/shard_map/ppermute | solution.py:25
  13.7 9.2 %collective-permute-done.far_ref = bf16[80,3584]{1,0:T(8,128)(2,1)S(1)} collective-permute-done((bf16[80,3584]{1,0:T(8,128)(2,1)S(1)}, bf16[80,3584]{1,0:T(8,128)(2,1)S(1)}, u32[]{:S(2)}, u32[]{:S(2)}) %collective-permute-start) | collective-permute-done | bytes 573472 | tf_op jit(solution)/shard_map/ppermute | solution.py:25
  22.8 4.7 %collective-permute-done.2.near_ref = bf16[48,3584]{1,0:T(8,128)(2,1)S(1)} collective-permute-done((bf16[48,3584]{1,0:T(8,128)(2,1)S(1)}, bf16[48,3584]{1,0:T(8,128)(2,1)S(1)}, u32[]{:S(2)}, u32[]{:S(2)}) %collective-permute-start.2) | collective-permute-done | bytes 344096 | tf_op jit(solution)/shard_map/ppermute | solution.py:25
  28.0 3.9 %expert_block.6 = (bf16[80,3584]{1,0:T(8,128)(2,1)S(1)}, bf16[80,3584]{1,0:T(8,128)(2,1)S(1)}) custom-call(bf16[80,3584]{1,0:T(8,128)(2,1)S(1)} %get-tuple-element.117.near_ref, bf16[80,3584]{1,0:T(8,128)(2,1)S(1)} %collective-permute-done.far_ref, bf16[10752,512]{1,0:T(8,128)(2,1)S(1)} %get-tuple-element.110.refs_0_, ...), custom_call_target="tpu_custom_call" | custom-call | flops 1024 | bytes 1024 | tf_op jit(solution)/shard_map/expert_block/pallas_call | solution.py:118
  31.9 10.4 %collective-permute-done.3.far_ref = bf16[48,3584]{1,0:T(8,128)(2,1)S(1)} collective-permute-done((bf16[48,3584]{1,0:T(8,128)(2,1)S(1)}, bf16[48,3584]{1,0:T(8,128)(2,1)S(1)}, u32[]{:S(2)}, u32[]{:S(2)}) %collective-permute-start.3) | collective-permute-done | bytes 344096 | tf_op jit(solution)/shard_map/ppermute | solution.py:25
  42.2 3.7 %expert_block.7 = (bf16[48,3584]{1,0:T(8,128)(2,1)S(1)}, bf16[48,3584]{1,0:T(8,128)(2,1)S(1)}) custom-call(bf16[48,3584]{1,0:T(8,128)(2,1)S(1)} %collective-permute-done.2.near_ref, bf16[48,3584]{1,0:T(8,128)(2,1)S(1)} %collective-permute-done.3.far_ref, bf16[10752,512]{1,0:T(8,128)(2,1)S(1)} %get-tuple-element.110.refs_0_, ...), custom_call_target="tpu_custom_call" | custom-call | flops 1024 | bytes 1024 | tf_op jit(solution)/shard_map/expert_block/pallas_call | solution.py:118
  46.0 3.9 %collective-permute-start.10 = (bf16[48,3584]{1,0:T(8,128)(2,1)S(1)}, bf16[48,3584]{1,0:T(8,128)(2,1)S(1)}, u32[]{:S(2)}, u32[]{:S(2)}) collective-permute-start(bf16[48,3584]{1,0:T(8,128)(2,1)S(1)} %get-tuple-element.148), channel_id=1, source_target_pairs={{0,12},{1,13},{2,14},{3,15},{4,8},{5,9},{6,10},{7,11},{8,4},{9,5},... | collective-permute-start | bytes 1032200 | tf_op jit(solution)/shard_map/ppermute | solution.py:25
  51.9 6.5 %collective-permute-done.7.far_ref = bf16[32,3584]{1,0:T(8,128)(2,1)S(1)} collective-permute-done((bf16[32,3584]{1,0:T(8,128)(2,1)S(1)}, bf16[32,3584]{1,0:T(8,128)(2,1)S(1)}, u32[]{:S(2)}, u32[]{:S(2)}) %collective-permute-start.7) | collective-permute-done | bytes 229408 | tf_op jit(solution)/shard_map/ppermute | solution.py:25
  58.5 4.0 %expert_block.8 = (bf16[32,3584]{1,0:T(8,128)(2,1)S(1)}, bf16[32,3584]{1,0:T(8,128)(2,1)S(1)}) custom-call(bf16[32,3584]{1,0:T(8,128)(2,1)S(1)} %collective-permute-done.4.near_ref, bf16[32,3584]{1,0:T(8,128)(2,1)S(1)} %collective-permute-done.7.far_ref, bf16[10752,512]{1,0:T(8,128)(2,1)S(1)} %get-tuple-element.110.refs_0_, ...), custom_call_target="tpu_custom_call" | custom-call | flops 1024 | bytes 1024 | tf_op jit(solution)/shard_map/expert_block/pallas_call | solution.py:118
  65.8 10.6 %collective-permute-done.9.refs_3_ = bf16[32,3584]{1,0:T(8,128)(2,1)S(1)} collective-permute-done((bf16[32,3584]{1,0:T(8,128)(2,1)S(1)}, bf16[32,3584]{1,0:T(8,128)(2,1)S(1)}, u32[]{:S(2)}, u32[]{:S(2)}) %collective-permute-start.9) | collective-permute-done | bytes 229408 | tf_op jit(solution)/shard_map/ppermute | solution.py:25
  76.7 3.9 %expert_block.9 = (bf16[48,3584]{1,0:T(8,128)(2,1)S(1)}, bf16[48,3584]{1,0:T(8,128)(2,1)S(1)}) custom-call(bf16[48,3584]{1,0:T(8,128)(2,1)S(1)} %collective-permute-done.10.near_ref, bf16[48,3584]{1,0:T(8,128)(2,1)S(1)} %collective-permute-done.13.far_ref, bf16[10752,512]{1,0:T(8,128)(2,1)S(1)} %get-tuple-element.110.refs_0_, ...), custom_call_target="tpu_custom_call" | custom-call | flops 1024 | bytes 1024 | tf_op jit(solution)/shard_map/expert_block/pallas_call | solution.py:118
  80.7 3.1 %collective-permute-start.14 = (bf16[80,3584]{1,0:T(8,128)(2,1)S(1)}, bf16[80,3584]{1,0:T(8,128)(2,1)S(1)}, u32[]{:S(2)}, u32[]{:S(2)}) collective-permute-start(bf16[80,3584]{1,0:T(8,128)(2,1)S(1)} %total.4), channel_id=1, source_target_pairs={{0,8},{1,9},{2,10},{3,11},{4,12},{5,13},{6,14},{7,15},{8,0},{9,1},... | collective-permute-start | bytes 1720328 | tf_op jit(solution)/shard_map/ppermute | solution.py:25
  85.8 3.8 %expert_block.10 = (bf16[80,3584]{1,0:T(8,128)(2,1)S(1)}, bf16[80,3584]{1,0:T(8,128)(2,1)S(1)}) custom-call(bf16[80,3584]{1,0:T(8,128)(2,1)S(1)} %collective-permute-done.6.near_ref, bf16[80,3584]{1,0:T(8,128)(2,1)S(1)} %collective-permute-done.12.far_ref, bf16[10752,512]{1,0:T(8,128)(2,1)S(1)} %get-tuple-element.110.refs_0_, ...), custom_call_target="tpu_custom_call" | custom-call | flops 1024 | bytes 1024 | tf_op jit(solution)/shard_map/expert_block/pallas_call | solution.py:118
  89.7 2.6 %collective-permute-done.15.far_ref = bf16[32,3584]{1,0:T(8,128)(2,1)S(1)} collective-permute-done((bf16[32,3584]{1,0:T(8,128)(2,1)S(1)}, bf16[32,3584]{1,0:T(8,128)(2,1)S(1)}, u32[]{:S(2)}, u32[]{:S(2)}) %collective-permute-start.15) | collective-permute-done | bytes 229408 | tf_op jit(solution)/shard_map/ppermute | solution.py:25
  92.3 4.0 %expert_block.11 = (bf16[32,3584]{1,0:T(8,128)(2,1)S(1)}, bf16[32,3584]{1,0:T(8,128)(2,1)S(1)}) custom-call(bf16[32,3584]{1,0:T(8,128)(2,1)S(1)} %collective-permute-done.11.near_ref, bf16[32,3584]{1,0:T(8,128)(2,1)S(1)} %collective-permute-done.15.far_ref, bf16[10752,512]{1,0:T(8,128)(2,1)S(1)} %get-tuple-element.110.refs_0_, ...), custom_call_target="tpu_custom_call" | custom-call | flops 1024 | bytes 1024 | tf_op jit(solution)/shard_map/expert_block/pallas_call | solution.py:118
  102.7 4.4 %collective-permute-done.14.refs_2_ = bf16[80,3584]{1,0:T(8,128)(2,1)S(1)} collective-permute-done((bf16[80,3584]{1,0:T(8,128)(2,1)S(1)}, bf16[80,3584]{1,0:T(8,128)(2,1)S(1)}, u32[]{:S(2)}, u32[]{:S(2)}) %collective-permute-start.14) | collective-permute-done | bytes 573472 | tf_op jit(solution)/shard_map/ppermute | solution.py:25
  110.7 9.0 %collective-permute-done.21 = bf16[32,3584]{1,0:T(8,128)(2,1)S(1)} collective-permute-done((bf16[32,3584]{1,0:T(8,128)(2,1)S(1)}, bf16[32,3584]{1,0:T(8,128)(2,1)S(1)}, u32[]{:S(2)}, u32[]{:S(2)}) %collective-permute-start.21) | collective-permute-done | bytes 229408 | tf_op jit(solution)/shard_map/ppermute | solution.py:25
  122.0 10.3 %collective-permute-done.23.refs_2_ = bf16[32,3584]{1,0:T(8,128)(2,1)S(1)} collective-permute-done((bf16[32,3584]{1,0:T(8,128)(2,1)S(1)}, bf16[32,3584]{1,0:T(8,128)(2,1)S(1)}, u32[]{:S(2)}, u32[]{:S(2)}) %collective-permute-start.23) | collective-permute-done | bytes 229408 | tf_op jit(solution)/shard_map/ppermute | solution.py:25
  132.7 9.3 %collective-permute-done.19.refs_0_ = bf16[80,3584]{1,0:T(8,128)(2,1)S(1)} collective-permute-done((bf16[80,3584]{1,0:T(8,128)(2,1)S(1)}, bf16[80,3584]{1,0:T(8,128)(2,1)S(1)}, u32[]{:S(2)}, u32[]{:S(2)}) %collective-permute-start.19) | collective-permute-done | bytes 573472 | tf_op jit(solution)/shard_map/ppermute | solution.py:25
  142.3 2.5 %score.1 = f32[16,16]{1,0:T(8,128)} custom-call(s32[1]{0:T(128)} %bitcast.own_ref, bf16[128,3584]{1,0:T(8,128)(2,1)S(1)} %copy-done, f32[1,3584]{1,0:T(1,128)S(1)} %broadcast_in_dim.12.gain_ref, s32[2,128]{1,0:T(2,128)S(1)} %bitcast.9, f32[2,128]{1,0:T(2,128)S(1)} %bitcast.10, bf16[128,3584]{1,0:T(8,128)(2,1)S(1)} %copy-done.1, f32[1,128]{1,0:T(1,128)S(1)} %bitcast.11, ...), custom_call_target="tpu_custom_call" | custom-call | flops 1024 | bytes 1024 | tf_op jit(solution)/shard_map/score/pallas_call | solution.py:181
  144.9 3.8 %all-to-all-start = ((f32[16,1,16]{2,1,0:T(1,128)}), f32[16,1,16]{2,1,0:T(1,128)S(1)}, u32[]{:S(2)}, u32[]{:S(2)}) async-start(f32[16,1,16]{2,1,0:T(1,128)} %bitcast.6), calls=%async_computation | async-start | bytes 16384 | tf_op jit(solution)/shard_map/all_to_all | solution.py:378
  148.9 6.2 %all-to-all-done = f32[16,1,16]{2,1,0:T(1,128)S(1)} async-done(((f32[16,1,16]{2,1,0:T(1,128)}), f32[16,1,16]{2,1,0:T(1,128)S(1)}, u32[]{:S(2)}, u32[]{:S(2)}) %all-to-all-start) | async-done | bytes 1056 | tf_op jit(solution)/shard_map/all_to_all | solution.py:378
  (67 shorter events, 25.4 us)
Async XLA Ops:
  5.9 22.1 %collective-permute-start.1 = (bf16[10752,512]{1,0:T(8,128)(2,1)S(1)}, bf16[10752,512]{1,0:T(8,128)(2,1)S(1)}, u32[]{:S(2)}, u32[]{:S(2)}) collective-permute-start(bf16[10752,512]{1,0:T(8,128)(2,1)S(1)} %get-tuple-element.110.refs_0_), channel_id=1, source_target_pairs={{0,1},{1,0},{2,3},{3,2},{4,5},{5,4},{6,7},{7,6},{8,9},{9,8},{10,11... | collective-permute-start | bytes 33030152 | tf_op jit(solution)/shard_map/ppermute | solution.py:25
  6.4 16.4 %collective-permute-start = (bf16[80,3584]{1,0:T(8,128)(2,1)S(1)}, bf16[80,3584]{1,0:T(8,128)(2,1)S(1)}, u32[]{:S(2)}, u32[]{:S(2)}) collective-permute-start(bf16[80,3584]{1,0:T(8,128)(2,1)S(1)} %get-tuple-element.117.near_ref), channel_id=1, source_target_pairs={{0,2},{1,3},{2,0},{3,1},{4,6},{5,7},{6,4},{7,5},{8,10},{9,11},{10,... | collective-permute-start | bytes 1720328 | tf_op jit(solution)/shard_map/ppermute | solution.py:25
  9.0 18.5 %collective-permute-start.2 = (bf16[48,3584]{1,0:T(8,128)(2,1)S(1)}, bf16[48,3584]{1,0:T(8,128)(2,1)S(1)}, u32[]{:S(2)}, u32[]{:S(2)}) collective-permute-start(bf16[48,3584]{1,0:T(8,128)(2,1)S(1)} %get-tuple-element.112), channel_id=1, source_target_pairs={{0,8},{1,9},{2,10},{3,11},{4,12},{5,13},{6,14},{7,15},{8,0},{9,1},... | collective-permute-start | bytes 1032200 | tf_op jit(solution)/shard_map/ppermute | solution.py:25
  11.6 34.4 %collective-permute-start.5 = (bf16[80,3584]{1,0:T(8,128)(2,1)S(1)}, bf16[80,3584]{1,0:T(8,128)(2,1)S(1)}, u32[]{:S(2)}, u32[]{:S(2)}) collective-permute-start(bf16[80,3584]{1,0:T(8,128)(2,1)S(1)} %get-tuple-element.134), channel_id=1, source_target_pairs={{0,2},{1,3},{2,0},{3,1},{4,6},{5,7},{6,4},{7,5},{8,10},{9,11},{10,... | collective-permute-start | bytes 1720328 | tf_op jit(solution)/shard_map/ppermute | solution.py:25
  12.1 33.9 %collective-permute-start.6 = (bf16[80,3584]{1,0:T(8,128)(2,1)S(1)}, bf16[80,3584]{1,0:T(8,128)(2,1)S(1)}, u32[]{:S(2)}, u32[]{:S(2)}) collective-permute-start(bf16[80,3584]{1,0:T(8,128)(2,1)S(1)} %get-tuple-element.134), channel_id=1, source_target_pairs={{0,4},{1,5},{2,6},{3,7},{4,0},{5,1},{6,2},{7,3},{8,12},{9,13},{10,... | collective-permute-start | bytes 1720328 | tf_op jit(solution)/shard_map/ppermute | solution.py:25
  27.5 14.7 %collective-permute-start.3 = (bf16[48,3584]{1,0:T(8,128)(2,1)S(1)}, bf16[48,3584]{1,0:T(8,128)(2,1)S(1)}, u32[]{:S(2)}, u32[]{:S(2)}) collective-permute-start(bf16[48,3584]{1,0:T(8,128)(2,1)S(1)} %collective-permute-done.2.near_ref), channel_id=1, source_target_pairs={{0,2},{1,3},{2,0},{3,1},{4,6},{5,7},{6,4},{7,5},{8,10},{9,11},{10,... | collective-permute-start | bytes 1032200 | tf_op jit(solution)/shard_map/ppermute | solution.py:25
  28.0 18.0 %collective-permute-start.4 = (bf16[32,3584]{1,0:T(8,128)(2,1)S(1)}, bf16[32,3584]{1,0:T(8,128)(2,1)S(1)}, u32[]{:S(2)}, u32[]{:S(2)}) collective-permute-start(bf16[32,3584]{1,0:T(8,128)(2,1)S(1)} %get-tuple-element.133), channel_id=1, source_target_pairs={{0,8},{1,9},{2,10},{3,11},{4,12},{5,13},{6,14},{7,15},{8,0},{9,1},... | collective-permute-start | bytes 688136 | tf_op jit(solution)/shard_map/ppermute | solution.py:25
  46.0 16.4 %collective-permute-start.10 = (bf16[48,3584]{1,0:T(8,128)(2,1)S(1)}, bf16[48,3584]{1,0:T(8,128)(2,1)S(1)}, u32[]{:S(2)}, u32[]{:S(2)}) collective-permute-start(bf16[48,3584]{1,0:T(8,128)(2,1)S(1)} %get-tuple-element.148), channel_id=1, source_target_pairs={{0,12},{1,13},{2,14},{3,15},{4,8},{5,9},{6,10},{7,11},{8,4},{9,5},... | collective-permute-start | bytes 1032200 | tf_op jit(solution)/shard_map/ppermute | solution.py:25
  49.9 8.5 %collective-permute-start.7 = (bf16[32,3584]{1,0:T(8,128)(2,1)S(1)}, bf16[32,3584]{1,0:T(8,128)(2,1)S(1)}, u32[]{:S(2)}, u32[]{:S(2)}) collective-permute-start(bf16[32,3584]{1,0:T(8,128)(2,1)S(1)} %collective-permute-done.4.near_ref), channel_id=1, source_target_pairs={{0,2},{1,3},{2,0},{3,1},{4,6},{5,7},{6,4},{7,5},{8,10},{9,11},{10,... | collective-permute-start | bytes 688136 | tf_op jit(solution)/shard_map/ppermute | solution.py:25
  51.4 29.2 %collective-permute-start.12 = (bf16[80,3584]{1,0:T(8,128)(2,1)S(1)}, bf16[80,3584]{1,0:T(8,128)(2,1)S(1)}, u32[]{:S(2)}, u32[]{:S(2)}) collective-permute-start(bf16[80,3584]{1,0:T(8,128)(2,1)S(1)} %collective-permute-done.5), channel_id=1, source_target_pairs={{0,4},{1,5},{2,6},{3,7},{4,0},{5,1},{6,2},{7,3},{8,12},{9,13},{10,... | collective-permute-start | bytes 1720328 | tf_op jit(solution)/shard_map/ppermute | solution.py:25
  51.4 14.4 %collective-permute-start.8 = (bf16[48,3584]{1,0:T(8,128)(2,1)S(1)}, bf16[48,3584]{1,0:T(8,128)(2,1)S(1)}, u32[]{:S(2)}, u32[]{:S(2)}) collective-permute-start(bf16[48,3584]{1,0:T(8,128)(2,1)S(1)} %get-tuple-element.145), channel_id=1, source_target_pairs={{0,2},{1,3},{2,0},{3,1},{4,6},{5,7},{6,4},{7,5},{8,10},{9,11},{10,... | collective-permute-start | bytes 1032200 | tf_op jit(solution)/shard_map/ppermute | solution.py:25
  62.5 14.3 %collective-permute-start.13 = (bf16[48,3584]{1,0:T(8,128)(2,1)S(1)}, bf16[48,3584]{1,0:T(8,128)(2,1)S(1)}, u32[]{:S(2)}, u32[]{:S(2)}) collective-permute-start(bf16[48,3584]{1,0:T(8,128)(2,1)S(1)} %collective-permute-done.10.near_ref), channel_id=1, source_target_pairs={{0,2},{1,3},{2,0},{3,1},{4,6},{5,7},{6,4},{7,5},{8,10},{9,11},{10,... | collective-permute-start | bytes 1032200 | tf_op jit(solution)/shard_map/ppermute | solution.py:25
  64.0 12.4 %collective-permute-start.9 = (bf16[32,3584]{1,0:T(8,128)(2,1)S(1)}, bf16[32,3584]{1,0:T(8,128)(2,1)S(1)}, u32[]{:S(2)}, u32[]{:S(2)}) collective-permute-start(bf16[32,3584]{1,0:T(8,128)(2,1)S(1)} %get-tuple-element.146), channel_id=1, source_target_pairs={{0,2},{1,3},{2,0},{3,1},{4,6},{5,7},{6,4},{7,5},{8,10},{9,11},{10,... | collective-permute-start | bytes 688136 | tf_op jit(solution)/shard_map/ppermute | solution.py:25
  64.5 16.1 %collective-permute-start.11 = (bf16[32,3584]{1,0:T(8,128)(2,1)S(1)}, bf16[32,3584]{1,0:T(8,128)(2,1)S(1)}, u32[]{:S(2)}, u32[]{:S(2)}) collective-permute-start(bf16[32,3584]{1,0:T(8,128)(2,1)S(1)} %get-tuple-element.156), channel_id=1, source_target_pairs={{0,12},{1,13},{2,14},{3,15},{4,8},{5,9},{6,10},{7,11},{8,4},{9,5},... | collective-permute-start | bytes 688136 | tf_op jit(solution)/shard_map/ppermute | solution.py:25
  80.7 26.5 %collective-permute-start.14 = (bf16[80,3584]{1,0:T(8,128)(2,1)S(1)}, bf16[80,3584]{1,0:T(8,128)(2,1)S(1)}, u32[]{:S(2)}, u32[]{:S(2)}) collective-permute-start(bf16[80,3584]{1,0:T(8,128)(2,1)S(1)} %total.4), channel_id=1, source_target_pairs={{0,8},{1,9},{2,10},{3,11},{4,12},{5,13},{6,14},{7,15},{8,0},{9,1},... | collective-permute-start | bytes 1720328 | tf_op jit(solution)/shard_map/ppermute | solution.py:25
  85.3 14.7 %collective-permute-start.16 = (bf16[48,3584]{1,0:T(8,128)(2,1)S(1)}, bf16[48,3584]{1,0:T(8,128)(2,1)S(1)}, u32[]{:S(2)}, u32[]{:S(2)}) collective-permute-start(bf16[48,3584]{1,0:T(8,128)(2,1)S(1)} %get-tuple-element.190), channel_id=1, source_target_pairs={{0,2},{1,3},{2,0},{3,1},{4,6},{5,7},{6,4},{7,5},{8,10},{9,11},{10,... | collective-permute-start | bytes 1032200 | tf_op jit(solution)/shard_map/ppermute | solution.py:25
  98.0 21.7 %collective-permute-start.20 = (bf16[48,3584]{1,0:T(8,128)(2,1)S(1)}, bf16[48,3584]{1,0:T(8,128)(2,1)S(1)}, u32[]{:S(2)}, u32[]{:S(2)}) collective-permute-start(bf16[48,3584]{1,0:T(8,128)(2,1)S(1)} %get-tuple-element.201), channel_id=1, source_target_pairs={{0,4},{1,5},{2,6},{3,7},{4,0},{5,1},{6,2},{7,3},{8,12},{9,13},{10,... | collective-permute-start | bytes 1032200 | tf_op jit(solution)/shard_map/ppermute | solution.py:25
  98.0 21.7 %collective-permute-start.21 = (bf16[32,3584]{1,0:T(8,128)(2,1)S(1)}, bf16[32,3584]{1,0:T(8,128)(2,1)S(1)}, u32[]{:S(2)}, u32[]{:S(2)}) collective-permute-start(bf16[32,3584]{1,0:T(8,128)(2,1)S(1)} %get-tuple-element.202), channel_id=1, source_target_pairs={{0,4},{1,5},{2,6},{3,7},{4,0},{5,1},{6,2},{7,3},{8,12},{9,13},{10,... | collective-permute-start | bytes 688136 | tf_op jit(solution)/shard_map/ppermute | solution.py:25
  107.2 25.2 %collective-permute-start.18 = (bf16[80,3584]{1,0:T(8,128)(2,1)S(1)}, bf16[80,3584]{1,0:T(8,128)(2,1)S(1)}, u32[]{:S(2)}, u32[]{:S(2)}) collective-permute-start(bf16[80,3584]{1,0:T(8,128)(2,1)S(1)} %get-tuple-element.198), channel_id=1, source_target_pairs={{0,2},{1,3},{2,0},{3,1},{4,6},{5,7},{6,4},{7,5},{8,10},{9,11},{10,... | collective-permute-start | bytes 1720328 | tf_op jit(solution)/shard_map/ppermute | solution.py:25
  108.7 33.2 %collective-permute-start.19 = (bf16[80,3584]{1,0:T(8,128)(2,1)S(1)}, bf16[80,3584]{1,0:T(8,128)(2,1)S(1)}, u32[]{:S(2)}, u32[]{:S(2)}) collective-permute-start(bf16[80,3584]{1,0:T(8,128)(2,1)S(1)} %get-tuple-element.200), channel_id=1, source_target_pairs={{0,4},{1,5},{2,6},{3,7},{4,0},{5,1},{6,2},{7,3},{8,12},{9,13},{10,... | collective-permute-start | bytes 1720328 | tf_op jit(solution)/shard_map/ppermute | solution.py:25
  108.7 33.5 %collective-permute-start.24 = (bf16[80,3584]{1,0:T(8,128)(2,1)S(1)}, bf16[80,3584]{1,0:T(8,128)(2,1)S(1)}, u32[]{:S(2)}, u32[]{:S(2)}) collective-permute-start(bf16[80,3584]{1,0:T(8,128)(2,1)S(1)} %total.5), channel_id=1, source_target_pairs={{0,12},{1,13},{2,14},{3,15},{4,8},{5,9},{6,10},{7,11},{8,4},{9,5},... | collective-permute-start | bytes 1720328 | tf_op jit(solution)/shard_map/ppermute | solution.py:25
  119.7 12.7 %collective-permute-start.22 = (bf16[48,3584]{1,0:T(8,128)(2,1)S(1)}, bf16[48,3584]{1,0:T(8,128)(2,1)S(1)}, u32[]{:S(2)}, u32[]{:S(2)}) collective-permute-start(bf16[48,3584]{1,0:T(8,128)(2,1)S(1)} %collective-permute-done.20), channel_id=1, source_target_pairs={{0,2},{1,3},{2,0},{3,1},{4,6},{5,7},{6,4},{7,5},{8,10},{9,11},{10,... | collective-permute-start | bytes 1032200 | tf_op jit(solution)/shard_map/ppermute | solution.py:25
  122.0 10.4 %collective-permute-start.23 = (bf16[32,3584]{1,0:T(8,128)(2,1)S(1)}, bf16[32,3584]{1,0:T(8,128)(2,1)S(1)}, u32[]{:S(2)}, u32[]{:S(2)}) collective-permute-start(bf16[32,3584]{1,0:T(8,128)(2,1)S(1)} %collective-permute-done.21), channel_id=1, source_target_pairs={{0,2},{1,3},{2,0},{3,1},{4,6},{5,7},{6,4},{7,5},{8,10},{9,11},{10,... | collective-permute-start | bytes 688136 | tf_op jit(solution)/shard_map/ppermute | solution.py:25
  144.9 10.2 %all-to-all-start = ((f32[16,1,16]{2,1,0:T(1,128)}), f32[16,1,16]{2,1,0:T(1,128)S(1)}, u32[]{:S(2)}, u32[]{:S(2)}) async-start(f32[16,1,16]{2,1,0:T(1,128)} %bitcast.6), calls=%async_computation | async-start | bytes 16384 | tf_op jit(solution)/shard_map/all_to_all | solution.py:378
  (11 other events, 349.9 us)

commit v10 on v8

--- a/solution.py
+++ b/solution.py
@@ -40,83 +40,105 @@
     return hit, slot
 
 
-def pack_kernel(own_ref, tokens_hbm, gain_ref, picks_hbm, gate_hbm, up_hbm, down_hbm, *refs):
-    *out_refs, weights_ref, tokens_ref, picks_ref, arrived = refs
-    width, hidden = gate_hbm.shape
+def pack_kernel(chunks, own_ref, tokens_hbm, gain_ref, picks_hbm, *refs):
+    *out_refs, tokens_ref, picks_ref, arrived = refs
     moves = [(tokens_hbm, tokens_ref), (picks_hbm, picks_ref)]
-    sources = [gate_hbm, up_hbm]
-    sources += [down_hbm.at[:, pl.ds(first, hidden)] for first in range(0, width, hidden)]
-    first = 0
-    for source in sources:
-        moves.append((source, weights_ref.at[pl.ds(first, source.shape[0]), :]))
-        first += source.shape[0]
     copies = [pltpu.make_async_copy(*move, arrived.at[n]) for n, move in enumerate(moves)]
     for copy in copies:
         copy.start()
-    copies[0].wait()
-    copies[1].wait()
+    for copy in copies:
+        copy.wait()
     tokens = tokens_ref.shape[0]
     values = tokens_ref[...].astype(F32)
     scale = lax.rsqrt(jnp.mean(values * values, axis=-1, keepdims=True) + EPS)
     normed = (values * scale * gain_ref[...]).astype(BF16)
-    _, slot = routing(own_ref[0], picks_ref[...], max(8, len(out_refs)))
-    for k, out_ref in enumerate(out_refs):
-        place = iota((out_ref.shape[0], tokens), 0)
-        chosen = (slot[k : k + 1, :] == place).astype(F32).astype(BF16)
-        out_ref[...] = jnp.dot(chosen, normed, preferred_element_type=F32).astype(BF16)
-    for copy in copies[2:]:
-        copy.wait()
-
-
-def pack(own, tokens, gain, picks, weights, experts, capacity):
-    width, hidden = weights[0].shape
+    _, slot = routing(own_ref[0], picks_ref[...], max(8, 1 + chunks[-1][-1]))
+    for blocks, out_ref in zip(chunks, out_refs):
+        count = out_ref.shape[0] // len(blocks)
+        place = iota((count, tokens), 0)
+        for n, k in enumerate(blocks):
+            chosen = (slot[k : k + 1, :] == place).astype(F32).astype(BF16)
+            rows = jnp.dot(chosen, normed, preferred_element_type=F32).astype(BF16)
+            out_ref[n * count : (n + 1) * count, :] = rows
+
+
+def in_hbm(*arrays):
+    return [pltpu.with_memory_space_constraint(array, pltpu.HBM) for array in arrays]
+
+
+def pack(own, tokens, gain, picks, chunks, capacity):
+    width = tokens.shape[1]
     smem = pl.BlockSpec(memory_space=pltpu.SMEM)
     vmem = pl.BlockSpec(memory_space=pltpu.VMEM)
     hbm = pl.BlockSpec(memory_space=pltpu.HBM)
-    shapes = [(capacity, width)] * experts + [(3 * width, hidden)]
-    there = [pltpu.with_memory_space_constraint(array, pltpu.HBM) for array in (tokens, picks, *weights)]
-    return pl.pallas_call(
-        pack_kernel,
-        out_shape=[jax.ShapeDtypeStruct(shape, BF16) for shape in shapes],
-        in_specs=[smem, hbm, vmem, hbm] + [hbm] * 3,
-        out_specs=[vmem] * len(shapes),
+    tokens, picks = in_hbm(tokens, picks)
+    return pl.pallas_call(
+        functools.partial(pack_kernel, chunks),
+        out_shape=[jax.ShapeDtypeStruct((len(blocks) * capacity, width), BF16) for blocks in chunks],
+        in_specs=[smem, hbm, vmem, hbm],
+        out_specs=[vmem] * len(chunks),
         scratch_shapes=[
             pltpu.VMEM(tokens.shape, BF16),
             pltpu.VMEM(picks.shape, jnp.int32),
-            pltpu.SemaphoreType.DMA((4 + width // hidden,)),
+            pltpu.SemaphoreType.DMA((2,)),
         ],
         compiler_params=pltpu.CompilerParams(vmem_limit_bytes=VMEM_LIMIT),
         cost_estimate=COST,
         name="pack",
-    )(own, there[0], gain, *there[1:])
-
-
-def expert_kernel(first, near_ref, far_ref, *refs):
+    )(own, tokens, gain, picks)
+
+
+def stage_kernel(count, *refs):
+    sources, there, arrived = refs[:count], refs[count:-1], refs[-1]
+    copies = [pltpu.make_async_copy(*move, arrived.at[n]) for n, move in enumerate(zip(sources, there))]
+    for copy in copies:
+        copy.start()
+    for copy in copies:
+        copy.wait()
+
+
+def stage(arrays, memory):
+    vmem = pl.BlockSpec(memory_space=pltpu.VMEM)
+    there = pl.BlockSpec(memory_space=memory)
+    return pl.pallas_call(
+        functools.partial(stage_kernel, len(arrays)),
+        out_shape=[pltpu.VMEM(array.shape, array.dtype) for array in arrays],
+        in_specs=[there] * len(arrays),
+        out_specs=[vmem] * len(arrays),
+        scratch_shapes=[pltpu.SemaphoreType.DMA((len(arrays),))],
+        compiler_params=pltpu.CompilerParams(vmem_limit_bytes=VMEM_LIMIT),
+        cost_estimate=COST,
+        name="stage",
+    )(*arrays)
+
+
+def expert_kernel(near_first, far_first, near_ref, far_ref, *refs):
     *weight_refs, mine_ref, theirs_ref, rows = refs
-    count = far_ref.shape[0]
-    rows[:count, :] = near_ref[first : first + count, :]
-    rows[count:, :] = far_ref[...]
-    width = rows.shape[1]
+    count, width = mine_ref.shape
+    rows[:count, :] = near_ref[near_first : near_first + count, :]
+    rows[count:, :] = far_ref[far_first : far_first + count, :]
     size = weight_refs[0].shape[1]
+    slices = [weight_refs[n : n + 3] for n in range(0, len(weight_refs), 3)]
     hidden = []
-    for ref in weight_refs:
-        gate = jnp.dot(rows[...], ref[:width, :], preferred_element_type=F32)
-        up = jnp.dot(rows[...], ref[width : 2 * width, :], preferred_element_type=F32)
+    for gate_ref, up_ref, _ in slices:
+        gate = jnp.dot(rows[...], gate_ref[...], preferred_element_type=F32)
+        up = jnp.dot(rows[...], up_ref[...], preferred_element_type=F32)
         hidden.append((jax.nn.silu(gate) * up).astype(BF16))
     for start in range(0, width, size):
+        cols = slice(start, start + size)
         part = sum(
-            jnp.dot(value, ref[pl.ds(2 * width + start, size), :], preferred_element_type=F32)
-            for value, ref in zip(hidden, weight_refs)
+            jnp.dot(value, down_ref[:, cols], preferred_element_type=F32)
+            for value, (_, _, down_ref) in zip(hidden, slices)
         ).astype(BF16)
-        mine_ref[:, start : start + size] = part[:count]
-        theirs_ref[:, start : start + size] = part[count:]
-
-
-def expert_block(near, first, far, weights):
-    count, width = far.shape
-    vmem = pl.BlockSpec(memory_space=pltpu.VMEM)
-    return pl.pallas_call(
-        functools.partial(expert_kernel, first),
+        mine_ref[:, cols] = part[:count]
+        theirs_ref[:, cols] = part[count:]
+
+
+def expert_block(near, far, weights, count, near_first=0, far_first=0):
+    width = far.shape[1]
+    vmem = pl.BlockSpec(memory_space=pltpu.VMEM)
+    return pl.pallas_call(
+        functools.partial(expert_kernel, near_first, far_first),
         out_shape=[jax.ShapeDtypeStruct((count, width), BF16)] * 2,
         in_specs=[vmem] * (2 + len(weights)),
         out_specs=[vmem] * 2,
@@ -208,17 +230,15 @@
         return lax.optimization_barrier((value, self.token))[0]
 
 
-def cut_kernel(whole_ref, *refs):
-    first = 0
-    for ref in refs:
-        ref[...] = whole_ref[first : first + ref.shape[0], :]
-        first += ref.shape[0]
+def cut_kernel(pieces, whole_ref, *refs):
+    for (first, count), ref in zip(pieces, refs):
+        ref[...] = whole_ref[first : first + count, :]
 
 
 def cut(whole, pieces):
     vmem = pl.BlockSpec(memory_space=pltpu.VMEM)
     return pl.pallas_call(
-        cut_kernel,
+        functools.partial(cut_kernel, pieces),
         out_shape=[jax.ShapeDtypeStruct((count, whole.shape[1]), BF16) for _, count in pieces],
         in_specs=[vmem],
         out_specs=[vmem] * len(pieces),
@@ -279,10 +299,12 @@
     picks_t = picks.T
     core, side = 1, 2
     cut_at = capacity * 5 // 8 // 16 * 16
-    pieces = [(0, cut_at), (cut_at, capacity - cut_at)] if cut_at else [(0, capacity)]
-    weights = (gate_weight, up_weight, down_weight)
-    *near, staged = pack(own, tokens, norm_gain[None, :], picks_t, weights, experts, capacity)
-    weights = [staged, swap(staged, core)]
+    pieces = ((0, cut_at), (cut_at, capacity - cut_at)) if cut_at else ((0, capacity),)
+    weights = [gate_weight, up_weight, down_weight]
+    swapped = [swap(weight, core) for weight in weights]
+    chunks = ((0, 1), (1,)) + tuple((k,) for k in range(2, experts))
+    both, *near = pack(own, tokens, norm_gain[None, :], picks_t, chunks, capacity)
+    near = [both, *near]
     order = Order(own)
     far, mine, theirs, back = {}, {}, {}, {}
 
@@ -297,17 +319,12 @@
 
     def work(k):
         mine[k], theirs[k] = [], []
-        for (first, _), piece in zip(pieces, far[k]):
+        for (first, count), piece in zip(pieces, far[k]):
             there = order.mark_one(piece)
-            if first == 0 and k == 2:
-                theirs[0] = order.mark(*theirs[0])
-            part, other = order.mark(*expert_block(order.late(near[k]), first, there, weights))
+            rows = (order.late(near[k]), there)
+            part, other = order.mark(*expert_block(*rows, weights, count, near_first=first))
             mine[k].append(part)
             theirs[k].append(swap(other, side))
-
-    def work_whole(k):
-        rows = (order.late(near[k]), 0, order.late(far[k]))
-        mine[k], theirs[k] = order.mark(*expert_block(*rows, weights))
 
     def home(k):
         theirs[k] = order.mark(*theirs[k])
@@ -319,42 +336,42 @@
     def arrive_back(k):
         back[k] = order.mark_one(back[k])
 
-    far[0], far[1] = swap(near[0], side), swap(near[1], side)
-    leave(1)
+    both_far = swap(both, side)
     leave(2)
-    far[0], weights[1] = order.mark(far[0], weights[1])
-    work_whole(0)
-    theirs[0] = [swap(theirs[0], side)]
-    mine[0] = [mine[0]]
+    weights = order.mark(*stage(in_hbm(*(order.late(weight) for weight in weights)), pltpu.HBM))
+    weights += order.mark(*stage(order.mark(*swapped), pl.ANY))
     arrive(2)
-    arrive(1)
-    far[1] = order.mark_one(far[1])
     for k in range(3, experts + 1):
         share(k - 1)
         if k < experts:
             leave(k)
         if k == 3:
-            far[1] = swap(order.late(far[1]), spread)
+            leave(1)
+            both_far = order.mark_one(both_far)
+            far[1] = swap(order.mark_one(cut(both_far, ((capacity, capacity),))[0]), spread)
+            mine[0], theirs[0] = order.mark(*expert_block(both, both_far, weights, capacity))
         if k > 3:
             home(k - 2)
             leave_back(k - 2)
         if k == experts:
-            far[1] = order.mark_one(far[1])
-            work_whole(1)
+            mine[1], theirs[1] = order.mark(*expert_block(near[1], far[1], weights, capacity))
             theirs[1] = [swap(piece, spread) for piece in order.mark(*cut(theirs[1], pieces))]
+            mine[1] = swap(mine[1], spread)
         work(k - 1)
         if k < experts:
             arrive(k)
+        if k == 3:
+            near[1], far[1] = order.mark(near[1], far[1])
         if k > 3:
             arrive_back(k - 2)
-    theirs[1] = order.mark(*theirs[1])
     home(experts - 1)
     leave_back(experts - 1)
-    mine[1] = [swap(order.late(mine[1]), spread)]
+    mine[1], *theirs[1] = order.mark(mine[1], *theirs[1])
+    mine[1] = [mine[1]]
     theirs[1] = [swap(order.late(piece), side) for piece in theirs[1]]
+    mine[0], theirs[0] = [mine[0]], [swap(order.late(theirs[0]), side)]
     arrive_back(experts - 1)
     home(0)
-    mine[1] = order.mark(*mine[1])
     home(1)
     blocks = [back[k] for k in range(experts)]
     local = score(

time: 147 us -> 174 us (1.18)
  waiting for transfers between devices: 73.3 us -> 102 us
  starting transfers between devices: 39 us -> 31.8 us
  Pallas kernels: 31.5 us -> 37.7 us
    ppermute x23 -> x24, waiting for transfers between devices: 67.1 us -> 95.7 us  [swap(): return lax.ppermute(value, 'expert', pairs)]
    pallas_call x10 -> x13, Pallas kernels: 27.8 us -> 34.1 us  [the longest x6 23.2 us: expert_block(): pl.pallas_call(functools.partial(expert_kernel, near_first, far_first), o...]
    ppermute x23 -> x24, starting transfers between devices: 34.6 us -> 28.4 us  [swap(): return lax.ppermute(value, 'expert', pairs)]
  transfers between devices with their start and end apart: 24 -> 25, of which waited for: 11 -> 9; matrix products, arithmetic and copies ran while one was open for 0% -> 1% of each run, Pallas kernels for 16% -> 20%
where the time goes in v10:
time: 174 us
  waiting for transfers between devices  102 us (59%)
  Pallas kernels  37.7 us (22%)
  starting transfers between devices  31.8 us (18%)
    ppermute x24, waiting for transfers between devices, swap(): return lax.ppermute(value, 'expert', pairs)  95.7 us
    ppermute x24, starting transfers between devices, swap(): return lax.ppermute(value, 'expert', pairs)  28.4 us
    pallas_call x6, Pallas kernels, expert_block(): pl.pallas_call(functools.partial(expert_kernel, near_first, far_first), o...  23.2 us
    pallas_call x2, Pallas kernels, stage(): pl.pallas_call(functools.partial(stage_kernel, len(arrays)), out_shape=[p...  8.45 us
    all_to_all x1, waiting for transfers between devices, per_device(): lax.all_to_all(local, 'expert', split_axis=0, concat_axis=0, tiled=True)  6.17 us
  transfers between devices with their start and end apart: 25, of which 9 were waited for; matrix products, arithmetic and copies ran while one was open for 1% of the time, Pallas kernels for 20%

profile of v10, /device:TPU:0, one launch (start us, length us, event | category | flops | bytes accessed | tf_op | source)
XLA Modules:
  0.0 174.1 jit_solution(15301025465267736222)
XLA Ops:
  2.4 2.2 %pack.1 = (bf16[160,3584]{1,0:T(8,128)(2,1)S(1)}, bf16[80,3584]{1,0:T(8,128)(2,1)S(1)}, bf16[80,3584]{1,0:T(8,128)(2,1)S(1)}, bf16[80,3584]{1,0:T(8,128)(2,1)S(1)}) custom-call(s32[1]{0:T(128)} %bitcast.own_ref, bf16[128,3584]{1,0:T(8,128)(2,1)} %tokens_ref.1, f32[1,3584]{1,0:T(1,128)S(1)} %broadcast_in_dim.15.gain_ref, s32[2,128]{1,0:T(2,128)} %bitcast.8), custom_call_target="tpu_custom_call" | custom-call | flops 1024 | bytes 1024 | tf_op jit(solution)/shard_map/pack/pallas_call | solution.py:75
  4.7 2.7 %collective-permute-start = (bf16[160,3584]{1,0:T(8,128)(2,1)S(1)}, bf16[160,3584]{1,0:T(8,128)(2,1)S(1)}, u32[]{:S(2)}, u32[]{:S(2)}) collective-permute-start(bf16[160,3584]{1,0:T(8,128)(2,1)S(1)} %get-tuple-element.126.near_ref), channel_id=1, source_target_pairs={{0,2},{1,3},{2,0},{3,1},{4,6},{5,7},{6,4},{7,5},{8,10},{9,11},{10,... | collective-permute-start | bytes 3440648 | tf_op jit(solution)/shard_map/ppermute | solution.py:25
  7.3 2.6 %collective-permute-start.1 = (bf16[80,3584]{1,0:T(8,128)(2,1)S(1)}, bf16[80,3584]{1,0:T(8,128)(2,1)S(1)}, u32[]{:S(2)}, u32[]{:S(2)}) collective-permute-start(bf16[80,3584]{1,0:T(8,128)(2,1)S(1)} %get-tuple-element.128), channel_id=1, source_target_pairs={{0,8},{1,9},{2,10},{3,11},{4,12},{5,13},{6,14},{7,15},{8,0},{9,1},... | collective-permute-start | bytes 1720328 | tf_op jit(solution)/shard_map/ppermute | solution.py:25
  9.9 4.2 %stage.2 = (bf16[3584,512]{1,0:T(8,128)(2,1)S(1)}, bf16[3584,512]{1,0:T(8,128)(2,1)S(1)}, bf16[512,3584]{1,0:T(8,128)(2,1)S(1)}) custom-call(bf16[3584,512]{1,0:T(8,128)(2,1)} %refs_0_, bf16[3584,512]{1,0:T(8,128)(2,1)} %refs_1_, bf16[512,3584]{1,0:T(8,128)(2,1)} %refs_2_), custom_call_target="tpu_custom_call" | custom-call | flops 1024 | bytes 1024 | tf_op jit(solution)/shard_map/stage/pallas_call | solution.py:103
  14.2 3.9 %collective-permute-done.4.refs_2_ = bf16[512,3584]{1,0:T(8,128)(2,1)} collective-permute-done((bf16[512,3584]{1,0:T(8,128)(2,1)}, bf16[512,3584]{1,0:T(8,128)(2,1)}, u32[]{:S(2)}, u32[]{:S(2)}) %collective-permute-start.4) | collective-permute-done | bytes 3670048 | tf_op jit(solution)/shard_map/ppermute | solution.py:25
  18.0 4.2 %stage.3 = (bf16[3584,512]{1,0:T(8,128)(2,1)S(1)}, bf16[3584,512]{1,0:T(8,128)(2,1)S(1)}, bf16[512,3584]{1,0:T(8,128)(2,1)S(1)}) custom-call(bf16[3584,512]{1,0:T(8,128)(2,1)} %collective-permute-done.2.refs_0_, bf16[3584,512]{1,0:T(8,128)(2,1)} %collective-permute-done.3.refs_1_, bf16[512,3584]{1,0:T(8,128)(2,1)} %collective-permute-done.4.refs_2_), custom_call_target="tpu_custom_call" | custom-call | flops 1024 | bytes 1024 | tf_op jit(solution)/shard_map/stage/pallas_call | solution.py:103
  22.3 13.3 %collective-permute-done.1.whole_ref.near_ref = bf16[80,3584]{1,0:T(8,128)(2,1)S(1)} collective-permute-done((bf16[80,3584]{1,0:T(8,128)(2,1)S(1)}, bf16[80,3584]{1,0:T(8,128)(2,1)S(1)}, u32[]{:S(2)}, u32[]{:S(2)}) %collective-permute-start.1) | collective-permute-done | bytes 573472 | tf_op jit(solution)/shard_map/ppermute | solution.py:25
  36.2 3.6 %collective-permute-start.7 = (bf16[80,3584]{1,0:T(8,128)(2,1)S(1)}, bf16[80,3584]{1,0:T(8,128)(2,1)S(1)}, u32[]{:S(2)}, u32[]{:S(2)}) collective-permute-start(bf16[80,3584]{1,0:T(8,128)(2,1)S(1)} %get-tuple-element.166), channel_id=1, source_target_pairs={{0,12},{1,13},{2,14},{3,15},{4,8},{5,9},{6,10},{7,11},{8,4},{9,5},... | collective-permute-start | bytes 1720328 | tf_op jit(solution)/shard_map/ppermute | solution.py:25
  43.3 3.8 %expert_block.6 = (bf16[80,3584]{1,0:T(8,128)(2,1)S(1)}, bf16[80,3584]{1,0:T(8,128)(2,1)S(1)}) custom-call(bf16[160,3584]{1,0:T(8,128)(2,1)S(1)} %get-tuple-element.126.near_ref, bf16[160,3584]{1,0:T(8,128)(2,1)S(1)} %collective-permute-done.far_ref.whole_ref, bf16[3584,512]{1,0:T(8,128)(2,1)S(1)} %get-tuple-element.150.refs_0_, ...), custom_call_target="tpu_custom_call" | custom-call | flops 1024 | bytes 1024 | tf_op jit(solution)/shard_map/expert_block/pallas_call | solution.py:140
  47.2 3.7 %expert_block.7 = (bf16[48,3584]{1,0:T(8,128)(2,1)S(1)}, bf16[48,3584]{1,0:T(8,128)(2,1)S(1)}) custom-call(bf16[80,3584]{1,0:T(8,128)(2,1)S(1)} %collective-permute-done.1.whole_ref.near_ref, bf16[48,3584]{1,0:T(8,128)(2,1)S(1)} %collective-permute-done.9.far_ref, bf16[3584,512]{1,0:T(8,128)(2,1)S(1)} %get-tuple-element.150.refs_0_, ...), custom_call_target="tpu_custom_call" | custom-call | flops 1024 | bytes 1024 | tf_op jit(solution)/shard_map/expert_block/pallas_call | solution.py:140
  51.5 4.0 %expert_block.8 = (bf16[32,3584]{1,0:T(8,128)(2,1)S(1)}, bf16[32,3584]{1,0:T(8,128)(2,1)S(1)}) custom-call(bf16[80,3584]{1,0:T(8,128)(2,1)S(1)} %collective-permute-done.1.whole_ref.near_ref, bf16[32,3584]{1,0:T(8,128)(2,1)S(1)} %collective-permute-done.8.far_ref, bf16[3584,512]{1,0:T(8,128)(2,1)S(1)} %get-tuple-element.150.refs_0_, ...), custom_call_target="tpu_custom_call" | custom-call | flops 1024 | bytes 1024 | tf_op jit(solution)/shard_map/expert_block/pallas_call | solution.py:140
  57.0 8.4 %collective-permute-done.5.near_ref = bf16[80,3584]{1,0:T(8,128)(2,1)S(1)} collective-permute-done((bf16[80,3584]{1,0:T(8,128)(2,1)S(1)}, bf16[80,3584]{1,0:T(8,128)(2,1)S(1)}, u32[]{:S(2)}, u32[]{:S(2)}) %collective-permute-start.5) | collective-permute-done | bytes 573472 | tf_op jit(solution)/shard_map/ppermute | solution.py:25
  65.4 11.9 %collective-permute-done.6.far_ref = bf16[80,3584]{1,0:T(8,128)(2,1)S(1)} collective-permute-done((bf16[80,3584]{1,0:T(8,128)(2,1)S(1)}, bf16[80,3584]{1,0:T(8,128)(2,1)S(1)}, u32[]{:S(2)}, u32[]{:S(2)}) %collective-permute-start.6) | collective-permute-done | bytes 573472 | tf_op jit(solution)/shard_map/ppermute | solution.py:25
  79.8 4.0 %expert_block.9 = (bf16[80,3584]{1,0:T(8,128)(2,1)S(1)}, bf16[80,3584]{1,0:T(8,128)(2,1)S(1)}) custom-call(bf16[80,3584]{1,0:T(8,128)(2,1)S(1)} %collective-permute-done.5.near_ref, bf16[80,3584]{1,0:T(8,128)(2,1)S(1)} %collective-permute-done.6.far_ref, bf16[3584,512]{1,0:T(8,128)(2,1)S(1)} %get-tuple-element.150.refs_0_, ...), custom_call_target="tpu_custom_call" | custom-call | flops 1024 | bytes 1024 | tf_op jit(solution)/shard_map/expert_block/pallas_call | solution.py:140
  86.2 3.1 %collective-permute-done.15.far_ref = bf16[48,3584]{1,0:T(8,128)(2,1)S(1)} collective-permute-done((bf16[48,3584]{1,0:T(8,128)(2,1)S(1)}, bf16[48,3584]{1,0:T(8,128)(2,1)S(1)}, u32[]{:S(2)}, u32[]{:S(2)}) %collective-permute-start.15) | collective-permute-done | bytes 344096 | tf_op jit(solution)/shard_map/ppermute | solution.py:25
  89.2 3.7 %expert_block.10 = (bf16[48,3584]{1,0:T(8,128)(2,1)S(1)}, bf16[48,3584]{1,0:T(8,128)(2,1)S(1)}) custom-call(bf16[80,3584]{1,0:T(8,128)(2,1)S(1)} %collective-permute-done.7.whole_ref.near_ref, bf16[48,3584]{1,0:T(8,128)(2,1)S(1)} %collective-permute-done.15.far_ref, bf16[3584,512]{1,0:T(8,128)(2,1)S(1)} %get-tuple-element.150.refs_0_, ...), custom_call_target="tpu_custom_call" | custom-call | flops 1024 | bytes 1024 | tf_op jit(solution)/shard_map/expert_block/pallas_call | solution.py:140
  95.5 4.0 %expert_block.11 = (bf16[32,3584]{1,0:T(8,128)(2,1)S(1)}, bf16[32,3584]{1,0:T(8,128)(2,1)S(1)}) custom-call(bf16[80,3584]{1,0:T(8,128)(2,1)S(1)} %collective-permute-done.7.whole_ref.near_ref, bf16[32,3584]{1,0:T(8,128)(2,1)S(1)} %collective-permute-done.16.far_ref, bf16[3584,512]{1,0:T(8,128)(2,1)S(1)} %get-tuple-element.150.refs_0_, ...), custom_call_target="tpu_custom_call" | custom-call | flops 1024 | bytes 1024 | tf_op jit(solution)/shard_map/expert_block/pallas_call | solution.py:140
  99.7 6.2 %collective-permute-done.19.refs_2_ = bf16[80,3584]{1,0:T(8,128)(2,1)S(1)} collective-permute-done((bf16[80,3584]{1,0:T(8,128)(2,1)S(1)}, bf16[80,3584]{1,0:T(8,128)(2,1)S(1)}, u32[]{:S(2)}, u32[]{:S(2)}) %collective-permute-start.19) | collective-permute-done | bytes 573472 | tf_op jit(solution)/shard_map/ppermute | solution.py:25
  106.2 2.7 %collective-permute-start.23 = (bf16[80,3584]{1,0:T(8,128)(2,1)S(1)}, bf16[80,3584]{1,0:T(8,128)(2,1)S(1)}, u32[]{:S(2)}, u32[]{:S(2)}) collective-permute-start(bf16[80,3584]{1,0:T(8,128)(2,1)S(1)} %total.5), channel_id=1, source_target_pairs={{0,12},{1,13},{2,14},{3,15},{4,8},{5,9},{6,10},{7,11},{8,4},{9,5},... | collective-permute-start | bytes 1720328 | tf_op jit(solution)/shard_map/ppermute | solution.py:25
  108.9 25.9 %collective-permute-done.14 = bf16[32,3584]{1,0:T(8,128)(2,1)S(1)} collective-permute-done((bf16[32,3584]{1,0:T(8,128)(2,1)S(1)}, bf16[32,3584]{1,0:T(8,128)(2,1)S(1)}, u32[]{:S(2)}, u32[]{:S(2)}) %collective-permute-start.14) | collective-permute-done | bytes 229408 | tf_op jit(solution)/shard_map/ppermute | solution.py:25
  137.3 23.0 %collective-permute-done.22.refs_2_ = bf16[32,3584]{1,0:T(8,128)(2,1)S(1)} collective-permute-done((bf16[32,3584]{1,0:T(8,128)(2,1)S(1)}, bf16[32,3584]{1,0:T(8,128)(2,1)S(1)}, u32[]{:S(2)}, u32[]{:S(2)}) %collective-permute-start.22) | collective-permute-done | bytes 229408 | tf_op jit(solution)/shard_map/ppermute | solution.py:25
  161.0 2.6 %score.1 = f32[16,16]{1,0:T(8,128)} custom-call(s32[1]{0:T(128)} %bitcast.own_ref, bf16[128,3584]{1,0:T(8,128)(2,1)S(1)} %copy-done, f32[1,3584]{1,0:T(1,128)S(1)} %broadcast_in_dim.12.gain_ref, s32[2,128]{1,0:T(2,128)S(1)} %bitcast.9, f32[2,128]{1,0:T(2,128)S(1)} %bitcast.10, bf16[128,3584]{1,0:T(8,128)(2,1)S(1)} %copy-done.1, f32[1,128]{1,0:T(1,128)S(1)} %bitcast.11, ...), custom_call_target="tpu_custom_call" | custom-call | flops 1024 | bytes 1024 | tf_op jit(solution)/shard_map/score/pallas_call | solution.py:203
  163.5 3.4 %all-to-all-start = ((f32[16,1,16]{2,1,0:T(1,128)}), f32[16,1,16]{2,1,0:T(1,128)S(1)}, u32[]{:S(2)}, u32[]{:S(2)}) async-start(f32[16,1,16]{2,1,0:T(1,128)} %bitcast.6), calls=%async_computation | async-start | bytes 16384 | tf_op jit(solution)/shard_map/all_to_all | solution.py:390
  167.2 6.2 %all-to-all-done = f32[16,1,16]{2,1,0:T(1,128)S(1)} async-done(((f32[16,1,16]{2,1,0:T(1,128)}), f32[16,1,16]{2,1,0:T(1,128)S(1)}, u32[]{:S(2)}, u32[]{:S(2)}) %all-to-all-start) | async-done | bytes 1056 | tf_op jit(solution)/shard_map/all_to_all | solution.py:390
  (70 shorter events, 19.9 us)
Async XLA Ops:
  0.6 13.5 %collective-permute-start.2 = (bf16[3584,512]{1,0:T(8,128)(2,1)}, bf16[3584,512]{1,0:T(8,128)(2,1)}, u32[]{:S(2)}, u32[]{:S(2)}) collective-permute-start(bf16[3584,512]{1,0:T(8,128)(2,1)} %refs_0_), channel_id=1, source_target_pairs={{0,1},{1,0},{2,3},{3,2},{4,5},{5,4},{6,7},{7,6},{8,9},{9,8},{10,11... | collective-permute-start | bytes 11010056 | tf_op jit(solution)/shard_map/ppermute | solution.py:25
  1.1 13.0 %collective-permute-start.3 = (bf16[3584,512]{1,0:T(8,128)(2,1)}, bf16[3584,512]{1,0:T(8,128)(2,1)}, u32[]{:S(2)}, u32[]{:S(2)}) collective-permute-start(bf16[3584,512]{1,0:T(8,128)(2,1)} %refs_1_), channel_id=1, source_target_pairs={{0,1},{1,0},{2,3},{3,2},{4,5},{5,4},{6,7},{7,6},{8,9},{9,8},{10,11... | collective-permute-start | bytes 11010056 | tf_op jit(solution)/shard_map/ppermute | solution.py:25
  1.2 16.8 %collective-permute-start.4 = (bf16[512,3584]{1,0:T(8,128)(2,1)}, bf16[512,3584]{1,0:T(8,128)(2,1)}, u32[]{:S(2)}, u32[]{:S(2)}) collective-permute-start(bf16[512,3584]{1,0:T(8,128)(2,1)} %refs_2_), channel_id=1, source_target_pairs={{0,1},{1,0},{2,3},{3,2},{4,5},{5,4},{6,7},{7,6},{8,9},{9,8},{10,11... | collective-permute-start | bytes 11010056 | tf_op jit(solution)/shard_map/ppermute | solution.py:25
  4.7 31.5 %collective-permute-start = (bf16[160,3584]{1,0:T(8,128)(2,1)S(1)}, bf16[160,3584]{1,0:T(8,128)(2,1)S(1)}, u32[]{:S(2)}, u32[]{:S(2)}) collective-permute-start(bf16[160,3584]{1,0:T(8,128)(2,1)S(1)} %get-tuple-element.126.near_ref), channel_id=1, source_target_pairs={{0,2},{1,3},{2,0},{3,1},{4,6},{5,7},{6,4},{7,5},{8,10},{9,11},{10,... | collective-permute-start | bytes 3440648 | tf_op jit(solution)/shard_map/ppermute | solution.py:25
  7.3 28.2 %collective-permute-start.1 = (bf16[80,3584]{1,0:T(8,128)(2,1)S(1)}, bf16[80,3584]{1,0:T(8,128)(2,1)S(1)}, u32[]{:S(2)}, u32[]{:S(2)}) collective-permute-start(bf16[80,3584]{1,0:T(8,128)(2,1)S(1)} %get-tuple-element.128), channel_id=1, source_target_pairs={{0,8},{1,9},{2,10},{3,11},{4,12},{5,13},{6,14},{7,15},{8,0},{9,1},... | collective-permute-start | bytes 1720328 | tf_op jit(solution)/shard_map/ppermute | solution.py:25
  35.6 11.6 %collective-permute-start.9 = (bf16[48,3584]{1,0:T(8,128)(2,1)S(1)}, bf16[48,3584]{1,0:T(8,128)(2,1)S(1)}, u32[]{:S(2)}, u32[]{:S(2)}) collective-permute-start(bf16[48,3584]{1,0:T(8,128)(2,1)S(1)} %get-tuple-element.170), channel_id=1, source_target_pairs={{0,2},{1,3},{2,0},{3,1},{4,6},{5,7},{6,4},{7,5},{8,10},{9,11},{10,... | collective-permute-start | bytes 1032200 | tf_op jit(solution)/shard_map/ppermute | solution.py:25
  36.2 20.8 %collective-permute-start.7 = (bf16[80,3584]{1,0:T(8,128)(2,1)S(1)}, bf16[80,3584]{1,0:T(8,128)(2,1)S(1)}, u32[]{:S(2)}, u32[]{:S(2)}) collective-permute-start(bf16[80,3584]{1,0:T(8,128)(2,1)S(1)} %get-tuple-element.166), channel_id=1, source_target_pairs={{0,12},{1,13},{2,14},{3,15},{4,8},{5,9},{6,10},{7,11},{8,4},{9,5},... | collective-permute-start | bytes 1720328 | tf_op jit(solution)/shard_map/ppermute | solution.py:25
  39.8 25.7 %collective-permute-start.5 = (bf16[80,3584]{1,0:T(8,128)(2,1)S(1)}, bf16[80,3584]{1,0:T(8,128)(2,1)S(1)}, u32[]{:S(2)}, u32[]{:S(2)}) collective-permute-start(bf16[80,3584]{1,0:T(8,128)(2,1)S(1)} %get-tuple-element.163), channel_id=1, source_target_pairs={{0,4},{1,5},{2,6},{3,7},{4,0},{5,1},{6,2},{7,3},{8,12},{9,13},{10,... | collective-permute-start | bytes 1720328 | tf_op jit(solution)/shard_map/ppermute | solution.py:25
  39.8 37.6 %collective-permute-start.6 = (bf16[80,3584]{1,0:T(8,128)(2,1)S(1)}, bf16[80,3584]{1,0:T(8,128)(2,1)S(1)}, u32[]{:S(2)}, u32[]{:S(2)}) collective-permute-start(bf16[80,3584]{1,0:T(8,128)(2,1)S(1)} %cut.5), channel_id=1, source_target_pairs={{0,4},{1,5},{2,6},{3,7},{4,0},{5,1},{6,2},{7,3},{8,12},{9,13},{10,... | collective-permute-start | bytes 1720328 | tf_op jit(solution)/shard_map/ppermute | solution.py:25
  41.8 9.7 %collective-permute-start.8 = (bf16[32,3584]{1,0:T(8,128)(2,1)S(1)}, bf16[32,3584]{1,0:T(8,128)(2,1)S(1)}, u32[]{:S(2)}, u32[]{:S(2)}) collective-permute-start(bf16[32,3584]{1,0:T(8,128)(2,1)S(1)} %get-tuple-element.168), channel_id=1, source_target_pairs={{0,2},{1,3},{2,0},{3,1},{4,6},{5,7},{6,4},{7,5},{8,10},{9,11},{10,... | collective-permute-start | bytes 688136 | tf_op jit(solution)/shard_map/ppermute | solution.py:25
  50.9 26.5 %collective-permute-start.10 = (bf16[48,3584]{1,0:T(8,128)(2,1)S(1)}, bf16[48,3584]{1,0:T(8,128)(2,1)S(1)}, u32[]{:S(2)}, u32[]{:S(2)}) collective-permute-start(bf16[48,3584]{1,0:T(8,128)(2,1)S(1)} %get-tuple-element.191), channel_id=1, source_target_pairs={{0,2},{1,3},{2,0},{3,1},{4,6},{5,7},{6,4},{7,5},{8,10},{9,11},{10,... | collective-permute-start | bytes 1032200 | tf_op jit(solution)/shard_map/ppermute | solution.py:25
  55.5 21.9 %collective-permute-start.11 = (bf16[32,3584]{1,0:T(8,128)(2,1)S(1)}, bf16[32,3584]{1,0:T(8,128)(2,1)S(1)}, u32[]{:S(2)}, u32[]{:S(2)}) collective-permute-start(bf16[32,3584]{1,0:T(8,128)(2,1)S(1)} %get-tuple-element.192), channel_id=1, source_target_pairs={{0,2},{1,3},{2,0},{3,1},{4,6},{5,7},{6,4},{7,5},{8,10},{9,11},{10,... | collective-permute-start | bytes 688136 | tf_op jit(solution)/shard_map/ppermute | solution.py:25
  77.6 28.3 %collective-permute-start.19 = (bf16[80,3584]{1,0:T(8,128)(2,1)S(1)}, bf16[80,3584]{1,0:T(8,128)(2,1)S(1)}, u32[]{:S(2)}, u32[]{:S(2)}) collective-permute-start(bf16[80,3584]{1,0:T(8,128)(2,1)S(1)} %total.4), channel_id=1, source_target_pairs={{0,8},{1,9},{2,10},{3,11},{4,12},{5,13},{6,14},{7,15},{8,0},{9,1},... | collective-permute-start | bytes 1720328 | tf_op jit(solution)/shard_map/ppermute | solution.py:25
  78.2 11.0 %collective-permute-start.15 = (bf16[48,3584]{1,0:T(8,128)(2,1)S(1)}, bf16[48,3584]{1,0:T(8,128)(2,1)S(1)}, u32[]{:S(2)}, u32[]{:S(2)}) collective-permute-start(bf16[48,3584]{1,0:T(8,128)(2,1)S(1)} %get-tuple-element.210), channel_id=1, source_target_pairs={{0,2},{1,3},{2,0},{3,1},{4,6},{5,7},{6,4},{7,5},{8,10},{9,11},{10,... | collective-permute-start | bytes 1032200 | tf_op jit(solution)/shard_map/ppermute | solution.py:25
  83.8 51.0 %collective-permute-start.12 = (bf16[80,3584]{1,0:T(8,128)(2,1)S(1)}, bf16[80,3584]{1,0:T(8,128)(2,1)S(1)}, u32[]{:S(2)}, u32[]{:S(2)}) collective-permute-start(bf16[80,3584]{1,0:T(8,128)(2,1)S(1)} %get-tuple-element.202), channel_id=1, source_target_pairs={{0,4},{1,5},{2,6},{3,7},{4,0},{5,1},{6,2},{7,3},{8,12},{9,13},{10,... | collective-permute-start | bytes 1720328 | tf_op jit(solution)/shard_map/ppermute | solution.py:25
  85.6 9.8 %collective-permute-start.16 = (bf16[32,3584]{1,0:T(8,128)(2,1)S(1)}, bf16[32,3584]{1,0:T(8,128)(2,1)S(1)}, u32[]{:S(2)}, u32[]{:S(2)}) collective-permute-start(bf16[32,3584]{1,0:T(8,128)(2,1)S(1)} %get-tuple-element.219), channel_id=1, source_target_pairs={{0,2},{1,3},{2,0},{3,1},{4,6},{5,7},{6,4},{7,5},{8,10},{9,11},{10,... | collective-permute-start | bytes 688136 | tf_op jit(solution)/shard_map/ppermute | solution.py:25
  93.0 12.9 %collective-permute-start.17 = (bf16[48,3584]{1,0:T(8,128)(2,1)S(1)}, bf16[48,3584]{1,0:T(8,128)(2,1)S(1)}, u32[]{:S(2)}, u32[]{:S(2)}) collective-permute-start(bf16[48,3584]{1,0:T(8,128)(2,1)S(1)} %get-tuple-element.227), channel_id=1, source_target_pairs={{0,2},{1,3},{2,0},{3,1},{4,6},{5,7},{6,4},{7,5},{8,10},{9,11},{10,... | collective-permute-start | bytes 1032200 | tf_op jit(solution)/shard_map/ppermute | solution.py:25
  94.5 40.2 %collective-permute-start.13 = (bf16[48,3584]{1,0:T(8,128)(2,1)S(1)}, bf16[48,3584]{1,0:T(8,128)(2,1)S(1)}, u32[]{:S(2)}, u32[]{:S(2)}) collective-permute-start(bf16[48,3584]{1,0:T(8,128)(2,1)S(1)} %get-tuple-element.207), channel_id=1, source_target_pairs={{0,4},{1,5},{2,6},{3,7},{4,0},{5,1},{6,2},{7,3},{8,12},{9,13},{10,... | collective-permute-start | bytes 1032200 | tf_op jit(solution)/shard_map/ppermute | solution.py:25
  105.9 28.9 %collective-permute-start.14 = (bf16[32,3584]{1,0:T(8,128)(2,1)S(1)}, bf16[32,3584]{1,0:T(8,128)(2,1)S(1)}, u32[]{:S(2)}, u32[]{:S(2)}) collective-permute-start(bf16[32,3584]{1,0:T(8,128)(2,1)S(1)} %get-tuple-element.208), channel_id=1, source_target_pairs={{0,4},{1,5},{2,6},{3,7},{4,0},{5,1},{6,2},{7,3},{8,12},{9,13},{10,... | collective-permute-start | bytes 688136 | tf_op jit(solution)/shard_map/ppermute | solution.py:25
  106.2 54.4 %collective-permute-start.23 = (bf16[80,3584]{1,0:T(8,128)(2,1)S(1)}, bf16[80,3584]{1,0:T(8,128)(2,1)S(1)}, u32[]{:S(2)}, u32[]{:S(2)}) collective-permute-start(bf16[80,3584]{1,0:T(8,128)(2,1)S(1)} %total.5), channel_id=1, source_target_pairs={{0,12},{1,13},{2,14},{3,15},{4,8},{5,9},{6,10},{7,11},{8,4},{9,5},... | collective-permute-start | bytes 1720328 | tf_op jit(solution)/shard_map/ppermute | solution.py:25
  134.8 25.8 %collective-permute-start.20 = (bf16[80,3584]{1,0:T(8,128)(2,1)S(1)}, bf16[80,3584]{1,0:T(8,128)(2,1)S(1)}, u32[]{:S(2)}, u32[]{:S(2)}) collective-permute-start(bf16[80,3584]{1,0:T(8,128)(2,1)S(1)} %get-tuple-element.237), channel_id=1, source_target_pairs={{0,2},{1,3},{2,0},{3,1},{4,6},{5,7},{6,4},{7,5},{8,10},{9,11},{10,... | collective-permute-start | bytes 1720328 | tf_op jit(solution)/shard_map/ppermute | solution.py:25
  135.3 25.0 %collective-permute-start.21 = (bf16[48,3584]{1,0:T(8,128)(2,1)S(1)}, bf16[48,3584]{1,0:T(8,128)(2,1)S(1)}, u32[]{:S(2)}, u32[]{:S(2)}) collective-permute-start(bf16[48,3584]{1,0:T(8,128)(2,1)S(1)} %collective-permute-done.13), channel_id=1, source_target_pairs={{0,2},{1,3},{2,0},{3,1},{4,6},{5,7},{6,4},{7,5},{8,10},{9,11},{10,... | collective-permute-start | bytes 1032200 | tf_op jit(solution)/shard_map/ppermute | solution.py:25
  136.8 23.5 %collective-permute-start.22 = (bf16[32,3584]{1,0:T(8,128)(2,1)S(1)}, bf16[32,3584]{1,0:T(8,128)(2,1)S(1)}, u32[]{:S(2)}, u32[]{:S(2)}) collective-permute-start(bf16[32,3584]{1,0:T(8,128)(2,1)S(1)} %collective-permute-done.14), channel_id=1, source_target_pairs={{0,2},{1,3},{2,0},{3,1},{4,6},{5,7},{6,4},{7,5},{8,10},{9,11},{10,... | collective-permute-start | bytes 688136 | tf_op jit(solution)/shard_map/ppermute | solution.py:25
  163.5 9.8 %all-to-all-start = ((f32[16,1,16]{2,1,0:T(1,128)}), f32[16,1,16]{2,1,0:T(1,128)S(1)}, u32[]{:S(2)}, u32[]{:S(2)}) async-start(f32[16,1,16]{2,1,0:T(1,128)} %bitcast.6), calls=%async_computation | async-start | bytes 16384 | tf_op jit(solution)/shard_map/all_to_all | solution.py:390
  (10 other events, 449.8 us)

commit v11 on v8

--- a/solution.py
+++ b/solution.py
@@ -299,8 +299,6 @@
         mine[k], theirs[k] = [], []
         for (first, _), piece in zip(pieces, far[k]):
             there = order.mark_one(piece)
-            if first == 0 and k == 2:
-                theirs[0] = order.mark(*theirs[0])
             part, other = order.mark(*expert_block(order.late(near[k]), first, there, weights))
             mine[k].append(part)
             theirs[k].append(swap(other, side))
@@ -319,16 +317,13 @@
     def arrive_back(k):
         back[k] = order.mark_one(back[k])
 
+    leave(2)
     far[0], far[1] = swap(near[0], side), swap(near[1], side)
     leave(1)
-    leave(2)
-    far[0], weights[1] = order.mark(far[0], weights[1])
-    work_whole(0)
-    theirs[0] = [swap(theirs[0], side)]
-    mine[0] = [mine[0]]
     arrive(2)
+    far[0] = order.mark_one(far[0])
+    far[1] = order.mark_one(far[1])
     arrive(1)
-    far[1] = order.mark_one(far[1])
     for k in range(3, experts + 1):
         share(k - 1)
         if k < experts:
@@ -341,21 +336,26 @@
         if k == experts:
             far[1] = order.mark_one(far[1])
             work_whole(1)
-            theirs[1] = [swap(piece, spread) for piece in order.mark(*cut(theirs[1], pieces))]
+            theirs[1] = swap(theirs[1], spread)
         work(k - 1)
+        if k == experts:
+            work_whole(0)
         if k < experts:
             arrive(k)
         if k > 3:
             arrive_back(k - 2)
-    theirs[1] = order.mark(*theirs[1])
     home(experts - 1)
     leave_back(experts - 1)
+    mine[0], theirs[0] = [mine[0]], [swap(order.late(theirs[0]), side)]
     mine[1] = [swap(order.late(mine[1]), spread)]
+    theirs[1] = order.mark(*cut(order.mark_one(theirs[1]), pieces))
     theirs[1] = [swap(order.late(piece), side) for piece in theirs[1]]
+    order = Order(own)
     arrive_back(experts - 1)
-    home(0)
+    theirs[0] = order.mark(*theirs[0])
     mine[1] = order.mark(*mine[1])
-    home(1)
+    own = order.token
+    back[0], back[1] = total(mine[0], theirs[0]), total(mine[1], theirs[1])
     blocks = [back[k] for k in range(experts)]
     local = score(
         own,

time: 147 us -> 143 us (0.973)
  starting transfers between devices: 39 us -> 33.8 us
    ppermute x23 -> x22, starting transfers between devices: 34.6 us -> 28.6 us  [swap(): return lax.ppermute(value, 'expert', pairs)]
    ppermute x23 -> x22, waiting for transfers between devices: 67.1 us -> 68.5 us  [swap(): return lax.ppermute(value, 'expert', pairs)]
  transfers between devices with their start and end apart: 24 -> 23, of which waited for: 11 -> 11; matrix products, arithmetic and copies ran while one was open for 0% -> 0% of each run, Pallas kernels for 16% -> 17%
where the time goes in v11:
time: 143 us
  waiting for transfers between devices  74.7 us (52%)
  starting transfers between devices  33.8 us (24%)
  Pallas kernels  31.5 us (22%)
    ppermute x22, waiting for transfers between devices, swap(): return lax.ppermute(value, 'expert', pairs)  68.5 us
    ppermute x22, starting transfers between devices, swap(): return lax.ppermute(value, 'expert', pairs)  28.6 us
    pallas_call x6, Pallas kernels, expert_block(): pl.pallas_call(functools.partial(expert_kernel, first), out_shape=[jax.Sh...  23.3 us
    all_to_all x1, waiting for transfers between devices, per_device(): lax.all_to_all(local, 'expert', split_axis=0, concat_axis=0, tiled=True)  6.21 us
    all_to_all x1, starting transfers between devices, per_device(): lax.all_to_all(local, 'expert', split_axis=0, concat_axis=0, tiled=True)  5.17 us
    pallas_call x1, Pallas kernels, pack(): pl.pallas_call(pack_kernel, out_shape=[jax.ShapeDtypeStruct(shape, BF16)...  4.5 us
  transfers between devices with their start and end apart: 23, of which 11 were waited for; matrix products, arithmetic and copies ran while one was open for 0% of the time, Pallas kernels for 17%

profile of v11, /device:TPU:0, one launch (start us, length us, event | category | flops | bytes accessed | tf_op | source)
XLA Modules:
  0.0 142.7 jit_solution(14782691377975020783)
XLA Ops:
  1.4 4.5 %pack.1 = (bf16[80,3584]{1,0:T(8,128)(2,1)S(1)}, bf16[80,3584]{1,0:T(8,128)(2,1)S(1)}, bf16[80,3584]{1,0:T(8,128)(2,1)S(1)}, bf16[80,3584]{1,0:T(8,128)(2,1)S(1)}, bf16[10752,512]{1,0:T(8,128)(2,1)S(1)}) custom-call(s32[1]{0:T(128)} %bitcast.own_ref, bf16[128,3584]{1,0:T(8,128)(2,1)} %tokens_ref.1, f32[1,3584]{1,0:T(1,128)S(1)} %broadcast_in_dim.12.gain_ref, ...), custom_call_target="tpu_custom_call" | custom-call | flops 1024 | bytes 1024 | tf_op jit(solution)/shard_map/pack/pallas_call | solution.py:78
  6.4 3.7 %collective-permute-start.3 = (bf16[80,3584]{1,0:T(8,128)(2,1)S(1)}, bf16[80,3584]{1,0:T(8,128)(2,1)S(1)}, u32[]{:S(2)}, u32[]{:S(2)}) collective-permute-start(bf16[80,3584]{1,0:T(8,128)(2,1)S(1)} %get-tuple-element.118), channel_id=1, source_target_pairs={{0,8},{1,9},{2,10},{3,11},{4,12},{5,13},{6,14},{7,15},{8,0},{9,1},... | collective-permute-start | bytes 1720328 | tf_op jit(solution)/shard_map/ppermute | solution.py:25
  13.7 22.4 %collective-permute-done.3.whole_ref.near_ref = bf16[80,3584]{1,0:T(8,128)(2,1)S(1)} collective-permute-done((bf16[80,3584]{1,0:T(8,128)(2,1)S(1)}, bf16[80,3584]{1,0:T(8,128)(2,1)S(1)}, u32[]{:S(2)}, u32[]{:S(2)}) %collective-permute-start.3) | collective-permute-done | bytes 573472 | tf_op jit(solution)/shard_map/ppermute | solution.py:25
  37.7 1.6 %collective-permute-start.5 = (bf16[48,3584]{1,0:T(8,128)(2,1)S(1)}, bf16[48,3584]{1,0:T(8,128)(2,1)S(1)}, u32[]{:S(2)}, u32[]{:S(2)}) collective-permute-start(bf16[48,3584]{1,0:T(8,128)(2,1)S(1)} %get-tuple-element.131), channel_id=1, source_target_pairs={{0,2},{1,3},{2,0},{3,1},{4,6},{5,7},{6,4},{7,5},{8,10},{9,11},{10,... | collective-permute-start | bytes 1032200 | tf_op jit(solution)/shard_map/ppermute | solution.py:25
  39.3 2.4 %collective-permute-start.10 = (bf16[80,3584]{1,0:T(8,128)(2,1)S(1)}, bf16[80,3584]{1,0:T(8,128)(2,1)S(1)}, u32[]{:S(2)}, u32[]{:S(2)}) collective-permute-start(bf16[80,3584]{1,0:T(8,128)(2,1)S(1)} %get-tuple-element.151), channel_id=1, source_target_pairs={{0,12},{1,13},{2,14},{3,15},{4,8},{5,9},{6,10},{7,11},{8,4},{9,5},... | collective-permute-start | bytes 1720328 | tf_op jit(solution)/shard_map/ppermute | solution.py:25
  42.2 6.5 %collective-permute-done.5.far_ref = bf16[48,3584]{1,0:T(8,128)(2,1)S(1)} collective-permute-done((bf16[48,3584]{1,0:T(8,128)(2,1)S(1)}, bf16[48,3584]{1,0:T(8,128)(2,1)S(1)}, u32[]{:S(2)}, u32[]{:S(2)}) %collective-permute-start.5) | collective-permute-done | bytes 344096 | tf_op jit(solution)/shard_map/ppermute | solution.py:25
  48.7 3.7 %expert_block.6 = (bf16[48,3584]{1,0:T(8,128)(2,1)S(1)}, bf16[48,3584]{1,0:T(8,128)(2,1)S(1)}) custom-call(bf16[80,3584]{1,0:T(8,128)(2,1)S(1)} %collective-permute-done.3.whole_ref.near_ref, bf16[48,3584]{1,0:T(8,128)(2,1)S(1)} %collective-permute-done.5.far_ref, bf16[10752,512]{1,0:T(8,128)(2,1)S(1)} %get-tuple-element.135.refs_0_, ...), custom_call_target="tpu_custom_call" | custom-call | flops 1024 | bytes 1024 | tf_op jit(solution)/shard_map/expert_block/pallas_call | solution.py:118
  52.4 1.7 %collective-permute-start.8 = (bf16[48,3584]{1,0:T(8,128)(2,1)S(1)}, bf16[48,3584]{1,0:T(8,128)(2,1)S(1)}, u32[]{:S(2)}, u32[]{:S(2)}) collective-permute-start(bf16[48,3584]{1,0:T(8,128)(2,1)S(1)} %get-tuple-element.148), channel_id=1, source_target_pairs={{0,2},{1,3},{2,0},{3,1},{4,6},{5,7},{6,4},{7,5},{8,10},{9,11},{10,... | collective-permute-start | bytes 1032200 | tf_op jit(solution)/shard_map/ppermute | solution.py:25
  54.1 4.0 %expert_block.7 = (bf16[32,3584]{1,0:T(8,128)(2,1)S(1)}, bf16[32,3584]{1,0:T(8,128)(2,1)S(1)}) custom-call(bf16[80,3584]{1,0:T(8,128)(2,1)S(1)} %collective-permute-done.3.whole_ref.near_ref, bf16[32,3584]{1,0:T(8,128)(2,1)S(1)} %collective-permute-done.7.far_ref, bf16[10752,512]{1,0:T(8,128)(2,1)S(1)} %get-tuple-element.135.refs_0_, ...), custom_call_target="tpu_custom_call" | custom-call | flops 1024 | bytes 1024 | tf_op jit(solution)/shard_map/expert_block/pallas_call | solution.py:118
  58.6 1.7 %collective-permute-start.11 = (bf16[48,3584]{1,0:T(8,128)(2,1)S(1)}, bf16[48,3584]{1,0:T(8,128)(2,1)S(1)}, u32[]{:S(2)}, u32[]{:S(2)}) collective-permute-start(bf16[48,3584]{1,0:T(8,128)(2,1)S(1)} %get-tuple-element.169), channel_id=1, source_target_pairs={{0,2},{1,3},{2,0},{3,1},{4,6},{5,7},{6,4},{7,5},{8,10},{9,11},{10,... | collective-permute-start | bytes 1032200 | tf_op jit(solution)/shard_map/ppermute | solution.py:25
  60.3 7.8 %collective-permute-done.9.refs_3_ = bf16[32,3584]{1,0:T(8,128)(2,1)S(1)} collective-permute-done((bf16[32,3584]{1,0:T(8,128)(2,1)S(1)}, bf16[32,3584]{1,0:T(8,128)(2,1)S(1)}, u32[]{:S(2)}, u32[]{:S(2)}) %collective-permute-start.9) | collective-permute-done | bytes 229408 | tf_op jit(solution)/shard_map/ppermute | solution.py:25
  68.5 1.8 %collective-permute-start.12 = (bf16[32,3584]{1,0:T(8,128)(2,1)S(1)}, bf16[32,3584]{1,0:T(8,128)(2,1)S(1)}, u32[]{:S(2)}, u32[]{:S(2)}) collective-permute-start(bf16[32,3584]{1,0:T(8,128)(2,1)S(1)} %get-tuple-element.178), channel_id=1, source_target_pairs={{0,2},{1,3},{2,0},{3,1},{4,6},{5,7},{6,4},{7,5},{8,10},{9,11},{10,... | collective-permute-start | bytes 688136 | tf_op jit(solution)/shard_map/ppermute | solution.py:25
  70.2 3.8 %expert_block.8 = (bf16[80,3584]{1,0:T(8,128)(2,1)S(1)}, bf16[80,3584]{1,0:T(8,128)(2,1)S(1)}) custom-call(bf16[80,3584]{1,0:T(8,128)(2,1)S(1)} %collective-permute-done.near_ref, bf16[80,3584]{1,0:T(8,128)(2,1)S(1)} %collective-permute-done.4.far_ref, bf16[10752,512]{1,0:T(8,128)(2,1)S(1)} %get-tuple-element.135.refs_0_, ...), custom_call_target="tpu_custom_call" | custom-call | flops 1024 | bytes 1024 | tf_op jit(solution)/shard_map/expert_block/pallas_call | solution.py:118
  74.5 3.9 %expert_block.9 = (bf16[48,3584]{1,0:T(8,128)(2,1)S(1)}, bf16[48,3584]{1,0:T(8,128)(2,1)S(1)}) custom-call(bf16[80,3584]{1,0:T(8,128)(2,1)S(1)} %collective-permute-done.10.whole_ref.near_ref, bf16[48,3584]{1,0:T(8,128)(2,1)S(1)} %collective-permute-done.11.far_ref, bf16[10752,512]{1,0:T(8,128)(2,1)S(1)} %get-tuple-element.135.refs_0_, ...), custom_call_target="tpu_custom_call" | custom-call | flops 1024 | bytes 1024 | tf_op jit(solution)/shard_map/expert_block/pallas_call | solution.py:118
  78.4 1.7 %collective-permute-start.13 = (bf16[48,3584]{1,0:T(8,128)(2,1)S(1)}, bf16[48,3584]{1,0:T(8,128)(2,1)S(1)}, u32[]{:S(2)}, u32[]{:S(2)}) collective-permute-start(bf16[48,3584]{1,0:T(8,128)(2,1)S(1)} %get-tuple-element.186), channel_id=1, source_target_pairs={{0,2},{1,3},{2,0},{3,1},{4,6},{5,7},{6,4},{7,5},{8,10},{9,11},{10,... | collective-permute-start | bytes 1032200 | tf_op jit(solution)/shard_map/ppermute | solution.py:25
  80.1 2.3 %collective-permute-start.19 = (bf16[80,3584]{1,0:T(8,128)(2,1)S(1)}, bf16[80,3584]{1,0:T(8,128)(2,1)S(1)}, u32[]{:S(2)}, u32[]{:S(2)}) collective-permute-start(bf16[80,3584]{1,0:T(8,128)(2,1)S(1)} %get-tuple-element.211), channel_id=1, source_target_pairs={{0,4},{1,5},{2,6},{3,7},{4,0},{5,1},{6,2},{7,3},{8,12},{9,13},{10,... | collective-permute-start | bytes 1720328 | tf_op jit(solution)/shard_map/ppermute | solution.py:25
  82.3 4.0 %expert_block.10 = (bf16[32,3584]{1,0:T(8,128)(2,1)S(1)}, bf16[32,3584]{1,0:T(8,128)(2,1)S(1)}) custom-call(bf16[80,3584]{1,0:T(8,128)(2,1)S(1)} %collective-permute-done.10.whole_ref.near_ref, bf16[32,3584]{1,0:T(8,128)(2,1)S(1)} %collective-permute-done.12.far_ref, bf16[10752,512]{1,0:T(8,128)(2,1)S(1)} %get-tuple-element.135.refs_0_, ...), custom_call_target="tpu_custom_call" | custom-call | flops 1024 | bytes 1024 | tf_op jit(solution)/shard_map/expert_block/pallas_call | solution.py:118
  87.9 3.8 %expert_block.11 = (bf16[80,3584]{1,0:T(8,128)(2,1)S(1)}, bf16[80,3584]{1,0:T(8,128)(2,1)S(1)}) custom-call(bf16[80,3584]{1,0:T(8,128)(2,1)S(1)} %get-tuple-element.190.near_ref, bf16[80,3584]{1,0:T(8,128)(2,1)S(1)} %collective-permute-done.2.far_ref, bf16[10752,512]{1,0:T(8,128)(2,1)S(1)} %get-tuple-element.135.refs_0_, ...), custom_call_target="tpu_custom_call" | custom-call | flops 1024 | bytes 1024 | tf_op jit(solution)/shard_map/expert_block/pallas_call | solution.py:118
  93.2 1.6 %collective-permute-start.18 = (bf16[80,3584]{1,0:T(8,128)(2,1)S(1)}, bf16[80,3584]{1,0:T(8,128)(2,1)S(1)}, u32[]{:S(2)}, u32[]{:S(2)}) collective-permute-start(bf16[80,3584]{1,0:T(8,128)(2,1)S(1)} %total.5), channel_id=1, source_target_pairs={{0,12},{1,13},{2,14},{3,15},{4,8},{5,9},{6,10},{7,11},{8,4},{9,5},... | collective-permute-start | bytes 1720328 | tf_op jit(solution)/shard_map/ppermute | solution.py:25
  96.3 19.3 %collective-permute-done.19.whole_ref = bf16[80,3584]{1,0:T(8,128)(2,1)S(1)} collective-permute-done((bf16[80,3584]{1,0:T(8,128)(2,1)S(1)}, bf16[80,3584]{1,0:T(8,128)(2,1)S(1)}, u32[]{:S(2)}, u32[]{:S(2)}) %collective-permute-start.19) | collective-permute-done | bytes 573472 | tf_op jit(solution)/shard_map/ppermute | solution.py:25
  118.1 8.2 %collective-permute-done.16.refs_0_ = bf16[80,3584]{1,0:T(8,128)(2,1)S(1)} collective-permute-done((bf16[80,3584]{1,0:T(8,128)(2,1)S(1)}, bf16[80,3584]{1,0:T(8,128)(2,1)S(1)}, u32[]{:S(2)}, u32[]{:S(2)}) %collective-permute-start.16) | collective-permute-done | bytes 573472 | tf_op jit(solution)/shard_map/ppermute | solution.py:25
  127.8 2.5 %score.1 = f32[16,16]{1,0:T(8,128)} custom-call(s32[1]{0:T(128)} %bitcast.own_ref, bf16[128,3584]{1,0:T(8,128)(2,1)S(1)} %copy-done, f32[1,3584]{1,0:T(1,128)S(1)} %broadcast_in_dim.13.gain_ref, s32[2,128]{1,0:T(2,128)S(1)} %bitcast.9, f32[2,128]{1,0:T(2,128)S(1)} %bitcast.10, bf16[128,3584]{1,0:T(8,128)(2,1)S(1)} %copy-done.1, f32[1,128]{1,0:T(1,128)S(1)} %bitcast.11, ...), custom_call_target="tpu_custom_call" | custom-call | flops 1024 | bytes 1024 | tf_op jit(solution)/shard_map/score/pallas_call | solution.py:181
  130.3 5.2 %all-to-all-start = ((f32[16,1,16]{2,1,0:T(1,128)}), f32[16,1,16]{2,1,0:T(1,128)S(1)}, u32[]{:S(2)}, u32[]{:S(2)}) async-start(f32[16,1,16]{2,1,0:T(1,128)} %bitcast.6), calls=%async_computation | async-start | bytes 16384 | tf_op jit(solution)/shard_map/all_to_all | solution.py:373
  135.7 6.2 %all-to-all-done = f32[16,1,16]{2,1,0:T(1,128)S(1)} async-done(((f32[16,1,16]{2,1,0:T(1,128)}), f32[16,1,16]{2,1,0:T(1,128)S(1)}, u32[]{:S(2)}, u32[]{:S(2)}) %all-to-all-start) | async-done | bytes 1056 | tf_op jit(solution)/shard_map/all_to_all | solution.py:373
  (63 shorter events, 17.6 us)
Async XLA Ops:
  5.9 42.8 %collective-permute-start.6 = (bf16[10752,512]{1,0:T(8,128)(2,1)S(1)}, bf16[10752,512]{1,0:T(8,128)(2,1)S(1)}, u32[]{:S(2)}, u32[]{:S(2)}) collective-permute-start(bf16[10752,512]{1,0:T(8,128)(2,1)S(1)} %get-tuple-element.135.refs_0_), channel_id=1, source_target_pairs={{0,1},{1,0},{2,3},{3,2},{4,5},{5,4},{6,7},{7,6},{8,9},{9,8},{10,11... | collective-permute-start | bytes 33030152 | tf_op jit(solution)/shard_map/ppermute | solution.py:25
  6.4 29.6 %collective-permute-start.3 = (bf16[80,3584]{1,0:T(8,128)(2,1)S(1)}, bf16[80,3584]{1,0:T(8,128)(2,1)S(1)}, u32[]{:S(2)}, u32[]{:S(2)}) collective-permute-start(bf16[80,3584]{1,0:T(8,128)(2,1)S(1)} %get-tuple-element.118), channel_id=1, source_target_pairs={{0,8},{1,9},{2,10},{3,11},{4,12},{5,13},{6,14},{7,15},{8,0},{9,1},... | collective-permute-start | bytes 1720328 | tf_op jit(solution)/shard_map/ppermute | solution.py:25
  10.1 26.0 %collective-permute-start.2 = (bf16[80,3584]{1,0:T(8,128)(2,1)S(1)}, bf16[80,3584]{1,0:T(8,128)(2,1)S(1)}, u32[]{:S(2)}, u32[]{:S(2)}) collective-permute-start(bf16[80,3584]{1,0:T(8,128)(2,1)S(1)} %get-tuple-element.190.near_ref), channel_id=1, source_target_pairs={{0,2},{1,3},{2,0},{3,1},{4,6},{5,7},{6,4},{7,5},{8,10},{9,11},{10,... | collective-permute-start | bytes 1720328 | tf_op jit(solution)/shard_map/ppermute | solution.py:25
  11.6 25.8 %collective-permute-start.1 = (bf16[80,3584]{1,0:T(8,128)(2,1)S(1)}, bf16[80,3584]{1,0:T(8,128)(2,1)S(1)}, u32[]{:S(2)}, u32[]{:S(2)}) collective-permute-start(bf16[80,3584]{1,0:T(8,128)(2,1)S(1)} %get-tuple-element.115), channel_id=1, source_target_pairs={{0,2},{1,3},{2,0},{3,1},{4,6},{5,7},{6,4},{7,5},{8,10},{9,11},{10,... | collective-permute-start | bytes 1720328 | tf_op jit(solution)/shard_map/ppermute | solution.py:25
  12.1 25.6 %collective-permute-start = (bf16[80,3584]{1,0:T(8,128)(2,1)S(1)}, bf16[80,3584]{1,0:T(8,128)(2,1)S(1)}, u32[]{:S(2)}, u32[]{:S(2)}) collective-permute-start(bf16[80,3584]{1,0:T(8,128)(2,1)S(1)} %get-tuple-element.115), channel_id=1, source_target_pairs={{0,4},{1,5},{2,6},{3,7},{4,0},{5,1},{6,2},{7,3},{8,12},{9,13},{10,... | collective-permute-start | bytes 1720328 | tf_op jit(solution)/shard_map/ppermute | solution.py:25
  37.7 11.0 %collective-permute-start.5 = (bf16[48,3584]{1,0:T(8,128)(2,1)S(1)}, bf16[48,3584]{1,0:T(8,128)(2,1)S(1)}, u32[]{:S(2)}, u32[]{:S(2)}) collective-permute-start(bf16[48,3584]{1,0:T(8,128)(2,1)S(1)} %get-tuple-element.131), channel_id=1, source_target_pairs={{0,2},{1,3},{2,0},{3,1},{4,6},{5,7},{6,4},{7,5},{8,10},{9,11},{10,... | collective-permute-start | bytes 1032200 | tf_op jit(solution)/shard_map/ppermute | solution.py:25
  39.3 19.3 %collective-permute-start.10 = (bf16[80,3584]{1,0:T(8,128)(2,1)S(1)}, bf16[80,3584]{1,0:T(8,128)(2,1)S(1)}, u32[]{:S(2)}, u32[]{:S(2)}) collective-permute-start(bf16[80,3584]{1,0:T(8,128)(2,1)S(1)} %get-tuple-element.151), channel_id=1, source_target_pairs={{0,12},{1,13},{2,14},{3,15},{4,8},{5,9},{6,10},{7,11},{8,4},{9,5},... | collective-permute-start | bytes 1720328 | tf_op jit(solution)/shard_map/ppermute | solution.py:25
  41.7 12.4 %collective-permute-start.7 = (bf16[32,3584]{1,0:T(8,128)(2,1)S(1)}, bf16[32,3584]{1,0:T(8,128)(2,1)S(1)}, u32[]{:S(2)}, u32[]{:S(2)}) collective-permute-start(bf16[32,3584]{1,0:T(8,128)(2,1)S(1)} %get-tuple-element.140), channel_id=1, source_target_pairs={{0,2},{1,3},{2,0},{3,1},{4,6},{5,7},{6,4},{7,5},{8,10},{9,11},{10,... | collective-permute-start | bytes 688136 | tf_op jit(solution)/shard_map/ppermute | solution.py:25
  42.2 28.0 %collective-permute-start.4 = (bf16[80,3584]{1,0:T(8,128)(2,1)S(1)}, bf16[80,3584]{1,0:T(8,128)(2,1)S(1)}, u32[]{:S(2)}, u32[]{:S(2)}) collective-permute-start(bf16[80,3584]{1,0:T(8,128)(2,1)S(1)} %collective-permute-done.1), channel_id=1, source_target_pairs={{0,4},{1,5},{2,6},{3,7},{4,0},{5,1},{6,2},{7,3},{8,12},{9,13},{10,... | collective-permute-start | bytes 1720328 | tf_op jit(solution)/shard_map/ppermute | solution.py:25
  52.4 15.7 %collective-permute-start.8 = (bf16[48,3584]{1,0:T(8,128)(2,1)S(1)}, bf16[48,3584]{1,0:T(8,128)(2,1)S(1)}, u32[]{:S(2)}, u32[]{:S(2)}) collective-permute-start(bf16[48,3584]{1,0:T(8,128)(2,1)S(1)} %get-tuple-element.148), channel_id=1, source_target_pairs={{0,2},{1,3},{2,0},{3,1},{4,6},{5,7},{6,4},{7,5},{8,10},{9,11},{10,... | collective-permute-start | bytes 1032200 | tf_op jit(solution)/shard_map/ppermute | solution.py:25
  58.1 10.0 %collective-permute-start.9 = (bf16[32,3584]{1,0:T(8,128)(2,1)S(1)}, bf16[32,3584]{1,0:T(8,128)(2,1)S(1)}, u32[]{:S(2)}, u32[]{:S(2)}) collective-permute-start(bf16[32,3584]{1,0:T(8,128)(2,1)S(1)} %get-tuple-element.149), channel_id=1, source_target_pairs={{0,2},{1,3},{2,0},{3,1},{4,6},{5,7},{6,4},{7,5},{8,10},{9,11},{10,... | collective-permute-start | bytes 688136 | tf_op jit(solution)/shard_map/ppermute | solution.py:25
  58.6 15.9 %collective-permute-start.11 = (bf16[48,3584]{1,0:T(8,128)(2,1)S(1)}, bf16[48,3584]{1,0:T(8,128)(2,1)S(1)}, u32[]{:S(2)}, u32[]{:S(2)}) collective-permute-start(bf16[48,3584]{1,0:T(8,128)(2,1)S(1)} %get-tuple-element.169), channel_id=1, source_target_pairs={{0,2},{1,3},{2,0},{3,1},{4,6},{5,7},{6,4},{7,5},{8,10},{9,11},{10,... | collective-permute-start | bytes 1032200 | tf_op jit(solution)/shard_map/ppermute | solution.py:25
  68.4 23.4 %collective-permute-start.15 = (bf16[80,3584]{1,0:T(8,128)(2,1)S(1)}, bf16[80,3584]{1,0:T(8,128)(2,1)S(1)}, u32[]{:S(2)}, u32[]{:S(2)}) collective-permute-start(bf16[80,3584]{1,0:T(8,128)(2,1)S(1)} %total.4), channel_id=1, source_target_pairs={{0,8},{1,9},{2,10},{3,11},{4,12},{5,13},{6,14},{7,15},{8,0},{9,1},... | collective-permute-start | bytes 1720328 | tf_op jit(solution)/shard_map/ppermute | solution.py:25
  68.5 13.9 %collective-permute-start.12 = (bf16[32,3584]{1,0:T(8,128)(2,1)S(1)}, bf16[32,3584]{1,0:T(8,128)(2,1)S(1)}, u32[]{:S(2)}, u32[]{:S(2)}) collective-permute-start(bf16[32,3584]{1,0:T(8,128)(2,1)S(1)} %get-tuple-element.178), channel_id=1, source_target_pairs={{0,2},{1,3},{2,0},{3,1},{4,6},{5,7},{6,4},{7,5},{8,10},{9,11},{10,... | collective-permute-start | bytes 688136 | tf_op jit(solution)/shard_map/ppermute | solution.py:25
  78.4 14.5 %collective-permute-start.13 = (bf16[48,3584]{1,0:T(8,128)(2,1)S(1)}, bf16[48,3584]{1,0:T(8,128)(2,1)S(1)}, u32[]{:S(2)}, u32[]{:S(2)}) collective-permute-start(bf16[48,3584]{1,0:T(8,128)(2,1)S(1)} %get-tuple-element.186), channel_id=1, source_target_pairs={{0,2},{1,3},{2,0},{3,1},{4,6},{5,7},{6,4},{7,5},{8,10},{9,11},{10,... | collective-permute-start | bytes 1032200 | tf_op jit(solution)/shard_map/ppermute | solution.py:25
  80.1 35.6 %collective-permute-start.19 = (bf16[80,3584]{1,0:T(8,128)(2,1)S(1)}, bf16[80,3584]{1,0:T(8,128)(2,1)S(1)}, u32[]{:S(2)}, u32[]{:S(2)}) collective-permute-start(bf16[80,3584]{1,0:T(8,128)(2,1)S(1)} %get-tuple-element.211), channel_id=1, source_target_pairs={{0,4},{1,5},{2,6},{3,7},{4,0},{5,1},{6,2},{7,3},{8,12},{9,13},{10,... | collective-permute-start | bytes 1720328 | tf_op jit(solution)/shard_map/ppermute | solution.py:25
  86.3 6.6 %collective-permute-start.14 = (bf16[32,3584]{1,0:T(8,128)(2,1)S(1)}, bf16[32,3584]{1,0:T(8,128)(2,1)S(1)}, u32[]{:S(2)}, u32[]{:S(2)}) collective-permute-start(bf16[32,3584]{1,0:T(8,128)(2,1)S(1)} %get-tuple-element.187), channel_id=1, source_target_pairs={{0,2},{1,3},{2,0},{3,1},{4,6},{5,7},{6,4},{7,5},{8,10},{9,11},{10,... | collective-permute-start | bytes 688136 | tf_op jit(solution)/shard_map/ppermute | solution.py:25
  91.7 36.0 %copy-start = (bf16[128,3584]{1,0:T(8,128)(2,1)S(1)}, bf16[128,3584]{1,0:T(8,128)(2,1)}, u32[]{:S(2)}) copy-start(bf16[128,3584]{1,0:T(8,128)(2,1)} %tokens_ref.1) | copy-start | bytes 2752516
  93.2 24.6 %collective-permute-start.18 = (bf16[80,3584]{1,0:T(8,128)(2,1)S(1)}, bf16[80,3584]{1,0:T(8,128)(2,1)S(1)}, u32[]{:S(2)}, u32[]{:S(2)}) collective-permute-start(bf16[80,3584]{1,0:T(8,128)(2,1)S(1)} %total.5), channel_id=1, source_target_pairs={{0,12},{1,13},{2,14},{3,15},{4,8},{5,9},{6,10},{7,11},{8,4},{9,5},... | collective-permute-start | bytes 1720328 | tf_op jit(solution)/shard_map/ppermute | solution.py:25
  94.8 23.0 %collective-permute-start.17 = (bf16[80,3584]{1,0:T(8,128)(2,1)S(1)}, bf16[80,3584]{1,0:T(8,128)(2,1)S(1)}, u32[]{:S(2)}, u32[]{:S(2)}) collective-permute-start(bf16[80,3584]{1,0:T(8,128)(2,1)S(1)} %get-tuple-element.203), channel_id=1, source_target_pairs={{0,2},{1,3},{2,0},{3,1},{4,6},{5,7},{6,4},{7,5},{8,10},{9,11},{10,... | collective-permute-start | bytes 1720328 | tf_op jit(solution)/shard_map/ppermute | solution.py:25
  96.3 30.0 %collective-permute-start.16 = (bf16[80,3584]{1,0:T(8,128)(2,1)S(1)}, bf16[80,3584]{1,0:T(8,128)(2,1)S(1)}, u32[]{:S(2)}, u32[]{:S(2)}) collective-permute-start(bf16[80,3584]{1,0:T(8,128)(2,1)S(1)} %get-tuple-element.201), channel_id=1, source_target_pairs={{0,4},{1,5},{2,6},{3,7},{4,0},{5,1},{6,2},{7,3},{8,12},{9,13},{10,... | collective-permute-start | bytes 1720328 | tf_op jit(solution)/shard_map/ppermute | solution.py:25
  115.7 11.8 %collective-permute-start.20 = (bf16[48,3584]{1,0:T(8,128)(2,1)S(1)}, bf16[48,3584]{1,0:T(8,128)(2,1)S(1)}, u32[]{:S(2)}, u32[]{:S(2)}) collective-permute-start(bf16[48,3584]{1,0:T(8,128)(2,1)S(1)} %get-tuple-element.218), channel_id=1, source_target_pairs={{0,2},{1,3},{2,0},{3,1},{4,6},{5,7},{6,4},{7,5},{8,10},{9,11},{10,... | collective-permute-start | bytes 1032200 | tf_op jit(solution)/shard_map/ppermute | solution.py:25
  117.2 10.3 %collective-permute-start.21 = (bf16[32,3584]{1,0:T(8,128)(2,1)S(1)}, bf16[32,3584]{1,0:T(8,128)(2,1)S(1)}, u32[]{:S(2)}, u32[]{:S(2)}) collective-permute-start(bf16[32,3584]{1,0:T(8,128)(2,1)S(1)} %get-tuple-element.220), channel_id=1, source_target_pairs={{0,2},{1,3},{2,0},{3,1},{4,6},{5,7},{6,4},{7,5},{8,10},{9,11},{10,... | collective-permute-start | bytes 688136 | tf_op jit(solution)/shard_map/ppermute | solution.py:25
  130.3 11.6 %all-to-all-start = ((f32[16,1,16]{2,1,0:T(1,128)}), f32[16,1,16]{2,1,0:T(1,128)S(1)}, u32[]{:S(2)}, u32[]{:S(2)}) async-start(f32[16,1,16]{2,1,0:T(1,128)} %bitcast.6), calls=%async_computation | async-start | bytes 16384 | tf_op jit(solution)/shard_map/all_to_all | solution.py:373
  (8 other events, 230.0 us)

commit v12 on v11

--- a/solution.py
+++ b/solution.py
@@ -40,10 +40,10 @@
     return hit, slot
 
 
-def pack_kernel(own_ref, tokens_hbm, gain_ref, picks_hbm, gate_hbm, up_hbm, down_hbm, *refs):
-    *out_refs, weights_ref, tokens_ref, picks_ref, arrived = refs
+def pack_kernel(own_ref, tokens_hbm, gain_hbm, picks_hbm, gate_hbm, up_hbm, down_hbm, *refs):
+    *out_refs, weights_ref, tokens_ref, gain_ref, picks_ref, arrived = refs
     width, hidden = gate_hbm.shape
-    moves = [(tokens_hbm, tokens_ref), (picks_hbm, picks_ref)]
+    moves = [(tokens_hbm, tokens_ref), (gain_hbm, gain_ref), (picks_hbm, picks_ref)]
     sources = [gate_hbm, up_hbm]
     sources += [down_hbm.at[:, pl.ds(first, hidden)] for first in range(0, width, hidden)]
     first = 0
@@ -53,18 +53,18 @@
     copies = [pltpu.make_async_copy(*move, arrived.at[n]) for n, move in enumerate(moves)]
     for copy in copies:
         copy.start()
-    copies[0].wait()
-    copies[1].wait()
+    for copy in copies[:3]:
+        copy.wait()
     tokens = tokens_ref.shape[0]
     values = tokens_ref[...].astype(F32)
     scale = lax.rsqrt(jnp.mean(values * values, axis=-1, keepdims=True) + EPS)
-    normed = (values * scale * gain_ref[...]).astype(BF16)
+    normed = (values * scale * gain_ref[...][None, :]).astype(BF16)
     _, slot = routing(own_ref[0], picks_ref[...], max(8, len(out_refs)))
     for k, out_ref in enumerate(out_refs):
         place = iota((out_ref.shape[0], tokens), 0)
         chosen = (slot[k : k + 1, :] == place).astype(F32).astype(BF16)
         out_ref[...] = jnp.dot(chosen, normed, preferred_element_type=F32).astype(BF16)
-    for copy in copies[2:]:
+    for copy in copies[3:]:
         copy.wait()
 
 
@@ -74,21 +74,22 @@
     vmem = pl.BlockSpec(memory_space=pltpu.VMEM)
     hbm = pl.BlockSpec(memory_space=pltpu.HBM)
     shapes = [(capacity, width)] * experts + [(3 * width, hidden)]
-    there = [pltpu.with_memory_space_constraint(array, pltpu.HBM) for array in (tokens, picks, *weights)]
+    there = [pltpu.with_memory_space_constraint(array, pltpu.HBM) for array in (tokens, gain, picks, *weights)]
     return pl.pallas_call(
         pack_kernel,
         out_shape=[jax.ShapeDtypeStruct(shape, BF16) for shape in shapes],
-        in_specs=[smem, hbm, vmem, hbm] + [hbm] * 3,
+        in_specs=[smem] + [hbm] * 6,
         out_specs=[vmem] * len(shapes),
         scratch_shapes=[
             pltpu.VMEM(tokens.shape, BF16),
+            pltpu.VMEM(gain.shape, F32),
             pltpu.VMEM(picks.shape, jnp.int32),
-            pltpu.SemaphoreType.DMA((4 + width // hidden,)),
+            pltpu.SemaphoreType.DMA((5 + width // hidden,)),
         ],
         compiler_params=pltpu.CompilerParams(vmem_limit_bytes=VMEM_LIMIT),
         cost_estimate=COST,
         name="pack",
-    )(own, there[0], gain, *there[1:])
+    )(own, *there)
 
 
 def expert_kernel(first, near_ref, far_ref, *refs):
@@ -159,7 +160,7 @@
     logit = jnp.zeros((tokens, 1), F32)
     for start in range(0, width, chunk):
         cols = slice(start, start + chunk)
-        final = (stream[:, cols] * scale * gain_ref[:, cols]).astype(BF16).astype(F32)
+        final = (stream[:, cols] * scale * gain_ref[cols][None, :]).astype(BF16).astype(F32)
         logit = logit + jnp.sum(final * target_ref[:, cols].astype(F32), axis=-1, keepdims=True)
     turn = iota((tokens, tokens), 0) == iota((tokens, tokens), 1)
     logit = jnp.sum(jnp.where(turn, logit, 0.0), axis=0, keepdims=True)
@@ -281,7 +282,7 @@
     cut_at = capacity * 5 // 8 // 16 * 16
     pieces = [(0, cut_at), (cut_at, capacity - cut_at)] if cut_at else [(0, capacity)]
     weights = (gate_weight, up_weight, down_weight)
-    *near, staged = pack(own, tokens, norm_gain[None, :], picks_t, weights, experts, capacity)
+    *near, staged = pack(own, tokens, norm_gain, picks_t, weights, experts, capacity)
     weights = [staged, swap(staged, core)]
     order = Order(own)
     far, mine, theirs, back = {}, {}, {}, {}
@@ -324,17 +325,21 @@
     far[0] = order.mark_one(far[0])
     far[1] = order.mark_one(far[1])
     arrive(1)
+    last = (capacity - 16, 16)
     for k in range(3, experts + 1):
+        if k > 3:
+            near[k - 1], *theirs[k - 2] = lax.optimization_barrier((near[k - 1], *theirs[k - 2]))
         share(k - 1)
         if k < experts:
             leave(k)
         if k == 3:
             far[1] = swap(order.late(far[1]), spread)
         if k > 3:
+            if k == experts:
+                far[1], *theirs[k - 2] = lax.optimization_barrier((far[1], *theirs[k - 2]))
             home(k - 2)
             leave_back(k - 2)
         if k == experts:
-            far[1] = order.mark_one(far[1])
             work_whole(1)
             theirs[1] = swap(theirs[1], spread)
         work(k - 1)
@@ -348,7 +353,7 @@
     leave_back(experts - 1)
     mine[0], theirs[0] = [mine[0]], [swap(order.late(theirs[0]), side)]
     mine[1] = [swap(order.late(mine[1]), spread)]
-    theirs[1] = order.mark(*cut(order.mark_one(theirs[1]), pieces))
+    theirs[1] = order.mark(*cut(order.mark_one(theirs[1]), [(0, last[0]), last]))
     theirs[1] = [swap(order.late(piece), side) for piece in theirs[1]]
     order = Order(own)
     arrive_back(experts - 1)
@@ -360,7 +365,7 @@
     local = score(
         own,
         tokens,
-        final_gain[None, :],
+        final_gain,
         picks_t,
         gates.T,
         target_rows,

time: 143 us -> 138 us (0.965)
  starting transfers between devices: 33.8 us -> 31.4 us
  waiting for transfers between devices: 74.7 us -> 72.5 us
    ppermute x22, waiting for transfers between devices: 68.5 us -> 66.3 us  [swap(): return lax.ppermute(value, 'expert', pairs)]
    all_to_all x1, starting transfers between devices: 5.17 us -> 3.51 us  [per_device(): lax.all_to_all(local, 'expert', split_axis=0, concat_axis=0, tiled=True)]
  transfers between devices with their start and end apart: 23 -> 23, of which waited for: 11 -> 9; matrix products, arithmetic and copies ran while one was open for 0% -> 0% of each run, Pallas kernels for 17% -> 18%
where the time goes in v12:
time: 138 us; the launch traced here: 137 us
  waiting for transfers between devices  72.5 us (53%)
  Pallas kernels  31.5 us (23%)
  starting transfers between devices  31.4 us (23%)
    ppermute x22, waiting for transfers between devices, swap(): return lax.ppermute(value, 'expert', pairs)  66.3 us
    ppermute x22, starting transfers between devices, swap(): return lax.ppermute(value, 'expert', pairs)  27.9 us
    pallas_call x6, Pallas kernels, expert_block(): pl.pallas_call(functools.partial(expert_kernel, first), out_shape=[jax.Sh...  23.3 us
    all_to_all x1, waiting for transfers between devices, per_device(): lax.all_to_all(local, 'expert', split_axis=0, concat_axis=0, tiled=True)  6.21 us
    pallas_call x1, Pallas kernels, pack(): pl.pallas_call(pack_kernel, out_shape=[jax.ShapeDtypeStruct(shape, BF16)...  4.53 us
    all_to_all x1, starting transfers between devices, per_device(): lax.all_to_all(local, 'expert', split_axis=0, concat_axis=0, tiled=True)  3.51 us
  transfers between devices with their start and end apart: 23, of which 9 were waited for; matrix products, arithmetic and copies ran while one was open for 0% of the time, Pallas kernels for 18%

profile of v12, /device:TPU:0, one launch (start us, length us, event | category | flops | bytes accessed | tf_op | source)
XLA Modules:
  0.0 137.4 jit_solution(4668348220117485802)
XLA Ops:
  0.6 4.5 %pack.1 = (bf16[80,3584]{1,0:T(8,128)(2,1)S(1)}, bf16[80,3584]{1,0:T(8,128)(2,1)S(1)}, bf16[80,3584]{1,0:T(8,128)(2,1)S(1)}, bf16[80,3584]{1,0:T(8,128)(2,1)S(1)}, bf16[10752,512]{1,0:T(8,128)(2,1)S(1)}) custom-call(s32[1]{0:T(128)} %bitcast.own_ref, bf16[128,3584]{1,0:T(8,128)(2,1)} %tokens_ref.1, f32[3584]{0:T(1024)} %gain_hbm.1, s32[2,128]{1,0:T(2,128)} %bitcast.8, ...), custom_call_target="tpu_custom_call" | custom-call | flops 1024 | bytes 1024 | tf_op jit(solution)/shard_map/pack/pallas_call | solution.py:78
  5.7 3.7 %collective-permute-start.3 = (bf16[80,3584]{1,0:T(8,128)(2,1)S(1)}, bf16[80,3584]{1,0:T(8,128)(2,1)S(1)}, u32[]{:S(2)}, u32[]{:S(2)}) collective-permute-start(bf16[80,3584]{1,0:T(8,128)(2,1)S(1)} %get-tuple-element.122), channel_id=1, source_target_pairs={{0,8},{1,9},{2,10},{3,11},{4,12},{5,13},{6,14},{7,15},{8,0},{9,1},... | collective-permute-start | bytes 1720328 | tf_op jit(solution)/shard_map/ppermute | solution.py:25
  13.0 22.4 %collective-permute-done.3.whole_ref.near_ref = bf16[80,3584]{1,0:T(8,128)(2,1)S(1)} collective-permute-done((bf16[80,3584]{1,0:T(8,128)(2,1)S(1)}, bf16[80,3584]{1,0:T(8,128)(2,1)S(1)}, u32[]{:S(2)}, u32[]{:S(2)}) %collective-permute-start.3) | collective-permute-done | bytes 573472 | tf_op jit(solution)/shard_map/ppermute | solution.py:25
  37.0 1.6 %collective-permute-start.4 = (bf16[48,3584]{1,0:T(8,128)(2,1)S(1)}, bf16[48,3584]{1,0:T(8,128)(2,1)S(1)}, u32[]{:S(2)}, u32[]{:S(2)}) collective-permute-start(bf16[48,3584]{1,0:T(8,128)(2,1)S(1)} %get-tuple-element.133), channel_id=1, source_target_pairs={{0,2},{1,3},{2,0},{3,1},{4,6},{5,7},{6,4},{7,5},{8,10},{9,11},{10,... | collective-permute-start | bytes 1032200 | tf_op jit(solution)/shard_map/ppermute | solution.py:25
  38.6 2.4 %collective-permute-start.8 = (bf16[80,3584]{1,0:T(8,128)(2,1)S(1)}, bf16[80,3584]{1,0:T(8,128)(2,1)S(1)}, u32[]{:S(2)}, u32[]{:S(2)}) collective-permute-start(bf16[80,3584]{1,0:T(8,128)(2,1)S(1)} %get-tuple-element.153), channel_id=1, source_target_pairs={{0,12},{1,13},{2,14},{3,15},{4,8},{5,9},{6,10},{7,11},{8,4},{9,5},... | collective-permute-start | bytes 1720328 | tf_op jit(solution)/shard_map/ppermute | solution.py:25
  41.5 6.5 %collective-permute-done.4.far_ref = bf16[48,3584]{1,0:T(8,128)(2,1)S(1)} collective-permute-done((bf16[48,3584]{1,0:T(8,128)(2,1)S(1)}, bf16[48,3584]{1,0:T(8,128)(2,1)S(1)}, u32[]{:S(2)}, u32[]{:S(2)}) %collective-permute-start.4) | collective-permute-done | bytes 344096 | tf_op jit(solution)/shard_map/ppermute | solution.py:25
  48.0 3.7 %expert_block.6 = (bf16[48,3584]{1,0:T(8,128)(2,1)S(1)}, bf16[48,3584]{1,0:T(8,128)(2,1)S(1)}) custom-call(bf16[80,3584]{1,0:T(8,128)(2,1)S(1)} %collective-permute-done.3.whole_ref.near_ref, bf16[48,3584]{1,0:T(8,128)(2,1)S(1)} %collective-permute-done.4.far_ref, bf16[10752,512]{1,0:T(8,128)(2,1)S(1)} %get-tuple-element.137.refs_0_, ...), custom_call_target="tpu_custom_call" | custom-call | flops 1024 | bytes 1024 | tf_op jit(solution)/shard_map/expert_block/pallas_call | solution.py:119
  51.7 1.7 %collective-permute-start.9 = (bf16[48,3584]{1,0:T(8,128)(2,1)S(1)}, bf16[48,3584]{1,0:T(8,128)(2,1)S(1)}, u32[]{:S(2)}, u32[]{:S(2)}) collective-permute-start(bf16[48,3584]{1,0:T(8,128)(2,1)S(1)} %get-tuple-element.156), channel_id=1, source_target_pairs={{0,2},{1,3},{2,0},{3,1},{4,6},{5,7},{6,4},{7,5},{8,10},{9,11},{10,... | collective-permute-start | bytes 1032200 | tf_op jit(solution)/shard_map/ppermute | solution.py:25
  53.4 4.0 %expert_block.7 = (bf16[32,3584]{1,0:T(8,128)(2,1)S(1)}, bf16[32,3584]{1,0:T(8,128)(2,1)S(1)}) custom-call(bf16[80,3584]{1,0:T(8,128)(2,1)S(1)} %collective-permute-done.3.whole_ref.near_ref, bf16[32,3584]{1,0:T(8,128)(2,1)S(1)} %collective-permute-done.6.far_ref, bf16[10752,512]{1,0:T(8,128)(2,1)S(1)} %get-tuple-element.137.refs_0_, ...), custom_call_target="tpu_custom_call" | custom-call | flops 1024 | bytes 1024 | tf_op jit(solution)/shard_map/expert_block/pallas_call | solution.py:119
  57.9 6.6 %collective-permute-done.10.refs_3_ = bf16[32,3584]{1,0:T(8,128)(2,1)S(1)} collective-permute-done((bf16[32,3584]{1,0:T(8,128)(2,1)S(1)}, bf16[32,3584]{1,0:T(8,128)(2,1)S(1)}, u32[]{:S(2)}, u32[]{:S(2)}) %collective-permute-start.10) | collective-permute-done | bytes 229408 | tf_op jit(solution)/shard_map/ppermute | solution.py:25
  64.5 1.8 %collective-permute-start.11 = (bf16[48,3584]{1,0:T(8,128)(2,1)S(1)}, bf16[48,3584]{1,0:T(8,128)(2,1)S(1)}, u32[]{:S(2)}, u32[]{:S(2)}) collective-permute-start(bf16[48,3584]{1,0:T(8,128)(2,1)S(1)} %get-tuple-element.178), channel_id=1, source_target_pairs={{0,2},{1,3},{2,0},{3,1},{4,6},{5,7},{6,4},{7,5},{8,10},{9,11},{10,... | collective-permute-start | bytes 1032200 | tf_op jit(solution)/shard_map/ppermute | solution.py:25
  68.2 3.8 %expert_block.8 = (bf16[80,3584]{1,0:T(8,128)(2,1)S(1)}, bf16[80,3584]{1,0:T(8,128)(2,1)S(1)}) custom-call(bf16[80,3584]{1,0:T(8,128)(2,1)S(1)} %collective-permute-done.near_ref, bf16[80,3584]{1,0:T(8,128)(2,1)S(1)} %collective-permute-done.7.far_ref, bf16[10752,512]{1,0:T(8,128)(2,1)S(1)} %get-tuple-element.137.refs_0_, ...), custom_call_target="tpu_custom_call" | custom-call | flops 1024 | bytes 1024 | tf_op jit(solution)/shard_map/expert_block/pallas_call | solution.py:119
  72.0 2.5 %collective-permute-start.19 = (bf16[80,3584]{1,0:T(8,128)(2,1)S(1)}, bf16[80,3584]{1,0:T(8,128)(2,1)S(1)}, u32[]{:S(2)}, u32[]{:S(2)}) collective-permute-start(bf16[80,3584]{1,0:T(8,128)(2,1)S(1)} %get-tuple-element.220), channel_id=1, source_target_pairs={{0,4},{1,5},{2,6},{3,7},{4,0},{5,1},{6,2},{7,3},{8,12},{9,13},{10,... | collective-permute-start | bytes 1720328 | tf_op jit(solution)/shard_map/ppermute | solution.py:25
  74.5 3.9 %expert_block.9 = (bf16[48,3584]{1,0:T(8,128)(2,1)S(1)}, bf16[48,3584]{1,0:T(8,128)(2,1)S(1)}) custom-call(bf16[80,3584]{1,0:T(8,128)(2,1)S(1)} %collective-permute-done.8.whole_ref.near_ref, bf16[48,3584]{1,0:T(8,128)(2,1)S(1)} %collective-permute-done.11.far_ref, bf16[10752,512]{1,0:T(8,128)(2,1)S(1)} %get-tuple-element.137.refs_0_, ...), custom_call_target="tpu_custom_call" | custom-call | flops 1024 | bytes 1024 | tf_op jit(solution)/shard_map/expert_block/pallas_call | solution.py:119
  79.9 4.0 %expert_block.10 = (bf16[32,3584]{1,0:T(8,128)(2,1)S(1)}, bf16[32,3584]{1,0:T(8,128)(2,1)S(1)}) custom-call(bf16[80,3584]{1,0:T(8,128)(2,1)S(1)} %collective-permute-done.8.whole_ref.near_ref, bf16[32,3584]{1,0:T(8,128)(2,1)S(1)} %collective-permute-done.12.far_ref, bf16[10752,512]{1,0:T(8,128)(2,1)S(1)} %get-tuple-element.137.refs_0_, ...), custom_call_target="tpu_custom_call" | custom-call | flops 1024 | bytes 1024 | tf_op jit(solution)/shard_map/expert_block/pallas_call | solution.py:119
  84.6 3.8 %expert_block.11 = (bf16[80,3584]{1,0:T(8,128)(2,1)S(1)}, bf16[80,3584]{1,0:T(8,128)(2,1)S(1)}) custom-call(bf16[80,3584]{1,0:T(8,128)(2,1)S(1)} %get-tuple-element.199.near_ref, bf16[80,3584]{1,0:T(8,128)(2,1)S(1)} %collective-permute-done.2.far_ref, bf16[10752,512]{1,0:T(8,128)(2,1)S(1)} %get-tuple-element.137.refs_0_, ...), custom_call_target="tpu_custom_call" | custom-call | flops 1024 | bytes 1024 | tf_op jit(solution)/shard_map/expert_block/pallas_call | solution.py:119
  88.5 5.3 %collective-permute-done.15.refs_2_ = bf16[80,3584]{1,0:T(8,128)(2,1)S(1)} collective-permute-done((bf16[80,3584]{1,0:T(8,128)(2,1)S(1)}, bf16[80,3584]{1,0:T(8,128)(2,1)S(1)}, u32[]{:S(2)}, u32[]{:S(2)}) %collective-permute-start.15) | collective-permute-done | bytes 573472 | tf_op jit(solution)/shard_map/ppermute | solution.py:25
  94.1 1.8 %collective-permute-start.18 = (bf16[80,3584]{1,0:T(8,128)(2,1)S(1)}, bf16[80,3584]{1,0:T(8,128)(2,1)S(1)}, u32[]{:S(2)}, u32[]{:S(2)}) collective-permute-start(bf16[80,3584]{1,0:T(8,128)(2,1)S(1)} %total.5), channel_id=1, source_target_pairs={{0,12},{1,13},{2,14},{3,15},{4,8},{5,9},{6,10},{7,11},{8,4},{9,5},... | collective-permute-start | bytes 1720328 | tf_op jit(solution)/shard_map/ppermute | solution.py:25
  97.5 14.5 %collective-permute-done.19.whole_ref = bf16[80,3584]{1,0:T(8,128)(2,1)S(1)} collective-permute-done((bf16[80,3584]{1,0:T(8,128)(2,1)S(1)}, bf16[80,3584]{1,0:T(8,128)(2,1)S(1)}, u32[]{:S(2)}, u32[]{:S(2)}) %collective-permute-start.19) | collective-permute-done | bytes 573472 | tf_op jit(solution)/shard_map/ppermute | solution.py:25
  112.1 2.0 %collective-permute-start.21 = (bf16[16,3584]{1,0:T(8,128)(2,1)S(1)}, bf16[16,3584]{1,0:T(8,128)(2,1)S(1)}, u32[]{:S(2)}, u32[]{:S(2)}) collective-permute-start(bf16[16,3584]{1,0:T(8,128)(2,1)S(1)} %get-tuple-element.229), channel_id=1, source_target_pairs={{0,2},{1,3},{2,0},{3,1},{4,6},{5,7},{6,4},{7,5},{8,10},{9,11},{10,... | collective-permute-start | bytes 344072 | tf_op jit(solution)/shard_map/ppermute | solution.py:25
  114.4 9.4 %collective-permute-done.16.refs_0_ = bf16[80,3584]{1,0:T(8,128)(2,1)S(1)} collective-permute-done((bf16[80,3584]{1,0:T(8,128)(2,1)S(1)}, bf16[80,3584]{1,0:T(8,128)(2,1)S(1)}, u32[]{:S(2)}, u32[]{:S(2)}) %collective-permute-start.16) | collective-permute-done | bytes 573472 | tf_op jit(solution)/shard_map/ppermute | solution.py:25
  124.2 2.5 %score.1 = f32[16,16]{1,0:T(8,128)} custom-call(s32[1]{0:T(128)} %bitcast.own_ref, bf16[128,3584]{1,0:T(8,128)(2,1)S(1)} %copy-done, f32[3584]{0:T(1024)S(1)} %copy-done.2, s32[2,128]{1,0:T(2,128)S(1)} %bitcast.9, f32[2,128]{1,0:T(2,128)S(1)} %bitcast.10, bf16[128,3584]{1,0:T(8,128)(2,1)S(1)} %copy-done.1, f32[1,128]{1,0:T(1,128)S(1)} %bitcast.11, ...), custom_call_target="tpu_custom_call" | custom-call | flops 1024 | bytes 1024 | tf_op jit(solution)/shard_map/score/pallas_call | solution.py:182
  126.7 3.5 %all-to-all-start = ((f32[16,1,16]{2,1,0:T(1,128)}), f32[16,1,16]{2,1,0:T(1,128)S(1)}, u32[]{:S(2)}, u32[]{:S(2)}) async-start(f32[16,1,16]{2,1,0:T(1,128)} %bitcast.6), calls=%async_computation | async-start | bytes 16384 | tf_op jit(solution)/shard_map/all_to_all | solution.py:378
  130.4 6.2 %all-to-all-done = f32[16,1,16]{2,1,0:T(1,128)S(1)} async-done(((f32[16,1,16]{2,1,0:T(1,128)}), f32[16,1,16]{2,1,0:T(1,128)S(1)}, u32[]{:S(2)}, u32[]{:S(2)}) %all-to-all-start) | async-done | bytes 1056 | tf_op jit(solution)/shard_map/all_to_all | solution.py:378
  (61 shorter events, 14.4 us)
Async XLA Ops:
  5.2 42.8 %collective-permute-start.5 = (bf16[10752,512]{1,0:T(8,128)(2,1)S(1)}, bf16[10752,512]{1,0:T(8,128)(2,1)S(1)}, u32[]{:S(2)}, u32[]{:S(2)}) collective-permute-start(bf16[10752,512]{1,0:T(8,128)(2,1)S(1)} %get-tuple-element.137.refs_0_), channel_id=1, source_target_pairs={{0,1},{1,0},{2,3},{3,2},{4,5},{5,4},{6,7},{7,6},{8,9},{9,8},{10,11... | collective-permute-start | bytes 33030152 | tf_op jit(solution)/shard_map/ppermute | solution.py:25
  5.7 29.6 %collective-permute-start.3 = (bf16[80,3584]{1,0:T(8,128)(2,1)S(1)}, bf16[80,3584]{1,0:T(8,128)(2,1)S(1)}, u32[]{:S(2)}, u32[]{:S(2)}) collective-permute-start(bf16[80,3584]{1,0:T(8,128)(2,1)S(1)} %get-tuple-element.122), channel_id=1, source_target_pairs={{0,8},{1,9},{2,10},{3,11},{4,12},{5,13},{6,14},{7,15},{8,0},{9,1},... | collective-permute-start | bytes 1720328 | tf_op jit(solution)/shard_map/ppermute | solution.py:25
  9.4 26.0 %collective-permute-start.2 = (bf16[80,3584]{1,0:T(8,128)(2,1)S(1)}, bf16[80,3584]{1,0:T(8,128)(2,1)S(1)}, u32[]{:S(2)}, u32[]{:S(2)}) collective-permute-start(bf16[80,3584]{1,0:T(8,128)(2,1)S(1)} %get-tuple-element.199.near_ref), channel_id=1, source_target_pairs={{0,2},{1,3},{2,0},{3,1},{4,6},{5,7},{6,4},{7,5},{8,10},{9,11},{10,... | collective-permute-start | bytes 1720328 | tf_op jit(solution)/shard_map/ppermute | solution.py:25
  10.9 25.8 %collective-permute-start.1 = (bf16[80,3584]{1,0:T(8,128)(2,1)S(1)}, bf16[80,3584]{1,0:T(8,128)(2,1)S(1)}, u32[]{:S(2)}, u32[]{:S(2)}) collective-permute-start(bf16[80,3584]{1,0:T(8,128)(2,1)S(1)} %get-tuple-element.119), channel_id=1, source_target_pairs={{0,2},{1,3},{2,0},{3,1},{4,6},{5,7},{6,4},{7,5},{8,10},{9,11},{10,... | collective-permute-start | bytes 1720328 | tf_op jit(solution)/shard_map/ppermute | solution.py:25
  11.4 25.6 %collective-permute-start = (bf16[80,3584]{1,0:T(8,128)(2,1)S(1)}, bf16[80,3584]{1,0:T(8,128)(2,1)S(1)}, u32[]{:S(2)}, u32[]{:S(2)}) collective-permute-start(bf16[80,3584]{1,0:T(8,128)(2,1)S(1)} %get-tuple-element.119), channel_id=1, source_target_pairs={{0,4},{1,5},{2,6},{3,7},{4,0},{5,1},{6,2},{7,3},{8,12},{9,13},{10,... | collective-permute-start | bytes 1720328 | tf_op jit(solution)/shard_map/ppermute | solution.py:25
  37.0 11.0 %collective-permute-start.4 = (bf16[48,3584]{1,0:T(8,128)(2,1)S(1)}, bf16[48,3584]{1,0:T(8,128)(2,1)S(1)}, u32[]{:S(2)}, u32[]{:S(2)}) collective-permute-start(bf16[48,3584]{1,0:T(8,128)(2,1)S(1)} %get-tuple-element.133), channel_id=1, source_target_pairs={{0,2},{1,3},{2,0},{3,1},{4,6},{5,7},{6,4},{7,5},{8,10},{9,11},{10,... | collective-permute-start | bytes 1032200 | tf_op jit(solution)/shard_map/ppermute | solution.py:25
  38.6 19.3 %collective-permute-start.8 = (bf16[80,3584]{1,0:T(8,128)(2,1)S(1)}, bf16[80,3584]{1,0:T(8,128)(2,1)S(1)}, u32[]{:S(2)}, u32[]{:S(2)}) collective-permute-start(bf16[80,3584]{1,0:T(8,128)(2,1)S(1)} %get-tuple-element.153), channel_id=1, source_target_pairs={{0,12},{1,13},{2,14},{3,15},{4,8},{5,9},{6,10},{7,11},{8,4},{9,5},... | collective-permute-start | bytes 1720328 | tf_op jit(solution)/shard_map/ppermute | solution.py:25
  41.0 12.4 %collective-permute-start.6 = (bf16[32,3584]{1,0:T(8,128)(2,1)S(1)}, bf16[32,3584]{1,0:T(8,128)(2,1)S(1)}, u32[]{:S(2)}, u32[]{:S(2)}) collective-permute-start(bf16[32,3584]{1,0:T(8,128)(2,1)S(1)} %get-tuple-element.142), channel_id=1, source_target_pairs={{0,2},{1,3},{2,0},{3,1},{4,6},{5,7},{6,4},{7,5},{8,10},{9,11},{10,... | collective-permute-start | bytes 688136 | tf_op jit(solution)/shard_map/ppermute | solution.py:25
  41.5 24.8 %collective-permute-start.7 = (bf16[80,3584]{1,0:T(8,128)(2,1)S(1)}, bf16[80,3584]{1,0:T(8,128)(2,1)S(1)}, u32[]{:S(2)}, u32[]{:S(2)}) collective-permute-start(bf16[80,3584]{1,0:T(8,128)(2,1)S(1)} %collective-permute-done.1), channel_id=1, source_target_pairs={{0,4},{1,5},{2,6},{3,7},{4,0},{5,1},{6,2},{7,3},{8,12},{9,13},{10,... | collective-permute-start | bytes 1720328 | tf_op jit(solution)/shard_map/ppermute | solution.py:25
  51.7 12.8 %collective-permute-start.9 = (bf16[48,3584]{1,0:T(8,128)(2,1)S(1)}, bf16[48,3584]{1,0:T(8,128)(2,1)S(1)}, u32[]{:S(2)}, u32[]{:S(2)}) collective-permute-start(bf16[48,3584]{1,0:T(8,128)(2,1)S(1)} %get-tuple-element.156), channel_id=1, source_target_pairs={{0,2},{1,3},{2,0},{3,1},{4,6},{5,7},{6,4},{7,5},{8,10},{9,11},{10,... | collective-permute-start | bytes 1032200 | tf_op jit(solution)/shard_map/ppermute | solution.py:25
  57.4 7.1 %collective-permute-start.10 = (bf16[32,3584]{1,0:T(8,128)(2,1)S(1)}, bf16[32,3584]{1,0:T(8,128)(2,1)S(1)}, u32[]{:S(2)}, u32[]{:S(2)}) collective-permute-start(bf16[32,3584]{1,0:T(8,128)(2,1)S(1)} %get-tuple-element.157), channel_id=1, source_target_pairs={{0,2},{1,3},{2,0},{3,1},{4,6},{5,7},{6,4},{7,5},{8,10},{9,11},{10,... | collective-permute-start | bytes 688136 | tf_op jit(solution)/shard_map/ppermute | solution.py:25
  64.5 10.0 %collective-permute-start.11 = (bf16[48,3584]{1,0:T(8,128)(2,1)S(1)}, bf16[48,3584]{1,0:T(8,128)(2,1)S(1)}, u32[]{:S(2)}, u32[]{:S(2)}) collective-permute-start(bf16[48,3584]{1,0:T(8,128)(2,1)S(1)} %get-tuple-element.178), channel_id=1, source_target_pairs={{0,2},{1,3},{2,0},{3,1},{4,6},{5,7},{6,4},{7,5},{8,10},{9,11},{10,... | collective-permute-start | bytes 1032200 | tf_op jit(solution)/shard_map/ppermute | solution.py:25
  66.6 27.2 %collective-permute-start.15 = (bf16[80,3584]{1,0:T(8,128)(2,1)S(1)}, bf16[80,3584]{1,0:T(8,128)(2,1)S(1)}, u32[]{:S(2)}, u32[]{:S(2)}) collective-permute-start(bf16[80,3584]{1,0:T(8,128)(2,1)S(1)} %total.4), channel_id=1, source_target_pairs={{0,8},{1,9},{2,10},{3,11},{4,12},{5,13},{6,14},{7,15},{8,0},{9,1},... | collective-permute-start | bytes 1720328 | tf_op jit(solution)/shard_map/ppermute | solution.py:25
  67.2 12.7 %collective-permute-start.12 = (bf16[32,3584]{1,0:T(8,128)(2,1)S(1)}, bf16[32,3584]{1,0:T(8,128)(2,1)S(1)}, u32[]{:S(2)}, u32[]{:S(2)}) collective-permute-start(bf16[32,3584]{1,0:T(8,128)(2,1)S(1)} %get-tuple-element.187), channel_id=1, source_target_pairs={{0,2},{1,3},{2,0},{3,1},{4,6},{5,7},{6,4},{7,5},{8,10},{9,11},{10,... | collective-permute-start | bytes 688136 | tf_op jit(solution)/shard_map/ppermute | solution.py:25
  72.0 39.9 %collective-permute-start.19 = (bf16[80,3584]{1,0:T(8,128)(2,1)S(1)}, bf16[80,3584]{1,0:T(8,128)(2,1)S(1)}, u32[]{:S(2)}, u32[]{:S(2)}) collective-permute-start(bf16[80,3584]{1,0:T(8,128)(2,1)S(1)} %get-tuple-element.220), channel_id=1, source_target_pairs={{0,4},{1,5},{2,6},{3,7},{4,0},{5,1},{6,2},{7,3},{8,12},{9,13},{10,... | collective-permute-start | bytes 1720328 | tf_op jit(solution)/shard_map/ppermute | solution.py:25
  78.4 15.4 %collective-permute-start.13 = (bf16[48,3584]{1,0:T(8,128)(2,1)S(1)}, bf16[48,3584]{1,0:T(8,128)(2,1)S(1)}, u32[]{:S(2)}, u32[]{:S(2)}) collective-permute-start(bf16[48,3584]{1,0:T(8,128)(2,1)S(1)} %get-tuple-element.195), channel_id=1, source_target_pairs={{0,2},{1,3},{2,0},{3,1},{4,6},{5,7},{6,4},{7,5},{8,10},{9,11},{10,... | collective-permute-start | bytes 1032200 | tf_op jit(solution)/shard_map/ppermute | solution.py:25
  83.9 9.9 %collective-permute-start.14 = (bf16[32,3584]{1,0:T(8,128)(2,1)S(1)}, bf16[32,3584]{1,0:T(8,128)(2,1)S(1)}, u32[]{:S(2)}, u32[]{:S(2)}) collective-permute-start(bf16[32,3584]{1,0:T(8,128)(2,1)S(1)} %get-tuple-element.196), channel_id=1, source_target_pairs={{0,2},{1,3},{2,0},{3,1},{4,6},{5,7},{6,4},{7,5},{8,10},{9,11},{10,... | collective-permute-start | bytes 688136 | tf_op jit(solution)/shard_map/ppermute | solution.py:25
  88.4 35.7 %copy-start = (bf16[128,3584]{1,0:T(8,128)(2,1)S(1)}, bf16[128,3584]{1,0:T(8,128)(2,1)}, u32[]{:S(2)}) copy-start(bf16[128,3584]{1,0:T(8,128)(2,1)} %tokens_ref.1) | copy-start | bytes 2752516
  94.1 20.0 %collective-permute-start.18 = (bf16[80,3584]{1,0:T(8,128)(2,1)S(1)}, bf16[80,3584]{1,0:T(8,128)(2,1)S(1)}, u32[]{:S(2)}, u32[]{:S(2)}) collective-permute-start(bf16[80,3584]{1,0:T(8,128)(2,1)S(1)} %total.5), channel_id=1, source_target_pairs={{0,12},{1,13},{2,14},{3,15},{4,8},{5,9},{6,10},{7,11},{8,4},{9,5},... | collective-permute-start | bytes 1720328 | tf_op jit(solution)/shard_map/ppermute | solution.py:25
  96.0 18.2 %collective-permute-start.17 = (bf16[80,3584]{1,0:T(8,128)(2,1)S(1)}, bf16[80,3584]{1,0:T(8,128)(2,1)S(1)}, u32[]{:S(2)}, u32[]{:S(2)}) collective-permute-start(bf16[80,3584]{1,0:T(8,128)(2,1)S(1)} %get-tuple-element.212), channel_id=1, source_target_pairs={{0,2},{1,3},{2,0},{3,1},{4,6},{5,7},{6,4},{7,5},{8,10},{9,11},{10,... | collective-permute-start | bytes 1720328 | tf_op jit(solution)/shard_map/ppermute | solution.py:25
  97.5 26.3 %collective-permute-start.16 = (bf16[80,3584]{1,0:T(8,128)(2,1)S(1)}, bf16[80,3584]{1,0:T(8,128)(2,1)S(1)}, u32[]{:S(2)}, u32[]{:S(2)}) collective-permute-start(bf16[80,3584]{1,0:T(8,128)(2,1)S(1)} %get-tuple-element.210), channel_id=1, source_target_pairs={{0,4},{1,5},{2,6},{3,7},{4,0},{5,1},{6,2},{7,3},{8,12},{9,13},{10,... | collective-permute-start | bytes 1720328 | tf_op jit(solution)/shard_map/ppermute | solution.py:25
  112.0 11.8 %collective-permute-start.20 = (bf16[64,3584]{1,0:T(8,128)(2,1)S(1)}, bf16[64,3584]{1,0:T(8,128)(2,1)S(1)}, u32[]{:S(2)}, u32[]{:S(2)}) collective-permute-start(bf16[64,3584]{1,0:T(8,128)(2,1)S(1)} %get-tuple-element.227), channel_id=1, source_target_pairs={{0,2},{1,3},{2,0},{3,1},{4,6},{5,7},{6,4},{7,5},{8,10},{9,11},{10,... | collective-permute-start | bytes 1376264 | tf_op jit(solution)/shard_map/ppermute | solution.py:25
  112.1 11.7 %collective-permute-start.21 = (bf16[16,3584]{1,0:T(8,128)(2,1)S(1)}, bf16[16,3584]{1,0:T(8,128)(2,1)S(1)}, u32[]{:S(2)}, u32[]{:S(2)}) collective-permute-start(bf16[16,3584]{1,0:T(8,128)(2,1)S(1)} %get-tuple-element.229), channel_id=1, source_target_pairs={{0,2},{1,3},{2,0},{3,1},{4,6},{5,7},{6,4},{7,5},{8,10},{9,11},{10,... | collective-permute-start | bytes 344072 | tf_op jit(solution)/shard_map/ppermute | solution.py:25
  126.7 9.9 %all-to-all-start = ((f32[16,1,16]{2,1,0:T(1,128)}), f32[16,1,16]{2,1,0:T(1,128)S(1)}, u32[]{:S(2)}, u32[]{:S(2)}) async-start(f32[16,1,16]{2,1,0:T(1,128)} %bitcast.6), calls=%async_computation | async-start | bytes 16384 | tf_op jit(solution)/shard_map/all_to_all | solution.py:378
  (8 other events, 232.8 us)

commit v13 on v12

--- a/solution.py
+++ b/solution.py
@@ -93,7 +93,8 @@
 
 
 def expert_kernel(first, near_ref, far_ref, *refs):
-    *weight_refs, mine_ref, theirs_ref, rows = refs
+    *refs, rows = refs
+    weight_refs, out_refs = refs[:2], refs[2:]
     count = far_ref.shape[0]
     rows[:count, :] = near_ref[first : first + count, :]
     rows[count:, :] = far_ref[...]
@@ -109,18 +110,21 @@
             jnp.dot(value, ref[pl.ds(2 * width + start, size), :], preferred_element_type=F32)
             for value, ref in zip(hidden, weight_refs)
         ).astype(BF16)
-        mine_ref[:, start : start + size] = part[:count]
-        theirs_ref[:, start : start + size] = part[count:]
-
-
-def expert_block(near, first, far, weights):
+        done = 0
+        for ref in out_refs:
+            ref[:, start : start + size] = part[done : done + ref.shape[0]]
+            done += ref.shape[0]
+
+
+def expert_block(near, first, far, weights, joined=False):
     count, width = far.shape
+    outs = [2 * count] if joined else [count, count]
     vmem = pl.BlockSpec(memory_space=pltpu.VMEM)
     return pl.pallas_call(
         functools.partial(expert_kernel, first),
-        out_shape=[jax.ShapeDtypeStruct((count, width), BF16)] * 2,
+        out_shape=[jax.ShapeDtypeStruct((rows, width), BF16) for rows in outs],
         in_specs=[vmem] * (2 + len(weights)),
-        out_specs=[vmem] * 2,
+        out_specs=[vmem] * len(outs),
         scratch_shapes=[pltpu.VMEM((2 * count, width), BF16)],
         compiler_params=pltpu.CompilerParams(vmem_limit_bytes=VMEM_LIMIT),
         cost_estimate=COST,
@@ -209,17 +213,15 @@
         return lax.optimization_barrier((value, self.token))[0]
 
 
-def cut_kernel(whole_ref, *refs):
-    first = 0
-    for ref in refs:
-        ref[...] = whole_ref[first : first + ref.shape[0], :]
-        first += ref.shape[0]
+def cut_kernel(pieces, whole_ref, *refs):
+    for (first, count), ref in zip(pieces, refs):
+        ref[...] = whole_ref[first : first + count, :]
 
 
 def cut(whole, pieces):
     vmem = pl.BlockSpec(memory_space=pltpu.VMEM)
     return pl.pallas_call(
-        cut_kernel,
+        functools.partial(cut_kernel, tuple(pieces)),
         out_shape=[jax.ShapeDtypeStruct((count, whole.shape[1]), BF16) for _, count in pieces],
         in_specs=[vmem],
         out_specs=[vmem] * len(pieces),
@@ -231,19 +233,20 @@
 
 def total_kernel(count, *refs):
     *refs, out_ref = refs
-    for side in (refs[:count], refs[count:]):
+    for n, side in enumerate((refs[:count], refs[count:])):
         first = 0
         for ref in side:
-            rows = slice(first, first + ref.shape[0])
-            if side[0] is refs[0]:
-                out_ref[rows, :] = ref[...]
-            else:
-                out_ref[rows, :] = (out_ref[rows, :].astype(F32) + ref[...].astype(F32)).astype(BF16)
-            first += ref.shape[0]
+            rows = min(ref.shape[0], out_ref.shape[0] - first)
+            there = slice(first, first + rows)
+            value = ref[:rows, :]
+            if n:
+                value = (out_ref[there, :].astype(F32) + value.astype(F32)).astype(BF16)
+            out_ref[there, :] = value
+            first += rows
 
 
 def total(ours, others):
-    rows = sum(piece.shape[0] for piece in ours)
+    rows = sum(piece.shape[0] for piece in others)
     vmem = pl.BlockSpec(memory_space=pltpu.VMEM)
     return pl.pallas_call(
         functools.partial(total_kernel, len(ours)),
@@ -325,7 +328,6 @@
     far[0] = order.mark_one(far[0])
     far[1] = order.mark_one(far[1])
     arrive(1)
-    last = (capacity - 16, 16)
     for k in range(3, experts + 1):
         if k > 3:
             near[k - 1], *theirs[k - 2] = lax.optimization_barrier((near[k - 1], *theirs[k - 2]))
@@ -335,14 +337,12 @@
         if k == 3:
             far[1] = swap(order.late(far[1]), spread)
         if k > 3:
-            if k == experts:
-                far[1], *theirs[k - 2] = lax.optimization_barrier((far[1], *theirs[k - 2]))
             home(k - 2)
             leave_back(k - 2)
-        if k == experts:
-            work_whole(1)
-            theirs[1] = swap(theirs[1], spread)
         work(k - 1)
+        if k == 3:
+            (joined,) = order.mark(*expert_block(order.late(near[1]), 0, order.late(far[1]), weights, joined=True))
+            mine[1] = [swap(joined, spread)]
         if k == experts:
             work_whole(0)
         if k < experts:
@@ -352,13 +352,14 @@
     home(experts - 1)
     leave_back(experts - 1)
     mine[0], theirs[0] = [mine[0]], [swap(order.late(theirs[0]), side)]
-    mine[1] = [swap(order.late(mine[1]), spread)]
-    theirs[1] = order.mark(*cut(order.mark_one(theirs[1]), [(0, last[0]), last]))
+    mine[1] = order.mark(*mine[1])
+    thirds = [(first, min(32, 2 * capacity - first)) for first in range(capacity, 2 * capacity, 32)]
+    theirs[1] = order.mark(*cut(mine[1][0], thirds))
     theirs[1] = [swap(order.late(piece), side) for piece in theirs[1]]
     order = Order(own)
     arrive_back(experts - 1)
     theirs[0] = order.mark(*theirs[0])
-    mine[1] = order.mark(*mine[1])
+    theirs[1] = order.mark(*theirs[1])
     own = order.token
     back[0], back[1] = total(mine[0], theirs[0]), total(mine[1], theirs[1])
     blocks = [back[k] for k in range(experts)]

time: 138 us -> 142 us (1.029)
  waiting for transfers between devices: 72.5 us -> 78.9 us
    ppermute x22, waiting for transfers between devices: 66.3 us -> 72.7 us  [swap(): return lax.ppermute(value, 'expert', pairs)]
    ppermute x22, starting transfers between devices: 27.9 us -> 26.1 us  [swap(): return lax.ppermute(value, 'expert', pairs)]
  transfers between devices with their start and end apart: 23 -> 23, of which waited for: 9 -> 11; matrix products, arithmetic and copies ran while one was open for 0% -> 0% of each run, Pallas kernels for 18% -> 17%
where the time goes in v13:
time: 142 us
  waiting for transfers between devices  78.9 us (56%)
  Pallas kernels  31.5 us (22%)
  starting transfers between devices  30 us (21%)
    ppermute x22, waiting for transfers between devices, swap(): return lax.ppermute(value, 'expert', pairs)  72.7 us
    ppermute x22, starting transfers between devices, swap(): return lax.ppermute(value, 'expert', pairs)  26.1 us
    pallas_call x6, Pallas kernels, expert_block(): pl.pallas_call(functools.partial(expert_kernel, first), out_shape=[jax.Sh...  23.2 us
    all_to_all x1, waiting for transfers between devices, per_device(): lax.all_to_all(local, 'expert', split_axis=0, concat_axis=0, tiled=True)  6.2 us
    pallas_call x1, Pallas kernels, pack(): pl.pallas_call(pack_kernel, out_shape=[jax.ShapeDtypeStruct(shape, BF16)...  4.53 us
    all_to_all x1, starting transfers between devices, per_device(): lax.all_to_all(local, 'expert', split_axis=0, concat_axis=0, tiled=True)  3.87 us
  transfers between devices with their start and end apart: 23, of which 11 were waited for; matrix products, arithmetic and copies ran while one was open for 0% of the time, Pallas kernels for 17%

profile of v13, /device:TPU:0, one launch (start us, length us, event | category | flops | bytes accessed | tf_op | source)
XLA Modules:
  0.0 142.3 jit_solution(12811233888087640485)
XLA Ops:
  0.6 4.5 %pack.1 = (bf16[80,3584]{1,0:T(8,128)(2,1)S(1)}, bf16[80,3584]{1,0:T(8,128)(2,1)S(1)}, bf16[80,3584]{1,0:T(8,128)(2,1)S(1)}, bf16[80,3584]{1,0:T(8,128)(2,1)S(1)}, bf16[10752,512]{1,0:T(8,128)(2,1)S(1)}) custom-call(s32[1]{0:T(128)} %bitcast.own_ref, bf16[128,3584]{1,0:T(8,128)(2,1)} %tokens_ref.1, f32[3584]{0:T(1024)} %gain_hbm.1, s32[2,128]{1,0:T(2,128)} %bitcast.8, ...), custom_call_target="tpu_custom_call" | custom-call | flops 1024 | bytes 1024 | tf_op jit(solution)/shard_map/pack/pallas_call | solution.py:78
  5.7 3.7 %collective-permute-start.3 = (bf16[80,3584]{1,0:T(8,128)(2,1)S(1)}, bf16[80,3584]{1,0:T(8,128)(2,1)S(1)}, u32[]{:S(2)}, u32[]{:S(2)}) collective-permute-start(bf16[80,3584]{1,0:T(8,128)(2,1)S(1)} %get-tuple-element.120), channel_id=1, source_target_pairs={{0,8},{1,9},{2,10},{3,11},{4,12},{5,13},{6,14},{7,15},{8,0},{9,1},... | collective-permute-start | bytes 1720328 | tf_op jit(solution)/shard_map/ppermute | solution.py:25
  13.0 22.4 %collective-permute-done.3.whole_ref.near_ref = bf16[80,3584]{1,0:T(8,128)(2,1)S(1)} collective-permute-done((bf16[80,3584]{1,0:T(8,128)(2,1)S(1)}, bf16[80,3584]{1,0:T(8,128)(2,1)S(1)}, u32[]{:S(2)}, u32[]{:S(2)}) %collective-permute-start.3) | collective-permute-done | bytes 573472 | tf_op jit(solution)/shard_map/ppermute | solution.py:25
  37.0 1.6 %collective-permute-start.5 = (bf16[48,3584]{1,0:T(8,128)(2,1)S(1)}, bf16[48,3584]{1,0:T(8,128)(2,1)S(1)}, u32[]{:S(2)}, u32[]{:S(2)}) collective-permute-start(bf16[48,3584]{1,0:T(8,128)(2,1)S(1)} %get-tuple-element.133), channel_id=1, source_target_pairs={{0,2},{1,3},{2,0},{3,1},{4,6},{5,7},{6,4},{7,5},{8,10},{9,11},{10,... | collective-permute-start | bytes 1032200 | tf_op jit(solution)/shard_map/ppermute | solution.py:25
  41.5 6.5 %collective-permute-done.5.far_ref = bf16[48,3584]{1,0:T(8,128)(2,1)S(1)} collective-permute-done((bf16[48,3584]{1,0:T(8,128)(2,1)S(1)}, bf16[48,3584]{1,0:T(8,128)(2,1)S(1)}, u32[]{:S(2)}, u32[]{:S(2)}) %collective-permute-start.5) | collective-permute-done | bytes 344096 | tf_op jit(solution)/shard_map/ppermute | solution.py:25
  48.0 3.7 %expert_block.6 = (bf16[48,3584]{1,0:T(8,128)(2,1)S(1)}, bf16[48,3584]{1,0:T(8,128)(2,1)S(1)}) custom-call(bf16[80,3584]{1,0:T(8,128)(2,1)S(1)} %collective-permute-done.3.whole_ref.near_ref, bf16[48,3584]{1,0:T(8,128)(2,1)S(1)} %collective-permute-done.5.far_ref, bf16[10752,512]{1,0:T(8,128)(2,1)S(1)} %get-tuple-element.137.refs_0_, ...), custom_call_target="tpu_custom_call" | custom-call | flops 1024 | bytes 1024 | tf_op jit(solution)/shard_map/expert_block/pallas_call | solution.py:123
  51.7 1.7 %collective-permute-start.10 = (bf16[48,3584]{1,0:T(8,128)(2,1)S(1)}, bf16[48,3584]{1,0:T(8,128)(2,1)S(1)}, u32[]{:S(2)}, u32[]{:S(2)}) collective-permute-start(bf16[48,3584]{1,0:T(8,128)(2,1)S(1)} %get-tuple-element.156), channel_id=1, source_target_pairs={{0,2},{1,3},{2,0},{3,1},{4,6},{5,7},{6,4},{7,5},{8,10},{9,11},{10,... | collective-permute-start | bytes 1032200 | tf_op jit(solution)/shard_map/ppermute | solution.py:25
  53.4 4.0 %expert_block.7 = (bf16[32,3584]{1,0:T(8,128)(2,1)S(1)}, bf16[32,3584]{1,0:T(8,128)(2,1)S(1)}) custom-call(bf16[80,3584]{1,0:T(8,128)(2,1)S(1)} %collective-permute-done.3.whole_ref.near_ref, bf16[32,3584]{1,0:T(8,128)(2,1)S(1)} %collective-permute-done.4.far_ref, bf16[10752,512]{1,0:T(8,128)(2,1)S(1)} %get-tuple-element.137.refs_0_, ...), custom_call_target="tpu_custom_call" | custom-call | flops 1024 | bytes 1024 | tf_op jit(solution)/shard_map/expert_block/pallas_call | solution.py:123
  57.9 3.8 %expert_block.8 = bf16[160,3584]{1,0:T(8,128)(2,1)S(1)} custom-call(bf16[80,3584]{1,0:T(8,128)(2,1)S(1)} %collective-permute-done.near_ref, bf16[80,3584]{1,0:T(8,128)(2,1)S(1)} %collective-permute-done.7.far_ref, bf16[10752,512]{1,0:T(8,128)(2,1)S(1)} %get-tuple-element.137.refs_0_, bf16[10752,512]{1,0:T(8,128)(2,1)S(1)} %collective-permute-done.6.refs_1_), custom_call_target="tpu_custom_call" | custom-call | flops 1024 | bytes 1024 | tf_op jit(solution)/shard_map/expert_block/pallas_call | solution.py:123
  63.0 4.2 %collective-permute-done.9.whole_ref.near_ref = bf16[80,3584]{1,0:T(8,128)(2,1)S(1)} collective-permute-done((bf16[80,3584]{1,0:T(8,128)(2,1)S(1)}, bf16[80,3584]{1,0:T(8,128)(2,1)S(1)}, u32[]{:S(2)}, u32[]{:S(2)}) %collective-permute-start.9) | collective-permute-done | bytes 573472 | tf_op jit(solution)/shard_map/ppermute | solution.py:25
  68.2 1.6 %collective-permute-start.13 = (bf16[32,3584]{1,0:T(8,128)(2,1)S(1)}, bf16[32,3584]{1,0:T(8,128)(2,1)S(1)}, u32[]{:S(2)}, u32[]{:S(2)}) collective-permute-start(bf16[32,3584]{1,0:T(8,128)(2,1)S(1)} %get-tuple-element.180), channel_id=1, source_target_pairs={{0,2},{1,3},{2,0},{3,1},{4,6},{5,7},{6,4},{7,5},{8,10},{9,11},{10,... | collective-permute-start | bytes 688136 | tf_op jit(solution)/shard_map/ppermute | solution.py:25
  69.8 7.2 %collective-permute-done.12.far_ref = bf16[48,3584]{1,0:T(8,128)(2,1)S(1)} collective-permute-done((bf16[48,3584]{1,0:T(8,128)(2,1)S(1)}, bf16[48,3584]{1,0:T(8,128)(2,1)S(1)}, u32[]{:S(2)}, u32[]{:S(2)}) %collective-permute-start.12) | collective-permute-done | bytes 344096 | tf_op jit(solution)/shard_map/ppermute | solution.py:25
  77.0 3.9 %expert_block.9 = (bf16[48,3584]{1,0:T(8,128)(2,1)S(1)}, bf16[48,3584]{1,0:T(8,128)(2,1)S(1)}) custom-call(bf16[80,3584]{1,0:T(8,128)(2,1)S(1)} %collective-permute-done.9.whole_ref.near_ref, bf16[48,3584]{1,0:T(8,128)(2,1)S(1)} %collective-permute-done.12.far_ref, bf16[10752,512]{1,0:T(8,128)(2,1)S(1)} %get-tuple-element.137.refs_0_, ...), custom_call_target="tpu_custom_call" | custom-call | flops 1024 | bytes 1024 | tf_op jit(solution)/shard_map/expert_block/pallas_call | solution.py:123
  81.4 4.0 %expert_block.10 = (bf16[32,3584]{1,0:T(8,128)(2,1)S(1)}, bf16[32,3584]{1,0:T(8,128)(2,1)S(1)}) custom-call(bf16[80,3584]{1,0:T(8,128)(2,1)S(1)} %collective-permute-done.9.whole_ref.near_ref, bf16[32,3584]{1,0:T(8,128)(2,1)S(1)} %collective-permute-done.13.far_ref, bf16[10752,512]{1,0:T(8,128)(2,1)S(1)} %get-tuple-element.137.refs_0_, ...), custom_call_target="tpu_custom_call" | custom-call | flops 1024 | bytes 1024 | tf_op jit(solution)/shard_map/expert_block/pallas_call | solution.py:123
  85.4 1.6 %collective-permute-start.15 = (bf16[32,3584]{1,0:T(8,128)(2,1)S(1)}, bf16[32,3584]{1,0:T(8,128)(2,1)S(1)}, u32[]{:S(2)}, u32[]{:S(2)}) collective-permute-start(bf16[32,3584]{1,0:T(8,128)(2,1)S(1)} %get-tuple-element.189), channel_id=1, source_target_pairs={{0,2},{1,3},{2,0},{3,1},{4,6},{5,7},{6,4},{7,5},{8,10},{9,11},{10,... | collective-permute-start | bytes 688136 | tf_op jit(solution)/shard_map/ppermute | solution.py:25
  87.0 3.8 %expert_block.11 = (bf16[80,3584]{1,0:T(8,128)(2,1)S(1)}, bf16[80,3584]{1,0:T(8,128)(2,1)S(1)}) custom-call(bf16[80,3584]{1,0:T(8,128)(2,1)S(1)} %get-tuple-element.192.near_ref, bf16[80,3584]{1,0:T(8,128)(2,1)S(1)} %collective-permute-done.2.far_ref, bf16[10752,512]{1,0:T(8,128)(2,1)S(1)} %get-tuple-element.137.refs_0_, ...), custom_call_target="tpu_custom_call" | custom-call | flops 1024 | bytes 1024 | tf_op jit(solution)/shard_map/expert_block/pallas_call | solution.py:123
  91.0 9.5 %collective-permute-done.16.refs_2_ = bf16[80,3584]{1,0:T(8,128)(2,1)S(1)} collective-permute-done((bf16[80,3584]{1,0:T(8,128)(2,1)S(1)}, bf16[80,3584]{1,0:T(8,128)(2,1)S(1)}, u32[]{:S(2)}, u32[]{:S(2)}) %collective-permute-start.16) | collective-permute-done | bytes 573472 | tf_op jit(solution)/shard_map/ppermute | solution.py:25
  100.7 1.8 %collective-permute-start.21 = (bf16[80,3584]{1,0:T(8,128)(2,1)S(1)}, bf16[80,3584]{1,0:T(8,128)(2,1)S(1)}, u32[]{:S(2)}, u32[]{:S(2)}) collective-permute-start(bf16[80,3584]{1,0:T(8,128)(2,1)S(1)} %total.5), channel_id=1, source_target_pairs={{0,12},{1,13},{2,14},{3,15},{4,8},{5,9},{6,10},{7,11},{8,4},{9,5},... | collective-permute-start | bytes 1720328 | tf_op jit(solution)/shard_map/ppermute | solution.py:25
  106.7 8.9 %collective-permute-done.21.refs_3_ = bf16[80,3584]{1,0:T(8,128)(2,1)S(1)} collective-permute-done((bf16[80,3584]{1,0:T(8,128)(2,1)S(1)}, bf16[80,3584]{1,0:T(8,128)(2,1)S(1)}, u32[]{:S(2)}, u32[]{:S(2)}) %collective-permute-start.21) | collective-permute-done | bytes 573472 | tf_op jit(solution)/shard_map/ppermute | solution.py:25
  115.7 2.8 %collective-permute-done.20.refs_1_ = bf16[80,3584]{1,0:T(8,128)(2,1)S(1)} collective-permute-done((bf16[80,3584]{1,0:T(8,128)(2,1)S(1)}, bf16[80,3584]{1,0:T(8,128)(2,1)S(1)}, u32[]{:S(2)}, u32[]{:S(2)}) %collective-permute-start.20) | collective-permute-done | bytes 573472 | tf_op jit(solution)/shard_map/ppermute | solution.py:25
  118.5 9.6 %collective-permute-done.19.refs_3_ = bf16[16,3584]{1,0:T(8,128)(2,1)S(1)} collective-permute-done((bf16[16,3584]{1,0:T(8,128)(2,1)S(1)}, bf16[16,3584]{1,0:T(8,128)(2,1)S(1)}, u32[]{:S(2)}, u32[]{:S(2)}) %collective-permute-start.19) | collective-permute-done | bytes 114720 | tf_op jit(solution)/shard_map/ppermute | solution.py:25
  128.7 2.5 %score.1 = f32[16,16]{1,0:T(8,128)} custom-call(s32[1]{0:T(128)} %bitcast.own_ref, bf16[128,3584]{1,0:T(8,128)(2,1)S(1)} %copy-done, f32[3584]{0:T(1024)S(1)} %copy-done.2, s32[2,128]{1,0:T(2,128)S(1)} %bitcast.9, f32[2,128]{1,0:T(2,128)S(1)} %bitcast.10, bf16[128,3584]{1,0:T(8,128)(2,1)S(1)} %copy-done.1, f32[1,128]{1,0:T(1,128)S(1)} %bitcast.11, ...), custom_call_target="tpu_custom_call" | custom-call | flops 1024 | bytes 1024 | tf_op jit(solution)/shard_map/score/pallas_call | solution.py:186
  131.3 3.9 %all-to-all-start = ((f32[16,1,16]{2,1,0:T(1,128)}), f32[16,1,16]{2,1,0:T(1,128)S(1)}, u32[]{:S(2)}, u32[]{:S(2)}) async-start(f32[16,1,16]{2,1,0:T(1,128)} %bitcast.6), calls=%async_computation | async-start | bytes 16384 | tf_op jit(solution)/shard_map/all_to_all | solution.py:379
  135.3 6.2 %all-to-all-done = f32[16,1,16]{2,1,0:T(1,128)S(1)} async-done(((f32[16,1,16]{2,1,0:T(1,128)}), f32[16,1,16]{2,1,0:T(1,128)S(1)}, u32[]{:S(2)}, u32[]{:S(2)}) %all-to-all-start) | async-done | bytes 1056 | tf_op jit(solution)/shard_map/all_to_all | solution.py:379
  (61 shorter events, 18.1 us)
Async XLA Ops:
  5.2 42.8 %collective-permute-start.6 = (bf16[10752,512]{1,0:T(8,128)(2,1)S(1)}, bf16[10752,512]{1,0:T(8,128)(2,1)S(1)}, u32[]{:S(2)}, u32[]{:S(2)}) collective-permute-start(bf16[10752,512]{1,0:T(8,128)(2,1)S(1)} %get-tuple-element.137.refs_0_), channel_id=1, source_target_pairs={{0,1},{1,0},{2,3},{3,2},{4,5},{5,4},{6,7},{7,6},{8,9},{9,8},{10,11... | collective-permute-start | bytes 33030152 | tf_op jit(solution)/shard_map/ppermute | solution.py:25
  5.7 29.6 %collective-permute-start.3 = (bf16[80,3584]{1,0:T(8,128)(2,1)S(1)}, bf16[80,3584]{1,0:T(8,128)(2,1)S(1)}, u32[]{:S(2)}, u32[]{:S(2)}) collective-permute-start(bf16[80,3584]{1,0:T(8,128)(2,1)S(1)} %get-tuple-element.120), channel_id=1, source_target_pairs={{0,8},{1,9},{2,10},{3,11},{4,12},{5,13},{6,14},{7,15},{8,0},{9,1},... | collective-permute-start | bytes 1720328 | tf_op jit(solution)/shard_map/ppermute | solution.py:25
  9.4 26.0 %collective-permute-start.2 = (bf16[80,3584]{1,0:T(8,128)(2,1)S(1)}, bf16[80,3584]{1,0:T(8,128)(2,1)S(1)}, u32[]{:S(2)}, u32[]{:S(2)}) collective-permute-start(bf16[80,3584]{1,0:T(8,128)(2,1)S(1)} %get-tuple-element.192.near_ref), channel_id=1, source_target_pairs={{0,2},{1,3},{2,0},{3,1},{4,6},{5,7},{6,4},{7,5},{8,10},{9,11},{10,... | collective-permute-start | bytes 1720328 | tf_op jit(solution)/shard_map/ppermute | solution.py:25
  10.9 25.8 %collective-permute-start.1 = (bf16[80,3584]{1,0:T(8,128)(2,1)S(1)}, bf16[80,3584]{1,0:T(8,128)(2,1)S(1)}, u32[]{:S(2)}, u32[]{:S(2)}) collective-permute-start(bf16[80,3584]{1,0:T(8,128)(2,1)S(1)} %get-tuple-element.117), channel_id=1, source_target_pairs={{0,2},{1,3},{2,0},{3,1},{4,6},{5,7},{6,4},{7,5},{8,10},{9,11},{10,... | collective-permute-start | bytes 1720328 | tf_op jit(solution)/shard_map/ppermute | solution.py:25
  11.4 25.6 %collective-permute-start = (bf16[80,3584]{1,0:T(8,128)(2,1)S(1)}, bf16[80,3584]{1,0:T(8,128)(2,1)S(1)}, u32[]{:S(2)}, u32[]{:S(2)}) collective-permute-start(bf16[80,3584]{1,0:T(8,128)(2,1)S(1)} %get-tuple-element.117), channel_id=1, source_target_pairs={{0,4},{1,5},{2,6},{3,7},{4,0},{5,1},{6,2},{7,3},{8,12},{9,13},{10,... | collective-permute-start | bytes 1720328 | tf_op jit(solution)/shard_map/ppermute | solution.py:25
  37.0 11.0 %collective-permute-start.5 = (bf16[48,3584]{1,0:T(8,128)(2,1)S(1)}, bf16[48,3584]{1,0:T(8,128)(2,1)S(1)}, u32[]{:S(2)}, u32[]{:S(2)}) collective-permute-start(bf16[48,3584]{1,0:T(8,128)(2,1)S(1)} %get-tuple-element.133), channel_id=1, source_target_pairs={{0,2},{1,3},{2,0},{3,1},{4,6},{5,7},{6,4},{7,5},{8,10},{9,11},{10,... | collective-permute-start | bytes 1032200 | tf_op jit(solution)/shard_map/ppermute | solution.py:25
  38.6 19.3 %collective-permute-start.7 = (bf16[80,3584]{1,0:T(8,128)(2,1)S(1)}, bf16[80,3584]{1,0:T(8,128)(2,1)S(1)}, u32[]{:S(2)}, u32[]{:S(2)}) collective-permute-start(bf16[80,3584]{1,0:T(8,128)(2,1)S(1)} %collective-permute-done.1), channel_id=1, source_target_pairs={{0,4},{1,5},{2,6},{3,7},{4,0},{5,1},{6,2},{7,3},{8,12},{9,13},{10,... | collective-permute-start | bytes 1720328 | tf_op jit(solution)/shard_map/ppermute | solution.py:25
  39.8 27.4 %collective-permute-start.9 = (bf16[80,3584]{1,0:T(8,128)(2,1)S(1)}, bf16[80,3584]{1,0:T(8,128)(2,1)S(1)}, u32[]{:S(2)}, u32[]{:S(2)}) collective-permute-start(bf16[80,3584]{1,0:T(8,128)(2,1)S(1)} %get-tuple-element.153), channel_id=1, source_target_pairs={{0,12},{1,13},{2,14},{3,15},{4,8},{5,9},{6,10},{7,11},{8,4},{9,5},... | collective-permute-start | bytes 1720328 | tf_op jit(solution)/shard_map/ppermute | solution.py:25
  41.0 12.4 %collective-permute-start.4 = (bf16[32,3584]{1,0:T(8,128)(2,1)S(1)}, bf16[32,3584]{1,0:T(8,128)(2,1)S(1)}, u32[]{:S(2)}, u32[]{:S(2)}) collective-permute-start(bf16[32,3584]{1,0:T(8,128)(2,1)S(1)} %get-tuple-element.131), channel_id=1, source_target_pairs={{0,2},{1,3},{2,0},{3,1},{4,6},{5,7},{6,4},{7,5},{8,10},{9,11},{10,... | collective-permute-start | bytes 688136 | tf_op jit(solution)/shard_map/ppermute | solution.py:25
  51.7 15.5 %collective-permute-start.10 = (bf16[48,3584]{1,0:T(8,128)(2,1)S(1)}, bf16[48,3584]{1,0:T(8,128)(2,1)S(1)}, u32[]{:S(2)}, u32[]{:S(2)}) collective-permute-start(bf16[48,3584]{1,0:T(8,128)(2,1)S(1)} %get-tuple-element.156), channel_id=1, source_target_pairs={{0,2},{1,3},{2,0},{3,1},{4,6},{5,7},{6,4},{7,5},{8,10},{9,11},{10,... | collective-permute-start | bytes 1032200 | tf_op jit(solution)/shard_map/ppermute | solution.py:25
  57.4 9.9 %collective-permute-start.11 = (bf16[32,3584]{1,0:T(8,128)(2,1)S(1)}, bf16[32,3584]{1,0:T(8,128)(2,1)S(1)}, u32[]{:S(2)}, u32[]{:S(2)}) collective-permute-start(bf16[32,3584]{1,0:T(8,128)(2,1)S(1)} %get-tuple-element.157), channel_id=1, source_target_pairs={{0,2},{1,3},{2,0},{3,1},{4,6},{5,7},{6,4},{7,5},{8,10},{9,11},{10,... | collective-permute-start | bytes 688136 | tf_op jit(solution)/shard_map/ppermute | solution.py:25
  61.7 41.4 %collective-permute-start.8 = (bf16[160,3584]{1,0:T(8,128)(2,1)S(1)}, bf16[160,3584]{1,0:T(8,128)(2,1)S(1)}, u32[]{:S(2)}, u32[]{:S(2)}) collective-permute-start(bf16[160,3584]{1,0:T(8,128)(2,1)S(1)} %expert_block.8), channel_id=1, source_target_pairs={{0,4},{1,5},{2,6},{3,7},{4,0},{5,1},{6,2},{7,3},{8,12},{9,13},{10,... | collective-permute-start | bytes 3440648 | tf_op jit(solution)/shard_map/ppermute | solution.py:25
  67.3 9.7 %collective-permute-start.12 = (bf16[48,3584]{1,0:T(8,128)(2,1)S(1)}, bf16[48,3584]{1,0:T(8,128)(2,1)S(1)}, u32[]{:S(2)}, u32[]{:S(2)}) collective-permute-start(bf16[48,3584]{1,0:T(8,128)(2,1)S(1)} %get-tuple-element.164), channel_id=1, source_target_pairs={{0,2},{1,3},{2,0},{3,1},{4,6},{5,7},{6,4},{7,5},{8,10},{9,11},{10,... | collective-permute-start | bytes 1032200 | tf_op jit(solution)/shard_map/ppermute | solution.py:25
  68.1 32.3 %collective-permute-start.16 = (bf16[80,3584]{1,0:T(8,128)(2,1)S(1)}, bf16[80,3584]{1,0:T(8,128)(2,1)S(1)}, u32[]{:S(2)}, u32[]{:S(2)}) collective-permute-start(bf16[80,3584]{1,0:T(8,128)(2,1)S(1)} %total.4), channel_id=1, source_target_pairs={{0,8},{1,9},{2,10},{3,11},{4,12},{5,13},{6,14},{7,15},{8,0},{9,1},... | collective-permute-start | bytes 1720328 | tf_op jit(solution)/shard_map/ppermute | solution.py:25
  68.2 13.2 %collective-permute-start.13 = (bf16[32,3584]{1,0:T(8,128)(2,1)S(1)}, bf16[32,3584]{1,0:T(8,128)(2,1)S(1)}, u32[]{:S(2)}, u32[]{:S(2)}) collective-permute-start(bf16[32,3584]{1,0:T(8,128)(2,1)S(1)} %get-tuple-element.180), channel_id=1, source_target_pairs={{0,2},{1,3},{2,0},{3,1},{4,6},{5,7},{6,4},{7,5},{8,10},{9,11},{10,... | collective-permute-start | bytes 688136 | tf_op jit(solution)/shard_map/ppermute | solution.py:25
  80.9 19.5 %collective-permute-start.14 = (bf16[48,3584]{1,0:T(8,128)(2,1)S(1)}, bf16[48,3584]{1,0:T(8,128)(2,1)S(1)}, u32[]{:S(2)}, u32[]{:S(2)}) collective-permute-start(bf16[48,3584]{1,0:T(8,128)(2,1)S(1)} %get-tuple-element.188), channel_id=1, source_target_pairs={{0,2},{1,3},{2,0},{3,1},{4,6},{5,7},{6,4},{7,5},{8,10},{9,11},{10,... | collective-permute-start | bytes 1032200 | tf_op jit(solution)/shard_map/ppermute | solution.py:25
  85.4 15.0 %collective-permute-start.15 = (bf16[32,3584]{1,0:T(8,128)(2,1)S(1)}, bf16[32,3584]{1,0:T(8,128)(2,1)S(1)}, u32[]{:S(2)}, u32[]{:S(2)}) collective-permute-start(bf16[32,3584]{1,0:T(8,128)(2,1)S(1)} %get-tuple-element.189), channel_id=1, source_target_pairs={{0,2},{1,3},{2,0},{3,1},{4,6},{5,7},{6,4},{7,5},{8,10},{9,11},{10,... | collective-permute-start | bytes 688136 | tf_op jit(solution)/shard_map/ppermute | solution.py:25
  90.9 37.8 %copy-start = (bf16[128,3584]{1,0:T(8,128)(2,1)S(1)}, bf16[128,3584]{1,0:T(8,128)(2,1)}, u32[]{:S(2)}) copy-start(bf16[128,3584]{1,0:T(8,128)(2,1)} %tokens_ref.1) | copy-start | bytes 2752516
  100.7 15.0 %collective-permute-start.21 = (bf16[80,3584]{1,0:T(8,128)(2,1)S(1)}, bf16[80,3584]{1,0:T(8,128)(2,1)S(1)}, u32[]{:S(2)}, u32[]{:S(2)}) collective-permute-start(bf16[80,3584]{1,0:T(8,128)(2,1)S(1)} %total.5), channel_id=1, source_target_pairs={{0,12},{1,13},{2,14},{3,15},{4,8},{5,9},{6,10},{7,11},{8,4},{9,5},... | collective-permute-start | bytes 1720328 | tf_op jit(solution)/shard_map/ppermute | solution.py:25
  102.5 15.9 %collective-permute-start.20 = (bf16[80,3584]{1,0:T(8,128)(2,1)S(1)}, bf16[80,3584]{1,0:T(8,128)(2,1)S(1)}, u32[]{:S(2)}, u32[]{:S(2)}) collective-permute-start(bf16[80,3584]{1,0:T(8,128)(2,1)S(1)} %get-tuple-element.216), channel_id=1, source_target_pairs={{0,2},{1,3},{2,0},{3,1},{4,6},{5,7},{6,4},{7,5},{8,10},{9,11},{10,... | collective-permute-start | bytes 1720328 | tf_op jit(solution)/shard_map/ppermute | solution.py:25
  103.1 25.0 %collective-permute-start.18 = (bf16[32,3584]{1,0:T(8,128)(2,1)S(1)}, bf16[32,3584]{1,0:T(8,128)(2,1)S(1)}, u32[]{:S(2)}, u32[]{:S(2)}) collective-permute-start(bf16[32,3584]{1,0:T(8,128)(2,1)S(1)} %get-tuple-element.212), channel_id=1, source_target_pairs={{0,2},{1,3},{2,0},{3,1},{4,6},{5,7},{6,4},{7,5},{8,10},{9,11},{10,... | collective-permute-start | bytes 688136 | tf_op jit(solution)/shard_map/ppermute | solution.py:25
  104.7 23.4 %collective-permute-start.17 = (bf16[32,3584]{1,0:T(8,128)(2,1)S(1)}, bf16[32,3584]{1,0:T(8,128)(2,1)S(1)}, u32[]{:S(2)}, u32[]{:S(2)}) collective-permute-start(bf16[32,3584]{1,0:T(8,128)(2,1)S(1)} %get-tuple-element.210), channel_id=1, source_target_pairs={{0,2},{1,3},{2,0},{3,1},{4,6},{5,7},{6,4},{7,5},{8,10},{9,11},{10,... | collective-permute-start | bytes 688136 | tf_op jit(solution)/shard_map/ppermute | solution.py:25
  105.2 22.9 %collective-permute-start.19 = (bf16[16,3584]{1,0:T(8,128)(2,1)S(1)}, bf16[16,3584]{1,0:T(8,128)(2,1)S(1)}, u32[]{:S(2)}, u32[]{:S(2)}) collective-permute-start(bf16[16,3584]{1,0:T(8,128)(2,1)S(1)} %get-tuple-element.214), channel_id=1, source_target_pairs={{0,2},{1,3},{2,0},{3,1},{4,6},{5,7},{6,4},{7,5},{8,10},{9,11},{10,... | collective-permute-start | bytes 344072 | tf_op jit(solution)/shard_map/ppermute | solution.py:25
  131.3 10.3 %all-to-all-start = ((f32[16,1,16]{2,1,0:T(1,128)}), f32[16,1,16]{2,1,0:T(1,128)S(1)}, u32[]{:S(2)}, u32[]{:S(2)}) async-start(f32[16,1,16]{2,1,0:T(1,128)} %bitcast.6), calls=%async_computation | async-start | bytes 16384 | tf_op jit(solution)/shard_map/all_to_all | solution.py:379
  (8 other events, 259.4 us)

commit v14 on v12

--- a/solution.py
+++ b/solution.py
@@ -321,10 +321,9 @@
     leave(2)
     far[0], far[1] = swap(near[0], side), swap(near[1], side)
     leave(1)
+    weights[1] = order.mark_one(weights[1])
     arrive(2)
     far[0] = order.mark_one(far[0])
-    far[1] = order.mark_one(far[1])
-    arrive(1)
     last = (capacity - 16, 16)
     for k in range(3, experts + 1):
         if k > 3:
@@ -333,6 +332,8 @@
         if k < experts:
             leave(k)
         if k == 3:
+            far[1] = order.mark_one(far[1])
+            arrive(1)
             far[1] = swap(order.late(far[1]), spread)
         if k > 3:
             if k == experts:

time: 138 us -> 137 us (level)
  transfers between devices with their start and end apart: 23 -> 23, of which waited for: 9 -> 10; matrix products, arithmetic and copies ran while one was open for 0% -> 0% of each run, Pallas kernels for 18% -> 18%
where the time goes in v14:
time: 137 us
  waiting for transfers between devices  72.6 us (53%)
  Pallas kernels  31.5 us (23%)
  starting transfers between devices  30.9 us (23%)
    ppermute x22, waiting for transfers between devices, swap(): return lax.ppermute(value, 'expert', pairs)  66.4 us
    ppermute x22, starting transfers between devices, swap(): return lax.ppermute(value, 'expert', pairs)  27 us
    pallas_call x6, Pallas kernels, expert_block(): pl.pallas_call(functools.partial(expert_kernel, first), out_shape=[jax.Sh...  23.2 us
    all_to_all x1, waiting for transfers between devices, per_device(): lax.all_to_all(local, 'expert', split_axis=0, concat_axis=0, tiled=True)  6.21 us
    pallas_call x1, Pallas kernels, pack(): pl.pallas_call(pack_kernel, out_shape=[jax.ShapeDtypeStruct(shape, BF16)...  4.53 us
    all_to_all x1, starting transfers between devices, per_device(): lax.all_to_all(local, 'expert', split_axis=0, concat_axis=0, tiled=True)  3.96 us
  transfers between devices with their start and end apart: 23, of which 10 were waited for; matrix products, arithmetic and copies ran while one was open for 0% of the time, Pallas kernels for 18%

profile of v14, /device:TPU:0, one launch (start us, length us, event | category | flops | bytes accessed | tf_op | source)
XLA Modules:
  0.0 137.0 jit_solution(18126484126744347790)
XLA Ops:
  0.6 4.5 %pack.1 = (bf16[80,3584]{1,0:T(8,128)(2,1)S(1)}, bf16[80,3584]{1,0:T(8,128)(2,1)S(1)}, bf16[80,3584]{1,0:T(8,128)(2,1)S(1)}, bf16[80,3584]{1,0:T(8,128)(2,1)S(1)}, bf16[10752,512]{1,0:T(8,128)(2,1)S(1)}) custom-call(s32[1]{0:T(128)} %bitcast.own_ref, bf16[128,3584]{1,0:T(8,128)(2,1)} %tokens_ref.1, f32[3584]{0:T(1024)} %gain_hbm.1, s32[2,128]{1,0:T(2,128)} %bitcast.8, ...), custom_call_target="tpu_custom_call" | custom-call | flops 1024 | bytes 1024 | tf_op jit(solution)/shard_map/pack/pallas_call | solution.py:78
  5.7 3.7 %collective-permute-start.2 = (bf16[80,3584]{1,0:T(8,128)(2,1)S(1)}, bf16[80,3584]{1,0:T(8,128)(2,1)S(1)}, u32[]{:S(2)}, u32[]{:S(2)}) collective-permute-start(bf16[80,3584]{1,0:T(8,128)(2,1)S(1)} %get-tuple-element.123), channel_id=1, source_target_pairs={{0,8},{1,9},{2,10},{3,11},{4,12},{5,13},{6,14},{7,15},{8,0},{9,1},... | collective-permute-start | bytes 1720328 | tf_op jit(solution)/shard_map/ppermute | solution.py:25
  13.0 9.3 %collective-permute-done.3.refs_1_ = bf16[10752,512]{1,0:T(8,128)(2,1)S(1)} collective-permute-done((bf16[10752,512]{1,0:T(8,128)(2,1)S(1)}, bf16[10752,512]{1,0:T(8,128)(2,1)S(1)}, u32[]{:S(2)}, u32[]{:S(2)}) %collective-permute-start.3) | collective-permute-done | bytes 11010080 | tf_op jit(solution)/shard_map/ppermute | solution.py:25
  22.2 13.1 %collective-permute-done.2.whole_ref.near_ref = bf16[80,3584]{1,0:T(8,128)(2,1)S(1)} collective-permute-done((bf16[80,3584]{1,0:T(8,128)(2,1)S(1)}, bf16[80,3584]{1,0:T(8,128)(2,1)S(1)}, u32[]{:S(2)}, u32[]{:S(2)}) %collective-permute-start.2) | collective-permute-done | bytes 573472 | tf_op jit(solution)/shard_map/ppermute | solution.py:25
  35.4 1.7 %collective-permute-start.5 = (bf16[48,3584]{1,0:T(8,128)(2,1)S(1)}, bf16[48,3584]{1,0:T(8,128)(2,1)S(1)}, u32[]{:S(2)}, u32[]{:S(2)}) collective-permute-start(bf16[48,3584]{1,0:T(8,128)(2,1)S(1)} %get-tuple-element.136), channel_id=1, source_target_pairs={{0,2},{1,3},{2,0},{3,1},{4,6},{5,7},{6,4},{7,5},{8,10},{9,11},{10,... | collective-permute-start | bytes 1032200 | tf_op jit(solution)/shard_map/ppermute | solution.py:25
  37.0 3.5 %collective-permute-start.8 = (bf16[80,3584]{1,0:T(8,128)(2,1)S(1)}, bf16[80,3584]{1,0:T(8,128)(2,1)S(1)}, u32[]{:S(2)}, u32[]{:S(2)}) collective-permute-start(bf16[80,3584]{1,0:T(8,128)(2,1)S(1)} %get-tuple-element.157), channel_id=1, source_target_pairs={{0,12},{1,13},{2,14},{3,15},{4,8},{5,9},{6,10},{7,11},{8,4},{9,5},... | collective-permute-start | bytes 1720328 | tf_op jit(solution)/shard_map/ppermute | solution.py:25
  41.0 5.4 %collective-permute-done.5.far_ref = bf16[48,3584]{1,0:T(8,128)(2,1)S(1)} collective-permute-done((bf16[48,3584]{1,0:T(8,128)(2,1)S(1)}, bf16[48,3584]{1,0:T(8,128)(2,1)S(1)}, u32[]{:S(2)}, u32[]{:S(2)}) %collective-permute-start.5) | collective-permute-done | bytes 344096 | tf_op jit(solution)/shard_map/ppermute | solution.py:25
  46.4 3.7 %expert_block.6 = (bf16[48,3584]{1,0:T(8,128)(2,1)S(1)}, bf16[48,3584]{1,0:T(8,128)(2,1)S(1)}) custom-call(bf16[80,3584]{1,0:T(8,128)(2,1)S(1)} %collective-permute-done.2.whole_ref.near_ref, bf16[48,3584]{1,0:T(8,128)(2,1)S(1)} %collective-permute-done.5.far_ref, bf16[10752,512]{1,0:T(8,128)(2,1)S(1)} %get-tuple-element.124.refs_0_, ...), custom_call_target="tpu_custom_call" | custom-call | flops 1024 | bytes 1024 | tf_op jit(solution)/shard_map/expert_block/pallas_call | solution.py:119
  50.1 1.7 %collective-permute-start.9 = (bf16[48,3584]{1,0:T(8,128)(2,1)S(1)}, bf16[48,3584]{1,0:T(8,128)(2,1)S(1)}, u32[]{:S(2)}, u32[]{:S(2)}) collective-permute-start(bf16[48,3584]{1,0:T(8,128)(2,1)S(1)} %get-tuple-element.160), channel_id=1, source_target_pairs={{0,2},{1,3},{2,0},{3,1},{4,6},{5,7},{6,4},{7,5},{8,10},{9,11},{10,... | collective-permute-start | bytes 1032200 | tf_op jit(solution)/shard_map/ppermute | solution.py:25
  51.8 4.0 %expert_block.7 = (bf16[32,3584]{1,0:T(8,128)(2,1)S(1)}, bf16[32,3584]{1,0:T(8,128)(2,1)S(1)}) custom-call(bf16[80,3584]{1,0:T(8,128)(2,1)S(1)} %collective-permute-done.2.whole_ref.near_ref, bf16[32,3584]{1,0:T(8,128)(2,1)S(1)} %collective-permute-done.6.far_ref, bf16[10752,512]{1,0:T(8,128)(2,1)S(1)} %get-tuple-element.124.refs_0_, ...), custom_call_target="tpu_custom_call" | custom-call | flops 1024 | bytes 1024 | tf_op jit(solution)/shard_map/expert_block/pallas_call | solution.py:119
  56.3 6.5 %collective-permute-done.10.refs_3_ = bf16[32,3584]{1,0:T(8,128)(2,1)S(1)} collective-permute-done((bf16[32,3584]{1,0:T(8,128)(2,1)S(1)}, bf16[32,3584]{1,0:T(8,128)(2,1)S(1)}, u32[]{:S(2)}, u32[]{:S(2)}) %collective-permute-start.10) | collective-permute-done | bytes 229408 | tf_op jit(solution)/shard_map/ppermute | solution.py:25
  64.1 1.7 %collective-permute-done.7.far_ref = bf16[80,3584]{1,0:T(8,128)(2,1)S(1)} collective-permute-done((bf16[80,3584]{1,0:T(8,128)(2,1)S(1)}, bf16[80,3584]{1,0:T(8,128)(2,1)S(1)}, u32[]{:S(2)}, u32[]{:S(2)}) %collective-permute-start.7) | collective-permute-done | bytes 573472 | tf_op jit(solution)/shard_map/ppermute | solution.py:25
  67.6 3.8 %expert_block.8 = (bf16[80,3584]{1,0:T(8,128)(2,1)S(1)}, bf16[80,3584]{1,0:T(8,128)(2,1)S(1)}) custom-call(bf16[80,3584]{1,0:T(8,128)(2,1)S(1)} %collective-permute-done.near_ref, bf16[80,3584]{1,0:T(8,128)(2,1)S(1)} %collective-permute-done.7.far_ref, bf16[10752,512]{1,0:T(8,128)(2,1)S(1)} %get-tuple-element.124.refs_0_, ...), custom_call_target="tpu_custom_call" | custom-call | flops 1024 | bytes 1024 | tf_op jit(solution)/shard_map/expert_block/pallas_call | solution.py:119
  71.4 2.5 %collective-permute-start.19 = (bf16[80,3584]{1,0:T(8,128)(2,1)S(1)}, bf16[80,3584]{1,0:T(8,128)(2,1)S(1)}, u32[]{:S(2)}, u32[]{:S(2)}) collective-permute-start(bf16[80,3584]{1,0:T(8,128)(2,1)S(1)} %get-tuple-element.224), channel_id=1, source_target_pairs={{0,4},{1,5},{2,6},{3,7},{4,0},{5,1},{6,2},{7,3},{8,12},{9,13},{10,... | collective-permute-start | bytes 1720328 | tf_op jit(solution)/shard_map/ppermute | solution.py:25
  74.0 3.9 %expert_block.9 = (bf16[48,3584]{1,0:T(8,128)(2,1)S(1)}, bf16[48,3584]{1,0:T(8,128)(2,1)S(1)}) custom-call(bf16[80,3584]{1,0:T(8,128)(2,1)S(1)} %collective-permute-done.8.whole_ref.near_ref, bf16[48,3584]{1,0:T(8,128)(2,1)S(1)} %collective-permute-done.11.far_ref, bf16[10752,512]{1,0:T(8,128)(2,1)S(1)} %get-tuple-element.124.refs_0_, ...), custom_call_target="tpu_custom_call" | custom-call | flops 1024 | bytes 1024 | tf_op jit(solution)/shard_map/expert_block/pallas_call | solution.py:119
  79.3 4.0 %expert_block.10 = (bf16[32,3584]{1,0:T(8,128)(2,1)S(1)}, bf16[32,3584]{1,0:T(8,128)(2,1)S(1)}) custom-call(bf16[80,3584]{1,0:T(8,128)(2,1)S(1)} %collective-permute-done.8.whole_ref.near_ref, bf16[32,3584]{1,0:T(8,128)(2,1)S(1)} %collective-permute-done.12.far_ref, bf16[10752,512]{1,0:T(8,128)(2,1)S(1)} %get-tuple-element.124.refs_0_, ...), custom_call_target="tpu_custom_call" | custom-call | flops 1024 | bytes 1024 | tf_op jit(solution)/shard_map/expert_block/pallas_call | solution.py:119
  84.0 3.8 %expert_block.11 = (bf16[80,3584]{1,0:T(8,128)(2,1)S(1)}, bf16[80,3584]{1,0:T(8,128)(2,1)S(1)}) custom-call(bf16[80,3584]{1,0:T(8,128)(2,1)S(1)} %get-tuple-element.203.near_ref, bf16[80,3584]{1,0:T(8,128)(2,1)S(1)} %collective-permute-done.4.far_ref, bf16[10752,512]{1,0:T(8,128)(2,1)S(1)} %get-tuple-element.124.refs_0_, ...), custom_call_target="tpu_custom_call" | custom-call | flops 1024 | bytes 1024 | tf_op jit(solution)/shard_map/expert_block/pallas_call | solution.py:119
  88.0 6.3 %collective-permute-done.15.refs_2_ = bf16[80,3584]{1,0:T(8,128)(2,1)S(1)} collective-permute-done((bf16[80,3584]{1,0:T(8,128)(2,1)S(1)}, bf16[80,3584]{1,0:T(8,128)(2,1)S(1)}, u32[]{:S(2)}, u32[]{:S(2)}) %collective-permute-start.15) | collective-permute-done | bytes 573472 | tf_op jit(solution)/shard_map/ppermute | solution.py:25
  96.4 1.7 %collective-permute-done.19.whole_ref = bf16[80,3584]{1,0:T(8,128)(2,1)S(1)} collective-permute-done((bf16[80,3584]{1,0:T(8,128)(2,1)S(1)}, bf16[80,3584]{1,0:T(8,128)(2,1)S(1)}, u32[]{:S(2)}, u32[]{:S(2)}) %collective-permute-start.19) | collective-permute-done | bytes 573472 | tf_op jit(solution)/shard_map/ppermute | solution.py:25
  100.3 12.0 %collective-permute-done.18.refs_3_ = bf16[80,3584]{1,0:T(8,128)(2,1)S(1)} collective-permute-done((bf16[80,3584]{1,0:T(8,128)(2,1)S(1)}, bf16[80,3584]{1,0:T(8,128)(2,1)S(1)}, u32[]{:S(2)}, u32[]{:S(2)}) %collective-permute-start.18) | collective-permute-done | bytes 573472 | tf_op jit(solution)/shard_map/ppermute | solution.py:25
  112.6 10.3 %collective-permute-done.16.refs_0_ = bf16[80,3584]{1,0:T(8,128)(2,1)S(1)} collective-permute-done((bf16[80,3584]{1,0:T(8,128)(2,1)S(1)}, bf16[80,3584]{1,0:T(8,128)(2,1)S(1)}, u32[]{:S(2)}, u32[]{:S(2)}) %collective-permute-start.16) | collective-permute-done | bytes 573472 | tf_op jit(solution)/shard_map/ppermute | solution.py:25
  123.3 2.5 %score.1 = f32[16,16]{1,0:T(8,128)} custom-call(s32[1]{0:T(128)} %bitcast.own_ref, bf16[128,3584]{1,0:T(8,128)(2,1)S(1)} %copy-done, f32[3584]{0:T(1024)S(1)} %copy-done.2, s32[2,128]{1,0:T(2,128)S(1)} %bitcast.9, f32[2,128]{1,0:T(2,128)S(1)} %bitcast.10, bf16[128,3584]{1,0:T(8,128)(2,1)S(1)} %copy-done.1, f32[1,128]{1,0:T(1,128)S(1)} %bitcast.11, ...), custom_call_target="tpu_custom_call" | custom-call | flops 1024 | bytes 1024 | tf_op jit(solution)/shard_map/score/pallas_call | solution.py:182
  125.8 4.0 %all-to-all-start = ((f32[16,1,16]{2,1,0:T(1,128)}), f32[16,1,16]{2,1,0:T(1,128)S(1)}, u32[]{:S(2)}, u32[]{:S(2)}) async-start(f32[16,1,16]{2,1,0:T(1,128)} %bitcast.6), calls=%async_computation | async-start | bytes 16384 | tf_op jit(solution)/shard_map/all_to_all | solution.py:379
  130.0 6.2 %all-to-all-done = f32[16,1,16]{2,1,0:T(1,128)S(1)} async-done(((f32[16,1,16]{2,1,0:T(1,128)}), f32[16,1,16]{2,1,0:T(1,128)S(1)}, u32[]{:S(2)}, u32[]{:S(2)}) %all-to-all-start) | async-done | bytes 1056 | tf_op jit(solution)/shard_map/all_to_all | solution.py:379
  (61 shorter events, 16.2 us)
Async XLA Ops:
  5.2 17.1 %collective-permute-start.3 = (bf16[10752,512]{1,0:T(8,128)(2,1)S(1)}, bf16[10752,512]{1,0:T(8,128)(2,1)S(1)}, u32[]{:S(2)}, u32[]{:S(2)}) collective-permute-start(bf16[10752,512]{1,0:T(8,128)(2,1)S(1)} %get-tuple-element.124.refs_0_), channel_id=1, source_target_pairs={{0,1},{1,0},{2,3},{3,2},{4,5},{5,4},{6,7},{7,6},{8,9},{9,8},{10,11... | collective-permute-start | bytes 33030152 | tf_op jit(solution)/shard_map/ppermute | solution.py:25
  5.7 29.6 %collective-permute-start.2 = (bf16[80,3584]{1,0:T(8,128)(2,1)S(1)}, bf16[80,3584]{1,0:T(8,128)(2,1)S(1)}, u32[]{:S(2)}, u32[]{:S(2)}) collective-permute-start(bf16[80,3584]{1,0:T(8,128)(2,1)S(1)} %get-tuple-element.123), channel_id=1, source_target_pairs={{0,8},{1,9},{2,10},{3,11},{4,12},{5,13},{6,14},{7,15},{8,0},{9,1},... | collective-permute-start | bytes 1720328 | tf_op jit(solution)/shard_map/ppermute | solution.py:25
  9.4 26.0 %collective-permute-start.4 = (bf16[80,3584]{1,0:T(8,128)(2,1)S(1)}, bf16[80,3584]{1,0:T(8,128)(2,1)S(1)}, u32[]{:S(2)}, u32[]{:S(2)}) collective-permute-start(bf16[80,3584]{1,0:T(8,128)(2,1)S(1)} %get-tuple-element.203.near_ref), channel_id=1, source_target_pairs={{0,2},{1,3},{2,0},{3,1},{4,6},{5,7},{6,4},{7,5},{8,10},{9,11},{10,... | collective-permute-start | bytes 1720328 | tf_op jit(solution)/shard_map/ppermute | solution.py:25
  10.9 30.1 %collective-permute-start.1 = (bf16[80,3584]{1,0:T(8,128)(2,1)S(1)}, bf16[80,3584]{1,0:T(8,128)(2,1)S(1)}, u32[]{:S(2)}, u32[]{:S(2)}) collective-permute-start(bf16[80,3584]{1,0:T(8,128)(2,1)S(1)} %get-tuple-element.121), channel_id=1, source_target_pairs={{0,2},{1,3},{2,0},{3,1},{4,6},{5,7},{6,4},{7,5},{8,10},{9,11},{10,... | collective-permute-start | bytes 1720328 | tf_op jit(solution)/shard_map/ppermute | solution.py:25
  11.4 29.6 %collective-permute-start = (bf16[80,3584]{1,0:T(8,128)(2,1)S(1)}, bf16[80,3584]{1,0:T(8,128)(2,1)S(1)}, u32[]{:S(2)}, u32[]{:S(2)}) collective-permute-start(bf16[80,3584]{1,0:T(8,128)(2,1)S(1)} %get-tuple-element.121), channel_id=1, source_target_pairs={{0,4},{1,5},{2,6},{3,7},{4,0},{5,1},{6,2},{7,3},{8,12},{9,13},{10,... | collective-permute-start | bytes 1720328 | tf_op jit(solution)/shard_map/ppermute | solution.py:25
  35.4 11.0 %collective-permute-start.5 = (bf16[48,3584]{1,0:T(8,128)(2,1)S(1)}, bf16[48,3584]{1,0:T(8,128)(2,1)S(1)}, u32[]{:S(2)}, u32[]{:S(2)}) collective-permute-start(bf16[48,3584]{1,0:T(8,128)(2,1)S(1)} %get-tuple-element.136), channel_id=1, source_target_pairs={{0,2},{1,3},{2,0},{3,1},{4,6},{5,7},{6,4},{7,5},{8,10},{9,11},{10,... | collective-permute-start | bytes 1032200 | tf_op jit(solution)/shard_map/ppermute | solution.py:25
  37.0 19.2 %collective-permute-start.8 = (bf16[80,3584]{1,0:T(8,128)(2,1)S(1)}, bf16[80,3584]{1,0:T(8,128)(2,1)S(1)}, u32[]{:S(2)}, u32[]{:S(2)}) collective-permute-start(bf16[80,3584]{1,0:T(8,128)(2,1)S(1)} %get-tuple-element.157), channel_id=1, source_target_pairs={{0,12},{1,13},{2,14},{3,15},{4,8},{5,9},{6,10},{7,11},{8,4},{9,5},... | collective-permute-start | bytes 1720328 | tf_op jit(solution)/shard_map/ppermute | solution.py:25
  40.5 11.3 %collective-permute-start.6 = (bf16[32,3584]{1,0:T(8,128)(2,1)S(1)}, bf16[32,3584]{1,0:T(8,128)(2,1)S(1)}, u32[]{:S(2)}, u32[]{:S(2)}) collective-permute-start(bf16[32,3584]{1,0:T(8,128)(2,1)S(1)} %get-tuple-element.146), channel_id=1, source_target_pairs={{0,2},{1,3},{2,0},{3,1},{4,6},{5,7},{6,4},{7,5},{8,10},{9,11},{10,... | collective-permute-start | bytes 688136 | tf_op jit(solution)/shard_map/ppermute | solution.py:25
  41.0 24.7 %collective-permute-start.7 = (bf16[80,3584]{1,0:T(8,128)(2,1)S(1)}, bf16[80,3584]{1,0:T(8,128)(2,1)S(1)}, u32[]{:S(2)}, u32[]{:S(2)}) collective-permute-start(bf16[80,3584]{1,0:T(8,128)(2,1)S(1)} %collective-permute-done.1), channel_id=1, source_target_pairs={{0,4},{1,5},{2,6},{3,7},{4,0},{5,1},{6,2},{7,3},{8,12},{9,13},{10,... | collective-permute-start | bytes 1720328 | tf_op jit(solution)/shard_map/ppermute | solution.py:25
  50.1 12.7 %collective-permute-start.9 = (bf16[48,3584]{1,0:T(8,128)(2,1)S(1)}, bf16[48,3584]{1,0:T(8,128)(2,1)S(1)}, u32[]{:S(2)}, u32[]{:S(2)}) collective-permute-start(bf16[48,3584]{1,0:T(8,128)(2,1)S(1)} %get-tuple-element.160), channel_id=1, source_target_pairs={{0,2},{1,3},{2,0},{3,1},{4,6},{5,7},{6,4},{7,5},{8,10},{9,11},{10,... | collective-permute-start | bytes 1032200 | tf_op jit(solution)/shard_map/ppermute | solution.py:25
  55.8 7.0 %collective-permute-start.10 = (bf16[32,3584]{1,0:T(8,128)(2,1)S(1)}, bf16[32,3584]{1,0:T(8,128)(2,1)S(1)}, u32[]{:S(2)}, u32[]{:S(2)}) collective-permute-start(bf16[32,3584]{1,0:T(8,128)(2,1)S(1)} %get-tuple-element.161), channel_id=1, source_target_pairs={{0,2},{1,3},{2,0},{3,1},{4,6},{5,7},{6,4},{7,5},{8,10},{9,11},{10,... | collective-permute-start | bytes 688136 | tf_op jit(solution)/shard_map/ppermute | solution.py:25
  62.8 11.2 %collective-permute-start.11 = (bf16[48,3584]{1,0:T(8,128)(2,1)S(1)}, bf16[48,3584]{1,0:T(8,128)(2,1)S(1)}, u32[]{:S(2)}, u32[]{:S(2)}) collective-permute-start(bf16[48,3584]{1,0:T(8,128)(2,1)S(1)} %get-tuple-element.182), channel_id=1, source_target_pairs={{0,2},{1,3},{2,0},{3,1},{4,6},{5,7},{6,4},{7,5},{8,10},{9,11},{10,... | collective-permute-start | bytes 1032200 | tf_op jit(solution)/shard_map/ppermute | solution.py:25
  66.0 28.2 %collective-permute-start.15 = (bf16[80,3584]{1,0:T(8,128)(2,1)S(1)}, bf16[80,3584]{1,0:T(8,128)(2,1)S(1)}, u32[]{:S(2)}, u32[]{:S(2)}) collective-permute-start(bf16[80,3584]{1,0:T(8,128)(2,1)S(1)} %total.4), channel_id=1, source_target_pairs={{0,8},{1,9},{2,10},{3,11},{4,12},{5,13},{6,14},{7,15},{8,0},{9,1},... | collective-permute-start | bytes 1720328 | tf_op jit(solution)/shard_map/ppermute | solution.py:25
  66.7 12.6 %collective-permute-start.12 = (bf16[32,3584]{1,0:T(8,128)(2,1)S(1)}, bf16[32,3584]{1,0:T(8,128)(2,1)S(1)}, u32[]{:S(2)}, u32[]{:S(2)}) collective-permute-start(bf16[32,3584]{1,0:T(8,128)(2,1)S(1)} %get-tuple-element.191), channel_id=1, source_target_pairs={{0,2},{1,3},{2,0},{3,1},{4,6},{5,7},{6,4},{7,5},{8,10},{9,11},{10,... | collective-permute-start | bytes 688136 | tf_op jit(solution)/shard_map/ppermute | solution.py:25
  71.4 26.7 %collective-permute-start.19 = (bf16[80,3584]{1,0:T(8,128)(2,1)S(1)}, bf16[80,3584]{1,0:T(8,128)(2,1)S(1)}, u32[]{:S(2)}, u32[]{:S(2)}) collective-permute-start(bf16[80,3584]{1,0:T(8,128)(2,1)S(1)} %get-tuple-element.224), channel_id=1, source_target_pairs={{0,4},{1,5},{2,6},{3,7},{4,0},{5,1},{6,2},{7,3},{8,12},{9,13},{10,... | collective-permute-start | bytes 1720328 | tf_op jit(solution)/shard_map/ppermute | solution.py:25
  77.9 16.4 %collective-permute-start.13 = (bf16[48,3584]{1,0:T(8,128)(2,1)S(1)}, bf16[48,3584]{1,0:T(8,128)(2,1)S(1)}, u32[]{:S(2)}, u32[]{:S(2)}) collective-permute-start(bf16[48,3584]{1,0:T(8,128)(2,1)S(1)} %get-tuple-element.199), channel_id=1, source_target_pairs={{0,2},{1,3},{2,0},{3,1},{4,6},{5,7},{6,4},{7,5},{8,10},{9,11},{10,... | collective-permute-start | bytes 1032200 | tf_op jit(solution)/shard_map/ppermute | solution.py:25
  83.2 11.1 %collective-permute-start.14 = (bf16[32,3584]{1,0:T(8,128)(2,1)S(1)}, bf16[32,3584]{1,0:T(8,128)(2,1)S(1)}, u32[]{:S(2)}, u32[]{:S(2)}) collective-permute-start(bf16[32,3584]{1,0:T(8,128)(2,1)S(1)} %get-tuple-element.200), channel_id=1, source_target_pairs={{0,2},{1,3},{2,0},{3,1},{4,6},{5,7},{6,4},{7,5},{8,10},{9,11},{10,... | collective-permute-start | bytes 688136 | tf_op jit(solution)/shard_map/ppermute | solution.py:25
  87.9 35.3 %copy-start = (bf16[128,3584]{1,0:T(8,128)(2,1)S(1)}, bf16[128,3584]{1,0:T(8,128)(2,1)}, u32[]{:S(2)}) copy-start(bf16[128,3584]{1,0:T(8,128)(2,1)} %tokens_ref.1) | copy-start | bytes 2752516
  94.6 17.7 %collective-permute-start.18 = (bf16[80,3584]{1,0:T(8,128)(2,1)S(1)}, bf16[80,3584]{1,0:T(8,128)(2,1)S(1)}, u32[]{:S(2)}, u32[]{:S(2)}) collective-permute-start(bf16[80,3584]{1,0:T(8,128)(2,1)S(1)} %total.5), channel_id=1, source_target_pairs={{0,12},{1,13},{2,14},{3,15},{4,8},{5,9},{6,10},{7,11},{8,4},{9,5},... | collective-permute-start | bytes 1720328 | tf_op jit(solution)/shard_map/ppermute | solution.py:25
  95.0 17.3 %collective-permute-start.17 = (bf16[80,3584]{1,0:T(8,128)(2,1)S(1)}, bf16[80,3584]{1,0:T(8,128)(2,1)S(1)}, u32[]{:S(2)}, u32[]{:S(2)}) collective-permute-start(bf16[80,3584]{1,0:T(8,128)(2,1)S(1)} %get-tuple-element.216), channel_id=1, source_target_pairs={{0,2},{1,3},{2,0},{3,1},{4,6},{5,7},{6,4},{7,5},{8,10},{9,11},{10,... | collective-permute-start | bytes 1720328 | tf_op jit(solution)/shard_map/ppermute | solution.py:25
  96.4 26.6 %collective-permute-start.16 = (bf16[80,3584]{1,0:T(8,128)(2,1)S(1)}, bf16[80,3584]{1,0:T(8,128)(2,1)S(1)}, u32[]{:S(2)}, u32[]{:S(2)}) collective-permute-start(bf16[80,3584]{1,0:T(8,128)(2,1)S(1)} %get-tuple-element.214), channel_id=1, source_target_pairs={{0,4},{1,5},{2,6},{3,7},{4,0},{5,1},{6,2},{7,3},{8,12},{9,13},{10,... | collective-permute-start | bytes 1720328 | tf_op jit(solution)/shard_map/ppermute | solution.py:25
  98.2 24.8 %collective-permute-start.20 = (bf16[64,3584]{1,0:T(8,128)(2,1)S(1)}, bf16[64,3584]{1,0:T(8,128)(2,1)S(1)}, u32[]{:S(2)}, u32[]{:S(2)}) collective-permute-start(bf16[64,3584]{1,0:T(8,128)(2,1)S(1)} %get-tuple-element.231), channel_id=1, source_target_pairs={{0,2},{1,3},{2,0},{3,1},{4,6},{5,7},{6,4},{7,5},{8,10},{9,11},{10,... | collective-permute-start | bytes 1376264 | tf_op jit(solution)/shard_map/ppermute | solution.py:25
  99.1 23.9 %collective-permute-start.21 = (bf16[16,3584]{1,0:T(8,128)(2,1)S(1)}, bf16[16,3584]{1,0:T(8,128)(2,1)S(1)}, u32[]{:S(2)}, u32[]{:S(2)}) collective-permute-start(bf16[16,3584]{1,0:T(8,128)(2,1)S(1)} %get-tuple-element.233), channel_id=1, source_target_pairs={{0,2},{1,3},{2,0},{3,1},{4,6},{5,7},{6,4},{7,5},{8,10},{9,11},{10,... | collective-permute-start | bytes 344072 | tf_op jit(solution)/shard_map/ppermute | solution.py:25
  125.8 10.4 %all-to-all-start = ((f32[16,1,16]{2,1,0:T(1,128)}), f32[16,1,16]{2,1,0:T(1,128)S(1)}, u32[]{:S(2)}, u32[]{:S(2)}) async-start(f32[16,1,16]{2,1,0:T(1,128)} %bitcast.6), calls=%async_computation | async-start | bytes 16384 | tf_op jit(solution)/shard_map/all_to_all | solution.py:379
  (8 other events, 244.4 us)

commit v15 on v14

--- a/solution.py
+++ b/solution.py
@@ -145,15 +145,15 @@
     spread = jnp.concatenate(parts, axis=0)
     coarse = spread.astype(BF16)
     fine = (spread - coarse.astype(F32)).astype(BF16)
+    halves = jnp.concatenate([coarse, fine], axis=1)
     chunk = width // 7 if width % 7 == 0 else width
     over_rows = (((0,), (0,)), ((), ()))
     squares = jnp.zeros((tokens, 1), F32)
     for start in range(0, width, chunk):
         cols = slice(start, start + chunk)
         rows = stacked[:, cols]
-        moe = lax.dot_general(coarse, rows, over_rows, preferred_element_type=F32)
-        moe = moe + lax.dot_general(fine, rows, over_rows, preferred_element_type=F32)
-        value = tokens_ref[:, cols].astype(F32) + moe
+        moe = lax.dot_general(halves, rows, over_rows, preferred_element_type=F32)
+        value = tokens_ref[:, cols].astype(F32) + (moe[:tokens] + moe[tokens:])
         stream[:, cols] = value
         squares = squares + jnp.sum(value * value, axis=-1, keepdims=True)
     scale = lax.rsqrt(squares / width + EPS)
@@ -327,7 +327,8 @@
     last = (capacity - 16, 16)
     for k in range(3, experts + 1):
         if k > 3:
-            near[k - 1], *theirs[k - 2] = lax.optimization_barrier((near[k - 1], *theirs[k - 2]))
+            held = (far[1], near[k - 1], *theirs[k - 2])
+            far[1], near[k - 1], *theirs[k - 2] = lax.optimization_barrier(held)
         share(k - 1)
         if k < experts:
             leave(k)
@@ -336,8 +337,6 @@
             arrive(1)
             far[1] = swap(order.late(far[1]), spread)
         if k > 3:
-            if k == experts:
-                far[1], *theirs[k - 2] = lax.optimization_barrier((far[1], *theirs[k - 2]))
             home(k - 2)
             leave_back(k - 2)
         if k == experts:

time: 137 us -> 138 us (level)
  transfers between devices with their start and end apart: 23 -> 23, of which waited for: 10 -> 10; matrix products, arithmetic and copies ran while one was open for 0% -> 0% of each run, Pallas kernels for 18% -> 17%
where the time goes in v15:
time: 138 us
  waiting for transfers between devices  73.9 us (54%)
  Pallas kernels  31.5 us (23%)
  starting transfers between devices  30.8 us (22%)
    ppermute x22, waiting for transfers between devices, swap(): return lax.ppermute(value, 'expert', pairs)  67.7 us
    ppermute x22, starting transfers between devices, swap(): return lax.ppermute(value, 'expert', pairs)  26.2 us
    pallas_call x6, Pallas kernels, expert_block(): pl.pallas_call(functools.partial(expert_kernel, first), out_shape=[jax.Sh...  23.2 us
    all_to_all x1, waiting for transfers between devices, per_device(): lax.all_to_all(local, 'expert', split_axis=0, concat_axis=0, tiled=True)  6.21 us
    all_to_all x1, starting transfers between devices, per_device(): lax.all_to_all(local, 'expert', split_axis=0, concat_axis=0, tiled=True)  4.56 us
    pallas_call x1, Pallas kernels, pack(): pl.pallas_call(pack_kernel, out_shape=[jax.ShapeDtypeStruct(shape, BF16)...  4.53 us
  transfers between devices with their start and end apart: 23, of which 10 were waited for; matrix products, arithmetic and copies ran while one was open for 0% of the time, Pallas kernels for 17%

profile of v15, /device:TPU:0, one launch (start us, length us, event | category | flops | bytes accessed | tf_op | source)
XLA Modules:
  0.0 138.1 jit_solution(1374817029862918595)
XLA Ops:
  0.6 4.5 %pack.1 = (bf16[80,3584]{1,0:T(8,128)(2,1)S(1)}, bf16[80,3584]{1,0:T(8,128)(2,1)S(1)}, bf16[80,3584]{1,0:T(8,128)(2,1)S(1)}, bf16[80,3584]{1,0:T(8,128)(2,1)S(1)}, bf16[10752,512]{1,0:T(8,128)(2,1)S(1)}) custom-call(s32[1]{0:T(128)} %bitcast.own_ref, bf16[128,3584]{1,0:T(8,128)(2,1)} %tokens_ref.1, f32[3584]{0:T(1024)} %gain_hbm.1, s32[2,128]{1,0:T(2,128)} %bitcast.8, ...), custom_call_target="tpu_custom_call" | custom-call | flops 1024 | bytes 1024 | tf_op jit(solution)/shard_map/pack/pallas_call | solution.py:78
  5.7 3.7 %collective-permute-start.2 = (bf16[80,3584]{1,0:T(8,128)(2,1)S(1)}, bf16[80,3584]{1,0:T(8,128)(2,1)S(1)}, u32[]{:S(2)}, u32[]{:S(2)}) collective-permute-start(bf16[80,3584]{1,0:T(8,128)(2,1)S(1)} %get-tuple-element.121), channel_id=1, source_target_pairs={{0,8},{1,9},{2,10},{3,11},{4,12},{5,13},{6,14},{7,15},{8,0},{9,1},... | collective-permute-start | bytes 1720328 | tf_op jit(solution)/shard_map/ppermute | solution.py:25
  13.0 9.3 %collective-permute-done.3.refs_1_ = bf16[10752,512]{1,0:T(8,128)(2,1)S(1)} collective-permute-done((bf16[10752,512]{1,0:T(8,128)(2,1)S(1)}, bf16[10752,512]{1,0:T(8,128)(2,1)S(1)}, u32[]{:S(2)}, u32[]{:S(2)}) %collective-permute-start.3) | collective-permute-done | bytes 11010080 | tf_op jit(solution)/shard_map/ppermute | solution.py:25
  22.2 13.1 %collective-permute-done.2.whole_ref.near_ref = bf16[80,3584]{1,0:T(8,128)(2,1)S(1)} collective-permute-done((bf16[80,3584]{1,0:T(8,128)(2,1)S(1)}, bf16[80,3584]{1,0:T(8,128)(2,1)S(1)}, u32[]{:S(2)}, u32[]{:S(2)}) %collective-permute-start.2) | collective-permute-done | bytes 573472 | tf_op jit(solution)/shard_map/ppermute | solution.py:25
  35.4 1.7 %collective-permute-start.5 = (bf16[48,3584]{1,0:T(8,128)(2,1)S(1)}, bf16[48,3584]{1,0:T(8,128)(2,1)S(1)}, u32[]{:S(2)}, u32[]{:S(2)}) collective-permute-start(bf16[48,3584]{1,0:T(8,128)(2,1)S(1)} %get-tuple-element.134), channel_id=1, source_target_pairs={{0,2},{1,3},{2,0},{3,1},{4,6},{5,7},{6,4},{7,5},{8,10},{9,11},{10,... | collective-permute-start | bytes 1032200 | tf_op jit(solution)/shard_map/ppermute | solution.py:25
  37.0 3.5 %collective-permute-start.8 = (bf16[80,3584]{1,0:T(8,128)(2,1)S(1)}, bf16[80,3584]{1,0:T(8,128)(2,1)S(1)}, u32[]{:S(2)}, u32[]{:S(2)}) collective-permute-start(bf16[80,3584]{1,0:T(8,128)(2,1)S(1)} %get-tuple-element.155), channel_id=1, source_target_pairs={{0,12},{1,13},{2,14},{3,15},{4,8},{5,9},{6,10},{7,11},{8,4},{9,5},... | collective-permute-start | bytes 1720328 | tf_op jit(solution)/shard_map/ppermute | solution.py:25
  41.0 5.4 %collective-permute-done.5.far_ref = bf16[48,3584]{1,0:T(8,128)(2,1)S(1)} collective-permute-done((bf16[48,3584]{1,0:T(8,128)(2,1)S(1)}, bf16[48,3584]{1,0:T(8,128)(2,1)S(1)}, u32[]{:S(2)}, u32[]{:S(2)}) %collective-permute-start.5) | collective-permute-done | bytes 344096 | tf_op jit(solution)/shard_map/ppermute | solution.py:25
  46.4 3.7 %expert_block.6 = (bf16[48,3584]{1,0:T(8,128)(2,1)S(1)}, bf16[48,3584]{1,0:T(8,128)(2,1)S(1)}) custom-call(bf16[80,3584]{1,0:T(8,128)(2,1)S(1)} %collective-permute-done.2.whole_ref.near_ref, bf16[48,3584]{1,0:T(8,128)(2,1)S(1)} %collective-permute-done.5.far_ref, bf16[10752,512]{1,0:T(8,128)(2,1)S(1)} %get-tuple-element.122.refs_0_, ...), custom_call_target="tpu_custom_call" | custom-call | flops 1024 | bytes 1024 | tf_op jit(solution)/shard_map/expert_block/pallas_call | solution.py:119
  50.1 1.7 %collective-permute-start.9 = (bf16[48,3584]{1,0:T(8,128)(2,1)S(1)}, bf16[48,3584]{1,0:T(8,128)(2,1)S(1)}, u32[]{:S(2)}, u32[]{:S(2)}) collective-permute-start(bf16[48,3584]{1,0:T(8,128)(2,1)S(1)} %get-tuple-element.158), channel_id=1, source_target_pairs={{0,2},{1,3},{2,0},{3,1},{4,6},{5,7},{6,4},{7,5},{8,10},{9,11},{10,... | collective-permute-start | bytes 1032200 | tf_op jit(solution)/shard_map/ppermute | solution.py:25
  51.8 4.0 %expert_block.7 = (bf16[32,3584]{1,0:T(8,128)(2,1)S(1)}, bf16[32,3584]{1,0:T(8,128)(2,1)S(1)}) custom-call(bf16[80,3584]{1,0:T(8,128)(2,1)S(1)} %collective-permute-done.2.whole_ref.near_ref, bf16[32,3584]{1,0:T(8,128)(2,1)S(1)} %collective-permute-done.6.far_ref, bf16[10752,512]{1,0:T(8,128)(2,1)S(1)} %get-tuple-element.122.refs_0_, ...), custom_call_target="tpu_custom_call" | custom-call | flops 1024 | bytes 1024 | tf_op jit(solution)/shard_map/expert_block/pallas_call | solution.py:119
  56.3 9.5 %collective-permute-done.7.far_ref = bf16[80,3584]{1,0:T(8,128)(2,1)S(1)} collective-permute-done((bf16[80,3584]{1,0:T(8,128)(2,1)S(1)}, bf16[80,3584]{1,0:T(8,128)(2,1)S(1)}, u32[]{:S(2)}, u32[]{:S(2)}) %collective-permute-start.7) | collective-permute-done | bytes 573472 | tf_op jit(solution)/shard_map/ppermute | solution.py:25
  68.8 3.8 %expert_block.8 = (bf16[80,3584]{1,0:T(8,128)(2,1)S(1)}, bf16[80,3584]{1,0:T(8,128)(2,1)S(1)}) custom-call(bf16[80,3584]{1,0:T(8,128)(2,1)S(1)} %collective-permute-done.near_ref, bf16[80,3584]{1,0:T(8,128)(2,1)S(1)} %collective-permute-done.7.far_ref, bf16[10752,512]{1,0:T(8,128)(2,1)S(1)} %get-tuple-element.122.refs_0_, ...), custom_call_target="tpu_custom_call" | custom-call | flops 1024 | bytes 1024 | tf_op jit(solution)/shard_map/expert_block/pallas_call | solution.py:119
  72.7 1.8 %collective-permute-start.19 = (bf16[80,3584]{1,0:T(8,128)(2,1)S(1)}, bf16[80,3584]{1,0:T(8,128)(2,1)S(1)}, u32[]{:S(2)}, u32[]{:S(2)}) collective-permute-start(bf16[80,3584]{1,0:T(8,128)(2,1)S(1)} %get-tuple-element.220), channel_id=1, source_target_pairs={{0,4},{1,5},{2,6},{3,7},{4,0},{5,1},{6,2},{7,3},{8,12},{9,13},{10,... | collective-permute-start | bytes 1720328 | tf_op jit(solution)/shard_map/ppermute | solution.py:25
  74.5 2.4 %collective-permute-done.11.far_ref = bf16[48,3584]{1,0:T(8,128)(2,1)S(1)} collective-permute-done((bf16[48,3584]{1,0:T(8,128)(2,1)S(1)}, bf16[48,3584]{1,0:T(8,128)(2,1)S(1)}, u32[]{:S(2)}, u32[]{:S(2)}) %collective-permute-start.11) | collective-permute-done | bytes 344096 | tf_op jit(solution)/shard_map/ppermute | solution.py:25
  76.8 3.9 %expert_block.9 = (bf16[48,3584]{1,0:T(8,128)(2,1)S(1)}, bf16[48,3584]{1,0:T(8,128)(2,1)S(1)}) custom-call(bf16[80,3584]{1,0:T(8,128)(2,1)S(1)} %collective-permute-done.8.whole_ref.near_ref, bf16[48,3584]{1,0:T(8,128)(2,1)S(1)} %collective-permute-done.11.far_ref, bf16[10752,512]{1,0:T(8,128)(2,1)S(1)} %get-tuple-element.122.refs_0_, ...), custom_call_target="tpu_custom_call" | custom-call | flops 1024 | bytes 1024 | tf_op jit(solution)/shard_map/expert_block/pallas_call | solution.py:119
  81.6 4.0 %expert_block.10 = (bf16[32,3584]{1,0:T(8,128)(2,1)S(1)}, bf16[32,3584]{1,0:T(8,128)(2,1)S(1)}) custom-call(bf16[80,3584]{1,0:T(8,128)(2,1)S(1)} %collective-permute-done.8.whole_ref.near_ref, bf16[32,3584]{1,0:T(8,128)(2,1)S(1)} %collective-permute-done.12.far_ref, bf16[10752,512]{1,0:T(8,128)(2,1)S(1)} %get-tuple-element.122.refs_0_, ...), custom_call_target="tpu_custom_call" | custom-call | flops 1024 | bytes 1024 | tf_op jit(solution)/shard_map/expert_block/pallas_call | solution.py:119
  86.9 3.8 %expert_block.11 = (bf16[80,3584]{1,0:T(8,128)(2,1)S(1)}, bf16[80,3584]{1,0:T(8,128)(2,1)S(1)}) custom-call(bf16[80,3584]{1,0:T(8,128)(2,1)S(1)} %get-tuple-element.199.near_ref, bf16[80,3584]{1,0:T(8,128)(2,1)S(1)} %collective-permute-done.4.far_ref, bf16[10752,512]{1,0:T(8,128)(2,1)S(1)} %get-tuple-element.122.refs_0_, ...), custom_call_target="tpu_custom_call" | custom-call | flops 1024 | bytes 1024 | tf_op jit(solution)/shard_map/expert_block/pallas_call | solution.py:119
  90.8 3.8 %collective-permute-done.15.refs_2_ = bf16[80,3584]{1,0:T(8,128)(2,1)S(1)} collective-permute-done((bf16[80,3584]{1,0:T(8,128)(2,1)S(1)}, bf16[80,3584]{1,0:T(8,128)(2,1)S(1)}, u32[]{:S(2)}, u32[]{:S(2)}) %collective-permute-start.15) | collective-permute-done | bytes 573472 | tf_op jit(solution)/shard_map/ppermute | solution.py:25
  96.8 2.0 %collective-permute-done.19.whole_ref = bf16[80,3584]{1,0:T(8,128)(2,1)S(1)} collective-permute-done((bf16[80,3584]{1,0:T(8,128)(2,1)S(1)}, bf16[80,3584]{1,0:T(8,128)(2,1)S(1)}, u32[]{:S(2)}, u32[]{:S(2)}) %collective-permute-start.19) | collective-permute-done | bytes 573472 | tf_op jit(solution)/shard_map/ppermute | solution.py:25
  100.9 11.7 %collective-permute-done.18.refs_3_ = bf16[80,3584]{1,0:T(8,128)(2,1)S(1)} collective-permute-done((bf16[80,3584]{1,0:T(8,128)(2,1)S(1)}, bf16[80,3584]{1,0:T(8,128)(2,1)S(1)}, u32[]{:S(2)}, u32[]{:S(2)}) %collective-permute-start.18) | collective-permute-done | bytes 573472 | tf_op jit(solution)/shard_map/ppermute | solution.py:25
  112.9 10.5 %collective-permute-done.16.refs_0_ = bf16[80,3584]{1,0:T(8,128)(2,1)S(1)} collective-permute-done((bf16[80,3584]{1,0:T(8,128)(2,1)S(1)}, bf16[80,3584]{1,0:T(8,128)(2,1)S(1)}, u32[]{:S(2)}, u32[]{:S(2)}) %collective-permute-start.16) | collective-permute-done | bytes 573472 | tf_op jit(solution)/shard_map/ppermute | solution.py:25
  123.8 2.5 %score.1 = f32[16,16]{1,0:T(8,128)} custom-call(s32[1]{0:T(128)} %bitcast.own_ref, bf16[128,3584]{1,0:T(8,128)(2,1)S(1)} %copy-done, f32[3584]{0:T(1024)S(1)} %copy-done.2, s32[2,128]{1,0:T(2,128)S(1)} %bitcast.9, f32[2,128]{1,0:T(2,128)S(1)} %bitcast.10, bf16[128,3584]{1,0:T(8,128)(2,1)S(1)} %copy-done.1, f32[1,128]{1,0:T(1,128)S(1)} %bitcast.11, ...), custom_call_target="tpu_custom_call" | custom-call | flops 1024 | bytes 1024 | tf_op jit(solution)/shard_map/score/pallas_call | solution.py:182
  126.3 4.6 %all-to-all-start = ((f32[16,1,16]{2,1,0:T(1,128)}), f32[16,1,16]{2,1,0:T(1,128)S(1)}, u32[]{:S(2)}, u32[]{:S(2)}) async-start(f32[16,1,16]{2,1,0:T(1,128)} %bitcast.6), calls=%async_computation | async-start | bytes 16384 | tf_op jit(solution)/shard_map/all_to_all | solution.py:378
  131.1 6.2 %all-to-all-done = f32[16,1,16]{2,1,0:T(1,128)S(1)} async-done(((f32[16,1,16]{2,1,0:T(1,128)}), f32[16,1,16]{2,1,0:T(1,128)S(1)}, u32[]{:S(2)}, u32[]{:S(2)}) %all-to-all-start) | async-done | bytes 1056 | tf_op jit(solution)/shard_map/all_to_all | solution.py:378
  (61 shorter events, 16.2 us)
Async XLA Ops:
  5.2 17.1 %collective-permute-start.3 = (bf16[10752,512]{1,0:T(8,128)(2,1)S(1)}, bf16[10752,512]{1,0:T(8,128)(2,1)S(1)}, u32[]{:S(2)}, u32[]{:S(2)}) collective-permute-start(bf16[10752,512]{1,0:T(8,128)(2,1)S(1)} %get-tuple-element.122.refs_0_), channel_id=1, source_target_pairs={{0,1},{1,0},{2,3},{3,2},{4,5},{5,4},{6,7},{7,6},{8,9},{9,8},{10,11... | collective-permute-start | bytes 33030152 | tf_op jit(solution)/shard_map/ppermute | solution.py:25
  5.7 29.6 %collective-permute-start.2 = (bf16[80,3584]{1,0:T(8,128)(2,1)S(1)}, bf16[80,3584]{1,0:T(8,128)(2,1)S(1)}, u32[]{:S(2)}, u32[]{:S(2)}) collective-permute-start(bf16[80,3584]{1,0:T(8,128)(2,1)S(1)} %get-tuple-element.121), channel_id=1, source_target_pairs={{0,8},{1,9},{2,10},{3,11},{4,12},{5,13},{6,14},{7,15},{8,0},{9,1},... | collective-permute-start | bytes 1720328 | tf_op jit(solution)/shard_map/ppermute | solution.py:25
  9.4 26.0 %collective-permute-start.4 = (bf16[80,3584]{1,0:T(8,128)(2,1)S(1)}, bf16[80,3584]{1,0:T(8,128)(2,1)S(1)}, u32[]{:S(2)}, u32[]{:S(2)}) collective-permute-start(bf16[80,3584]{1,0:T(8,128)(2,1)S(1)} %get-tuple-element.199.near_ref), channel_id=1, source_target_pairs={{0,2},{1,3},{2,0},{3,1},{4,6},{5,7},{6,4},{7,5},{8,10},{9,11},{10,... | collective-permute-start | bytes 1720328 | tf_op jit(solution)/shard_map/ppermute | solution.py:25
  10.9 26.1 %collective-permute-start.1 = (bf16[80,3584]{1,0:T(8,128)(2,1)S(1)}, bf16[80,3584]{1,0:T(8,128)(2,1)S(1)}, u32[]{:S(2)}, u32[]{:S(2)}) collective-permute-start(bf16[80,3584]{1,0:T(8,128)(2,1)S(1)} %get-tuple-element.119), channel_id=1, source_target_pairs={{0,2},{1,3},{2,0},{3,1},{4,6},{5,7},{6,4},{7,5},{8,10},{9,11},{10,... | collective-permute-start | bytes 1720328 | tf_op jit(solution)/shard_map/ppermute | solution.py:25
  11.4 25.6 %collective-permute-start = (bf16[80,3584]{1,0:T(8,128)(2,1)S(1)}, bf16[80,3584]{1,0:T(8,128)(2,1)S(1)}, u32[]{:S(2)}, u32[]{:S(2)}) collective-permute-start(bf16[80,3584]{1,0:T(8,128)(2,1)S(1)} %get-tuple-element.119), channel_id=1, source_target_pairs={{0,4},{1,5},{2,6},{3,7},{4,0},{5,1},{6,2},{7,3},{8,12},{9,13},{10,... | collective-permute-start | bytes 1720328 | tf_op jit(solution)/shard_map/ppermute | solution.py:25
  35.4 11.0 %collective-permute-start.5 = (bf16[48,3584]{1,0:T(8,128)(2,1)S(1)}, bf16[48,3584]{1,0:T(8,128)(2,1)S(1)}, u32[]{:S(2)}, u32[]{:S(2)}) collective-permute-start(bf16[48,3584]{1,0:T(8,128)(2,1)S(1)} %get-tuple-element.134), channel_id=1, source_target_pairs={{0,2},{1,3},{2,0},{3,1},{4,6},{5,7},{6,4},{7,5},{8,10},{9,11},{10,... | collective-permute-start | bytes 1032200 | tf_op jit(solution)/shard_map/ppermute | solution.py:25
  37.0 19.2 %collective-permute-start.8 = (bf16[80,3584]{1,0:T(8,128)(2,1)S(1)}, bf16[80,3584]{1,0:T(8,128)(2,1)S(1)}, u32[]{:S(2)}, u32[]{:S(2)}) collective-permute-start(bf16[80,3584]{1,0:T(8,128)(2,1)S(1)} %get-tuple-element.155), channel_id=1, source_target_pairs={{0,12},{1,13},{2,14},{3,15},{4,8},{5,9},{6,10},{7,11},{8,4},{9,5},... | collective-permute-start | bytes 1720328 | tf_op jit(solution)/shard_map/ppermute | solution.py:25
  40.5 25.3 %collective-permute-start.7 = (bf16[80,3584]{1,0:T(8,128)(2,1)S(1)}, bf16[80,3584]{1,0:T(8,128)(2,1)S(1)}, u32[]{:S(2)}, u32[]{:S(2)}) collective-permute-start(bf16[80,3584]{1,0:T(8,128)(2,1)S(1)} %collective-permute-done.1), channel_id=1, source_target_pairs={{0,4},{1,5},{2,6},{3,7},{4,0},{5,1},{6,2},{7,3},{8,12},{9,13},{10,... | collective-permute-start | bytes 1720328 | tf_op jit(solution)/shard_map/ppermute | solution.py:25
  40.5 11.3 %collective-permute-start.6 = (bf16[32,3584]{1,0:T(8,128)(2,1)S(1)}, bf16[32,3584]{1,0:T(8,128)(2,1)S(1)}, u32[]{:S(2)}, u32[]{:S(2)}) collective-permute-start(bf16[32,3584]{1,0:T(8,128)(2,1)S(1)} %get-tuple-element.144), channel_id=1, source_target_pairs={{0,2},{1,3},{2,0},{3,1},{4,6},{5,7},{6,4},{7,5},{8,10},{9,11},{10,... | collective-permute-start | bytes 688136 | tf_op jit(solution)/shard_map/ppermute | solution.py:25
  50.1 15.7 %collective-permute-start.9 = (bf16[48,3584]{1,0:T(8,128)(2,1)S(1)}, bf16[48,3584]{1,0:T(8,128)(2,1)S(1)}, u32[]{:S(2)}, u32[]{:S(2)}) collective-permute-start(bf16[48,3584]{1,0:T(8,128)(2,1)S(1)} %get-tuple-element.158), channel_id=1, source_target_pairs={{0,2},{1,3},{2,0},{3,1},{4,6},{5,7},{6,4},{7,5},{8,10},{9,11},{10,... | collective-permute-start | bytes 1032200 | tf_op jit(solution)/shard_map/ppermute | solution.py:25
  55.8 10.0 %collective-permute-start.10 = (bf16[32,3584]{1,0:T(8,128)(2,1)S(1)}, bf16[32,3584]{1,0:T(8,128)(2,1)S(1)}, u32[]{:S(2)}, u32[]{:S(2)}) collective-permute-start(bf16[32,3584]{1,0:T(8,128)(2,1)S(1)} %get-tuple-element.159), channel_id=1, source_target_pairs={{0,2},{1,3},{2,0},{3,1},{4,6},{5,7},{6,4},{7,5},{8,10},{9,11},{10,... | collective-permute-start | bytes 688136 | tf_op jit(solution)/shard_map/ppermute | solution.py:25
  65.8 11.0 %collective-permute-start.11 = (bf16[48,3584]{1,0:T(8,128)(2,1)S(1)}, bf16[48,3584]{1,0:T(8,128)(2,1)S(1)}, u32[]{:S(2)}, u32[]{:S(2)}) collective-permute-start(bf16[48,3584]{1,0:T(8,128)(2,1)S(1)} %get-tuple-element.178), channel_id=1, source_target_pairs={{0,2},{1,3},{2,0},{3,1},{4,6},{5,7},{6,4},{7,5},{8,10},{9,11},{10,... | collective-permute-start | bytes 1032200 | tf_op jit(solution)/shard_map/ppermute | solution.py:25
  67.0 27.7 %collective-permute-start.15 = (bf16[80,3584]{1,0:T(8,128)(2,1)S(1)}, bf16[80,3584]{1,0:T(8,128)(2,1)S(1)}, u32[]{:S(2)}, u32[]{:S(2)}) collective-permute-start(bf16[80,3584]{1,0:T(8,128)(2,1)S(1)} %total.4), channel_id=1, source_target_pairs={{0,8},{1,9},{2,10},{3,11},{4,12},{5,13},{6,14},{7,15},{8,0},{9,1},... | collective-permute-start | bytes 1720328 | tf_op jit(solution)/shard_map/ppermute | solution.py:25
  67.6 14.0 %collective-permute-start.12 = (bf16[32,3584]{1,0:T(8,128)(2,1)S(1)}, bf16[32,3584]{1,0:T(8,128)(2,1)S(1)}, u32[]{:S(2)}, u32[]{:S(2)}) collective-permute-start(bf16[32,3584]{1,0:T(8,128)(2,1)S(1)} %get-tuple-element.187), channel_id=1, source_target_pairs={{0,2},{1,3},{2,0},{3,1},{4,6},{5,7},{6,4},{7,5},{8,10},{9,11},{10,... | collective-permute-start | bytes 688136 | tf_op jit(solution)/shard_map/ppermute | solution.py:25
  72.7 26.1 %collective-permute-start.19 = (bf16[80,3584]{1,0:T(8,128)(2,1)S(1)}, bf16[80,3584]{1,0:T(8,128)(2,1)S(1)}, u32[]{:S(2)}, u32[]{:S(2)}) collective-permute-start(bf16[80,3584]{1,0:T(8,128)(2,1)S(1)} %get-tuple-element.220), channel_id=1, source_target_pairs={{0,4},{1,5},{2,6},{3,7},{4,0},{5,1},{6,2},{7,3},{8,12},{9,13},{10,... | collective-permute-start | bytes 1720328 | tf_op jit(solution)/shard_map/ppermute | solution.py:25
  80.7 13.9 %collective-permute-start.13 = (bf16[48,3584]{1,0:T(8,128)(2,1)S(1)}, bf16[48,3584]{1,0:T(8,128)(2,1)S(1)}, u32[]{:S(2)}, u32[]{:S(2)}) collective-permute-start(bf16[48,3584]{1,0:T(8,128)(2,1)S(1)} %get-tuple-element.195), channel_id=1, source_target_pairs={{0,2},{1,3},{2,0},{3,1},{4,6},{5,7},{6,4},{7,5},{8,10},{9,11},{10,... | collective-permute-start | bytes 1032200 | tf_op jit(solution)/shard_map/ppermute | solution.py:25
  85.6 9.1 %collective-permute-start.14 = (bf16[32,3584]{1,0:T(8,128)(2,1)S(1)}, bf16[32,3584]{1,0:T(8,128)(2,1)S(1)}, u32[]{:S(2)}, u32[]{:S(2)}) collective-permute-start(bf16[32,3584]{1,0:T(8,128)(2,1)S(1)} %get-tuple-element.196), channel_id=1, source_target_pairs={{0,2},{1,3},{2,0},{3,1},{4,6},{5,7},{6,4},{7,5},{8,10},{9,11},{10,... | collective-permute-start | bytes 688136 | tf_op jit(solution)/shard_map/ppermute | solution.py:25
  90.7 33.0 %copy-start = (bf16[128,3584]{1,0:T(8,128)(2,1)S(1)}, bf16[128,3584]{1,0:T(8,128)(2,1)}, u32[]{:S(2)}) copy-start(bf16[128,3584]{1,0:T(8,128)(2,1)} %tokens_ref.1) | copy-start | bytes 2752516
  94.9 17.7 %collective-permute-start.18 = (bf16[80,3584]{1,0:T(8,128)(2,1)S(1)}, bf16[80,3584]{1,0:T(8,128)(2,1)S(1)}, u32[]{:S(2)}, u32[]{:S(2)}) collective-permute-start(bf16[80,3584]{1,0:T(8,128)(2,1)S(1)} %total.5), channel_id=1, source_target_pairs={{0,12},{1,13},{2,14},{3,15},{4,8},{5,9},{6,10},{7,11},{8,4},{9,5},... | collective-permute-start | bytes 1720328 | tf_op jit(solution)/shard_map/ppermute | solution.py:25
  95.3 17.3 %collective-permute-start.17 = (bf16[80,3584]{1,0:T(8,128)(2,1)S(1)}, bf16[80,3584]{1,0:T(8,128)(2,1)S(1)}, u32[]{:S(2)}, u32[]{:S(2)}) collective-permute-start(bf16[80,3584]{1,0:T(8,128)(2,1)S(1)} %get-tuple-element.212), channel_id=1, source_target_pairs={{0,2},{1,3},{2,0},{3,1},{4,6},{5,7},{6,4},{7,5},{8,10},{9,11},{10,... | collective-permute-start | bytes 1720328 | tf_op jit(solution)/shard_map/ppermute | solution.py:25
  96.8 26.6 %collective-permute-start.16 = (bf16[80,3584]{1,0:T(8,128)(2,1)S(1)}, bf16[80,3584]{1,0:T(8,128)(2,1)S(1)}, u32[]{:S(2)}, u32[]{:S(2)}) collective-permute-start(bf16[80,3584]{1,0:T(8,128)(2,1)S(1)} %get-tuple-element.210), channel_id=1, source_target_pairs={{0,4},{1,5},{2,6},{3,7},{4,0},{5,1},{6,2},{7,3},{8,12},{9,13},{10,... | collective-permute-start | bytes 1720328 | tf_op jit(solution)/shard_map/ppermute | solution.py:25
  98.8 24.6 %collective-permute-start.20 = (bf16[64,3584]{1,0:T(8,128)(2,1)S(1)}, bf16[64,3584]{1,0:T(8,128)(2,1)S(1)}, u32[]{:S(2)}, u32[]{:S(2)}) collective-permute-start(bf16[64,3584]{1,0:T(8,128)(2,1)S(1)} %get-tuple-element.227), channel_id=1, source_target_pairs={{0,2},{1,3},{2,0},{3,1},{4,6},{5,7},{6,4},{7,5},{8,10},{9,11},{10,... | collective-permute-start | bytes 1376264 | tf_op jit(solution)/shard_map/ppermute | solution.py:25
  99.9 23.6 %collective-permute-start.21 = (bf16[16,3584]{1,0:T(8,128)(2,1)S(1)}, bf16[16,3584]{1,0:T(8,128)(2,1)S(1)}, u32[]{:S(2)}, u32[]{:S(2)}) collective-permute-start(bf16[16,3584]{1,0:T(8,128)(2,1)S(1)} %get-tuple-element.229), channel_id=1, source_target_pairs={{0,2},{1,3},{2,0},{3,1},{4,6},{5,7},{6,4},{7,5},{8,10},{9,11},{10,... | collective-permute-start | bytes 344072 | tf_op jit(solution)/shard_map/ppermute | solution.py:25
  126.3 11.0 %all-to-all-start = ((f32[16,1,16]{2,1,0:T(1,128)}), f32[16,1,16]{2,1,0:T(1,128)S(1)}, u32[]{:S(2)}, u32[]{:S(2)}) async-start(f32[16,1,16]{2,1,0:T(1,128)} %bitcast.6), calls=%async_computation | async-start | bytes 16384 | tf_op jit(solution)/shard_map/all_to_all | solution.py:378
  (8 other events, 230.8 us)

commit v16 on v14

--- a/solution.py
+++ b/solution.py
@@ -374,9 +374,13 @@
         segment_ids[None, :],
         blocks,
         capacity,
-        (devices, ref_logps.shape[0]),
+        (devices // 2, ref_logps.shape[0]),
     )
-    gathered = lax.all_to_all(local, "expert", split_axis=0, concat_axis=0, tiled=True)
+    local = local + swap(local, core)
+    cores = [list(range(first, devices, 2)) for first in range(2)]
+    gathered = lax.all_to_all(
+        local, "expert", split_axis=0, concat_axis=0, axis_index_groups=cores, tiled=True
+    )
     sequence_logps = jnp.sum(gathered, axis=0)
     margin = sequence_logps[0::2] - ref_logps[0::2] - (sequence_logps[1::2] - ref_logps[1::2])
     pair_loss = -jax.nn.log_sigmoid(BETA * margin)

time: 137 us -> 138 us (level)
    ppermute x22 -> x23, waiting for transfers between devices: 66.4 us -> 67.5 us  [swap(): return lax.ppermute(value, 'expert', pairs)]
    ppermute x22 -> x23, starting transfers between devices: 27 us -> 27 us  [swap(): return lax.ppermute(value, 'expert', pairs)]
  transfers between devices with their start and end apart: 23 -> 24, of which waited for: 10 -> 11; matrix products, arithmetic and copies ran while one was open for 0% -> 0% of each run, Pallas kernels for 18% -> 18%
where the time goes in v16:
time: 138 us
  waiting for transfers between devices  73.8 us (53%)
  Pallas kernels  30.9 us (22%)
  starting transfers between devices  30.9 us (22%)
    ppermute x23, waiting for transfers between devices, swap(): return lax.ppermute(value, 'expert', pairs)  67.5 us
    ppermute x23, starting transfers between devices, swap(): return lax.ppermute(value, 'expert', pairs)  27 us
    pallas_call x6, Pallas kernels, expert_block(): pl.pallas_call(functools.partial(expert_kernel, first), out_shape=[jax.Sh...  23.3 us
    all_to_all x1, waiting for transfers between devices, per_device(): lax.all_to_all(local, 'expert', split_axis=0, concat_axis=0, axis_index_g...  6.27 us
    pallas_call x1, Pallas kernels, pack(): pl.pallas_call(pack_kernel, out_shape=[jax.ShapeDtypeStruct(shape, BF16)...  4.53 us
    all_to_all x1, starting transfers between devices, per_device(): lax.all_to_all(local, 'expert', split_axis=0, concat_axis=0, axis_index_g...  3.87 us
  transfers between devices with their start and end apart: 24, of which 11 were waited for; matrix products, arithmetic and copies ran while one was open for 0% of the time, Pallas kernels for 18%

profile of v16, /device:TPU:0, one launch (start us, length us, event | category | flops | bytes accessed | tf_op | source)
XLA Modules:
  0.0 138.1 jit_solution(5011110544162531503)
XLA Ops:
  0.6 4.5 %pack.1 = (bf16[80,3584]{1,0:T(8,128)(2,1)S(1)}, bf16[80,3584]{1,0:T(8,128)(2,1)S(1)}, bf16[80,3584]{1,0:T(8,128)(2,1)S(1)}, bf16[80,3584]{1,0:T(8,128)(2,1)S(1)}, bf16[10752,512]{1,0:T(8,128)(2,1)S(1)}) custom-call(s32[1]{0:T(128)} %bitcast.own_ref, bf16[128,3584]{1,0:T(8,128)(2,1)} %tokens_ref.1, f32[3584]{0:T(1024)} %gain_hbm.1, s32[2,128]{1,0:T(2,128)} %bitcast.8, ...), custom_call_target="tpu_custom_call" | custom-call | flops 1024 | bytes 1024 | tf_op jit(solution)/shard_map/pack/pallas_call | solution.py:78
  5.7 3.7 %collective-permute-start.2 = (bf16[80,3584]{1,0:T(8,128)(2,1)S(1)}, bf16[80,3584]{1,0:T(8,128)(2,1)S(1)}, u32[]{:S(2)}, u32[]{:S(2)}) collective-permute-start(bf16[80,3584]{1,0:T(8,128)(2,1)S(1)} %get-tuple-element.123), channel_id=1, source_target_pairs={{0,8},{1,9},{2,10},{3,11},{4,12},{5,13},{6,14},{7,15},{8,0},{9,1},... | collective-permute-start | bytes 1720328 | tf_op jit(solution)/shard_map/ppermute | solution.py:25
  13.0 9.3 %collective-permute-done.3.refs_1_ = bf16[10752,512]{1,0:T(8,128)(2,1)S(1)} collective-permute-done((bf16[10752,512]{1,0:T(8,128)(2,1)S(1)}, bf16[10752,512]{1,0:T(8,128)(2,1)S(1)}, u32[]{:S(2)}, u32[]{:S(2)}) %collective-permute-start.3) | collective-permute-done | bytes 11010080 | tf_op jit(solution)/shard_map/ppermute | solution.py:25
  22.2 13.1 %collective-permute-done.2.whole_ref.near_ref = bf16[80,3584]{1,0:T(8,128)(2,1)S(1)} collective-permute-done((bf16[80,3584]{1,0:T(8,128)(2,1)S(1)}, bf16[80,3584]{1,0:T(8,128)(2,1)S(1)}, u32[]{:S(2)}, u32[]{:S(2)}) %collective-permute-start.2) | collective-permute-done | bytes 573472 | tf_op jit(solution)/shard_map/ppermute | solution.py:25
  35.4 1.7 %collective-permute-start.5 = (bf16[48,3584]{1,0:T(8,128)(2,1)S(1)}, bf16[48,3584]{1,0:T(8,128)(2,1)S(1)}, u32[]{:S(2)}, u32[]{:S(2)}) collective-permute-start(bf16[48,3584]{1,0:T(8,128)(2,1)S(1)} %get-tuple-element.136), channel_id=1, source_target_pairs={{0,2},{1,3},{2,0},{3,1},{4,6},{5,7},{6,4},{7,5},{8,10},{9,11},{10,... | collective-permute-start | bytes 1032200 | tf_op jit(solution)/shard_map/ppermute | solution.py:25
  37.0 3.5 %collective-permute-start.8 = (bf16[80,3584]{1,0:T(8,128)(2,1)S(1)}, bf16[80,3584]{1,0:T(8,128)(2,1)S(1)}, u32[]{:S(2)}, u32[]{:S(2)}) collective-permute-start(bf16[80,3584]{1,0:T(8,128)(2,1)S(1)} %get-tuple-element.157), channel_id=1, source_target_pairs={{0,12},{1,13},{2,14},{3,15},{4,8},{5,9},{6,10},{7,11},{8,4},{9,5},... | collective-permute-start | bytes 1720328 | tf_op jit(solution)/shard_map/ppermute | solution.py:25
  41.0 5.4 %collective-permute-done.5.far_ref = bf16[48,3584]{1,0:T(8,128)(2,1)S(1)} collective-permute-done((bf16[48,3584]{1,0:T(8,128)(2,1)S(1)}, bf16[48,3584]{1,0:T(8,128)(2,1)S(1)}, u32[]{:S(2)}, u32[]{:S(2)}) %collective-permute-start.5) | collective-permute-done | bytes 344096 | tf_op jit(solution)/shard_map/ppermute | solution.py:25
  46.4 3.7 %expert_block.6 = (bf16[48,3584]{1,0:T(8,128)(2,1)S(1)}, bf16[48,3584]{1,0:T(8,128)(2,1)S(1)}) custom-call(bf16[80,3584]{1,0:T(8,128)(2,1)S(1)} %collective-permute-done.2.whole_ref.near_ref, bf16[48,3584]{1,0:T(8,128)(2,1)S(1)} %collective-permute-done.5.far_ref, bf16[10752,512]{1,0:T(8,128)(2,1)S(1)} %get-tuple-element.124.refs_0_, ...), custom_call_target="tpu_custom_call" | custom-call | flops 1024 | bytes 1024 | tf_op jit(solution)/shard_map/expert_block/pallas_call | solution.py:119
  50.1 1.7 %collective-permute-start.9 = (bf16[48,3584]{1,0:T(8,128)(2,1)S(1)}, bf16[48,3584]{1,0:T(8,128)(2,1)S(1)}, u32[]{:S(2)}, u32[]{:S(2)}) collective-permute-start(bf16[48,3584]{1,0:T(8,128)(2,1)S(1)} %get-tuple-element.160), channel_id=1, source_target_pairs={{0,2},{1,3},{2,0},{3,1},{4,6},{5,7},{6,4},{7,5},{8,10},{9,11},{10,... | collective-permute-start | bytes 1032200 | tf_op jit(solution)/shard_map/ppermute | solution.py:25
  51.8 4.0 %expert_block.7 = (bf16[32,3584]{1,0:T(8,128)(2,1)S(1)}, bf16[32,3584]{1,0:T(8,128)(2,1)S(1)}) custom-call(bf16[80,3584]{1,0:T(8,128)(2,1)S(1)} %collective-permute-done.2.whole_ref.near_ref, bf16[32,3584]{1,0:T(8,128)(2,1)S(1)} %collective-permute-done.6.far_ref, bf16[10752,512]{1,0:T(8,128)(2,1)S(1)} %get-tuple-element.124.refs_0_, ...), custom_call_target="tpu_custom_call" | custom-call | flops 1024 | bytes 1024 | tf_op jit(solution)/shard_map/expert_block/pallas_call | solution.py:119
  56.3 6.5 %collective-permute-done.10.refs_3_ = bf16[32,3584]{1,0:T(8,128)(2,1)S(1)} collective-permute-done((bf16[32,3584]{1,0:T(8,128)(2,1)S(1)}, bf16[32,3584]{1,0:T(8,128)(2,1)S(1)}, u32[]{:S(2)}, u32[]{:S(2)}) %collective-permute-start.10) | collective-permute-done | bytes 229408 | tf_op jit(solution)/shard_map/ppermute | solution.py:25
  64.1 1.7 %collective-permute-done.7.far_ref = bf16[80,3584]{1,0:T(8,128)(2,1)S(1)} collective-permute-done((bf16[80,3584]{1,0:T(8,128)(2,1)S(1)}, bf16[80,3584]{1,0:T(8,128)(2,1)S(1)}, u32[]{:S(2)}, u32[]{:S(2)}) %collective-permute-start.7) | collective-permute-done | bytes 573472 | tf_op jit(solution)/shard_map/ppermute | solution.py:25
  67.6 3.9 %expert_block.8 = (bf16[80,3584]{1,0:T(8,128)(2,1)S(1)}, bf16[80,3584]{1,0:T(8,128)(2,1)S(1)}) custom-call(bf16[80,3584]{1,0:T(8,128)(2,1)S(1)} %collective-permute-done.near_ref, bf16[80,3584]{1,0:T(8,128)(2,1)S(1)} %collective-permute-done.7.far_ref, bf16[10752,512]{1,0:T(8,128)(2,1)S(1)} %get-tuple-element.124.refs_0_, ...), custom_call_target="tpu_custom_call" | custom-call | flops 1024 | bytes 1024 | tf_op jit(solution)/shard_map/expert_block/pallas_call | solution.py:119
  71.5 2.5 %collective-permute-start.19 = (bf16[80,3584]{1,0:T(8,128)(2,1)S(1)}, bf16[80,3584]{1,0:T(8,128)(2,1)S(1)}, u32[]{:S(2)}, u32[]{:S(2)}) collective-permute-start(bf16[80,3584]{1,0:T(8,128)(2,1)S(1)} %get-tuple-element.224), channel_id=1, source_target_pairs={{0,4},{1,5},{2,6},{3,7},{4,0},{5,1},{6,2},{7,3},{8,12},{9,13},{10,... | collective-permute-start | bytes 1720328 | tf_op jit(solution)/shard_map/ppermute | solution.py:25
  74.0 3.9 %expert_block.9 = (bf16[48,3584]{1,0:T(8,128)(2,1)S(1)}, bf16[48,3584]{1,0:T(8,128)(2,1)S(1)}) custom-call(bf16[80,3584]{1,0:T(8,128)(2,1)S(1)} %collective-permute-done.8.whole_ref.near_ref, bf16[48,3584]{1,0:T(8,128)(2,1)S(1)} %collective-permute-done.11.far_ref, bf16[10752,512]{1,0:T(8,128)(2,1)S(1)} %get-tuple-element.124.refs_0_, ...), custom_call_target="tpu_custom_call" | custom-call | flops 1024 | bytes 1024 | tf_op jit(solution)/shard_map/expert_block/pallas_call | solution.py:119
  79.3 4.0 %expert_block.10 = (bf16[32,3584]{1,0:T(8,128)(2,1)S(1)}, bf16[32,3584]{1,0:T(8,128)(2,1)S(1)}) custom-call(bf16[80,3584]{1,0:T(8,128)(2,1)S(1)} %collective-permute-done.8.whole_ref.near_ref, bf16[32,3584]{1,0:T(8,128)(2,1)S(1)} %collective-permute-done.12.far_ref, bf16[10752,512]{1,0:T(8,128)(2,1)S(1)} %get-tuple-element.124.refs_0_, ...), custom_call_target="tpu_custom_call" | custom-call | flops 1024 | bytes 1024 | tf_op jit(solution)/shard_map/expert_block/pallas_call | solution.py:119
  84.0 3.9 %expert_block.11 = (bf16[80,3584]{1,0:T(8,128)(2,1)S(1)}, bf16[80,3584]{1,0:T(8,128)(2,1)S(1)}) custom-call(bf16[80,3584]{1,0:T(8,128)(2,1)S(1)} %get-tuple-element.203.near_ref, bf16[80,3584]{1,0:T(8,128)(2,1)S(1)} %collective-permute-done.4.far_ref, bf16[10752,512]{1,0:T(8,128)(2,1)S(1)} %get-tuple-element.124.refs_0_, ...), custom_call_target="tpu_custom_call" | custom-call | flops 1024 | bytes 1024 | tf_op jit(solution)/shard_map/expert_block/pallas_call | solution.py:119
  88.0 6.3 %collective-permute-done.15.refs_2_ = bf16[80,3584]{1,0:T(8,128)(2,1)S(1)} collective-permute-done((bf16[80,3584]{1,0:T(8,128)(2,1)S(1)}, bf16[80,3584]{1,0:T(8,128)(2,1)S(1)}, u32[]{:S(2)}, u32[]{:S(2)}) %collective-permute-start.15) | collective-permute-done | bytes 573472 | tf_op jit(solution)/shard_map/ppermute | solution.py:25
  96.4 1.7 %collective-permute-done.19.whole_ref = bf16[80,3584]{1,0:T(8,128)(2,1)S(1)} collective-permute-done((bf16[80,3584]{1,0:T(8,128)(2,1)S(1)}, bf16[80,3584]{1,0:T(8,128)(2,1)S(1)}, u32[]{:S(2)}, u32[]{:S(2)}) %collective-permute-start.19) | collective-permute-done | bytes 573472 | tf_op jit(solution)/shard_map/ppermute | solution.py:25
  100.3 12.0 %collective-permute-done.18.refs_3_ = bf16[80,3584]{1,0:T(8,128)(2,1)S(1)} collective-permute-done((bf16[80,3584]{1,0:T(8,128)(2,1)S(1)}, bf16[80,3584]{1,0:T(8,128)(2,1)S(1)}, u32[]{:S(2)}, u32[]{:S(2)}) %collective-permute-start.18) | collective-permute-done | bytes 573472 | tf_op jit(solution)/shard_map/ppermute | solution.py:25
  112.6 10.3 %collective-permute-done.16.refs_0_ = bf16[80,3584]{1,0:T(8,128)(2,1)S(1)} collective-permute-done((bf16[80,3584]{1,0:T(8,128)(2,1)S(1)}, bf16[80,3584]{1,0:T(8,128)(2,1)S(1)}, u32[]{:S(2)}, u32[]{:S(2)}) %collective-permute-start.16) | collective-permute-done | bytes 573472 | tf_op jit(solution)/shard_map/ppermute | solution.py:25
  123.3 1.9 %score.1 = f32[8,16]{1,0:T(8,128)S(1)} custom-call(s32[1]{0:T(128)} %bitcast.own_ref, bf16[128,3584]{1,0:T(8,128)(2,1)S(1)} %copy-done, f32[3584]{0:T(1024)S(1)} %copy-done.2, s32[2,128]{1,0:T(2,128)S(1)} %bitcast.9, f32[2,128]{1,0:T(2,128)S(1)} %bitcast.10, bf16[128,3584]{1,0:T(8,128)(2,1)S(1)} %copy-done.1, f32[1,128]{1,0:T(1,128)S(1)} %bitcast.11, ...), custom_call_target="tpu_custom_call" | custom-call | flops 1024 | bytes 1024 | tf_op jit(solution)/shard_map/score/pallas_call | solution.py:182
  127.0 3.9 %all-to-all-start = ((f32[8,1,16]{2,1,0:T(1,128)}), f32[8,1,16]{2,1,0:T(1,128)S(1)}, u32[]{:S(2)}, u32[]{:S(2)}) async-start(f32[8,1,16]{2,1,0:T(1,128)} %bitcast.6), calls=%async_computation | async-start | bytes 8192 | tf_op jit(solution)/shard_map/all_to_all | solution.py:381
  131.0 6.3 %all-to-all-done = f32[8,1,16]{2,1,0:T(1,128)S(1)} async-done(((f32[8,1,16]{2,1,0:T(1,128)}), f32[8,1,16]{2,1,0:T(1,128)S(1)}, u32[]{:S(2)}, u32[]{:S(2)}) %all-to-all-start) | async-done | bytes 544 | tf_op jit(solution)/shard_map/all_to_all | solution.py:381
  (64 shorter events, 18.0 us)
Async XLA Ops:
  5.2 17.1 %collective-permute-start.3 = (bf16[10752,512]{1,0:T(8,128)(2,1)S(1)}, bf16[10752,512]{1,0:T(8,128)(2,1)S(1)}, u32[]{:S(2)}, u32[]{:S(2)}) collective-permute-start(bf16[10752,512]{1,0:T(8,128)(2,1)S(1)} %get-tuple-element.124.refs_0_), channel_id=1, source_target_pairs={{0,1},{1,0},{2,3},{3,2},{4,5},{5,4},{6,7},{7,6},{8,9},{9,8},{10,11... | collective-permute-start | bytes 33030152 | tf_op jit(solution)/shard_map/ppermute | solution.py:25
  5.7 29.6 %collective-permute-start.2 = (bf16[80,3584]{1,0:T(8,128)(2,1)S(1)}, bf16[80,3584]{1,0:T(8,128)(2,1)S(1)}, u32[]{:S(2)}, u32[]{:S(2)}) collective-permute-start(bf16[80,3584]{1,0:T(8,128)(2,1)S(1)} %get-tuple-element.123), channel_id=1, source_target_pairs={{0,8},{1,9},{2,10},{3,11},{4,12},{5,13},{6,14},{7,15},{8,0},{9,1},... | collective-permute-start | bytes 1720328 | tf_op jit(solution)/shard_map/ppermute | solution.py:25
  9.4 26.0 %collective-permute-start.4 = (bf16[80,3584]{1,0:T(8,128)(2,1)S(1)}, bf16[80,3584]{1,0:T(8,128)(2,1)S(1)}, u32[]{:S(2)}, u32[]{:S(2)}) collective-permute-start(bf16[80,3584]{1,0:T(8,128)(2,1)S(1)} %get-tuple-element.203.near_ref), channel_id=1, source_target_pairs={{0,2},{1,3},{2,0},{3,1},{4,6},{5,7},{6,4},{7,5},{8,10},{9,11},{10,... | collective-permute-start | bytes 1720328 | tf_op jit(solution)/shard_map/ppermute | solution.py:25
  10.9 30.1 %collective-permute-start.1 = (bf16[80,3584]{1,0:T(8,128)(2,1)S(1)}, bf16[80,3584]{1,0:T(8,128)(2,1)S(1)}, u32[]{:S(2)}, u32[]{:S(2)}) collective-permute-start(bf16[80,3584]{1,0:T(8,128)(2,1)S(1)} %get-tuple-element.121), channel_id=1, source_target_pairs={{0,2},{1,3},{2,0},{3,1},{4,6},{5,7},{6,4},{7,5},{8,10},{9,11},{10,... | collective-permute-start | bytes 1720328 | tf_op jit(solution)/shard_map/ppermute | solution.py:25
  11.4 29.6 %collective-permute-start = (bf16[80,3584]{1,0:T(8,128)(2,1)S(1)}, bf16[80,3584]{1,0:T(8,128)(2,1)S(1)}, u32[]{:S(2)}, u32[]{:S(2)}) collective-permute-start(bf16[80,3584]{1,0:T(8,128)(2,1)S(1)} %get-tuple-element.121), channel_id=1, source_target_pairs={{0,4},{1,5},{2,6},{3,7},{4,0},{5,1},{6,2},{7,3},{8,12},{9,13},{10,... | collective-permute-start | bytes 1720328 | tf_op jit(solution)/shard_map/ppermute | solution.py:25
  35.4 11.0 %collective-permute-start.5 = (bf16[48,3584]{1,0:T(8,128)(2,1)S(1)}, bf16[48,3584]{1,0:T(8,128)(2,1)S(1)}, u32[]{:S(2)}, u32[]{:S(2)}) collective-permute-start(bf16[48,3584]{1,0:T(8,128)(2,1)S(1)} %get-tuple-element.136), channel_id=1, source_target_pairs={{0,2},{1,3},{2,0},{3,1},{4,6},{5,7},{6,4},{7,5},{8,10},{9,11},{10,... | collective-permute-start | bytes 1032200 | tf_op jit(solution)/shard_map/ppermute | solution.py:25
  37.0 19.2 %collective-permute-start.8 = (bf16[80,3584]{1,0:T(8,128)(2,1)S(1)}, bf16[80,3584]{1,0:T(8,128)(2,1)S(1)}, u32[]{:S(2)}, u32[]{:S(2)}) collective-permute-start(bf16[80,3584]{1,0:T(8,128)(2,1)S(1)} %get-tuple-element.157), channel_id=1, source_target_pairs={{0,12},{1,13},{2,14},{3,15},{4,8},{5,9},{6,10},{7,11},{8,4},{9,5},... | collective-permute-start | bytes 1720328 | tf_op jit(solution)/shard_map/ppermute | solution.py:25
  40.5 11.3 %collective-permute-start.6 = (bf16[32,3584]{1,0:T(8,128)(2,1)S(1)}, bf16[32,3584]{1,0:T(8,128)(2,1)S(1)}, u32[]{:S(2)}, u32[]{:S(2)}) collective-permute-start(bf16[32,3584]{1,0:T(8,128)(2,1)S(1)} %get-tuple-element.146), channel_id=1, source_target_pairs={{0,2},{1,3},{2,0},{3,1},{4,6},{5,7},{6,4},{7,5},{8,10},{9,11},{10,... | collective-permute-start | bytes 688136 | tf_op jit(solution)/shard_map/ppermute | solution.py:25
  41.0 24.7 %collective-permute-start.7 = (bf16[80,3584]{1,0:T(8,128)(2,1)S(1)}, bf16[80,3584]{1,0:T(8,128)(2,1)S(1)}, u32[]{:S(2)}, u32[]{:S(2)}) collective-permute-start(bf16[80,3584]{1,0:T(8,128)(2,1)S(1)} %collective-permute-done.1), channel_id=1, source_target_pairs={{0,4},{1,5},{2,6},{3,7},{4,0},{5,1},{6,2},{7,3},{8,12},{9,13},{10,... | collective-permute-start | bytes 1720328 | tf_op jit(solution)/shard_map/ppermute | solution.py:25
  50.1 12.7 %collective-permute-start.9 = (bf16[48,3584]{1,0:T(8,128)(2,1)S(1)}, bf16[48,3584]{1,0:T(8,128)(2,1)S(1)}, u32[]{:S(2)}, u32[]{:S(2)}) collective-permute-start(bf16[48,3584]{1,0:T(8,128)(2,1)S(1)} %get-tuple-element.160), channel_id=1, source_target_pairs={{0,2},{1,3},{2,0},{3,1},{4,6},{5,7},{6,4},{7,5},{8,10},{9,11},{10,... | collective-permute-start | bytes 1032200 | tf_op jit(solution)/shard_map/ppermute | solution.py:25
  55.8 7.0 %collective-permute-start.10 = (bf16[32,3584]{1,0:T(8,128)(2,1)S(1)}, bf16[32,3584]{1,0:T(8,128)(2,1)S(1)}, u32[]{:S(2)}, u32[]{:S(2)}) collective-permute-start(bf16[32,3584]{1,0:T(8,128)(2,1)S(1)} %get-tuple-element.161), channel_id=1, source_target_pairs={{0,2},{1,3},{2,0},{3,1},{4,6},{5,7},{6,4},{7,5},{8,10},{9,11},{10,... | collective-permute-start | bytes 688136 | tf_op jit(solution)/shard_map/ppermute | solution.py:25
  62.8 11.2 %collective-permute-start.11 = (bf16[48,3584]{1,0:T(8,128)(2,1)S(1)}, bf16[48,3584]{1,0:T(8,128)(2,1)S(1)}, u32[]{:S(2)}, u32[]{:S(2)}) collective-permute-start(bf16[48,3584]{1,0:T(8,128)(2,1)S(1)} %get-tuple-element.182), channel_id=1, source_target_pairs={{0,2},{1,3},{2,0},{3,1},{4,6},{5,7},{6,4},{7,5},{8,10},{9,11},{10,... | collective-permute-start | bytes 1032200 | tf_op jit(solution)/shard_map/ppermute | solution.py:25
  66.0 28.2 %collective-permute-start.15 = (bf16[80,3584]{1,0:T(8,128)(2,1)S(1)}, bf16[80,3584]{1,0:T(8,128)(2,1)S(1)}, u32[]{:S(2)}, u32[]{:S(2)}) collective-permute-start(bf16[80,3584]{1,0:T(8,128)(2,1)S(1)} %total.4), channel_id=1, source_target_pairs={{0,8},{1,9},{2,10},{3,11},{4,12},{5,13},{6,14},{7,15},{8,0},{9,1},... | collective-permute-start | bytes 1720328 | tf_op jit(solution)/shard_map/ppermute | solution.py:25
  66.7 12.6 %collective-permute-start.12 = (bf16[32,3584]{1,0:T(8,128)(2,1)S(1)}, bf16[32,3584]{1,0:T(8,128)(2,1)S(1)}, u32[]{:S(2)}, u32[]{:S(2)}) collective-permute-start(bf16[32,3584]{1,0:T(8,128)(2,1)S(1)} %get-tuple-element.191), channel_id=1, source_target_pairs={{0,2},{1,3},{2,0},{3,1},{4,6},{5,7},{6,4},{7,5},{8,10},{9,11},{10,... | collective-permute-start | bytes 688136 | tf_op jit(solution)/shard_map/ppermute | solution.py:25
  71.5 26.7 %collective-permute-start.19 = (bf16[80,3584]{1,0:T(8,128)(2,1)S(1)}, bf16[80,3584]{1,0:T(8,128)(2,1)S(1)}, u32[]{:S(2)}, u32[]{:S(2)}) collective-permute-start(bf16[80,3584]{1,0:T(8,128)(2,1)S(1)} %get-tuple-element.224), channel_id=1, source_target_pairs={{0,4},{1,5},{2,6},{3,7},{4,0},{5,1},{6,2},{7,3},{8,12},{9,13},{10,... | collective-permute-start | bytes 1720328 | tf_op jit(solution)/shard_map/ppermute | solution.py:25
  77.9 16.4 %collective-permute-start.13 = (bf16[48,3584]{1,0:T(8,128)(2,1)S(1)}, bf16[48,3584]{1,0:T(8,128)(2,1)S(1)}, u32[]{:S(2)}, u32[]{:S(2)}) collective-permute-start(bf16[48,3584]{1,0:T(8,128)(2,1)S(1)} %get-tuple-element.199), channel_id=1, source_target_pairs={{0,2},{1,3},{2,0},{3,1},{4,6},{5,7},{6,4},{7,5},{8,10},{9,11},{10,... | collective-permute-start | bytes 1032200 | tf_op jit(solution)/shard_map/ppermute | solution.py:25
  83.2 11.1 %collective-permute-start.14 = (bf16[32,3584]{1,0:T(8,128)(2,1)S(1)}, bf16[32,3584]{1,0:T(8,128)(2,1)S(1)}, u32[]{:S(2)}, u32[]{:S(2)}) collective-permute-start(bf16[32,3584]{1,0:T(8,128)(2,1)S(1)} %get-tuple-element.200), channel_id=1, source_target_pairs={{0,2},{1,3},{2,0},{3,1},{4,6},{5,7},{6,4},{7,5},{8,10},{9,11},{10,... | collective-permute-start | bytes 688136 | tf_op jit(solution)/shard_map/ppermute | solution.py:25
  94.6 17.7 %collective-permute-start.18 = (bf16[80,3584]{1,0:T(8,128)(2,1)S(1)}, bf16[80,3584]{1,0:T(8,128)(2,1)S(1)}, u32[]{:S(2)}, u32[]{:S(2)}) collective-permute-start(bf16[80,3584]{1,0:T(8,128)(2,1)S(1)} %total.5), channel_id=1, source_target_pairs={{0,12},{1,13},{2,14},{3,15},{4,8},{5,9},{6,10},{7,11},{8,4},{9,5},... | collective-permute-start | bytes 1720328 | tf_op jit(solution)/shard_map/ppermute | solution.py:25
  95.0 17.3 %collective-permute-start.17 = (bf16[80,3584]{1,0:T(8,128)(2,1)S(1)}, bf16[80,3584]{1,0:T(8,128)(2,1)S(1)}, u32[]{:S(2)}, u32[]{:S(2)}) collective-permute-start(bf16[80,3584]{1,0:T(8,128)(2,1)S(1)} %get-tuple-element.216), channel_id=1, source_target_pairs={{0,2},{1,3},{2,0},{3,1},{4,6},{5,7},{6,4},{7,5},{8,10},{9,11},{10,... | collective-permute-start | bytes 1720328 | tf_op jit(solution)/shard_map/ppermute | solution.py:25
  96.4 26.5 %collective-permute-start.16 = (bf16[80,3584]{1,0:T(8,128)(2,1)S(1)}, bf16[80,3584]{1,0:T(8,128)(2,1)S(1)}, u32[]{:S(2)}, u32[]{:S(2)}) collective-permute-start(bf16[80,3584]{1,0:T(8,128)(2,1)S(1)} %get-tuple-element.214), channel_id=1, source_target_pairs={{0,4},{1,5},{2,6},{3,7},{4,0},{5,1},{6,2},{7,3},{8,12},{9,13},{10,... | collective-permute-start | bytes 1720328 | tf_op jit(solution)/shard_map/ppermute | solution.py:25
  98.2 24.8 %collective-permute-start.20 = (bf16[64,3584]{1,0:T(8,128)(2,1)S(1)}, bf16[64,3584]{1,0:T(8,128)(2,1)S(1)}, u32[]{:S(2)}, u32[]{:S(2)}) collective-permute-start(bf16[64,3584]{1,0:T(8,128)(2,1)S(1)} %get-tuple-element.231), channel_id=1, source_target_pairs={{0,2},{1,3},{2,0},{3,1},{4,6},{5,7},{6,4},{7,5},{8,10},{9,11},{10,... | collective-permute-start | bytes 1376264 | tf_op jit(solution)/shard_map/ppermute | solution.py:25
  99.1 23.9 %collective-permute-start.21 = (bf16[16,3584]{1,0:T(8,128)(2,1)S(1)}, bf16[16,3584]{1,0:T(8,128)(2,1)S(1)}, u32[]{:S(2)}, u32[]{:S(2)}) collective-permute-start(bf16[16,3584]{1,0:T(8,128)(2,1)S(1)} %get-tuple-element.233), channel_id=1, source_target_pairs={{0,2},{1,3},{2,0},{3,1},{4,6},{5,7},{6,4},{7,5},{8,10},{9,11},{10,... | collective-permute-start | bytes 344072 | tf_op jit(solution)/shard_map/ppermute | solution.py:25
  125.2 1.2 collective-permute-start.22
  127.0 10.3 %all-to-all-start = ((f32[8,1,16]{2,1,0:T(1,128)}), f32[8,1,16]{2,1,0:T(1,128)S(1)}, u32[]{:S(2)}, u32[]{:S(2)}) async-start(f32[8,1,16]{2,1,0:T(1,128)} %bitcast.6), calls=%async_computation | async-start | bytes 8192 | tf_op jit(solution)/shard_map/all_to_all | solution.py:381
  (9 other events, 280.6 us)

commit v17 on v14

--- a/solution.py
+++ b/solution.py
@@ -229,6 +229,28 @@
     )(whole)
 
 
+def join_kernel(*refs):
+    *refs, out_ref = refs
+    first = 0
+    for ref in refs:
+        out_ref[first : first + ref.shape[0], :] = ref[...]
+        first += ref.shape[0]
+
+
+def join(arrays):
+    vmem = pl.BlockSpec(memory_space=pltpu.VMEM)
+    rows = sum(array.shape[0] for array in arrays)
+    return pl.pallas_call(
+        join_kernel,
+        out_shape=jax.ShapeDtypeStruct((rows, arrays[0].shape[1]), BF16),
+        in_specs=[vmem] * len(arrays),
+        out_specs=vmem,
+        compiler_params=pltpu.CompilerParams(vmem_limit_bytes=VMEM_LIMIT),
+        cost_estimate=COST,
+        name="join",
+    )(*arrays)
+
+
 def total_kernel(count, *refs):
     *refs, out_ref = refs
     for side in (refs[:count], refs[count:]):
@@ -301,6 +323,8 @@
         for (first, _), piece in zip(pieces, far[k]):
             there = order.mark_one(piece)
             part, other = order.mark(*expert_block(order.late(near[k]), first, there, weights))
+            if k == 2 and first:
+                far[0], far[1], other = lax.optimization_barrier((far[0], far[1], other))
             mine[k].append(part)
             theirs[k].append(swap(other, side))
 
@@ -319,11 +343,13 @@
         back[k] = order.mark_one(back[k])
 
     leave(2)
-    far[0], far[1] = swap(near[0], side), swap(near[1], side)
+    far[1] = [swap(piece, side) for piece in cut(near[1], pieces)]
     leave(1)
-    weights[1] = order.mark_one(weights[1])
+    *far[1], weights[1] = order.mark(*far[1], weights[1])
+    far[1] = swap(join(far[1]), spread)
+    near[0], weights[1] = lax.optimization_barrier((near[0], weights[1]))
+    far[0] = swap(near[0], side)
     arrive(2)
-    far[0] = order.mark_one(far[0])
     last = (capacity - 16, 16)
     for k in range(3, experts + 1):
         if k > 3:
@@ -332,12 +358,8 @@
         if k < experts:
             leave(k)
         if k == 3:
-            far[1] = order.mark_one(far[1])
             arrive(1)
-            far[1] = swap(order.late(far[1]), spread)
         if k > 3:
-            if k == experts:
-                far[1], *theirs[k - 2] = lax.optimization_barrier((far[1], *theirs[k - 2]))
             home(k - 2)
             leave_back(k - 2)
         if k == experts:

time: 137 us -> 135 us (0.985)
  waiting for transfers between devices: 72.6 us -> 58.3 us
  starting transfers between devices: 30.9 us -> 43.3 us
    ppermute x22 -> x23, waiting for transfers between devices: 66.4 us -> 52.1 us  [swap(): return lax.ppermute(value, 'expert', pairs)]
    ppermute x22 -> x23, starting transfers between devices: 27 us -> 39.9 us  [swap(): return lax.ppermute(value, 'expert', pairs)]
  transfers between devices with their start and end apart: 23 -> 24, of which waited for: 10 -> 10; matrix products, arithmetic and copies ran while one was open for 0% -> 0% of each run, Pallas kernels for 18% -> 18%
where the time goes in v17:
time: 135 us
  waiting for transfers between devices  58.3 us (43%)
  starting transfers between devices  43.3 us (32%)
  Pallas kernels  31.7 us (23%)
    ppermute x23, waiting for transfers between devices, swap(): return lax.ppermute(value, 'expert', pairs)  52.1 us
    ppermute x23, starting transfers between devices, swap(): return lax.ppermute(value, 'expert', pairs)  39.9 us
    pallas_call x6, Pallas kernels, expert_block(): pl.pallas_call(functools.partial(expert_kernel, first), out_shape=[jax.Sh...  23.3 us
    all_to_all x1, waiting for transfers between devices, per_device(): lax.all_to_all(local, 'expert', split_axis=0, concat_axis=0, tiled=True)  6.15 us
    pallas_call x1, Pallas kernels, pack(): pl.pallas_call(pack_kernel, out_shape=[jax.ShapeDtypeStruct(shape, BF16)...  4.53 us
    all_to_all x1, starting transfers between devices, per_device(): lax.all_to_all(local, 'expert', split_axis=0, concat_axis=0, tiled=True)  3.42 us
  transfers between devices with their start and end apart: 24, of which 10 were waited for; matrix products, arithmetic and copies ran while one was open for 0% of the time, Pallas kernels for 18%

profile of v17, /device:TPU:0, one launch (start us, length us, event | category | flops | bytes accessed | tf_op | source)
XLA Modules:
  0.0 135.2 jit_solution(7220732674787085383)
XLA Ops:
  0.6 4.5 %pack.1 = (bf16[80,3584]{1,0:T(8,128)(2,1)S(1)}, bf16[80,3584]{1,0:T(8,128)(2,1)S(1)}, bf16[80,3584]{1,0:T(8,128)(2,1)S(1)}, bf16[80,3584]{1,0:T(8,128)(2,1)S(1)}, bf16[10752,512]{1,0:T(8,128)(2,1)S(1)}) custom-call(s32[1]{0:T(128)} %bitcast.own_ref, bf16[128,3584]{1,0:T(8,128)(2,1)} %tokens_ref.1, f32[3584]{0:T(1024)} %gain_hbm.1, s32[2,128]{1,0:T(2,128)} %bitcast.8, ...), custom_call_target="tpu_custom_call" | custom-call | flops 1024 | bytes 1024 | tf_op jit(solution)/shard_map/pack/pallas_call | solution.py:78
  5.7 3.7 %collective-permute-start.1 = (bf16[80,3584]{1,0:T(8,128)(2,1)S(1)}, bf16[80,3584]{1,0:T(8,128)(2,1)S(1)}, u32[]{:S(2)}, u32[]{:S(2)}) collective-permute-start(bf16[80,3584]{1,0:T(8,128)(2,1)S(1)} %get-tuple-element.124), channel_id=1, source_target_pairs={{0,8},{1,9},{2,10},{3,11},{4,12},{5,13},{6,14},{7,15},{8,0},{9,1},... | collective-permute-start | bytes 1720328 | tf_op jit(solution)/shard_map/ppermute | solution.py:25
  13.1 11.4 %collective-permute-done.3.refs_1_ = bf16[32,3584]{1,0:T(8,128)(2,1)S(1)} collective-permute-done((bf16[32,3584]{1,0:T(8,128)(2,1)S(1)}, bf16[32,3584]{1,0:T(8,128)(2,1)S(1)}, u32[]{:S(2)}, u32[]{:S(2)}) %collective-permute-start.3) | collective-permute-done | bytes 229408 | tf_op jit(solution)/shard_map/ppermute | solution.py:25
  27.7 7.6 %collective-permute-done.1.whole_ref.near_ref = bf16[80,3584]{1,0:T(8,128)(2,1)S(1)} collective-permute-done((bf16[80,3584]{1,0:T(8,128)(2,1)S(1)}, bf16[80,3584]{1,0:T(8,128)(2,1)S(1)}, u32[]{:S(2)}, u32[]{:S(2)}) %collective-permute-start.1) | collective-permute-done | bytes 573472 | tf_op jit(solution)/shard_map/ppermute | solution.py:25
  37.0 3.5 %collective-permute-start.7 = (bf16[80,3584]{1,0:T(8,128)(2,1)S(1)}, bf16[80,3584]{1,0:T(8,128)(2,1)S(1)}, u32[]{:S(2)}, u32[]{:S(2)}) collective-permute-start(bf16[80,3584]{1,0:T(8,128)(2,1)S(1)} %get-tuple-element.157), channel_id=1, source_target_pairs={{0,12},{1,13},{2,14},{3,15},{4,8},{5,9},{6,10},{7,11},{8,4},{9,5},... | collective-permute-start | bytes 1720328 | tf_op jit(solution)/shard_map/ppermute | solution.py:25
  41.0 6.0 %collective-permute-done.5.far_ref = bf16[48,3584]{1,0:T(8,128)(2,1)S(1)} collective-permute-done((bf16[48,3584]{1,0:T(8,128)(2,1)S(1)}, bf16[48,3584]{1,0:T(8,128)(2,1)S(1)}, u32[]{:S(2)}, u32[]{:S(2)}) %collective-permute-start.5) | collective-permute-done | bytes 344096 | tf_op jit(solution)/shard_map/ppermute | solution.py:25
  47.0 3.7 %expert_block.6 = (bf16[48,3584]{1,0:T(8,128)(2,1)S(1)}, bf16[48,3584]{1,0:T(8,128)(2,1)S(1)}) custom-call(bf16[80,3584]{1,0:T(8,128)(2,1)S(1)} %collective-permute-done.1.whole_ref.near_ref, bf16[48,3584]{1,0:T(8,128)(2,1)S(1)} %collective-permute-done.5.far_ref, bf16[10752,512]{1,0:T(8,128)(2,1)S(1)} %get-tuple-element.127.refs_0_, ...), custom_call_target="tpu_custom_call" | custom-call | flops 1024 | bytes 1024 | tf_op jit(solution)/shard_map/expert_block/pallas_call | solution.py:119
  52.4 4.0 %expert_block.7 = (bf16[32,3584]{1,0:T(8,128)(2,1)S(1)}, bf16[32,3584]{1,0:T(8,128)(2,1)S(1)}) custom-call(bf16[80,3584]{1,0:T(8,128)(2,1)S(1)} %collective-permute-done.1.whole_ref.near_ref, bf16[32,3584]{1,0:T(8,128)(2,1)S(1)} %collective-permute-done.6.far_ref, bf16[10752,512]{1,0:T(8,128)(2,1)S(1)} %get-tuple-element.127.refs_0_, ...), custom_call_target="tpu_custom_call" | custom-call | flops 1024 | bytes 1024 | tf_op jit(solution)/shard_map/expert_block/pallas_call | solution.py:119
  56.4 5.0 %collective-permute-done.10.far_ref = bf16[80,3584]{1,0:T(8,128)(2,1)S(1)} collective-permute-done((bf16[80,3584]{1,0:T(8,128)(2,1)S(1)}, bf16[80,3584]{1,0:T(8,128)(2,1)S(1)}, u32[]{:S(2)}, u32[]{:S(2)}) %collective-permute-start.10) | collective-permute-done | bytes 573472 | tf_op jit(solution)/shard_map/ppermute | solution.py:25
  61.5 8.4 %collective-permute-done.11.refs_3_ = bf16[32,3584]{1,0:T(8,128)(2,1)S(1)} collective-permute-done((bf16[32,3584]{1,0:T(8,128)(2,1)S(1)}, bf16[32,3584]{1,0:T(8,128)(2,1)S(1)}, u32[]{:S(2)}, u32[]{:S(2)}) %collective-permute-start.11) | collective-permute-done | bytes 229408 | tf_op jit(solution)/shard_map/ppermute | solution.py:25
  70.4 2.1 %collective-permute-start.13 = (bf16[32,3584]{1,0:T(8,128)(2,1)S(1)}, bf16[32,3584]{1,0:T(8,128)(2,1)S(1)}, u32[]{:S(2)}, u32[]{:S(2)}) collective-permute-start(bf16[32,3584]{1,0:T(8,128)(2,1)S(1)} %get-tuple-element.193), channel_id=1, source_target_pairs={{0,2},{1,3},{2,0},{3,1},{4,6},{5,7},{6,4},{7,5},{8,10},{9,11},{10,... | collective-permute-start | bytes 688136 | tf_op jit(solution)/shard_map/ppermute | solution.py:25
  72.4 3.9 %expert_block.8 = (bf16[80,3584]{1,0:T(8,128)(2,1)S(1)}, bf16[80,3584]{1,0:T(8,128)(2,1)S(1)}) custom-call(bf16[80,3584]{1,0:T(8,128)(2,1)S(1)} %collective-permute-done.near_ref, bf16[80,3584]{1,0:T(8,128)(2,1)S(1)} %collective-permute-done.10.far_ref, bf16[10752,512]{1,0:T(8,128)(2,1)S(1)} %get-tuple-element.127.refs_0_, ...), custom_call_target="tpu_custom_call" | custom-call | flops 1024 | bytes 1024 | tf_op jit(solution)/shard_map/expert_block/pallas_call | solution.py:119
  76.3 2.7 %collective-permute-start.20 = (bf16[80,3584]{1,0:T(8,128)(2,1)S(1)}, bf16[80,3584]{1,0:T(8,128)(2,1)S(1)}, u32[]{:S(2)}, u32[]{:S(2)}) collective-permute-start(bf16[80,3584]{1,0:T(8,128)(2,1)S(1)} %get-tuple-element.226), channel_id=1, source_target_pairs={{0,4},{1,5},{2,6},{3,7},{4,0},{5,1},{6,2},{7,3},{8,12},{9,13},{10,... | collective-permute-start | bytes 1720328 | tf_op jit(solution)/shard_map/ppermute | solution.py:25
  79.1 3.9 %expert_block.9 = (bf16[48,3584]{1,0:T(8,128)(2,1)S(1)}, bf16[48,3584]{1,0:T(8,128)(2,1)S(1)}) custom-call(bf16[80,3584]{1,0:T(8,128)(2,1)S(1)} %collective-permute-done.7.whole_ref.near_ref, bf16[48,3584]{1,0:T(8,128)(2,1)S(1)} %collective-permute-done.12.far_ref, bf16[10752,512]{1,0:T(8,128)(2,1)S(1)} %get-tuple-element.127.refs_0_, ...), custom_call_target="tpu_custom_call" | custom-call | flops 1024 | bytes 1024 | tf_op jit(solution)/shard_map/expert_block/pallas_call | solution.py:119
  83.1 4.0 %expert_block.10 = (bf16[32,3584]{1,0:T(8,128)(2,1)S(1)}, bf16[32,3584]{1,0:T(8,128)(2,1)S(1)}) custom-call(bf16[80,3584]{1,0:T(8,128)(2,1)S(1)} %collective-permute-done.7.whole_ref.near_ref, bf16[32,3584]{1,0:T(8,128)(2,1)S(1)} %collective-permute-done.13.far_ref, bf16[10752,512]{1,0:T(8,128)(2,1)S(1)} %get-tuple-element.127.refs_0_, ...), custom_call_target="tpu_custom_call" | custom-call | flops 1024 | bytes 1024 | tf_op jit(solution)/shard_map/expert_block/pallas_call | solution.py:119
  87.0 2.1 %collective-permute-start.15 = (bf16[32,3584]{1,0:T(8,128)(2,1)S(1)}, bf16[32,3584]{1,0:T(8,128)(2,1)S(1)}, u32[]{:S(2)}, u32[]{:S(2)}) collective-permute-start(bf16[32,3584]{1,0:T(8,128)(2,1)S(1)} %get-tuple-element.202), channel_id=1, source_target_pairs={{0,2},{1,3},{2,0},{3,1},{4,6},{5,7},{6,4},{7,5},{8,10},{9,11},{10,... | collective-permute-start | bytes 688136 | tf_op jit(solution)/shard_map/ppermute | solution.py:25
  89.1 3.9 %expert_block.11 = (bf16[80,3584]{1,0:T(8,128)(2,1)S(1)}, bf16[80,3584]{1,0:T(8,128)(2,1)S(1)}) custom-call(bf16[80,3584]{1,0:T(8,128)(2,1)S(1)} %get-tuple-element.205.near_ref, bf16[80,3584]{1,0:T(8,128)(2,1)S(1)} %collective-permute-done.9.far_ref, bf16[10752,512]{1,0:T(8,128)(2,1)S(1)} %get-tuple-element.127.refs_0_, ...), custom_call_target="tpu_custom_call" | custom-call | flops 1024 | bytes 1024 | tf_op jit(solution)/shard_map/expert_block/pallas_call | solution.py:119
  95.1 2.0 %collective-permute-start.18 = (bf16[80,3584]{1,0:T(8,128)(2,1)S(1)}, bf16[80,3584]{1,0:T(8,128)(2,1)S(1)}, u32[]{:S(2)}, u32[]{:S(2)}) collective-permute-start(bf16[80,3584]{1,0:T(8,128)(2,1)S(1)} %get-tuple-element.218), channel_id=1, source_target_pairs={{0,2},{1,3},{2,0},{3,1},{4,6},{5,7},{6,4},{7,5},{8,10},{9,11},{10,... | collective-permute-start | bytes 1720328 | tf_op jit(solution)/shard_map/ppermute | solution.py:25
  97.2 10.6 %collective-permute-start.21 = (bf16[64,3584]{1,0:T(8,128)(2,1)S(1)}, bf16[64,3584]{1,0:T(8,128)(2,1)S(1)}, u32[]{:S(2)}, u32[]{:S(2)}) collective-permute-start(bf16[64,3584]{1,0:T(8,128)(2,1)S(1)} %get-tuple-element.233), channel_id=1, source_target_pairs={{0,2},{1,3},{2,0},{3,1},{4,6},{5,7},{6,4},{7,5},{8,10},{9,11},{10,... | collective-permute-start | bytes 1376264 | tf_op jit(solution)/shard_map/ppermute | solution.py:25
  107.9 3.4 %collective-permute-done.19.refs_3_ = bf16[80,3584]{1,0:T(8,128)(2,1)S(1)} collective-permute-done((bf16[80,3584]{1,0:T(8,128)(2,1)S(1)}, bf16[80,3584]{1,0:T(8,128)(2,1)S(1)}, u32[]{:S(2)}, u32[]{:S(2)}) %collective-permute-start.19) | collective-permute-done | bytes 573472 | tf_op jit(solution)/shard_map/ppermute | solution.py:25
  111.5 8.8 %collective-permute-done.17.refs_0_ = bf16[80,3584]{1,0:T(8,128)(2,1)S(1)} collective-permute-done((bf16[80,3584]{1,0:T(8,128)(2,1)S(1)}, bf16[80,3584]{1,0:T(8,128)(2,1)S(1)}, u32[]{:S(2)}, u32[]{:S(2)}) %collective-permute-start.17) | collective-permute-done | bytes 573472 | tf_op jit(solution)/shard_map/ppermute | solution.py:25
  122.1 2.6 %score.1 = f32[16,16]{1,0:T(8,128)} custom-call(s32[1]{0:T(128)} %bitcast.own_ref, bf16[128,3584]{1,0:T(8,128)(2,1)S(1)} %copy-done, f32[3584]{0:T(1024)S(1)} %copy-done.2, s32[2,128]{1,0:T(2,128)S(1)} %bitcast.9, f32[2,128]{1,0:T(2,128)S(1)} %bitcast.10, bf16[128,3584]{1,0:T(8,128)(2,1)S(1)} %copy-done.1, f32[1,128]{1,0:T(1,128)S(1)} %bitcast.11, ...), custom_call_target="tpu_custom_call" | custom-call | flops 1024 | bytes 1024 | tf_op jit(solution)/shard_map/score/pallas_call | solution.py:182
  124.6 3.4 %all-to-all-start = ((f32[16,1,16]{2,1,0:T(1,128)}), f32[16,1,16]{2,1,0:T(1,128)S(1)}, u32[]{:S(2)}, u32[]{:S(2)}) async-start(f32[16,1,16]{2,1,0:T(1,128)} %bitcast.6), calls=%async_computation | async-start | bytes 16384 | tf_op jit(solution)/shard_map/all_to_all | solution.py:401
  128.3 6.1 %all-to-all-done = f32[16,1,16]{2,1,0:T(1,128)S(1)} async-done(((f32[16,1,16]{2,1,0:T(1,128)}), f32[16,1,16]{2,1,0:T(1,128)S(1)}, u32[]{:S(2)}, u32[]{:S(2)}) %all-to-all-start) | async-done | bytes 1056 | tf_op jit(solution)/shard_map/all_to_all | solution.py:401
  (65 shorter events, 17.0 us)
Async XLA Ops:
  5.2 19.3 %collective-permute-start.4 = (bf16[10752,512]{1,0:T(8,128)(2,1)S(1)}, bf16[10752,512]{1,0:T(8,128)(2,1)S(1)}, u32[]{:S(2)}, u32[]{:S(2)}) collective-permute-start(bf16[10752,512]{1,0:T(8,128)(2,1)S(1)} %get-tuple-element.127.refs_0_), channel_id=1, source_target_pairs={{0,1},{1,0},{2,3},{3,2},{4,5},{5,4},{6,7},{7,6},{8,9},{9,8},{10,11... | collective-permute-start | bytes 33030152 | tf_op jit(solution)/shard_map/ppermute | solution.py:25
  5.7 29.6 %collective-permute-start.1 = (bf16[80,3584]{1,0:T(8,128)(2,1)S(1)}, bf16[80,3584]{1,0:T(8,128)(2,1)S(1)}, u32[]{:S(2)}, u32[]{:S(2)}) collective-permute-start(bf16[80,3584]{1,0:T(8,128)(2,1)S(1)} %get-tuple-element.124), channel_id=1, source_target_pairs={{0,8},{1,9},{2,10},{3,11},{4,12},{5,13},{6,14},{7,15},{8,0},{9,1},... | collective-permute-start | bytes 1720328 | tf_op jit(solution)/shard_map/ppermute | solution.py:25
  9.4 15.1 %collective-permute-start.2 = (bf16[48,3584]{1,0:T(8,128)(2,1)S(1)}, bf16[48,3584]{1,0:T(8,128)(2,1)S(1)}, u32[]{:S(2)}, u32[]{:S(2)}) collective-permute-start(bf16[48,3584]{1,0:T(8,128)(2,1)S(1)} %get-tuple-element.125), channel_id=1, source_target_pairs={{0,2},{1,3},{2,0},{3,1},{4,6},{5,7},{6,4},{7,5},{8,10},{9,11},{10,... | collective-permute-start | bytes 1032200 | tf_op jit(solution)/shard_map/ppermute | solution.py:25
  11.0 29.5 %collective-permute-start = (bf16[80,3584]{1,0:T(8,128)(2,1)S(1)}, bf16[80,3584]{1,0:T(8,128)(2,1)S(1)}, u32[]{:S(2)}, u32[]{:S(2)}) collective-permute-start(bf16[80,3584]{1,0:T(8,128)(2,1)S(1)} %get-tuple-element.122.whole_ref), channel_id=1, source_target_pairs={{0,4},{1,5},{2,6},{3,7},{4,0},{5,1},{6,2},{7,3},{8,12},{9,13},{10,... | collective-permute-start | bytes 1720328 | tf_op jit(solution)/shard_map/ppermute | solution.py:25
  12.6 12.0 %collective-permute-start.3 = (bf16[32,3584]{1,0:T(8,128)(2,1)S(1)}, bf16[32,3584]{1,0:T(8,128)(2,1)S(1)}, u32[]{:S(2)}, u32[]{:S(2)}) collective-permute-start(bf16[32,3584]{1,0:T(8,128)(2,1)S(1)} %get-tuple-element.126), channel_id=1, source_target_pairs={{0,2},{1,3},{2,0},{3,1},{4,6},{5,7},{6,4},{7,5},{8,10},{9,11},{10,... | collective-permute-start | bytes 688136 | tf_op jit(solution)/shard_map/ppermute | solution.py:25
  24.5 31.9 %collective-permute-start.9 = (bf16[80,3584]{1,0:T(8,128)(2,1)S(1)}, bf16[80,3584]{1,0:T(8,128)(2,1)S(1)}, u32[]{:S(2)}, u32[]{:S(2)}) collective-permute-start(bf16[80,3584]{1,0:T(8,128)(2,1)S(1)} %get-tuple-element.205.near_ref), channel_id=1, source_target_pairs={{0,2},{1,3},{2,0},{3,1},{4,6},{5,7},{6,4},{7,5},{8,10},{9,11},{10,... | collective-permute-start | bytes 1720328 | tf_op jit(solution)/shard_map/ppermute | solution.py:25
  26.1 35.4 %collective-permute-start.10 = (bf16[80,3584]{1,0:T(8,128)(2,1)S(1)}, bf16[80,3584]{1,0:T(8,128)(2,1)S(1)}, u32[]{:S(2)}, u32[]{:S(2)}) collective-permute-start(bf16[80,3584]{1,0:T(8,128)(2,1)S(1)} %join.1), channel_id=1, source_target_pairs={{0,4},{1,5},{2,6},{3,7},{4,0},{5,1},{6,2},{7,3},{8,12},{9,13},{10,... | collective-permute-start | bytes 1720328 | tf_op jit(solution)/shard_map/ppermute | solution.py:25
  35.4 11.6 %collective-permute-start.5 = (bf16[48,3584]{1,0:T(8,128)(2,1)S(1)}, bf16[48,3584]{1,0:T(8,128)(2,1)S(1)}, u32[]{:S(2)}, u32[]{:S(2)}) collective-permute-start(bf16[48,3584]{1,0:T(8,128)(2,1)S(1)} %get-tuple-element.136), channel_id=1, source_target_pairs={{0,2},{1,3},{2,0},{3,1},{4,6},{5,7},{6,4},{7,5},{8,10},{9,11},{10,... | collective-permute-start | bytes 1032200 | tf_op jit(solution)/shard_map/ppermute | solution.py:25
  37.0 24.4 %collective-permute-start.7 = (bf16[80,3584]{1,0:T(8,128)(2,1)S(1)}, bf16[80,3584]{1,0:T(8,128)(2,1)S(1)}, u32[]{:S(2)}, u32[]{:S(2)}) collective-permute-start(bf16[80,3584]{1,0:T(8,128)(2,1)S(1)} %get-tuple-element.157), channel_id=1, source_target_pairs={{0,12},{1,13},{2,14},{3,15},{4,8},{5,9},{6,10},{7,11},{8,4},{9,5},... | collective-permute-start | bytes 1720328 | tf_op jit(solution)/shard_map/ppermute | solution.py:25
  40.5 11.9 %collective-permute-start.6 = (bf16[32,3584]{1,0:T(8,128)(2,1)S(1)}, bf16[32,3584]{1,0:T(8,128)(2,1)S(1)}, u32[]{:S(2)}, u32[]{:S(2)}) collective-permute-start(bf16[32,3584]{1,0:T(8,128)(2,1)S(1)} %get-tuple-element.148), channel_id=1, source_target_pairs={{0,2},{1,3},{2,0},{3,1},{4,6},{5,7},{6,4},{7,5},{8,10},{9,11},{10,... | collective-permute-start | bytes 688136 | tf_op jit(solution)/shard_map/ppermute | solution.py:25
  50.7 10.8 %collective-permute-start.8 = (bf16[48,3584]{1,0:T(8,128)(2,1)S(1)}, bf16[48,3584]{1,0:T(8,128)(2,1)S(1)}, u32[]{:S(2)}, u32[]{:S(2)}) collective-permute-start(bf16[48,3584]{1,0:T(8,128)(2,1)S(1)} %get-tuple-element.160), channel_id=1, source_target_pairs={{0,2},{1,3},{2,0},{3,1},{4,6},{5,7},{6,4},{7,5},{8,10},{9,11},{10,... | collective-permute-start | bytes 1032200 | tf_op jit(solution)/shard_map/ppermute | solution.py:25
  61.4 8.4 %collective-permute-start.11 = (bf16[32,3584]{1,0:T(8,128)(2,1)S(1)}, bf16[32,3584]{1,0:T(8,128)(2,1)S(1)}, u32[]{:S(2)}, u32[]{:S(2)}) collective-permute-start(bf16[32,3584]{1,0:T(8,128)(2,1)S(1)} %get-tuple-element.165), channel_id=1, source_target_pairs={{0,2},{1,3},{2,0},{3,1},{4,6},{5,7},{6,4},{7,5},{8,10},{9,11},{10,... | collective-permute-start | bytes 688136 | tf_op jit(solution)/shard_map/ppermute | solution.py:25
  69.9 9.1 %collective-permute-start.12 = (bf16[48,3584]{1,0:T(8,128)(2,1)S(1)}, bf16[48,3584]{1,0:T(8,128)(2,1)S(1)}, u32[]{:S(2)}, u32[]{:S(2)}) collective-permute-start(bf16[48,3584]{1,0:T(8,128)(2,1)S(1)} %get-tuple-element.184), channel_id=1, source_target_pairs={{0,2},{1,3},{2,0},{3,1},{4,6},{5,7},{6,4},{7,5},{8,10},{9,11},{10,... | collective-permute-start | bytes 1032200 | tf_op jit(solution)/shard_map/ppermute | solution.py:25
  70.3 22.8 %collective-permute-start.16 = (bf16[80,3584]{1,0:T(8,128)(2,1)S(1)}, bf16[80,3584]{1,0:T(8,128)(2,1)S(1)}, u32[]{:S(2)}, u32[]{:S(2)}) collective-permute-start(bf16[80,3584]{1,0:T(8,128)(2,1)S(1)} %total.4), channel_id=1, source_target_pairs={{0,8},{1,9},{2,10},{3,11},{4,12},{5,13},{6,14},{7,15},{8,0},{9,1},... | collective-permute-start | bytes 1720328 | tf_op jit(solution)/shard_map/ppermute | solution.py:25
  70.4 12.7 %collective-permute-start.13 = (bf16[32,3584]{1,0:T(8,128)(2,1)S(1)}, bf16[32,3584]{1,0:T(8,128)(2,1)S(1)}, u32[]{:S(2)}, u32[]{:S(2)}) collective-permute-start(bf16[32,3584]{1,0:T(8,128)(2,1)S(1)} %get-tuple-element.193), channel_id=1, source_target_pairs={{0,2},{1,3},{2,0},{3,1},{4,6},{5,7},{6,4},{7,5},{8,10},{9,11},{10,... | collective-permute-start | bytes 688136 | tf_op jit(solution)/shard_map/ppermute | solution.py:25
  76.3 20.8 %collective-permute-start.20 = (bf16[80,3584]{1,0:T(8,128)(2,1)S(1)}, bf16[80,3584]{1,0:T(8,128)(2,1)S(1)}, u32[]{:S(2)}, u32[]{:S(2)}) collective-permute-start(bf16[80,3584]{1,0:T(8,128)(2,1)S(1)} %get-tuple-element.226), channel_id=1, source_target_pairs={{0,4},{1,5},{2,6},{3,7},{4,0},{5,1},{6,2},{7,3},{8,12},{9,13},{10,... | collective-permute-start | bytes 1720328 | tf_op jit(solution)/shard_map/ppermute | solution.py:25
  83.0 10.2 %collective-permute-start.14 = (bf16[48,3584]{1,0:T(8,128)(2,1)S(1)}, bf16[48,3584]{1,0:T(8,128)(2,1)S(1)}, u32[]{:S(2)}, u32[]{:S(2)}) collective-permute-start(bf16[48,3584]{1,0:T(8,128)(2,1)S(1)} %get-tuple-element.201), channel_id=1, source_target_pairs={{0,2},{1,3},{2,0},{3,1},{4,6},{5,7},{6,4},{7,5},{8,10},{9,11},{10,... | collective-permute-start | bytes 1032200 | tf_op jit(solution)/shard_map/ppermute | solution.py:25
  87.0 6.1 %collective-permute-start.15 = (bf16[32,3584]{1,0:T(8,128)(2,1)S(1)}, bf16[32,3584]{1,0:T(8,128)(2,1)S(1)}, u32[]{:S(2)}, u32[]{:S(2)}) collective-permute-start(bf16[32,3584]{1,0:T(8,128)(2,1)S(1)} %get-tuple-element.202), channel_id=1, source_target_pairs={{0,2},{1,3},{2,0},{3,1},{4,6},{5,7},{6,4},{7,5},{8,10},{9,11},{10,... | collective-permute-start | bytes 688136 | tf_op jit(solution)/shard_map/ppermute | solution.py:25
  93.4 17.8 %collective-permute-start.19 = (bf16[80,3584]{1,0:T(8,128)(2,1)S(1)}, bf16[80,3584]{1,0:T(8,128)(2,1)S(1)}, u32[]{:S(2)}, u32[]{:S(2)}) collective-permute-start(bf16[80,3584]{1,0:T(8,128)(2,1)S(1)} %total.5), channel_id=1, source_target_pairs={{0,12},{1,13},{2,14},{3,15},{4,8},{5,9},{6,10},{7,11},{8,4},{9,5},... | collective-permute-start | bytes 1720328 | tf_op jit(solution)/shard_map/ppermute | solution.py:25
  95.1 16.2 %collective-permute-start.18 = (bf16[80,3584]{1,0:T(8,128)(2,1)S(1)}, bf16[80,3584]{1,0:T(8,128)(2,1)S(1)}, u32[]{:S(2)}, u32[]{:S(2)}) collective-permute-start(bf16[80,3584]{1,0:T(8,128)(2,1)S(1)} %get-tuple-element.218), channel_id=1, source_target_pairs={{0,2},{1,3},{2,0},{3,1},{4,6},{5,7},{6,4},{7,5},{8,10},{9,11},{10,... | collective-permute-start | bytes 1720328 | tf_op jit(solution)/shard_map/ppermute | solution.py:25
  97.1 23.3 %collective-permute-start.17 = (bf16[80,3584]{1,0:T(8,128)(2,1)S(1)}, bf16[80,3584]{1,0:T(8,128)(2,1)S(1)}, u32[]{:S(2)}, u32[]{:S(2)}) collective-permute-start(bf16[80,3584]{1,0:T(8,128)(2,1)S(1)} %get-tuple-element.216), channel_id=1, source_target_pairs={{0,4},{1,5},{2,6},{3,7},{4,0},{5,1},{6,2},{7,3},{8,12},{9,13},{10,... | collective-permute-start | bytes 1720328 | tf_op jit(solution)/shard_map/ppermute | solution.py:25
  97.2 24.6 %collective-permute-start.21 = (bf16[64,3584]{1,0:T(8,128)(2,1)S(1)}, bf16[64,3584]{1,0:T(8,128)(2,1)S(1)}, u32[]{:S(2)}, u32[]{:S(2)}) collective-permute-start(bf16[64,3584]{1,0:T(8,128)(2,1)S(1)} %get-tuple-element.233), channel_id=1, source_target_pairs={{0,2},{1,3},{2,0},{3,1},{4,6},{5,7},{6,4},{7,5},{8,10},{9,11},{10,... | collective-permute-start | bytes 1376264 | tf_op jit(solution)/shard_map/ppermute | solution.py:25
  107.8 13.9 %collective-permute-start.22 = (bf16[16,3584]{1,0:T(8,128)(2,1)S(1)}, bf16[16,3584]{1,0:T(8,128)(2,1)S(1)}, u32[]{:S(2)}, u32[]{:S(2)}) collective-permute-start(bf16[16,3584]{1,0:T(8,128)(2,1)S(1)} %get-tuple-element.235), channel_id=1, source_target_pairs={{0,2},{1,3},{2,0},{3,1},{4,6},{5,7},{6,4},{7,5},{8,10},{9,11},{10,... | collective-permute-start | bytes 344072 | tf_op jit(solution)/shard_map/ppermute | solution.py:25
  124.6 9.8 %all-to-all-start = ((f32[16,1,16]{2,1,0:T(1,128)}), f32[16,1,16]{2,1,0:T(1,128)S(1)}, u32[]{:S(2)}, u32[]{:S(2)}) async-start(f32[16,1,16]{2,1,0:T(1,128)} %bitcast.6), calls=%async_computation | async-start | bytes 16384 | tf_op jit(solution)/shard_map/all_to_all | solution.py:401
  (9 other events, 234.9 us)

commit v18 on v17

--- a/solution.py
+++ b/solution.py
@@ -94,9 +94,10 @@
 
 def expert_kernel(first, near_ref, far_ref, *refs):
     *weight_refs, mine_ref, theirs_ref, rows = refs
-    count = far_ref.shape[0]
-    rows[:count, :] = near_ref[first : first + count, :]
-    rows[count:, :] = far_ref[...]
+    count = mine_ref.shape[0]
+    split = 2 * count - far_ref.shape[0]
+    rows[:split, :] = near_ref[first : first + split, :]
+    rows[split:, :] = far_ref[...]
     width = rows.shape[1]
     size = weight_refs[0].shape[1]
     hidden = []
@@ -113,8 +114,8 @@
         theirs_ref[:, start : start + size] = part[count:]
 
 
-def expert_block(near, first, far, weights):
-    count, width = far.shape
+def expert_block(near, first, far, weights, count):
+    width = far.shape[1]
     vmem = pl.BlockSpec(memory_space=pltpu.VMEM)
     return pl.pallas_call(
         functools.partial(expert_kernel, first),
@@ -209,17 +210,15 @@
         return lax.optimization_barrier((value, self.token))[0]
 
 
-def cut_kernel(whole_ref, *refs):
-    first = 0
-    for ref in refs:
-        ref[...] = whole_ref[first : first + ref.shape[0], :]
-        first += ref.shape[0]
+def cut_kernel(pieces, whole_ref, *refs):
+    for (first, count), ref in zip(pieces, refs):
+        ref[...] = whole_ref[first : first + count, :]
 
 
 def cut(whole, pieces):
     vmem = pl.BlockSpec(memory_space=pltpu.VMEM)
     return pl.pallas_call(
-        cut_kernel,
+        functools.partial(cut_kernel, tuple(pieces)),
         out_shape=[jax.ShapeDtypeStruct((count, whole.shape[1]), BF16) for _, count in pieces],
         in_specs=[vmem],
         out_specs=[vmem] * len(pieces),
@@ -320,17 +319,17 @@
 
     def work(k):
         mine[k], theirs[k] = [], []
-        for (first, _), piece in zip(pieces, far[k]):
+        for (first, count), piece in zip(pieces, far[k]):
             there = order.mark_one(piece)
-            part, other = order.mark(*expert_block(order.late(near[k]), first, there, weights))
+            part, other = order.mark(*expert_block(order.late(near[k]), first, there, weights, count))
             if k == 2 and first:
-                far[0], far[1], other = lax.optimization_barrier((far[0], far[1], other))
+                far[0], other = lax.optimization_barrier((far[0], other))
             mine[k].append(part)
             theirs[k].append(swap(other, side))
 
     def work_whole(k):
         rows = (order.late(near[k]), 0, order.late(far[k]))
-        mine[k], theirs[k] = order.mark(*expert_block(*rows, weights))
+        mine[k], theirs[k] = order.mark(*expert_block(*rows, weights, capacity))
 
     def home(k):
         theirs[k] = order.mark(*theirs[k])
@@ -343,17 +342,20 @@
         back[k] = order.mark_one(back[k])
 
     leave(2)
-    far[1] = [swap(piece, side) for piece in cut(near[1], pieces)]
+    tail_rows = 32 if capacity > 32 else capacity // 2
+    *far[1], near[1], tail = cut(near[1], (*pieces, (0, capacity - tail_rows), (capacity - tail_rows, tail_rows)))
+    far[1] = [swap(piece, side) for piece in far[1]]
     leave(1)
     *far[1], weights[1] = order.mark(*far[1], weights[1])
-    far[1] = swap(join(far[1]), spread)
+    far[1] = swap(join([tail, *far[1]]), spread)
     near[0], weights[1] = lax.optimization_barrier((near[0], weights[1]))
     far[0] = swap(near[0], side)
     arrive(2)
     last = (capacity - 16, 16)
     for k in range(3, experts + 1):
         if k > 3:
-            near[k - 1], *theirs[k - 2] = lax.optimization_barrier((near[k - 1], *theirs[k - 2]))
+            held = (far[1], near[k - 1], *theirs[k - 2])
+            far[1], near[k - 1], *theirs[k - 2] = lax.optimization_barrier(held)
         share(k - 1)
         if k < experts:
             leave(k)

time: 135 us -> 138 us (1.022)
  waiting for transfers between devices: 58.3 us -> 66.1 us
  starting transfers between devices: 43.3 us -> 38.5 us
    ppermute x23, waiting for transfers between devices: 52.1 us -> 59.9 us  [swap(): return lax.ppermute(value, 'expert', pairs)]
    ppermute x23, starting transfers between devices: 39.9 us -> 34.7 us  [swap(): return lax.ppermute(value, 'expert', pairs)]
  transfers between devices with their start and end apart: 24 -> 24, of which waited for: 10 -> 13; matrix products, arithmetic and copies ran while one was open for 0% -> 0% of each run, Pallas kernels for 18% -> 18%
where the time goes in v18:
time: 138 us
  waiting for transfers between devices  66.1 us (48%)
  starting transfers between devices  38.5 us (28%)
  Pallas kernels  31.7 us (23%)
    ppermute x23, waiting for transfers between devices, swap(): return lax.ppermute(value, 'expert', pairs)  59.9 us
    ppermute x23, starting transfers between devices, swap(): return lax.ppermute(value, 'expert', pairs)  34.7 us
    pallas_call x6, Pallas kernels, expert_block(): pl.pallas_call(functools.partial(expert_kernel, first), out_shape=[jax.Sh...  23.3 us
    all_to_all x1, waiting for transfers between devices, per_device(): lax.all_to_all(local, 'expert', split_axis=0, concat_axis=0, tiled=True)  6.19 us
    pallas_call x1, Pallas kernels, pack(): pl.pallas_call(pack_kernel, out_shape=[jax.ShapeDtypeStruct(shape, BF16)...  4.53 us
    all_to_all x1, starting transfers between devices, per_device(): lax.all_to_all(local, 'expert', split_axis=0, concat_axis=0, tiled=True)  3.85 us
  transfers between devices with their start and end apart: 24, of which 13 were waited for; matrix products, arithmetic and copies ran while one was open for 0% of the time, Pallas kernels for 18%

profile of v18, /device:TPU:0, one launch (start us, length us, event | category | flops | bytes accessed | tf_op | source)
XLA Modules:
  0.0 138.3 jit_solution(15542675768656085697)
XLA Ops:
  0.6 4.5 %pack.1 = (bf16[80,3584]{1,0:T(8,128)(2,1)S(1)}, bf16[80,3584]{1,0:T(8,128)(2,1)S(1)}, bf16[80,3584]{1,0:T(8,128)(2,1)S(1)}, bf16[80,3584]{1,0:T(8,128)(2,1)S(1)}, bf16[10752,512]{1,0:T(8,128)(2,1)S(1)}) custom-call(s32[1]{0:T(128)} %bitcast.own_ref, bf16[128,3584]{1,0:T(8,128)(2,1)} %tokens_ref.1, f32[3584]{0:T(1024)} %gain_hbm.1, s32[2,128]{1,0:T(2,128)} %bitcast.8, ...), custom_call_target="tpu_custom_call" | custom-call | flops 1024 | bytes 1024 | tf_op jit(solution)/shard_map/pack/pallas_call | solution.py:78
  5.7 3.7 %collective-permute-start.1 = (bf16[80,3584]{1,0:T(8,128)(2,1)S(1)}, bf16[80,3584]{1,0:T(8,128)(2,1)S(1)}, u32[]{:S(2)}, u32[]{:S(2)}) collective-permute-start(bf16[80,3584]{1,0:T(8,128)(2,1)S(1)} %get-tuple-element.127), channel_id=1, source_target_pairs={{0,8},{1,9},{2,10},{3,11},{4,12},{5,13},{6,14},{7,15},{8,0},{9,1},... | collective-permute-start | bytes 1720328 | tf_op jit(solution)/shard_map/ppermute | solution.py:25
  13.1 11.4 %collective-permute-done.3.refs_2_ = bf16[32,3584]{1,0:T(8,128)(2,1)S(1)} collective-permute-done((bf16[32,3584]{1,0:T(8,128)(2,1)S(1)}, bf16[32,3584]{1,0:T(8,128)(2,1)S(1)}, u32[]{:S(2)}, u32[]{:S(2)}) %collective-permute-start.3) | collective-permute-done | bytes 229408 | tf_op jit(solution)/shard_map/ppermute | solution.py:25
  27.8 7.5 %collective-permute-done.1.whole_ref.near_ref = bf16[80,3584]{1,0:T(8,128)(2,1)S(1)} collective-permute-done((bf16[80,3584]{1,0:T(8,128)(2,1)S(1)}, bf16[80,3584]{1,0:T(8,128)(2,1)S(1)}, u32[]{:S(2)}, u32[]{:S(2)}) %collective-permute-start.1) | collective-permute-done | bytes 573472 | tf_op jit(solution)/shard_map/ppermute | solution.py:25
  37.0 3.5 %collective-permute-start.8 = (bf16[80,3584]{1,0:T(8,128)(2,1)S(1)}, bf16[80,3584]{1,0:T(8,128)(2,1)S(1)}, u32[]{:S(2)}, u32[]{:S(2)}) collective-permute-start(bf16[80,3584]{1,0:T(8,128)(2,1)S(1)} %get-tuple-element.163), channel_id=1, source_target_pairs={{0,12},{1,13},{2,14},{3,15},{4,8},{5,9},{6,10},{7,11},{8,4},{9,5},... | collective-permute-start | bytes 1720328 | tf_op jit(solution)/shard_map/ppermute | solution.py:25
  41.0 6.0 %collective-permute-done.5.far_ref = bf16[48,3584]{1,0:T(8,128)(2,1)S(1)} collective-permute-done((bf16[48,3584]{1,0:T(8,128)(2,1)S(1)}, bf16[48,3584]{1,0:T(8,128)(2,1)S(1)}, u32[]{:S(2)}, u32[]{:S(2)}) %collective-permute-start.5) | collective-permute-done | bytes 344096 | tf_op jit(solution)/shard_map/ppermute | solution.py:25
  47.0 3.7 %expert_block.6 = (bf16[48,3584]{1,0:T(8,128)(2,1)S(1)}, bf16[48,3584]{1,0:T(8,128)(2,1)S(1)}) custom-call(bf16[80,3584]{1,0:T(8,128)(2,1)S(1)} %collective-permute-done.1.whole_ref.near_ref, bf16[48,3584]{1,0:T(8,128)(2,1)S(1)} %collective-permute-done.5.far_ref, bf16[10752,512]{1,0:T(8,128)(2,1)S(1)} %get-tuple-element.130.refs_0_, ...), custom_call_target="tpu_custom_call" | custom-call | flops 1024 | bytes 1024 | tf_op jit(solution)/shard_map/expert_block/pallas_call | solution.py:120
  52.4 4.0 %expert_block.7 = (bf16[32,3584]{1,0:T(8,128)(2,1)S(1)}, bf16[32,3584]{1,0:T(8,128)(2,1)S(1)}) custom-call(bf16[80,3584]{1,0:T(8,128)(2,1)S(1)} %collective-permute-done.1.whole_ref.near_ref, bf16[32,3584]{1,0:T(8,128)(2,1)S(1)} %collective-permute-done.6.far_ref, bf16[10752,512]{1,0:T(8,128)(2,1)S(1)} %get-tuple-element.130.refs_0_, ...), custom_call_target="tpu_custom_call" | custom-call | flops 1024 | bytes 1024 | tf_op jit(solution)/shard_map/expert_block/pallas_call | solution.py:120
  56.9 4.1 %collective-permute-done.8.whole_ref.near_ref = bf16[80,3584]{1,0:T(8,128)(2,1)S(1)} collective-permute-done((bf16[80,3584]{1,0:T(8,128)(2,1)S(1)}, bf16[80,3584]{1,0:T(8,128)(2,1)S(1)}, u32[]{:S(2)}, u32[]{:S(2)}) %collective-permute-start.8) | collective-permute-done | bytes 573472 | tf_op jit(solution)/shard_map/ppermute | solution.py:25
  61.2 2.8 %collective-permute-done.11.refs_3_ = bf16[32,3584]{1,0:T(8,128)(2,1)S(1)} collective-permute-done((bf16[32,3584]{1,0:T(8,128)(2,1)S(1)}, bf16[32,3584]{1,0:T(8,128)(2,1)S(1)}, u32[]{:S(2)}, u32[]{:S(2)}) %collective-permute-start.11) | collective-permute-done | bytes 229408 | tf_op jit(solution)/shard_map/ppermute | solution.py:25
  66.7 1.9 %collective-permute-start.16 = (bf16[80,3584]{1,0:T(8,128)(2,1)S(1)}, bf16[80,3584]{1,0:T(8,128)(2,1)S(1)}, u32[]{:S(2)}, u32[]{:S(2)}) collective-permute-start(bf16[80,3584]{1,0:T(8,128)(2,1)S(1)} %total.4), channel_id=1, source_target_pairs={{0,8},{1,9},{2,10},{3,11},{4,12},{5,13},{6,14},{7,15},{8,0},{9,1},... | collective-permute-start | bytes 1720328 | tf_op jit(solution)/shard_map/ppermute | solution.py:25
  69.0 3.8 %expert_block.8 = (bf16[80,3584]{1,0:T(8,128)(2,1)S(1)}, bf16[80,3584]{1,0:T(8,128)(2,1)S(1)}) custom-call(bf16[48,3584]{1,0:T(8,128)(2,1)S(1)} %collective-permute-done.near_ref, bf16[112,3584]{1,0:T(8,128)(2,1)S(1)} %collective-permute-done.7.far_ref, bf16[10752,512]{1,0:T(8,128)(2,1)S(1)} %get-tuple-element.130.refs_0_, ...), custom_call_target="tpu_custom_call" | custom-call | flops 1024 | bytes 1024 | tf_op jit(solution)/shard_map/expert_block/pallas_call | solution.py:120
  72.9 2.3 %collective-permute-start.20 = (bf16[80,3584]{1,0:T(8,128)(2,1)S(1)}, bf16[80,3584]{1,0:T(8,128)(2,1)S(1)}, u32[]{:S(2)}, u32[]{:S(2)}) collective-permute-start(bf16[80,3584]{1,0:T(8,128)(2,1)S(1)} %get-tuple-element.230), channel_id=1, source_target_pairs={{0,4},{1,5},{2,6},{3,7},{4,0},{5,1},{6,2},{7,3},{8,12},{9,13},{10,... | collective-permute-start | bytes 1720328 | tf_op jit(solution)/shard_map/ppermute | solution.py:25
  75.7 3.9 %expert_block.9 = (bf16[48,3584]{1,0:T(8,128)(2,1)S(1)}, bf16[48,3584]{1,0:T(8,128)(2,1)S(1)}) custom-call(bf16[80,3584]{1,0:T(8,128)(2,1)S(1)} %collective-permute-done.8.whole_ref.near_ref, bf16[48,3584]{1,0:T(8,128)(2,1)S(1)} %collective-permute-done.12.far_ref, bf16[10752,512]{1,0:T(8,128)(2,1)S(1)} %get-tuple-element.130.refs_0_, ...), custom_call_target="tpu_custom_call" | custom-call | flops 1024 | bytes 1024 | tf_op jit(solution)/shard_map/expert_block/pallas_call | solution.py:120
  81.3 4.0 %expert_block.10 = (bf16[32,3584]{1,0:T(8,128)(2,1)S(1)}, bf16[32,3584]{1,0:T(8,128)(2,1)S(1)}) custom-call(bf16[80,3584]{1,0:T(8,128)(2,1)S(1)} %collective-permute-done.8.whole_ref.near_ref, bf16[32,3584]{1,0:T(8,128)(2,1)S(1)} %collective-permute-done.13.far_ref, bf16[10752,512]{1,0:T(8,128)(2,1)S(1)} %get-tuple-element.130.refs_0_, ...), custom_call_target="tpu_custom_call" | custom-call | flops 1024 | bytes 1024 | tf_op jit(solution)/shard_map/expert_block/pallas_call | solution.py:120
  85.8 3.9 %expert_block.11 = (bf16[80,3584]{1,0:T(8,128)(2,1)S(1)}, bf16[80,3584]{1,0:T(8,128)(2,1)S(1)}) custom-call(bf16[80,3584]{1,0:T(8,128)(2,1)S(1)} %get-tuple-element.209.near_ref, bf16[80,3584]{1,0:T(8,128)(2,1)S(1)} %collective-permute-done.10.far_ref, bf16[10752,512]{1,0:T(8,128)(2,1)S(1)} %get-tuple-element.130.refs_0_, ...), custom_call_target="tpu_custom_call" | custom-call | flops 1024 | bytes 1024 | tf_op jit(solution)/shard_map/expert_block/pallas_call | solution.py:120
  89.8 4.9 %collective-permute-done.16.refs_2_ = bf16[80,3584]{1,0:T(8,128)(2,1)S(1)} collective-permute-done((bf16[80,3584]{1,0:T(8,128)(2,1)S(1)}, bf16[80,3584]{1,0:T(8,128)(2,1)S(1)}, u32[]{:S(2)}, u32[]{:S(2)}) %collective-permute-start.16) | collective-permute-done | bytes 573472 | tf_op jit(solution)/shard_map/ppermute | solution.py:25
  94.9 2.5 %collective-permute-start.19 = (bf16[80,3584]{1,0:T(8,128)(2,1)S(1)}, bf16[80,3584]{1,0:T(8,128)(2,1)S(1)}, u32[]{:S(2)}, u32[]{:S(2)}) collective-permute-start(bf16[80,3584]{1,0:T(8,128)(2,1)S(1)} %total.5), channel_id=1, source_target_pairs={{0,12},{1,13},{2,14},{3,15},{4,8},{5,9},{6,10},{7,11},{8,4},{9,5},... | collective-permute-start | bytes 1720328 | tf_op jit(solution)/shard_map/ppermute | solution.py:25
  98.3 11.7 %collective-permute-done.20.whole_ref = bf16[80,3584]{1,0:T(8,128)(2,1)S(1)} collective-permute-done((bf16[80,3584]{1,0:T(8,128)(2,1)S(1)}, bf16[80,3584]{1,0:T(8,128)(2,1)S(1)}, u32[]{:S(2)}, u32[]{:S(2)}) %collective-permute-start.20) | collective-permute-done | bytes 573472 | tf_op jit(solution)/shard_map/ppermute | solution.py:25
  110.0 4.0 %collective-permute-start.21 = (bf16[64,3584]{1,0:T(8,128)(2,1)S(1)}, bf16[64,3584]{1,0:T(8,128)(2,1)S(1)}, u32[]{:S(2)}, u32[]{:S(2)}) collective-permute-start(bf16[64,3584]{1,0:T(8,128)(2,1)S(1)} %get-tuple-element.237), channel_id=1, source_target_pairs={{0,2},{1,3},{2,0},{3,1},{4,6},{5,7},{6,4},{7,5},{8,10},{9,11},{10,... | collective-permute-start | bytes 1376264 | tf_op jit(solution)/shard_map/ppermute | solution.py:25
  114.4 9.1 %collective-permute-done.17.refs_0_ = bf16[80,3584]{1,0:T(8,128)(2,1)S(1)} collective-permute-done((bf16[80,3584]{1,0:T(8,128)(2,1)S(1)}, bf16[80,3584]{1,0:T(8,128)(2,1)S(1)}, u32[]{:S(2)}, u32[]{:S(2)}) %collective-permute-start.17) | collective-permute-done | bytes 573472 | tf_op jit(solution)/shard_map/ppermute | solution.py:25
  124.7 2.6 %score.1 = f32[16,16]{1,0:T(8,128)} custom-call(s32[1]{0:T(128)} %bitcast.own_ref, bf16[128,3584]{1,0:T(8,128)(2,1)S(1)} %copy-done, f32[3584]{0:T(1024)S(1)} %copy-done.2, s32[2,128]{1,0:T(2,128)S(1)} %bitcast.9, f32[2,128]{1,0:T(2,128)S(1)} %bitcast.10, bf16[128,3584]{1,0:T(8,128)(2,1)S(1)} %copy-done.1, f32[1,128]{1,0:T(1,128)S(1)} %bitcast.11, ...), custom_call_target="tpu_custom_call" | custom-call | flops 1024 | bytes 1024 | tf_op jit(solution)/shard_map/score/pallas_call | solution.py:183
  127.2 3.9 %all-to-all-start = ((f32[16,1,16]{2,1,0:T(1,128)}), f32[16,1,16]{2,1,0:T(1,128)S(1)}, u32[]{:S(2)}, u32[]{:S(2)}) async-start(f32[16,1,16]{2,1,0:T(1,128)} %bitcast.6), calls=%async_computation | async-start | bytes 16384 | tf_op jit(solution)/shard_map/all_to_all | solution.py:403
  131.3 6.2 %all-to-all-done = f32[16,1,16]{2,1,0:T(1,128)S(1)} async-done(((f32[16,1,16]{2,1,0:T(1,128)}), f32[16,1,16]{2,1,0:T(1,128)S(1)}, u32[]{:S(2)}, u32[]{:S(2)}) %all-to-all-start) | async-done | bytes 1056 | tf_op jit(solution)/shard_map/all_to_all | solution.py:403
  (65 shorter events, 21.4 us)
Async XLA Ops:
  5.2 19.4 %collective-permute-start.4 = (bf16[10752,512]{1,0:T(8,128)(2,1)S(1)}, bf16[10752,512]{1,0:T(8,128)(2,1)S(1)}, u32[]{:S(2)}, u32[]{:S(2)}) collective-permute-start(bf16[10752,512]{1,0:T(8,128)(2,1)S(1)} %get-tuple-element.130.refs_0_), channel_id=1, source_target_pairs={{0,1},{1,0},{2,3},{3,2},{4,5},{5,4},{6,7},{7,6},{8,9},{9,8},{10,11... | collective-permute-start | bytes 33030152 | tf_op jit(solution)/shard_map/ppermute | solution.py:25
  5.7 29.6 %collective-permute-start.1 = (bf16[80,3584]{1,0:T(8,128)(2,1)S(1)}, bf16[80,3584]{1,0:T(8,128)(2,1)S(1)}, u32[]{:S(2)}, u32[]{:S(2)}) collective-permute-start(bf16[80,3584]{1,0:T(8,128)(2,1)S(1)} %get-tuple-element.127), channel_id=1, source_target_pairs={{0,8},{1,9},{2,10},{3,11},{4,12},{5,13},{6,14},{7,15},{8,0},{9,1},... | collective-permute-start | bytes 1720328 | tf_op jit(solution)/shard_map/ppermute | solution.py:25
  9.4 15.1 %collective-permute-start.2 = (bf16[48,3584]{1,0:T(8,128)(2,1)S(1)}, bf16[48,3584]{1,0:T(8,128)(2,1)S(1)}, u32[]{:S(2)}, u32[]{:S(2)}) collective-permute-start(bf16[48,3584]{1,0:T(8,128)(2,1)S(1)} %get-tuple-element.128), channel_id=1, source_target_pairs={{0,2},{1,3},{2,0},{3,1},{4,6},{5,7},{6,4},{7,5},{8,10},{9,11},{10,... | collective-permute-start | bytes 1032200 | tf_op jit(solution)/shard_map/ppermute | solution.py:25
  11.1 13.5 %collective-permute-start.3 = (bf16[32,3584]{1,0:T(8,128)(2,1)S(1)}, bf16[32,3584]{1,0:T(8,128)(2,1)S(1)}, u32[]{:S(2)}, u32[]{:S(2)}) collective-permute-start(bf16[32,3584]{1,0:T(8,128)(2,1)S(1)} %get-tuple-element.129), channel_id=1, source_target_pairs={{0,2},{1,3},{2,0},{3,1},{4,6},{5,7},{6,4},{7,5},{8,10},{9,11},{10,... | collective-permute-start | bytes 688136 | tf_op jit(solution)/shard_map/ppermute | solution.py:25
  11.5 29.0 %collective-permute-start = (bf16[48,3584]{1,0:T(8,128)(2,1)S(1)}, bf16[48,3584]{1,0:T(8,128)(2,1)S(1)}, u32[]{:S(2)}, u32[]{:S(2)}) collective-permute-start(bf16[48,3584]{1,0:T(8,128)(2,1)S(1)} %get-tuple-element.125), channel_id=1, source_target_pairs={{0,4},{1,5},{2,6},{3,7},{4,0},{5,1},{6,2},{7,3},{8,12},{9,13},{10,... | collective-permute-start | bytes 1032200 | tf_op jit(solution)/shard_map/ppermute | solution.py:25
  24.6 31.9 %collective-permute-start.10 = (bf16[80,3584]{1,0:T(8,128)(2,1)S(1)}, bf16[80,3584]{1,0:T(8,128)(2,1)S(1)}, u32[]{:S(2)}, u32[]{:S(2)}) collective-permute-start(bf16[80,3584]{1,0:T(8,128)(2,1)S(1)} %get-tuple-element.209.near_ref), channel_id=1, source_target_pairs={{0,2},{1,3},{2,0},{3,1},{4,6},{5,7},{6,4},{7,5},{8,10},{9,11},{10,... | collective-permute-start | bytes 1720328 | tf_op jit(solution)/shard_map/ppermute | solution.py:25
  26.1 38.6 %collective-permute-start.7 = (bf16[112,3584]{1,0:T(8,128)(2,1)S(1)}, bf16[112,3584]{1,0:T(8,128)(2,1)S(1)}, u32[]{:S(2)}, u32[]{:S(2)}) collective-permute-start(bf16[112,3584]{1,0:T(8,128)(2,1)S(1)} %join.1), channel_id=1, source_target_pairs={{0,4},{1,5},{2,6},{3,7},{4,0},{5,1},{6,2},{7,3},{8,12},{9,13},{10,... | collective-permute-start | bytes 2408456 | tf_op jit(solution)/shard_map/ppermute | solution.py:25
  35.4 11.7 %collective-permute-start.5 = (bf16[48,3584]{1,0:T(8,128)(2,1)S(1)}, bf16[48,3584]{1,0:T(8,128)(2,1)S(1)}, u32[]{:S(2)}, u32[]{:S(2)}) collective-permute-start(bf16[48,3584]{1,0:T(8,128)(2,1)S(1)} %get-tuple-element.139), channel_id=1, source_target_pairs={{0,2},{1,3},{2,0},{3,1},{4,6},{5,7},{6,4},{7,5},{8,10},{9,11},{10,... | collective-permute-start | bytes 1032200 | tf_op jit(solution)/shard_map/ppermute | solution.py:25
  37.0 24.1 %collective-permute-start.8 = (bf16[80,3584]{1,0:T(8,128)(2,1)S(1)}, bf16[80,3584]{1,0:T(8,128)(2,1)S(1)}, u32[]{:S(2)}, u32[]{:S(2)}) collective-permute-start(bf16[80,3584]{1,0:T(8,128)(2,1)S(1)} %get-tuple-element.163), channel_id=1, source_target_pairs={{0,12},{1,13},{2,14},{3,15},{4,8},{5,9},{6,10},{7,11},{8,4},{9,5},... | collective-permute-start | bytes 1720328 | tf_op jit(solution)/shard_map/ppermute | solution.py:25
  40.5 11.9 %collective-permute-start.6 = (bf16[32,3584]{1,0:T(8,128)(2,1)S(1)}, bf16[32,3584]{1,0:T(8,128)(2,1)S(1)}, u32[]{:S(2)}, u32[]{:S(2)}) collective-permute-start(bf16[32,3584]{1,0:T(8,128)(2,1)S(1)} %get-tuple-element.151), channel_id=1, source_target_pairs={{0,2},{1,3},{2,0},{3,1},{4,6},{5,7},{6,4},{7,5},{8,10},{9,11},{10,... | collective-permute-start | bytes 688136 | tf_op jit(solution)/shard_map/ppermute | solution.py:25
  50.8 10.4 %collective-permute-start.9 = (bf16[48,3584]{1,0:T(8,128)(2,1)S(1)}, bf16[48,3584]{1,0:T(8,128)(2,1)S(1)}, u32[]{:S(2)}, u32[]{:S(2)}) collective-permute-start(bf16[48,3584]{1,0:T(8,128)(2,1)S(1)} %get-tuple-element.166), channel_id=1, source_target_pairs={{0,2},{1,3},{2,0},{3,1},{4,6},{5,7},{6,4},{7,5},{8,10},{9,11},{10,... | collective-permute-start | bytes 1032200 | tf_op jit(solution)/shard_map/ppermute | solution.py:25
  56.4 7.6 %collective-permute-start.11 = (bf16[32,3584]{1,0:T(8,128)(2,1)S(1)}, bf16[32,3584]{1,0:T(8,128)(2,1)S(1)}, u32[]{:S(2)}, u32[]{:S(2)}) collective-permute-start(bf16[32,3584]{1,0:T(8,128)(2,1)S(1)} %get-tuple-element.169), channel_id=1, source_target_pairs={{0,2},{1,3},{2,0},{3,1},{4,6},{5,7},{6,4},{7,5},{8,10},{9,11},{10,... | collective-permute-start | bytes 688136 | tf_op jit(solution)/shard_map/ppermute | solution.py:25
  64.8 11.0 %collective-permute-start.12 = (bf16[48,3584]{1,0:T(8,128)(2,1)S(1)}, bf16[48,3584]{1,0:T(8,128)(2,1)S(1)}, u32[]{:S(2)}, u32[]{:S(2)}) collective-permute-start(bf16[48,3584]{1,0:T(8,128)(2,1)S(1)} %get-tuple-element.188), channel_id=1, source_target_pairs={{0,2},{1,3},{2,0},{3,1},{4,6},{5,7},{6,4},{7,5},{8,10},{9,11},{10,... | collective-permute-start | bytes 1032200 | tf_op jit(solution)/shard_map/ppermute | solution.py:25
  66.7 28.0 %collective-permute-start.16 = (bf16[80,3584]{1,0:T(8,128)(2,1)S(1)}, bf16[80,3584]{1,0:T(8,128)(2,1)S(1)}, u32[]{:S(2)}, u32[]{:S(2)}) collective-permute-start(bf16[80,3584]{1,0:T(8,128)(2,1)S(1)} %total.4), channel_id=1, source_target_pairs={{0,8},{1,9},{2,10},{3,11},{4,12},{5,13},{6,14},{7,15},{8,0},{9,1},... | collective-permute-start | bytes 1720328 | tf_op jit(solution)/shard_map/ppermute | solution.py:25
  68.5 12.8 %collective-permute-start.13 = (bf16[32,3584]{1,0:T(8,128)(2,1)S(1)}, bf16[32,3584]{1,0:T(8,128)(2,1)S(1)}, u32[]{:S(2)}, u32[]{:S(2)}) collective-permute-start(bf16[32,3584]{1,0:T(8,128)(2,1)S(1)} %get-tuple-element.197), channel_id=1, source_target_pairs={{0,2},{1,3},{2,0},{3,1},{4,6},{5,7},{6,4},{7,5},{8,10},{9,11},{10,... | collective-permute-start | bytes 688136 | tf_op jit(solution)/shard_map/ppermute | solution.py:25
  72.9 37.1 %collective-permute-start.20 = (bf16[80,3584]{1,0:T(8,128)(2,1)S(1)}, bf16[80,3584]{1,0:T(8,128)(2,1)S(1)}, u32[]{:S(2)}, u32[]{:S(2)}) collective-permute-start(bf16[80,3584]{1,0:T(8,128)(2,1)S(1)} %get-tuple-element.230), channel_id=1, source_target_pairs={{0,4},{1,5},{2,6},{3,7},{4,0},{5,1},{6,2},{7,3},{8,12},{9,13},{10,... | collective-permute-start | bytes 1720328 | tf_op jit(solution)/shard_map/ppermute | solution.py:25
  79.7 15.0 %collective-permute-start.14 = (bf16[48,3584]{1,0:T(8,128)(2,1)S(1)}, bf16[48,3584]{1,0:T(8,128)(2,1)S(1)}, u32[]{:S(2)}, u32[]{:S(2)}) collective-permute-start(bf16[48,3584]{1,0:T(8,128)(2,1)S(1)} %get-tuple-element.205), channel_id=1, source_target_pairs={{0,2},{1,3},{2,0},{3,1},{4,6},{5,7},{6,4},{7,5},{8,10},{9,11},{10,... | collective-permute-start | bytes 1032200 | tf_op jit(solution)/shard_map/ppermute | solution.py:25
  85.3 9.4 %collective-permute-start.15 = (bf16[32,3584]{1,0:T(8,128)(2,1)S(1)}, bf16[32,3584]{1,0:T(8,128)(2,1)S(1)}, u32[]{:S(2)}, u32[]{:S(2)}) collective-permute-start(bf16[32,3584]{1,0:T(8,128)(2,1)S(1)} %get-tuple-element.206), channel_id=1, source_target_pairs={{0,2},{1,3},{2,0},{3,1},{4,6},{5,7},{6,4},{7,5},{8,10},{9,11},{10,... | collective-permute-start | bytes 688136 | tf_op jit(solution)/shard_map/ppermute | solution.py:25
  94.9 19.1 %collective-permute-start.19 = (bf16[80,3584]{1,0:T(8,128)(2,1)S(1)}, bf16[80,3584]{1,0:T(8,128)(2,1)S(1)}, u32[]{:S(2)}, u32[]{:S(2)}) collective-permute-start(bf16[80,3584]{1,0:T(8,128)(2,1)S(1)} %total.5), channel_id=1, source_target_pairs={{0,12},{1,13},{2,14},{3,15},{4,8},{5,9},{6,10},{7,11},{8,4},{9,5},... | collective-permute-start | bytes 1720328 | tf_op jit(solution)/shard_map/ppermute | solution.py:25
  97.5 16.6 %collective-permute-start.18 = (bf16[80,3584]{1,0:T(8,128)(2,1)S(1)}, bf16[80,3584]{1,0:T(8,128)(2,1)S(1)}, u32[]{:S(2)}, u32[]{:S(2)}) collective-permute-start(bf16[80,3584]{1,0:T(8,128)(2,1)S(1)} %get-tuple-element.222), channel_id=1, source_target_pairs={{0,2},{1,3},{2,0},{3,1},{4,6},{5,7},{6,4},{7,5},{8,10},{9,11},{10,... | collective-permute-start | bytes 1720328 | tf_op jit(solution)/shard_map/ppermute | solution.py:25
  98.3 25.2 %collective-permute-start.17 = (bf16[80,3584]{1,0:T(8,128)(2,1)S(1)}, bf16[80,3584]{1,0:T(8,128)(2,1)S(1)}, u32[]{:S(2)}, u32[]{:S(2)}) collective-permute-start(bf16[80,3584]{1,0:T(8,128)(2,1)S(1)} %get-tuple-element.220), channel_id=1, source_target_pairs={{0,4},{1,5},{2,6},{3,7},{4,0},{5,1},{6,2},{7,3},{8,12},{9,13},{10,... | collective-permute-start | bytes 1720328 | tf_op jit(solution)/shard_map/ppermute | solution.py:25
  110.0 14.3 %collective-permute-start.21 = (bf16[64,3584]{1,0:T(8,128)(2,1)S(1)}, bf16[64,3584]{1,0:T(8,128)(2,1)S(1)}, u32[]{:S(2)}, u32[]{:S(2)}) collective-permute-start(bf16[64,3584]{1,0:T(8,128)(2,1)S(1)} %get-tuple-element.237), channel_id=1, source_target_pairs={{0,2},{1,3},{2,0},{3,1},{4,6},{5,7},{6,4},{7,5},{8,10},{9,11},{10,... | collective-permute-start | bytes 1376264 | tf_op jit(solution)/shard_map/ppermute | solution.py:25
  114.0 10.3 %collective-permute-start.22 = (bf16[16,3584]{1,0:T(8,128)(2,1)S(1)}, bf16[16,3584]{1,0:T(8,128)(2,1)S(1)}, u32[]{:S(2)}, u32[]{:S(2)}) collective-permute-start(bf16[16,3584]{1,0:T(8,128)(2,1)S(1)} %get-tuple-element.239), channel_id=1, source_target_pairs={{0,2},{1,3},{2,0},{3,1},{4,6},{5,7},{6,4},{7,5},{8,10},{9,11},{10,... | collective-permute-start | bytes 344072 | tf_op jit(solution)/shard_map/ppermute | solution.py:25
  127.2 10.2 %all-to-all-start = ((f32[16,1,16]{2,1,0:T(1,128)}), f32[16,1,16]{2,1,0:T(1,128)S(1)}, u32[]{:S(2)}, u32[]{:S(2)}) async-start(f32[16,1,16]{2,1,0:T(1,128)} %bitcast.6), calls=%async_computation | async-start | bytes 16384 | tf_op jit(solution)/shard_map/all_to_all | solution.py:403
  (9 other events, 266.3 us)

commit v19 on v17

--- a/solution.py
+++ b/solution.py
@@ -324,7 +324,8 @@
             there = order.mark_one(piece)
             part, other = order.mark(*expert_block(order.late(near[k]), first, there, weights))
             if k == 2 and first:
-                far[0], far[1], other = lax.optimization_barrier((far[0], far[1], other))
+                far[1], other = lax.optimization_barrier((far[1], other))
+                far[0], other = lax.optimization_barrier((far[0], other))
             mine[k].append(part)
             theirs[k].append(swap(other, side))
 
@@ -346,8 +347,9 @@
     far[1] = [swap(piece, side) for piece in cut(near[1], pieces)]
     leave(1)
     *far[1], weights[1] = order.mark(*far[1], weights[1])
-    far[1] = swap(join(far[1]), spread)
-    near[0], weights[1] = lax.optimization_barrier((near[0], weights[1]))
+    far[1] = join(far[1])
+    near[0], far[1] = lax.optimization_barrier((near[0], far[1]))
+    far[1] = swap(far[1], spread)
     far[0] = swap(near[0], side)
     arrive(2)
     last = (capacity - 16, 16)

time: 135 us -> 136 us (level)
  waiting for transfers between devices: 58.3 us -> 67.9 us
  starting transfers between devices: 43.3 us -> 34.6 us
    ppermute x23, waiting for transfers between devices: 52.1 us -> 61.8 us  [swap(): return lax.ppermute(value, 'expert', pairs)]
    ppermute x23, starting transfers between devices: 39.9 us -> 31.1 us  [swap(): return lax.ppermute(value, 'expert', pairs)]
where the time goes in v19:
time: 136 us
  waiting for transfers between devices  67.9 us (50%)
  starting transfers between devices  34.6 us (25%)
  Pallas kernels  31.7 us (23%)
    ppermute x23, waiting for transfers between devices, swap(): return lax.ppermute(value, 'expert', pairs)  61.8 us
    ppermute x23, starting transfers between devices, swap(): return lax.ppermute(value, 'expert', pairs)  31.1 us
    pallas_call x6, Pallas kernels, expert_block(): pl.pallas_call(functools.partial(expert_kernel, first), out_shape=[jax.Sh...  23.3 us
    all_to_all x1, waiting for transfers between devices, per_device(): lax.all_to_all(local, 'expert', split_axis=0, concat_axis=0, tiled=True)  6.15 us
    pallas_call x1, Pallas kernels, pack(): pl.pallas_call(pack_kernel, out_shape=[jax.ShapeDtypeStruct(shape, BF16)...  4.53 us
    all_to_all x1, starting transfers between devices, per_device(): lax.all_to_all(local, 'expert', split_axis=0, concat_axis=0, tiled=True)  3.42 us
  transfers between devices with their start and end apart: 24, of which 10 were waited for; matrix products, arithmetic and copies ran while one was open for 0% of the time, Pallas kernels for 18%

profile of v19, /device:TPU:0, one launch (start us, length us, event | category | flops | bytes accessed | tf_op | source)
XLA Modules:
  0.0 136.1 jit_solution(4628997646272330035)
XLA Ops:
  0.6 4.5 %pack.1 = (bf16[80,3584]{1,0:T(8,128)(2,1)S(1)}, bf16[80,3584]{1,0:T(8,128)(2,1)S(1)}, bf16[80,3584]{1,0:T(8,128)(2,1)S(1)}, bf16[80,3584]{1,0:T(8,128)(2,1)S(1)}, bf16[10752,512]{1,0:T(8,128)(2,1)S(1)}) custom-call(s32[1]{0:T(128)} %bitcast.own_ref, bf16[128,3584]{1,0:T(8,128)(2,1)} %tokens_ref.1, f32[3584]{0:T(1024)} %gain_hbm.1, s32[2,128]{1,0:T(2,128)} %bitcast.8, ...), custom_call_target="tpu_custom_call" | custom-call | flops 1024 | bytes 1024 | tf_op jit(solution)/shard_map/pack/pallas_call | solution.py:78
  5.7 3.7 %collective-permute-start.1 = (bf16[80,3584]{1,0:T(8,128)(2,1)S(1)}, bf16[80,3584]{1,0:T(8,128)(2,1)S(1)}, u32[]{:S(2)}, u32[]{:S(2)}) collective-permute-start(bf16[80,3584]{1,0:T(8,128)(2,1)S(1)} %get-tuple-element.125), channel_id=1, source_target_pairs={{0,8},{1,9},{2,10},{3,11},{4,12},{5,13},{6,14},{7,15},{8,0},{9,1},... | collective-permute-start | bytes 1720328 | tf_op jit(solution)/shard_map/ppermute | solution.py:25
  13.1 11.4 %collective-permute-done.3.refs_1_ = bf16[32,3584]{1,0:T(8,128)(2,1)S(1)} collective-permute-done((bf16[32,3584]{1,0:T(8,128)(2,1)S(1)}, bf16[32,3584]{1,0:T(8,128)(2,1)S(1)}, u32[]{:S(2)}, u32[]{:S(2)}) %collective-permute-start.3) | collective-permute-done | bytes 229408 | tf_op jit(solution)/shard_map/ppermute | solution.py:25
  27.7 7.6 %collective-permute-done.1.whole_ref.near_ref = bf16[80,3584]{1,0:T(8,128)(2,1)S(1)} collective-permute-done((bf16[80,3584]{1,0:T(8,128)(2,1)S(1)}, bf16[80,3584]{1,0:T(8,128)(2,1)S(1)}, u32[]{:S(2)}, u32[]{:S(2)}) %collective-permute-start.1) | collective-permute-done | bytes 573472 | tf_op jit(solution)/shard_map/ppermute | solution.py:25
  37.0 3.5 %collective-permute-start.7 = (bf16[80,3584]{1,0:T(8,128)(2,1)S(1)}, bf16[80,3584]{1,0:T(8,128)(2,1)S(1)}, u32[]{:S(2)}, u32[]{:S(2)}) collective-permute-start(bf16[80,3584]{1,0:T(8,128)(2,1)S(1)} %get-tuple-element.156), channel_id=1, source_target_pairs={{0,12},{1,13},{2,14},{3,15},{4,8},{5,9},{6,10},{7,11},{8,4},{9,5},... | collective-permute-start | bytes 1720328 | tf_op jit(solution)/shard_map/ppermute | solution.py:25
  41.0 8.5 %collective-permute-done.5.far_ref = bf16[48,3584]{1,0:T(8,128)(2,1)S(1)} collective-permute-done((bf16[48,3584]{1,0:T(8,128)(2,1)S(1)}, bf16[48,3584]{1,0:T(8,128)(2,1)S(1)}, u32[]{:S(2)}, u32[]{:S(2)}) %collective-permute-start.5) | collective-permute-done | bytes 344096 | tf_op jit(solution)/shard_map/ppermute | solution.py:25
  49.5 3.7 %expert_block.6 = (bf16[48,3584]{1,0:T(8,128)(2,1)S(1)}, bf16[48,3584]{1,0:T(8,128)(2,1)S(1)}) custom-call(bf16[80,3584]{1,0:T(8,128)(2,1)S(1)} %collective-permute-done.1.whole_ref.near_ref, bf16[48,3584]{1,0:T(8,128)(2,1)S(1)} %collective-permute-done.5.far_ref, bf16[10752,512]{1,0:T(8,128)(2,1)S(1)} %get-tuple-element.128.refs_0_, ...), custom_call_target="tpu_custom_call" | custom-call | flops 1024 | bytes 1024 | tf_op jit(solution)/shard_map/expert_block/pallas_call | solution.py:119
  54.8 4.0 %expert_block.7 = (bf16[32,3584]{1,0:T(8,128)(2,1)S(1)}, bf16[32,3584]{1,0:T(8,128)(2,1)S(1)}) custom-call(bf16[80,3584]{1,0:T(8,128)(2,1)S(1)} %collective-permute-done.1.whole_ref.near_ref, bf16[32,3584]{1,0:T(8,128)(2,1)S(1)} %collective-permute-done.6.far_ref, bf16[10752,512]{1,0:T(8,128)(2,1)S(1)} %get-tuple-element.128.refs_0_, ...), custom_call_target="tpu_custom_call" | custom-call | flops 1024 | bytes 1024 | tf_op jit(solution)/shard_map/expert_block/pallas_call | solution.py:119
  58.8 2.6 %collective-permute-done.10.far_ref = bf16[80,3584]{1,0:T(8,128)(2,1)S(1)} collective-permute-done((bf16[80,3584]{1,0:T(8,128)(2,1)S(1)}, bf16[80,3584]{1,0:T(8,128)(2,1)S(1)}, u32[]{:S(2)}, u32[]{:S(2)}) %collective-permute-start.10) | collective-permute-done | bytes 573472 | tf_op jit(solution)/shard_map/ppermute | solution.py:25
  63.0 6.9 %collective-permute-done.11.refs_3_ = bf16[32,3584]{1,0:T(8,128)(2,1)S(1)} collective-permute-done((bf16[32,3584]{1,0:T(8,128)(2,1)S(1)}, bf16[32,3584]{1,0:T(8,128)(2,1)S(1)}, u32[]{:S(2)}, u32[]{:S(2)}) %collective-permute-start.11) | collective-permute-done | bytes 229408 | tf_op jit(solution)/shard_map/ppermute | solution.py:25
  70.4 2.1 %collective-permute-start.13 = (bf16[32,3584]{1,0:T(8,128)(2,1)S(1)}, bf16[32,3584]{1,0:T(8,128)(2,1)S(1)}, u32[]{:S(2)}, u32[]{:S(2)}) collective-permute-start(bf16[32,3584]{1,0:T(8,128)(2,1)S(1)} %get-tuple-element.195), channel_id=1, source_target_pairs={{0,2},{1,3},{2,0},{3,1},{4,6},{5,7},{6,4},{7,5},{8,10},{9,11},{10,... | collective-permute-start | bytes 688136 | tf_op jit(solution)/shard_map/ppermute | solution.py:25
  72.5 3.9 %expert_block.8 = (bf16[80,3584]{1,0:T(8,128)(2,1)S(1)}, bf16[80,3584]{1,0:T(8,128)(2,1)S(1)}) custom-call(bf16[80,3584]{1,0:T(8,128)(2,1)S(1)} %collective-permute-done.near_ref, bf16[80,3584]{1,0:T(8,128)(2,1)S(1)} %collective-permute-done.10.far_ref, bf16[10752,512]{1,0:T(8,128)(2,1)S(1)} %get-tuple-element.128.refs_0_, ...), custom_call_target="tpu_custom_call" | custom-call | flops 1024 | bytes 1024 | tf_op jit(solution)/shard_map/expert_block/pallas_call | solution.py:119
  76.3 2.7 %collective-permute-start.20 = (bf16[80,3584]{1,0:T(8,128)(2,1)S(1)}, bf16[80,3584]{1,0:T(8,128)(2,1)S(1)}, u32[]{:S(2)}, u32[]{:S(2)}) collective-permute-start(bf16[80,3584]{1,0:T(8,128)(2,1)S(1)} %get-tuple-element.228), channel_id=1, source_target_pairs={{0,4},{1,5},{2,6},{3,7},{4,0},{5,1},{6,2},{7,3},{8,12},{9,13},{10,... | collective-permute-start | bytes 1720328 | tf_op jit(solution)/shard_map/ppermute | solution.py:25
  79.1 3.9 %expert_block.9 = (bf16[48,3584]{1,0:T(8,128)(2,1)S(1)}, bf16[48,3584]{1,0:T(8,128)(2,1)S(1)}) custom-call(bf16[80,3584]{1,0:T(8,128)(2,1)S(1)} %collective-permute-done.7.whole_ref.near_ref, bf16[48,3584]{1,0:T(8,128)(2,1)S(1)} %collective-permute-done.12.far_ref, bf16[10752,512]{1,0:T(8,128)(2,1)S(1)} %get-tuple-element.128.refs_0_, ...), custom_call_target="tpu_custom_call" | custom-call | flops 1024 | bytes 1024 | tf_op jit(solution)/shard_map/expert_block/pallas_call | solution.py:119
  83.1 4.0 %expert_block.10 = (bf16[32,3584]{1,0:T(8,128)(2,1)S(1)}, bf16[32,3584]{1,0:T(8,128)(2,1)S(1)}) custom-call(bf16[80,3584]{1,0:T(8,128)(2,1)S(1)} %collective-permute-done.7.whole_ref.near_ref, bf16[32,3584]{1,0:T(8,128)(2,1)S(1)} %collective-permute-done.13.far_ref, bf16[10752,512]{1,0:T(8,128)(2,1)S(1)} %get-tuple-element.128.refs_0_, ...), custom_call_target="tpu_custom_call" | custom-call | flops 1024 | bytes 1024 | tf_op jit(solution)/shard_map/expert_block/pallas_call | solution.py:119
  87.1 2.1 %collective-permute-start.15 = (bf16[32,3584]{1,0:T(8,128)(2,1)S(1)}, bf16[32,3584]{1,0:T(8,128)(2,1)S(1)}, u32[]{:S(2)}, u32[]{:S(2)}) collective-permute-start(bf16[32,3584]{1,0:T(8,128)(2,1)S(1)} %get-tuple-element.204), channel_id=1, source_target_pairs={{0,2},{1,3},{2,0},{3,1},{4,6},{5,7},{6,4},{7,5},{8,10},{9,11},{10,... | collective-permute-start | bytes 688136 | tf_op jit(solution)/shard_map/ppermute | solution.py:25
  89.1 3.9 %expert_block.11 = (bf16[80,3584]{1,0:T(8,128)(2,1)S(1)}, bf16[80,3584]{1,0:T(8,128)(2,1)S(1)}) custom-call(bf16[80,3584]{1,0:T(8,128)(2,1)S(1)} %get-tuple-element.207.near_ref, bf16[80,3584]{1,0:T(8,128)(2,1)S(1)} %collective-permute-done.9.far_ref, bf16[10752,512]{1,0:T(8,128)(2,1)S(1)} %get-tuple-element.128.refs_0_, ...), custom_call_target="tpu_custom_call" | custom-call | flops 1024 | bytes 1024 | tf_op jit(solution)/shard_map/expert_block/pallas_call | solution.py:119
  93.4 2.0 %collective-permute-start.19 = (bf16[80,3584]{1,0:T(8,128)(2,1)S(1)}, bf16[80,3584]{1,0:T(8,128)(2,1)S(1)}, u32[]{:S(2)}, u32[]{:S(2)}) collective-permute-start(bf16[80,3584]{1,0:T(8,128)(2,1)S(1)} %total.5), channel_id=1, source_target_pairs={{0,12},{1,13},{2,14},{3,15},{4,8},{5,9},{6,10},{7,11},{8,4},{9,5},... | collective-permute-start | bytes 1720328 | tf_op jit(solution)/shard_map/ppermute | solution.py:25
  97.1 14.8 %collective-permute-done.20.whole_ref = bf16[80,3584]{1,0:T(8,128)(2,1)S(1)} collective-permute-done((bf16[80,3584]{1,0:T(8,128)(2,1)S(1)}, bf16[80,3584]{1,0:T(8,128)(2,1)S(1)}, u32[]{:S(2)}, u32[]{:S(2)}) %collective-permute-start.20) | collective-permute-done | bytes 573472 | tf_op jit(solution)/shard_map/ppermute | solution.py:25
  112.0 2.0 %collective-permute-start.21 = (bf16[64,3584]{1,0:T(8,128)(2,1)S(1)}, bf16[64,3584]{1,0:T(8,128)(2,1)S(1)}, u32[]{:S(2)}, u32[]{:S(2)}) collective-permute-start(bf16[64,3584]{1,0:T(8,128)(2,1)S(1)} %get-tuple-element.235), channel_id=1, source_target_pairs={{0,2},{1,3},{2,0},{3,1},{4,6},{5,7},{6,4},{7,5},{8,10},{9,11},{10,... | collective-permute-start | bytes 1376264 | tf_op jit(solution)/shard_map/ppermute | solution.py:25
  114.3 8.3 %collective-permute-done.17.refs_0_ = bf16[80,3584]{1,0:T(8,128)(2,1)S(1)} collective-permute-done((bf16[80,3584]{1,0:T(8,128)(2,1)S(1)}, bf16[80,3584]{1,0:T(8,128)(2,1)S(1)}, u32[]{:S(2)}, u32[]{:S(2)}) %collective-permute-start.17) | collective-permute-done | bytes 573472 | tf_op jit(solution)/shard_map/ppermute | solution.py:25
  123.0 2.6 %score.1 = f32[16,16]{1,0:T(8,128)} custom-call(s32[1]{0:T(128)} %bitcast.own_ref, bf16[128,3584]{1,0:T(8,128)(2,1)S(1)} %copy-done, f32[3584]{0:T(1024)S(1)} %copy-done.2, s32[2,128]{1,0:T(2,128)S(1)} %bitcast.9, f32[2,128]{1,0:T(2,128)S(1)} %bitcast.10, bf16[128,3584]{1,0:T(8,128)(2,1)S(1)} %copy-done.1, f32[1,128]{1,0:T(1,128)S(1)} %bitcast.11, ...), custom_call_target="tpu_custom_call" | custom-call | flops 1024 | bytes 1024 | tf_op jit(solution)/shard_map/score/pallas_call | solution.py:182
  125.6 3.4 %all-to-all-start = ((f32[16,1,16]{2,1,0:T(1,128)}), f32[16,1,16]{2,1,0:T(1,128)S(1)}, u32[]{:S(2)}, u32[]{:S(2)}) async-start(f32[16,1,16]{2,1,0:T(1,128)} %bitcast.6), calls=%async_computation | async-start | bytes 16384 | tf_op jit(solution)/shard_map/all_to_all | solution.py:403
  129.2 6.1 %all-to-all-done = f32[16,1,16]{2,1,0:T(1,128)S(1)} async-done(((f32[16,1,16]{2,1,0:T(1,128)}), f32[16,1,16]{2,1,0:T(1,128)S(1)}, u32[]{:S(2)}, u32[]{:S(2)}) %all-to-all-start) | async-done | bytes 1056 | tf_op jit(solution)/shard_map/all_to_all | solution.py:403
  (65 shorter events, 17.1 us)
Async XLA Ops:
  5.2 19.3 %collective-permute-start.4 = (bf16[10752,512]{1,0:T(8,128)(2,1)S(1)}, bf16[10752,512]{1,0:T(8,128)(2,1)S(1)}, u32[]{:S(2)}, u32[]{:S(2)}) collective-permute-start(bf16[10752,512]{1,0:T(8,128)(2,1)S(1)} %get-tuple-element.128.refs_0_), channel_id=1, source_target_pairs={{0,1},{1,0},{2,3},{3,2},{4,5},{5,4},{6,7},{7,6},{8,9},{9,8},{10,11... | collective-permute-start | bytes 33030152 | tf_op jit(solution)/shard_map/ppermute | solution.py:25
  5.7 29.6 %collective-permute-start.1 = (bf16[80,3584]{1,0:T(8,128)(2,1)S(1)}, bf16[80,3584]{1,0:T(8,128)(2,1)S(1)}, u32[]{:S(2)}, u32[]{:S(2)}) collective-permute-start(bf16[80,3584]{1,0:T(8,128)(2,1)S(1)} %get-tuple-element.125), channel_id=1, source_target_pairs={{0,8},{1,9},{2,10},{3,11},{4,12},{5,13},{6,14},{7,15},{8,0},{9,1},... | collective-permute-start | bytes 1720328 | tf_op jit(solution)/shard_map/ppermute | solution.py:25
  9.4 15.1 %collective-permute-start.2 = (bf16[48,3584]{1,0:T(8,128)(2,1)S(1)}, bf16[48,3584]{1,0:T(8,128)(2,1)S(1)}, u32[]{:S(2)}, u32[]{:S(2)}) collective-permute-start(bf16[48,3584]{1,0:T(8,128)(2,1)S(1)} %get-tuple-element.126), channel_id=1, source_target_pairs={{0,2},{1,3},{2,0},{3,1},{4,6},{5,7},{6,4},{7,5},{8,10},{9,11},{10,... | collective-permute-start | bytes 1032200 | tf_op jit(solution)/shard_map/ppermute | solution.py:25
  11.0 29.5 %collective-permute-start = (bf16[80,3584]{1,0:T(8,128)(2,1)S(1)}, bf16[80,3584]{1,0:T(8,128)(2,1)S(1)}, u32[]{:S(2)}, u32[]{:S(2)}) collective-permute-start(bf16[80,3584]{1,0:T(8,128)(2,1)S(1)} %get-tuple-element.123.whole_ref), channel_id=1, source_target_pairs={{0,4},{1,5},{2,6},{3,7},{4,0},{5,1},{6,2},{7,3},{8,12},{9,13},{10,... | collective-permute-start | bytes 1720328 | tf_op jit(solution)/shard_map/ppermute | solution.py:25
  12.6 12.0 %collective-permute-start.3 = (bf16[32,3584]{1,0:T(8,128)(2,1)S(1)}, bf16[32,3584]{1,0:T(8,128)(2,1)S(1)}, u32[]{:S(2)}, u32[]{:S(2)}) collective-permute-start(bf16[32,3584]{1,0:T(8,128)(2,1)S(1)} %get-tuple-element.127), channel_id=1, source_target_pairs={{0,2},{1,3},{2,0},{3,1},{4,6},{5,7},{6,4},{7,5},{8,10},{9,11},{10,... | collective-permute-start | bytes 688136 | tf_op jit(solution)/shard_map/ppermute | solution.py:25
  24.6 36.9 %collective-permute-start.10 = (bf16[80,3584]{1,0:T(8,128)(2,1)S(1)}, bf16[80,3584]{1,0:T(8,128)(2,1)S(1)}, u32[]{:S(2)}, u32[]{:S(2)}) collective-permute-start(bf16[80,3584]{1,0:T(8,128)(2,1)S(1)} %join.1), channel_id=1, source_target_pairs={{0,4},{1,5},{2,6},{3,7},{4,0},{5,1},{6,2},{7,3},{8,12},{9,13},{10,... | collective-permute-start | bytes 1720328 | tf_op jit(solution)/shard_map/ppermute | solution.py:25
  26.2 35.2 %collective-permute-start.9 = (bf16[80,3584]{1,0:T(8,128)(2,1)S(1)}, bf16[80,3584]{1,0:T(8,128)(2,1)S(1)}, u32[]{:S(2)}, u32[]{:S(2)}) collective-permute-start(bf16[80,3584]{1,0:T(8,128)(2,1)S(1)} %get-tuple-element.207.near_ref), channel_id=1, source_target_pairs={{0,2},{1,3},{2,0},{3,1},{4,6},{5,7},{6,4},{7,5},{8,10},{9,11},{10,... | collective-permute-start | bytes 1720328 | tf_op jit(solution)/shard_map/ppermute | solution.py:25
  35.4 14.1 %collective-permute-start.5 = (bf16[48,3584]{1,0:T(8,128)(2,1)S(1)}, bf16[48,3584]{1,0:T(8,128)(2,1)S(1)}, u32[]{:S(2)}, u32[]{:S(2)}) collective-permute-start(bf16[48,3584]{1,0:T(8,128)(2,1)S(1)} %get-tuple-element.137), channel_id=1, source_target_pairs={{0,2},{1,3},{2,0},{3,1},{4,6},{5,7},{6,4},{7,5},{8,10},{9,11},{10,... | collective-permute-start | bytes 1032200 | tf_op jit(solution)/shard_map/ppermute | solution.py:25
  37.0 24.4 %collective-permute-start.7 = (bf16[80,3584]{1,0:T(8,128)(2,1)S(1)}, bf16[80,3584]{1,0:T(8,128)(2,1)S(1)}, u32[]{:S(2)}, u32[]{:S(2)}) collective-permute-start(bf16[80,3584]{1,0:T(8,128)(2,1)S(1)} %get-tuple-element.156), channel_id=1, source_target_pairs={{0,12},{1,13},{2,14},{3,15},{4,8},{5,9},{6,10},{7,11},{8,4},{9,5},... | collective-permute-start | bytes 1720328 | tf_op jit(solution)/shard_map/ppermute | solution.py:25
  40.5 14.3 %collective-permute-start.6 = (bf16[32,3584]{1,0:T(8,128)(2,1)S(1)}, bf16[32,3584]{1,0:T(8,128)(2,1)S(1)}, u32[]{:S(2)}, u32[]{:S(2)}) collective-permute-start(bf16[32,3584]{1,0:T(8,128)(2,1)S(1)} %get-tuple-element.147), channel_id=1, source_target_pairs={{0,2},{1,3},{2,0},{3,1},{4,6},{5,7},{6,4},{7,5},{8,10},{9,11},{10,... | collective-permute-start | bytes 688136 | tf_op jit(solution)/shard_map/ppermute | solution.py:25
  53.2 9.8 %collective-permute-start.8 = (bf16[48,3584]{1,0:T(8,128)(2,1)S(1)}, bf16[48,3584]{1,0:T(8,128)(2,1)S(1)}, u32[]{:S(2)}, u32[]{:S(2)}) collective-permute-start(bf16[48,3584]{1,0:T(8,128)(2,1)S(1)} %get-tuple-element.159), channel_id=1, source_target_pairs={{0,2},{1,3},{2,0},{3,1},{4,6},{5,7},{6,4},{7,5},{8,10},{9,11},{10,... | collective-permute-start | bytes 1032200 | tf_op jit(solution)/shard_map/ppermute | solution.py:25
  61.4 8.5 %collective-permute-start.11 = (bf16[32,3584]{1,0:T(8,128)(2,1)S(1)}, bf16[32,3584]{1,0:T(8,128)(2,1)S(1)}, u32[]{:S(2)}, u32[]{:S(2)}) collective-permute-start(bf16[32,3584]{1,0:T(8,128)(2,1)S(1)} %get-tuple-element.167), channel_id=1, source_target_pairs={{0,2},{1,3},{2,0},{3,1},{4,6},{5,7},{6,4},{7,5},{8,10},{9,11},{10,... | collective-permute-start | bytes 688136 | tf_op jit(solution)/shard_map/ppermute | solution.py:25
  70.0 9.1 %collective-permute-start.12 = (bf16[48,3584]{1,0:T(8,128)(2,1)S(1)}, bf16[48,3584]{1,0:T(8,128)(2,1)S(1)}, u32[]{:S(2)}, u32[]{:S(2)}) collective-permute-start(bf16[48,3584]{1,0:T(8,128)(2,1)S(1)} %get-tuple-element.186), channel_id=1, source_target_pairs={{0,2},{1,3},{2,0},{3,1},{4,6},{5,7},{6,4},{7,5},{8,10},{9,11},{10,... | collective-permute-start | bytes 1032200 | tf_op jit(solution)/shard_map/ppermute | solution.py:25
  70.3 22.8 %collective-permute-start.16 = (bf16[80,3584]{1,0:T(8,128)(2,1)S(1)}, bf16[80,3584]{1,0:T(8,128)(2,1)S(1)}, u32[]{:S(2)}, u32[]{:S(2)}) collective-permute-start(bf16[80,3584]{1,0:T(8,128)(2,1)S(1)} %total.4), channel_id=1, source_target_pairs={{0,8},{1,9},{2,10},{3,11},{4,12},{5,13},{6,14},{7,15},{8,0},{9,1},... | collective-permute-start | bytes 1720328 | tf_op jit(solution)/shard_map/ppermute | solution.py:25
  70.4 12.7 %collective-permute-start.13 = (bf16[32,3584]{1,0:T(8,128)(2,1)S(1)}, bf16[32,3584]{1,0:T(8,128)(2,1)S(1)}, u32[]{:S(2)}, u32[]{:S(2)}) collective-permute-start(bf16[32,3584]{1,0:T(8,128)(2,1)S(1)} %get-tuple-element.195), channel_id=1, source_target_pairs={{0,2},{1,3},{2,0},{3,1},{4,6},{5,7},{6,4},{7,5},{8,10},{9,11},{10,... | collective-permute-start | bytes 688136 | tf_op jit(solution)/shard_map/ppermute | solution.py:25
  76.3 35.6 %collective-permute-start.20 = (bf16[80,3584]{1,0:T(8,128)(2,1)S(1)}, bf16[80,3584]{1,0:T(8,128)(2,1)S(1)}, u32[]{:S(2)}, u32[]{:S(2)}) collective-permute-start(bf16[80,3584]{1,0:T(8,128)(2,1)S(1)} %get-tuple-element.228), channel_id=1, source_target_pairs={{0,4},{1,5},{2,6},{3,7},{4,0},{5,1},{6,2},{7,3},{8,12},{9,13},{10,... | collective-permute-start | bytes 1720328 | tf_op jit(solution)/shard_map/ppermute | solution.py:25
  83.0 10.2 %collective-permute-start.14 = (bf16[48,3584]{1,0:T(8,128)(2,1)S(1)}, bf16[48,3584]{1,0:T(8,128)(2,1)S(1)}, u32[]{:S(2)}, u32[]{:S(2)}) collective-permute-start(bf16[48,3584]{1,0:T(8,128)(2,1)S(1)} %get-tuple-element.203), channel_id=1, source_target_pairs={{0,2},{1,3},{2,0},{3,1},{4,6},{5,7},{6,4},{7,5},{8,10},{9,11},{10,... | collective-permute-start | bytes 1032200 | tf_op jit(solution)/shard_map/ppermute | solution.py:25
  87.1 6.1 %collective-permute-start.15 = (bf16[32,3584]{1,0:T(8,128)(2,1)S(1)}, bf16[32,3584]{1,0:T(8,128)(2,1)S(1)}, u32[]{:S(2)}, u32[]{:S(2)}) collective-permute-start(bf16[32,3584]{1,0:T(8,128)(2,1)S(1)} %get-tuple-element.204), channel_id=1, source_target_pairs={{0,2},{1,3},{2,0},{3,1},{4,6},{5,7},{6,4},{7,5},{8,10},{9,11},{10,... | collective-permute-start | bytes 688136 | tf_op jit(solution)/shard_map/ppermute | solution.py:25
  93.4 20.6 %collective-permute-start.19 = (bf16[80,3584]{1,0:T(8,128)(2,1)S(1)}, bf16[80,3584]{1,0:T(8,128)(2,1)S(1)}, u32[]{:S(2)}, u32[]{:S(2)}) collective-permute-start(bf16[80,3584]{1,0:T(8,128)(2,1)S(1)} %total.5), channel_id=1, source_target_pairs={{0,12},{1,13},{2,14},{3,15},{4,8},{5,9},{6,10},{7,11},{8,4},{9,5},... | collective-permute-start | bytes 1720328 | tf_op jit(solution)/shard_map/ppermute | solution.py:25
  95.4 18.7 %collective-permute-start.18 = (bf16[80,3584]{1,0:T(8,128)(2,1)S(1)}, bf16[80,3584]{1,0:T(8,128)(2,1)S(1)}, u32[]{:S(2)}, u32[]{:S(2)}) collective-permute-start(bf16[80,3584]{1,0:T(8,128)(2,1)S(1)} %get-tuple-element.220), channel_id=1, source_target_pairs={{0,2},{1,3},{2,0},{3,1},{4,6},{5,7},{6,4},{7,5},{8,10},{9,11},{10,... | collective-permute-start | bytes 1720328 | tf_op jit(solution)/shard_map/ppermute | solution.py:25
  97.1 25.5 %collective-permute-start.17 = (bf16[80,3584]{1,0:T(8,128)(2,1)S(1)}, bf16[80,3584]{1,0:T(8,128)(2,1)S(1)}, u32[]{:S(2)}, u32[]{:S(2)}) collective-permute-start(bf16[80,3584]{1,0:T(8,128)(2,1)S(1)} %get-tuple-element.218), channel_id=1, source_target_pairs={{0,4},{1,5},{2,6},{3,7},{4,0},{5,1},{6,2},{7,3},{8,12},{9,13},{10,... | collective-permute-start | bytes 1720328 | tf_op jit(solution)/shard_map/ppermute | solution.py:25
  112.0 10.7 %collective-permute-start.21 = (bf16[64,3584]{1,0:T(8,128)(2,1)S(1)}, bf16[64,3584]{1,0:T(8,128)(2,1)S(1)}, u32[]{:S(2)}, u32[]{:S(2)}) collective-permute-start(bf16[64,3584]{1,0:T(8,128)(2,1)S(1)} %get-tuple-element.235), channel_id=1, source_target_pairs={{0,2},{1,3},{2,0},{3,1},{4,6},{5,7},{6,4},{7,5},{8,10},{9,11},{10,... | collective-permute-start | bytes 1376264 | tf_op jit(solution)/shard_map/ppermute | solution.py:25
  113.9 8.7 %collective-permute-start.22 = (bf16[16,3584]{1,0:T(8,128)(2,1)S(1)}, bf16[16,3584]{1,0:T(8,128)(2,1)S(1)}, u32[]{:S(2)}, u32[]{:S(2)}) collective-permute-start(bf16[16,3584]{1,0:T(8,128)(2,1)S(1)} %get-tuple-element.237), channel_id=1, source_target_pairs={{0,2},{1,3},{2,0},{3,1},{4,6},{5,7},{6,4},{7,5},{8,10},{9,11},{10,... | collective-permute-start | bytes 344072 | tf_op jit(solution)/shard_map/ppermute | solution.py:25
  125.6 9.8 %all-to-all-start = ((f32[16,1,16]{2,1,0:T(1,128)}), f32[16,1,16]{2,1,0:T(1,128)S(1)}, u32[]{:S(2)}, u32[]{:S(2)}) async-start(f32[16,1,16]{2,1,0:T(1,128)} %bitcast.6), calls=%async_computation | async-start | bytes 16384 | tf_op jit(solution)/shard_map/all_to_all | solution.py:403
  (9 other events, 227.4 us)

commit v20 on v17

--- a/solution.py
+++ b/solution.py
@@ -350,7 +350,7 @@
     near[0], weights[1] = lax.optimization_barrier((near[0], weights[1]))
     far[0] = swap(near[0], side)
     arrive(2)
-    last = (capacity - 16, 16)
+    last = pieces[-1]
     for k in range(3, experts + 1):
         if k > 3:
             near[k - 1], *theirs[k - 2] = lax.optimization_barrier((near[k - 1], *theirs[k - 2]))

time: 135 us -> 141 us (1.044)
  waiting for transfers between devices: 58.3 us -> 71.9 us
  starting transfers between devices: 43.3 us -> 35.7 us
    ppermute x23, waiting for transfers between devices: 52.1 us -> 65.7 us  [swap(): return lax.ppermute(value, 'expert', pairs)]
    ppermute x23, starting transfers between devices: 39.9 us -> 30.2 us  [swap(): return lax.ppermute(value, 'expert', pairs)]
    all_to_all x1, starting transfers between devices: 3.42 us -> 5.47 us  [per_device(): lax.all_to_all(local, 'expert', split_axis=0, concat_axis=0, tiled=True)]
  transfers between devices with their start and end apart: 24 -> 24, of which waited for: 10 -> 11; matrix products, arithmetic and copies ran while one was open for 0% -> 0% of each run, Pallas kernels for 18% -> 17%
where the time goes in v20:
time: 141 us
  waiting for transfers between devices  71.9 us (51%)
  starting transfers between devices  35.7 us (25%)
  Pallas kernels  31.7 us (22%)
    ppermute x23, waiting for transfers between devices, swap(): return lax.ppermute(value, 'expert', pairs)  65.7 us
    ppermute x23, starting transfers between devices, swap(): return lax.ppermute(value, 'expert', pairs)  30.2 us
    pallas_call x6, Pallas kernels, expert_block(): pl.pallas_call(functools.partial(expert_kernel, first), out_shape=[jax.Sh...  23.3 us
    all_to_all x1, waiting for transfers between devices, per_device(): lax.all_to_all(local, 'expert', split_axis=0, concat_axis=0, tiled=True)  6.19 us
    all_to_all x1, starting transfers between devices, per_device(): lax.all_to_all(local, 'expert', split_axis=0, concat_axis=0, tiled=True)  5.47 us
    pallas_call x1, Pallas kernels, pack(): pl.pallas_call(pack_kernel, out_shape=[jax.ShapeDtypeStruct(shape, BF16)...  4.53 us
  transfers between devices with their start and end apart: 24, of which 11 were waited for; matrix products, arithmetic and copies ran while one was open for 0% of the time, Pallas kernels for 17%

profile of v20, /device:TPU:0, one launch (start us, length us, event | category | flops | bytes accessed | tf_op | source)
XLA Modules:
  0.0 141.2 jit_solution(4515532350259815052)
XLA Ops:
  0.6 4.5 %pack.1 = (bf16[80,3584]{1,0:T(8,128)(2,1)S(1)}, bf16[80,3584]{1,0:T(8,128)(2,1)S(1)}, bf16[80,3584]{1,0:T(8,128)(2,1)S(1)}, bf16[80,3584]{1,0:T(8,128)(2,1)S(1)}, bf16[10752,512]{1,0:T(8,128)(2,1)S(1)}) custom-call(s32[1]{0:T(128)} %bitcast.own_ref, bf16[128,3584]{1,0:T(8,128)(2,1)} %tokens_ref.1, f32[3584]{0:T(1024)} %gain_hbm.1, s32[2,128]{1,0:T(2,128)} %bitcast.8, ...), custom_call_target="tpu_custom_call" | custom-call | flops 1024 | bytes 1024 | tf_op jit(solution)/shard_map/pack/pallas_call | solution.py:78
  5.7 3.7 %collective-permute-start.1 = (bf16[80,3584]{1,0:T(8,128)(2,1)S(1)}, bf16[80,3584]{1,0:T(8,128)(2,1)S(1)}, u32[]{:S(2)}, u32[]{:S(2)}) collective-permute-start(bf16[80,3584]{1,0:T(8,128)(2,1)S(1)} %get-tuple-element.124), channel_id=1, source_target_pairs={{0,8},{1,9},{2,10},{3,11},{4,12},{5,13},{6,14},{7,15},{8,0},{9,1},... | collective-permute-start | bytes 1720328 | tf_op jit(solution)/shard_map/ppermute | solution.py:25
  13.1 11.4 %collective-permute-done.3.refs_1_ = bf16[32,3584]{1,0:T(8,128)(2,1)S(1)} collective-permute-done((bf16[32,3584]{1,0:T(8,128)(2,1)S(1)}, bf16[32,3584]{1,0:T(8,128)(2,1)S(1)}, u32[]{:S(2)}, u32[]{:S(2)}) %collective-permute-start.3) | collective-permute-done | bytes 229408 | tf_op jit(solution)/shard_map/ppermute | solution.py:25
  27.7 7.6 %collective-permute-done.1.whole_ref.near_ref = bf16[80,3584]{1,0:T(8,128)(2,1)S(1)} collective-permute-done((bf16[80,3584]{1,0:T(8,128)(2,1)S(1)}, bf16[80,3584]{1,0:T(8,128)(2,1)S(1)}, u32[]{:S(2)}, u32[]{:S(2)}) %collective-permute-start.1) | collective-permute-done | bytes 573472 | tf_op jit(solution)/shard_map/ppermute | solution.py:25
  37.0 3.5 %collective-permute-start.7 = (bf16[80,3584]{1,0:T(8,128)(2,1)S(1)}, bf16[80,3584]{1,0:T(8,128)(2,1)S(1)}, u32[]{:S(2)}, u32[]{:S(2)}) collective-permute-start(bf16[80,3584]{1,0:T(8,128)(2,1)S(1)} %get-tuple-element.157), channel_id=1, source_target_pairs={{0,12},{1,13},{2,14},{3,15},{4,8},{5,9},{6,10},{7,11},{8,4},{9,5},... | collective-permute-start | bytes 1720328 | tf_op jit(solution)/shard_map/ppermute | solution.py:25
  41.0 6.0 %collective-permute-done.5.far_ref = bf16[48,3584]{1,0:T(8,128)(2,1)S(1)} collective-permute-done((bf16[48,3584]{1,0:T(8,128)(2,1)S(1)}, bf16[48,3584]{1,0:T(8,128)(2,1)S(1)}, u32[]{:S(2)}, u32[]{:S(2)}) %collective-permute-start.5) | collective-permute-done | bytes 344096 | tf_op jit(solution)/shard_map/ppermute | solution.py:25
  47.0 3.7 %expert_block.6 = (bf16[48,3584]{1,0:T(8,128)(2,1)S(1)}, bf16[48,3584]{1,0:T(8,128)(2,1)S(1)}) custom-call(bf16[80,3584]{1,0:T(8,128)(2,1)S(1)} %collective-permute-done.1.whole_ref.near_ref, bf16[48,3584]{1,0:T(8,128)(2,1)S(1)} %collective-permute-done.5.far_ref, bf16[10752,512]{1,0:T(8,128)(2,1)S(1)} %get-tuple-element.127.refs_0_, ...), custom_call_target="tpu_custom_call" | custom-call | flops 1024 | bytes 1024 | tf_op jit(solution)/shard_map/expert_block/pallas_call | solution.py:119
  50.7 1.7 %collective-permute-start.8 = (bf16[48,3584]{1,0:T(8,128)(2,1)S(1)}, bf16[48,3584]{1,0:T(8,128)(2,1)S(1)}, u32[]{:S(2)}, u32[]{:S(2)}) collective-permute-start(bf16[48,3584]{1,0:T(8,128)(2,1)S(1)} %get-tuple-element.160), channel_id=1, source_target_pairs={{0,2},{1,3},{2,0},{3,1},{4,6},{5,7},{6,4},{7,5},{8,10},{9,11},{10,... | collective-permute-start | bytes 1032200 | tf_op jit(solution)/shard_map/ppermute | solution.py:25
  52.4 4.0 %expert_block.7 = (bf16[32,3584]{1,0:T(8,128)(2,1)S(1)}, bf16[32,3584]{1,0:T(8,128)(2,1)S(1)}) custom-call(bf16[80,3584]{1,0:T(8,128)(2,1)S(1)} %collective-permute-done.1.whole_ref.near_ref, bf16[32,3584]{1,0:T(8,128)(2,1)S(1)} %collective-permute-done.6.far_ref, bf16[10752,512]{1,0:T(8,128)(2,1)S(1)} %get-tuple-element.127.refs_0_, ...), custom_call_target="tpu_custom_call" | custom-call | flops 1024 | bytes 1024 | tf_op jit(solution)/shard_map/expert_block/pallas_call | solution.py:119
  56.4 5.0 %collective-permute-done.10.far_ref = bf16[80,3584]{1,0:T(8,128)(2,1)S(1)} collective-permute-done((bf16[80,3584]{1,0:T(8,128)(2,1)S(1)}, bf16[80,3584]{1,0:T(8,128)(2,1)S(1)}, u32[]{:S(2)}, u32[]{:S(2)}) %collective-permute-start.10) | collective-permute-done | bytes 573472 | tf_op jit(solution)/shard_map/ppermute | solution.py:25
  61.5 8.4 %collective-permute-done.11.refs_3_ = bf16[32,3584]{1,0:T(8,128)(2,1)S(1)} collective-permute-done((bf16[32,3584]{1,0:T(8,128)(2,1)S(1)}, bf16[32,3584]{1,0:T(8,128)(2,1)S(1)}, u32[]{:S(2)}, u32[]{:S(2)}) %collective-permute-start.11) | collective-permute-done | bytes 229408 | tf_op jit(solution)/shard_map/ppermute | solution.py:25
  70.4 2.1 %collective-permute-start.13 = (bf16[32,3584]{1,0:T(8,128)(2,1)S(1)}, bf16[32,3584]{1,0:T(8,128)(2,1)S(1)}, u32[]{:S(2)}, u32[]{:S(2)}) collective-permute-start(bf16[32,3584]{1,0:T(8,128)(2,1)S(1)} %get-tuple-element.193), channel_id=1, source_target_pairs={{0,2},{1,3},{2,0},{3,1},{4,6},{5,7},{6,4},{7,5},{8,10},{9,11},{10,... | collective-permute-start | bytes 688136 | tf_op jit(solution)/shard_map/ppermute | solution.py:25
  72.4 3.9 %expert_block.8 = (bf16[80,3584]{1,0:T(8,128)(2,1)S(1)}, bf16[80,3584]{1,0:T(8,128)(2,1)S(1)}) custom-call(bf16[80,3584]{1,0:T(8,128)(2,1)S(1)} %collective-permute-done.near_ref, bf16[80,3584]{1,0:T(8,128)(2,1)S(1)} %collective-permute-done.10.far_ref, bf16[10752,512]{1,0:T(8,128)(2,1)S(1)} %get-tuple-element.127.refs_0_, ...), custom_call_target="tpu_custom_call" | custom-call | flops 1024 | bytes 1024 | tf_op jit(solution)/shard_map/expert_block/pallas_call | solution.py:119
  77.6 3.9 %expert_block.9 = (bf16[48,3584]{1,0:T(8,128)(2,1)S(1)}, bf16[48,3584]{1,0:T(8,128)(2,1)S(1)}) custom-call(bf16[80,3584]{1,0:T(8,128)(2,1)S(1)} %collective-permute-done.7.whole_ref.near_ref, bf16[48,3584]{1,0:T(8,128)(2,1)S(1)} %collective-permute-done.12.far_ref, bf16[10752,512]{1,0:T(8,128)(2,1)S(1)} %get-tuple-element.127.refs_0_, ...), custom_call_target="tpu_custom_call" | custom-call | flops 1024 | bytes 1024 | tf_op jit(solution)/shard_map/expert_block/pallas_call | solution.py:119
  83.0 4.0 %expert_block.10 = (bf16[32,3584]{1,0:T(8,128)(2,1)S(1)}, bf16[32,3584]{1,0:T(8,128)(2,1)S(1)}) custom-call(bf16[80,3584]{1,0:T(8,128)(2,1)S(1)} %collective-permute-done.7.whole_ref.near_ref, bf16[32,3584]{1,0:T(8,128)(2,1)S(1)} %collective-permute-done.13.far_ref, bf16[10752,512]{1,0:T(8,128)(2,1)S(1)} %get-tuple-element.127.refs_0_, ...), custom_call_target="tpu_custom_call" | custom-call | flops 1024 | bytes 1024 | tf_op jit(solution)/shard_map/expert_block/pallas_call | solution.py:119
  87.0 2.0 %collective-permute-start.15 = (bf16[32,3584]{1,0:T(8,128)(2,1)S(1)}, bf16[32,3584]{1,0:T(8,128)(2,1)S(1)}, u32[]{:S(2)}, u32[]{:S(2)}) collective-permute-start(bf16[32,3584]{1,0:T(8,128)(2,1)S(1)} %get-tuple-element.202), channel_id=1, source_target_pairs={{0,2},{1,3},{2,0},{3,1},{4,6},{5,7},{6,4},{7,5},{8,10},{9,11},{10,... | collective-permute-start | bytes 688136 | tf_op jit(solution)/shard_map/ppermute | solution.py:25
  89.0 3.9 %expert_block.11 = (bf16[80,3584]{1,0:T(8,128)(2,1)S(1)}, bf16[80,3584]{1,0:T(8,128)(2,1)S(1)}) custom-call(bf16[80,3584]{1,0:T(8,128)(2,1)S(1)} %get-tuple-element.205.near_ref, bf16[80,3584]{1,0:T(8,128)(2,1)S(1)} %collective-permute-done.9.far_ref, bf16[10752,512]{1,0:T(8,128)(2,1)S(1)} %get-tuple-element.127.refs_0_, ...), custom_call_target="tpu_custom_call" | custom-call | flops 1024 | bytes 1024 | tf_op jit(solution)/shard_map/expert_block/pallas_call | solution.py:119
  93.4 1.7 %collective-permute-start.19 = (bf16[80,3584]{1,0:T(8,128)(2,1)S(1)}, bf16[80,3584]{1,0:T(8,128)(2,1)S(1)}, u32[]{:S(2)}, u32[]{:S(2)}) collective-permute-start(bf16[80,3584]{1,0:T(8,128)(2,1)S(1)} %total.5), channel_id=1, source_target_pairs={{0,12},{1,13},{2,14},{3,15},{4,8},{5,9},{6,10},{7,11},{8,4},{9,5},... | collective-permute-start | bytes 1720328 | tf_op jit(solution)/shard_map/ppermute | solution.py:25
  95.1 1.9 %collective-permute-start.18 = (bf16[80,3584]{1,0:T(8,128)(2,1)S(1)}, bf16[80,3584]{1,0:T(8,128)(2,1)S(1)}, u32[]{:S(2)}, u32[]{:S(2)}) collective-permute-start(bf16[80,3584]{1,0:T(8,128)(2,1)S(1)} %get-tuple-element.218), channel_id=1, source_target_pairs={{0,2},{1,3},{2,0},{3,1},{4,6},{5,7},{6,4},{7,5},{8,10},{9,11},{10,... | collective-permute-start | bytes 1720328 | tf_op jit(solution)/shard_map/ppermute | solution.py:25
  97.4 18.4 %collective-permute-done.20.whole_ref = bf16[80,3584]{1,0:T(8,128)(2,1)S(1)} collective-permute-done((bf16[80,3584]{1,0:T(8,128)(2,1)S(1)}, bf16[80,3584]{1,0:T(8,128)(2,1)S(1)}, u32[]{:S(2)}, u32[]{:S(2)}) %collective-permute-start.20) | collective-permute-done | bytes 573472 | tf_op jit(solution)/shard_map/ppermute | solution.py:25
  118.2 6.7 %collective-permute-done.17.refs_0_ = bf16[80,3584]{1,0:T(8,128)(2,1)S(1)} collective-permute-done((bf16[80,3584]{1,0:T(8,128)(2,1)S(1)}, bf16[80,3584]{1,0:T(8,128)(2,1)S(1)}, u32[]{:S(2)}, u32[]{:S(2)}) %collective-permute-start.17) | collective-permute-done | bytes 573472 | tf_op jit(solution)/shard_map/ppermute | solution.py:25
  126.0 2.6 %score.1 = f32[16,16]{1,0:T(8,128)} custom-call(s32[1]{0:T(128)} %bitcast.own_ref, bf16[128,3584]{1,0:T(8,128)(2,1)S(1)} %copy-done, f32[3584]{0:T(1024)S(1)} %copy-done.2, s32[2,128]{1,0:T(2,128)S(1)} %bitcast.9, f32[2,128]{1,0:T(2,128)S(1)} %bitcast.10, bf16[128,3584]{1,0:T(8,128)(2,1)S(1)} %copy-done.1, f32[1,128]{1,0:T(1,128)S(1)} %bitcast.11, ...), custom_call_target="tpu_custom_call" | custom-call | flops 1024 | bytes 1024 | tf_op jit(solution)/shard_map/score/pallas_call | solution.py:182
  128.5 5.5 %all-to-all-start = ((f32[16,1,16]{2,1,0:T(1,128)}), f32[16,1,16]{2,1,0:T(1,128)S(1)}, u32[]{:S(2)}, u32[]{:S(2)}) async-start(f32[16,1,16]{2,1,0:T(1,128)} %bitcast.6), calls=%async_computation | async-start | bytes 16384 | tf_op jit(solution)/shard_map/all_to_all | solution.py:401
  134.2 6.2 %all-to-all-done = f32[16,1,16]{2,1,0:T(1,128)S(1)} async-done(((f32[16,1,16]{2,1,0:T(1,128)}), f32[16,1,16]{2,1,0:T(1,128)S(1)}, u32[]{:S(2)}, u32[]{:S(2)}) %all-to-all-start) | async-done | bytes 1056 | tf_op jit(solution)/shard_map/all_to_all | solution.py:401
  (65 shorter events, 18.0 us)
Async XLA Ops:
  5.2 19.3 %collective-permute-start.4 = (bf16[10752,512]{1,0:T(8,128)(2,1)S(1)}, bf16[10752,512]{1,0:T(8,128)(2,1)S(1)}, u32[]{:S(2)}, u32[]{:S(2)}) collective-permute-start(bf16[10752,512]{1,0:T(8,128)(2,1)S(1)} %get-tuple-element.127.refs_0_), channel_id=1, source_target_pairs={{0,1},{1,0},{2,3},{3,2},{4,5},{5,4},{6,7},{7,6},{8,9},{9,8},{10,11... | collective-permute-start | bytes 33030152 | tf_op jit(solution)/shard_map/ppermute | solution.py:25
  5.7 29.6 %collective-permute-start.1 = (bf16[80,3584]{1,0:T(8,128)(2,1)S(1)}, bf16[80,3584]{1,0:T(8,128)(2,1)S(1)}, u32[]{:S(2)}, u32[]{:S(2)}) collective-permute-start(bf16[80,3584]{1,0:T(8,128)(2,1)S(1)} %get-tuple-element.124), channel_id=1, source_target_pairs={{0,8},{1,9},{2,10},{3,11},{4,12},{5,13},{6,14},{7,15},{8,0},{9,1},... | collective-permute-start | bytes 1720328 | tf_op jit(solution)/shard_map/ppermute | solution.py:25
  9.4 15.1 %collective-permute-start.2 = (bf16[48,3584]{1,0:T(8,128)(2,1)S(1)}, bf16[48,3584]{1,0:T(8,128)(2,1)S(1)}, u32[]{:S(2)}, u32[]{:S(2)}) collective-permute-start(bf16[48,3584]{1,0:T(8,128)(2,1)S(1)} %get-tuple-element.125), channel_id=1, source_target_pairs={{0,2},{1,3},{2,0},{3,1},{4,6},{5,7},{6,4},{7,5},{8,10},{9,11},{10,... | collective-permute-start | bytes 1032200 | tf_op jit(solution)/shard_map/ppermute | solution.py:25
  11.0 29.5 %collective-permute-start = (bf16[80,3584]{1,0:T(8,128)(2,1)S(1)}, bf16[80,3584]{1,0:T(8,128)(2,1)S(1)}, u32[]{:S(2)}, u32[]{:S(2)}) collective-permute-start(bf16[80,3584]{1,0:T(8,128)(2,1)S(1)} %get-tuple-element.122.whole_ref), channel_id=1, source_target_pairs={{0,4},{1,5},{2,6},{3,7},{4,0},{5,1},{6,2},{7,3},{8,12},{9,13},{10,... | collective-permute-start | bytes 1720328 | tf_op jit(solution)/shard_map/ppermute | solution.py:25
  12.6 12.0 %collective-permute-start.3 = (bf16[32,3584]{1,0:T(8,128)(2,1)S(1)}, bf16[32,3584]{1,0:T(8,128)(2,1)S(1)}, u32[]{:S(2)}, u32[]{:S(2)}) collective-permute-start(bf16[32,3584]{1,0:T(8,128)(2,1)S(1)} %get-tuple-element.126), channel_id=1, source_target_pairs={{0,2},{1,3},{2,0},{3,1},{4,6},{5,7},{6,4},{7,5},{8,10},{9,11},{10,... | collective-permute-start | bytes 688136 | tf_op jit(solution)/shard_map/ppermute | solution.py:25
  24.5 31.9 %collective-permute-start.9 = (bf16[80,3584]{1,0:T(8,128)(2,1)S(1)}, bf16[80,3584]{1,0:T(8,128)(2,1)S(1)}, u32[]{:S(2)}, u32[]{:S(2)}) collective-permute-start(bf16[80,3584]{1,0:T(8,128)(2,1)S(1)} %get-tuple-element.205.near_ref), channel_id=1, source_target_pairs={{0,2},{1,3},{2,0},{3,1},{4,6},{5,7},{6,4},{7,5},{8,10},{9,11},{10,... | collective-permute-start | bytes 1720328 | tf_op jit(solution)/shard_map/ppermute | solution.py:25
  26.1 35.4 %collective-permute-start.10 = (bf16[80,3584]{1,0:T(8,128)(2,1)S(1)}, bf16[80,3584]{1,0:T(8,128)(2,1)S(1)}, u32[]{:S(2)}, u32[]{:S(2)}) collective-permute-start(bf16[80,3584]{1,0:T(8,128)(2,1)S(1)} %join.1), channel_id=1, source_target_pairs={{0,4},{1,5},{2,6},{3,7},{4,0},{5,1},{6,2},{7,3},{8,12},{9,13},{10,... | collective-permute-start | bytes 1720328 | tf_op jit(solution)/shard_map/ppermute | solution.py:25
  35.4 11.6 %collective-permute-start.5 = (bf16[48,3584]{1,0:T(8,128)(2,1)S(1)}, bf16[48,3584]{1,0:T(8,128)(2,1)S(1)}, u32[]{:S(2)}, u32[]{:S(2)}) collective-permute-start(bf16[48,3584]{1,0:T(8,128)(2,1)S(1)} %get-tuple-element.136), channel_id=1, source_target_pairs={{0,2},{1,3},{2,0},{3,1},{4,6},{5,7},{6,4},{7,5},{8,10},{9,11},{10,... | collective-permute-start | bytes 1032200 | tf_op jit(solution)/shard_map/ppermute | solution.py:25
  37.0 24.4 %collective-permute-start.7 = (bf16[80,3584]{1,0:T(8,128)(2,1)S(1)}, bf16[80,3584]{1,0:T(8,128)(2,1)S(1)}, u32[]{:S(2)}, u32[]{:S(2)}) collective-permute-start(bf16[80,3584]{1,0:T(8,128)(2,1)S(1)} %get-tuple-element.157), channel_id=1, source_target_pairs={{0,12},{1,13},{2,14},{3,15},{4,8},{5,9},{6,10},{7,11},{8,4},{9,5},... | collective-permute-start | bytes 1720328 | tf_op jit(solution)/shard_map/ppermute | solution.py:25
  40.5 11.9 %collective-permute-start.6 = (bf16[32,3584]{1,0:T(8,128)(2,1)S(1)}, bf16[32,3584]{1,0:T(8,128)(2,1)S(1)}, u32[]{:S(2)}, u32[]{:S(2)}) collective-permute-start(bf16[32,3584]{1,0:T(8,128)(2,1)S(1)} %get-tuple-element.148), channel_id=1, source_target_pairs={{0,2},{1,3},{2,0},{3,1},{4,6},{5,7},{6,4},{7,5},{8,10},{9,11},{10,... | collective-permute-start | bytes 688136 | tf_op jit(solution)/shard_map/ppermute | solution.py:25
  50.7 10.8 %collective-permute-start.8 = (bf16[48,3584]{1,0:T(8,128)(2,1)S(1)}, bf16[48,3584]{1,0:T(8,128)(2,1)S(1)}, u32[]{:S(2)}, u32[]{:S(2)}) collective-permute-start(bf16[48,3584]{1,0:T(8,128)(2,1)S(1)} %get-tuple-element.160), channel_id=1, source_target_pairs={{0,2},{1,3},{2,0},{3,1},{4,6},{5,7},{6,4},{7,5},{8,10},{9,11},{10,... | collective-permute-start | bytes 1032200 | tf_op jit(solution)/shard_map/ppermute | solution.py:25
  61.4 8.4 %collective-permute-start.11 = (bf16[32,3584]{1,0:T(8,128)(2,1)S(1)}, bf16[32,3584]{1,0:T(8,128)(2,1)S(1)}, u32[]{:S(2)}, u32[]{:S(2)}) collective-permute-start(bf16[32,3584]{1,0:T(8,128)(2,1)S(1)} %get-tuple-element.165), channel_id=1, source_target_pairs={{0,2},{1,3},{2,0},{3,1},{4,6},{5,7},{6,4},{7,5},{8,10},{9,11},{10,... | collective-permute-start | bytes 688136 | tf_op jit(solution)/shard_map/ppermute | solution.py:25
  69.9 7.7 %collective-permute-start.12 = (bf16[48,3584]{1,0:T(8,128)(2,1)S(1)}, bf16[48,3584]{1,0:T(8,128)(2,1)S(1)}, u32[]{:S(2)}, u32[]{:S(2)}) collective-permute-start(bf16[48,3584]{1,0:T(8,128)(2,1)S(1)} %get-tuple-element.184), channel_id=1, source_target_pairs={{0,2},{1,3},{2,0},{3,1},{4,6},{5,7},{6,4},{7,5},{8,10},{9,11},{10,... | collective-permute-start | bytes 1032200 | tf_op jit(solution)/shard_map/ppermute | solution.py:25
  70.3 22.7 %collective-permute-start.16 = (bf16[80,3584]{1,0:T(8,128)(2,1)S(1)}, bf16[80,3584]{1,0:T(8,128)(2,1)S(1)}, u32[]{:S(2)}, u32[]{:S(2)}) collective-permute-start(bf16[80,3584]{1,0:T(8,128)(2,1)S(1)} %total.4), channel_id=1, source_target_pairs={{0,8},{1,9},{2,10},{3,11},{4,12},{5,13},{6,14},{7,15},{8,0},{9,1},... | collective-permute-start | bytes 1720328 | tf_op jit(solution)/shard_map/ppermute | solution.py:25
  70.4 12.7 %collective-permute-start.13 = (bf16[32,3584]{1,0:T(8,128)(2,1)S(1)}, bf16[32,3584]{1,0:T(8,128)(2,1)S(1)}, u32[]{:S(2)}, u32[]{:S(2)}) collective-permute-start(bf16[32,3584]{1,0:T(8,128)(2,1)S(1)} %get-tuple-element.193), channel_id=1, source_target_pairs={{0,2},{1,3},{2,0},{3,1},{4,6},{5,7},{6,4},{7,5},{8,10},{9,11},{10,... | collective-permute-start | bytes 688136 | tf_op jit(solution)/shard_map/ppermute | solution.py:25
  81.5 11.6 %collective-permute-start.14 = (bf16[48,3584]{1,0:T(8,128)(2,1)S(1)}, bf16[48,3584]{1,0:T(8,128)(2,1)S(1)}, u32[]{:S(2)}, u32[]{:S(2)}) collective-permute-start(bf16[48,3584]{1,0:T(8,128)(2,1)S(1)} %get-tuple-element.201), channel_id=1, source_target_pairs={{0,2},{1,3},{2,0},{3,1},{4,6},{5,7},{6,4},{7,5},{8,10},{9,11},{10,... | collective-permute-start | bytes 1032200 | tf_op jit(solution)/shard_map/ppermute | solution.py:25
  81.6 34.2 %collective-permute-start.20 = (bf16[80,3584]{1,0:T(8,128)(2,1)S(1)}, bf16[80,3584]{1,0:T(8,128)(2,1)S(1)}, u32[]{:S(2)}, u32[]{:S(2)}) collective-permute-start(bf16[80,3584]{1,0:T(8,128)(2,1)S(1)} %get-tuple-element.226), channel_id=1, source_target_pairs={{0,4},{1,5},{2,6},{3,7},{4,0},{5,1},{6,2},{7,3},{8,12},{9,13},{10,... | collective-permute-start | bytes 1720328 | tf_op jit(solution)/shard_map/ppermute | solution.py:25
  87.0 6.1 %collective-permute-start.15 = (bf16[32,3584]{1,0:T(8,128)(2,1)S(1)}, bf16[32,3584]{1,0:T(8,128)(2,1)S(1)}, u32[]{:S(2)}, u32[]{:S(2)}) collective-permute-start(bf16[32,3584]{1,0:T(8,128)(2,1)S(1)} %get-tuple-element.202), channel_id=1, source_target_pairs={{0,2},{1,3},{2,0},{3,1},{4,6},{5,7},{6,4},{7,5},{8,10},{9,11},{10,... | collective-permute-start | bytes 688136 | tf_op jit(solution)/shard_map/ppermute | solution.py:25
  93.4 24.5 %collective-permute-start.19 = (bf16[80,3584]{1,0:T(8,128)(2,1)S(1)}, bf16[80,3584]{1,0:T(8,128)(2,1)S(1)}, u32[]{:S(2)}, u32[]{:S(2)}) collective-permute-start(bf16[80,3584]{1,0:T(8,128)(2,1)S(1)} %total.5), channel_id=1, source_target_pairs={{0,12},{1,13},{2,14},{3,15},{4,8},{5,9},{6,10},{7,11},{8,4},{9,5},... | collective-permute-start | bytes 1720328 | tf_op jit(solution)/shard_map/ppermute | solution.py:25
  95.1 22.9 %collective-permute-start.18 = (bf16[80,3584]{1,0:T(8,128)(2,1)S(1)}, bf16[80,3584]{1,0:T(8,128)(2,1)S(1)}, u32[]{:S(2)}, u32[]{:S(2)}) collective-permute-start(bf16[80,3584]{1,0:T(8,128)(2,1)S(1)} %get-tuple-element.218), channel_id=1, source_target_pairs={{0,2},{1,3},{2,0},{3,1},{4,6},{5,7},{6,4},{7,5},{8,10},{9,11},{10,... | collective-permute-start | bytes 1720328 | tf_op jit(solution)/shard_map/ppermute | solution.py:25
  97.0 27.9 %collective-permute-start.17 = (bf16[80,3584]{1,0:T(8,128)(2,1)S(1)}, bf16[80,3584]{1,0:T(8,128)(2,1)S(1)}, u32[]{:S(2)}, u32[]{:S(2)}) collective-permute-start(bf16[80,3584]{1,0:T(8,128)(2,1)S(1)} %get-tuple-element.216), channel_id=1, source_target_pairs={{0,4},{1,5},{2,6},{3,7},{4,0},{5,1},{6,2},{7,3},{8,12},{9,13},{10,... | collective-permute-start | bytes 1720328 | tf_op jit(solution)/shard_map/ppermute | solution.py:25
  115.8 9.8 %collective-permute-start.21 = (bf16[48,3584]{1,0:T(8,128)(2,1)S(1)}, bf16[48,3584]{1,0:T(8,128)(2,1)S(1)}, u32[]{:S(2)}, u32[]{:S(2)}) collective-permute-start(bf16[48,3584]{1,0:T(8,128)(2,1)S(1)} %get-tuple-element.233), channel_id=1, source_target_pairs={{0,2},{1,3},{2,0},{3,1},{4,6},{5,7},{6,4},{7,5},{8,10},{9,11},{10,... | collective-permute-start | bytes 1032200 | tf_op jit(solution)/shard_map/ppermute | solution.py:25
  116.7 8.9 %collective-permute-start.22 = (bf16[32,3584]{1,0:T(8,128)(2,1)S(1)}, bf16[32,3584]{1,0:T(8,128)(2,1)S(1)}, u32[]{:S(2)}, u32[]{:S(2)}) collective-permute-start(bf16[32,3584]{1,0:T(8,128)(2,1)S(1)} %get-tuple-element.235), channel_id=1, source_target_pairs={{0,2},{1,3},{2,0},{3,1},{4,6},{5,7},{6,4},{7,5},{8,10},{9,11},{10,... | collective-permute-start | bytes 688136 | tf_op jit(solution)/shard_map/ppermute | solution.py:25
  128.5 11.9 %all-to-all-start = ((f32[16,1,16]{2,1,0:T(1,128)}), f32[16,1,16]{2,1,0:T(1,128)S(1)}, u32[]{:S(2)}, u32[]{:S(2)}) async-start(f32[16,1,16]{2,1,0:T(1,128)} %bitcast.6), calls=%async_computation | async-start | bytes 16384 | tf_op jit(solution)/shard_map/all_to_all | solution.py:401
  (9 other events, 249.7 us)
